TPU v7x, 256 devices: a whole 4x4x8 slice. The times are simulated.
256 devices in a mesh: dp: 16 (over z, core), fsdp: 16 (over y, x).
Axes of the slice: x: 4, y: 4, z: 8, core: 2. Of those that a mesh axis runs over, the one named last changes fastest.
Arguments:
- tokens: bfloat16 [65536, 8192], P(('dp', 'fsdp')), may hold values from -6 to 6
- cotangent: bfloat16 [65536, 1024], P(('dp', 'fsdp')), may hold values from -6 to 6
- value_weight: bfloat16 [8192, 1024], P('fsdp'), may hold values from -0.1875 to 0.1875
- adapter_down_weight: bfloat16 [64, 8192, 64], P('dp', 'fsdp'), may hold values from -0.0625 to 0.0625
- adapter_up_weight: bfloat16 [64, 64, 1024], P('dp', None, 'fsdp'), may hold values from -0.1875 to 0.1875
- segment_tenant: int32 [16, 8], replicated, may hold values from 0 to 63, as said below
- segment_lengths: int32 [16, 8], replicated, may hold values from 1 to 2048, 4096 in all within a row
- tenant_stored_row: int32 [64], replicated, may hold values from 0 to 63, as said below
Outputs:
- input_gradient: bfloat16 [65536, 8192], P(('dp', 'fsdp'))
- adapter_down_gradient: float32 [64, 8192, 64], P('dp', 'fsdp')
- adapter_up_gradient: float32 [64, 64, 1024], P('dp', None, 'fsdp')
Inputs may be any that keep to these rules, and one draw needn't show every extreme that they name: `segment_tenant`: the 8 tenants of one bin are distinct, and the packer places them so that their stored rows tenant_stored_row[t] lie in 8 different blocks of 4 consecutive rows (no bin draws two tenants whose adapters one dp index owns). A permutation of the tenants: tenant t's adapters are row tenant_stored_row[t] of adapter_down_weight and adapter_up_weight.
All inputs are finite; a program needn't handle non-finite values.
Results may differ from a plain program's by a relative error of at most 0.018.
Values may be sent and summed in bfloat16 or wider, within the bound.
No kernel may reach another device: no remote copies, remote signals or barrier semaphores. Data moves between devices by JAX's collectives and lax.ppermute only.
A program may use at most 128 MiB of HBM per device.

v0:
```python
import jax
import jax.numpy as jnp
from jax import lax
from jax.sharding import PartitionSpec as P

ADAPTER_SCALE = 2.0


def slot_columns(lengths_row, positions, rank_space_width):
    seg_ends = jnp.cumsum(lengths_row)
    starts = seg_ends - lengths_row
    inside = (positions[:, None] >= starts[None, :]) & (positions[:, None] < seg_ends[None, :])
    return jnp.repeat(inside, rank_space_width, axis=1)


def local(
    tokens,
    cotangent,
    value_weight,
    adapter_down_weight,
    adapter_up_weight,
    segment_tenant,
    segment_lengths,
    tenant_stored_row,
):
    local_token_count, model_width_piece, rank_space_width = adapter_down_weight.shape
    value_width_piece = adapter_up_weight.shape[2]
    bin_count, slot_count = segment_tenant.shape
    rows_here = tokens.shape[0]
    groups = lax.axis_size("fsdp")
    me_bin = lax.axis_index("dp")
    me_piece = lax.axis_index("fsdp")
    gradient_norm_value = (groups * rows_here) ** (-0.5)
    zero_constant = jnp.zeros((), jnp.bfloat16)
    contract_last = (((1,), (1,)), ((), ()))
    contract_first = (((0,), (0,)), ((), ()))
    matches = (
        segment_tenant[:, :, None]
        == jnp.arange(tenant_stored_row.shape[0], dtype=jnp.int32)[None, None, :]
    )
    stored = jnp.sum(jnp.where(matches, tenant_stored_row[None, None, :], 0), axis=2)
    my_stored = lax.dynamic_index_in_dim(stored, me_bin, 0, keepdims=False)
    table_down, table_up = (
        lax.all_gather(adapter_down_weight, "dp", axis=0, tiled=True),
        lax.all_gather(adapter_up_weight, "dp", axis=0, tiled=True),
    )
    segment_down_weight = jnp.take(table_down, my_stored, axis=0)
    segment_up_weight = jnp.take(table_up, my_stored, axis=0)
    down_cols = jnp.transpose(segment_down_weight, (1, 0, 2)).reshape(
        model_width_piece, slot_count * rank_space_width
    )
    up_rows = segment_up_weight.reshape(slot_count * rank_space_width, value_width_piece)
    down_full, up_full = (
        lax.all_gather(down_cols, "fsdp", axis=0, tiled=True),
        lax.all_gather(up_rows, "fsdp", axis=1, tiled=True),
    )
    my_lengths = lax.dynamic_index_in_dim(segment_lengths, me_bin, 0, keepdims=False)
    positions = me_piece * rows_here + jnp.arange(rows_here, dtype=jnp.int32)
    broadcast_row_mask = slot_columns(my_lengths, positions, rank_space_width)
    low_rank = jnp.where(
        broadcast_row_mask,
        jnp.dot(tokens, down_full, preferred_element_type=jnp.float32).astype(jnp.bfloat16),
        zero_constant,
    )
    matrix_product = lax.dot_general(
        cotangent, up_full, contract_last, preferred_element_type=jnp.float32
    )
    rank_space_gradient = jnp.where(
        broadcast_row_mask, (ADAPTER_SCALE * matrix_product).astype(jnp.bfloat16), zero_constant
    )
    base_term = lax.dot_general(
        cotangent,
        lax.all_gather(value_weight, "fsdp", axis=0, tiled=True),
        contract_last,
        preferred_element_type=jnp.float32,
    )
    adapter_term = lax.dot_general(
        rank_space_gradient, down_full, contract_last, preferred_element_type=jnp.float32
    )
    input_gradient = (base_term + adapter_term).astype(jnp.bfloat16)
    part_down = lax.dot_general(
        tokens, rank_space_gradient, contract_first, preferred_element_type=jnp.float32
    )
    partial_up_gradient = ADAPTER_SCALE * lax.dot_general(
        low_rank, cotangent, contract_first, preferred_element_type=jnp.float32
    )
    sum_down, sum_up = (
        lax.psum_scatter(
            part_down.astype(jnp.bfloat16), "fsdp", scatter_dimension=0, tiled=True
        ).astype(jnp.float32),
        lax.psum_scatter(
            partial_up_gradient.astype(jnp.bfloat16), "fsdp", scatter_dimension=1, tiled=True
        ).astype(jnp.float32),
    )
    bin_down = jnp.transpose(
        sum_down.astype(jnp.bfloat16).reshape(model_width_piece, slot_count, rank_space_width),
        (1, 0, 2),
    )
    bin_up = sum_up.astype(jnp.bfloat16).reshape(slot_count, rank_space_width, value_width_piece)
    segment_placement = (
        my_stored[:, None] == jnp.arange(bin_count * local_token_count, dtype=jnp.int32)[None, :]
    ).astype(jnp.bfloat16)
    table_down = jnp.einsum(
        "st,sdr->tdr", segment_placement, bin_down, preferred_element_type=jnp.float32
    )
    table_up = jnp.einsum(
        "st,srv->trv", segment_placement, bin_up, preferred_element_type=jnp.float32
    )
    down_grad, up_grad = (
        lax.psum_scatter(
            table_down.astype(jnp.bfloat16), "dp", scatter_dimension=0, tiled=True
        ).astype(jnp.float32),
        lax.psum_scatter(
            table_up.astype(jnp.bfloat16), "dp", scatter_dimension=0, tiled=True
        ).astype(jnp.float32),
    )
    return (input_gradient, down_grad * gradient_norm_value, up_grad * gradient_norm_value)


def solution(mesh):
    placed = (
        P(("dp", "fsdp"), None),
        P(("dp", "fsdp"), None),
        P("fsdp", None),
        P("dp", "fsdp", None),
        P("dp", None, "fsdp"),
        P(),
        P(),
        P(),
    )
    return jax.shard_map(
        local,
        mesh=mesh,
        in_specs=placed,
        out_specs=(P(("dp", "fsdp"), None), P("dp", "fsdp", None), P("dp", None, "fsdp")),
        check_vma=False,
    )
```

profile of v0, /device:TPU:1, one launch (start us, length us, event | category | flops | bytes accessed | tf_op | source)
XLA Modules:
  0.0 626.8 jit_solution(17753394289822480714)
XLA Ops:
  8.7 1.1 select_reduce_fusion
  9.9 46.4 %all-gather.9.cloned.1.call-done = bf16[64,512,64]{1,2,0:T(8,128)(2,1)} async-done(((bf16[4,512,64]{1,2,0:T(8,128)(2,1)}), bf16[64,512,64]{1,2,0:T(8,128)(2,1)}) %all-gather.9.cloned.1.call-update) | async-done | bytes 4194320 | tf_op jit(solution)/shard_map/all_gather | solution.py:44
  56.2 2.8 gather_fusion.1
  59.0 0.9 broadcast_select_fusion
  60.1 19.3 %all_gather.16 = bf16[64,64,64]{2,1,0:T(8,128)(2,1)S(1)} all-gather(bf16[4,64,64]{2,1,0:T(8,128)(2,1)} %param.12), channel_id=1, replica_groups=mesh['dp'=16,'fsdp'=16] {'dp'}, dimensions={0}, use_global_device_ids=true | all-gather | bytes 557056 | tf_op jit(solution)/shard_map/all_gather | solution.py:45
  80.8 0.8 constant_dynamic-slice_fusion.1
  82.0 58.8 %all-gather.11.cloned.1.call-done = bf16[8192,512]{0,1:T(8,128)(2,1)} async-done(((bf16[512,512]{0,1:T(8,128)(2,1)}), bf16[8192,512]{0,1:T(8,128)(2,1)}) %all-gather.11.cloned.1.call-update) | async-done | bytes 8388624 | tf_op jit(solution)/shard_map/all_gather | solution.py:54
  140.8 8.8 %multiply_convert_fusion = bf16[512,1024]{0,1:T(8,128)(2,1)} fusion(bf16[256,1024]{1,0:T(8,128)(2,1)S(1)} %copy-done, pred[256,512]{0,1:T(32,128)(4,1)S(1)} %bitcast.57, bf16[8192,512]{0,1:T(8,128)(2,1)} %all-gather.11.cloned.1.call-done, bf16[256,8192]{1,0:T(8,128)(2,1)} %param.8), kind=kOutput, calls=%fused_computation.7 | convolution fusion | flops 2417229824 | bytes 14286848 | tf_op jit(solution)/shard_map/dot_general | solution.py:84
  149.6 40.8 %all-gather.7.cloned.1.call-done = bf16[512,1024]{0,1:T(8,128)(2,1)} async-done(((bf16[512,64]{0,1:T(8,128)(2,1)}), bf16[512,1024]{0,1:T(8,128)(2,1)}) %all-gather.7.cloned.1.call-update) | async-done | bytes 1048592 | tf_op jit(solution)/shard_map/all_gather | solution.py:55
  190.4 1.7 fusion.5
  192.1 7.8 %fusion = bf16[8192,512]{0,1:T(8,128)(2,1)} fusion(bf16[256,512]{0,1:T(8,128)(2,1)S(1)} %fusion.5, bf16[256,8192]{1,0:T(8,128)(2,1)} %param.8), kind=kOutput, calls=%fused_computation.3 | convolution fusion | flops 2151677952 | bytes 12845056 | tf_op jit(solution)/shard_map/dot_general | solution.py:81
  199.9 71.4 %reduce-scatter.9.cloned.1.call-done = bf16[512,64]{0,1:T(8,128)(2,1)} async-done(((bf16[512,1024]{0,1:T(8,128)(2,1)}), bf16[512,64]{0,1:T(8,128)(2,1)}) %reduce-scatter.9.cloned.1.call-update) | async-done | bytes 65552 | tf_op jit(solution)/shard_map/reduce_scatter | solution.py:91
  271.4 1.0 reshape.78
  273.1 1.7 copy.30
  274.8 90.5 %reduce-scatter.5.cloned.1.call-done = bf16[512,512]{0,1:T(8,128)(2,1)} async-done(((bf16[8192,512]{0,1:T(8,128)(2,1)}), bf16[512,512]{0,1:T(8,128)(2,1)}) %reduce-scatter.5.cloned.1.call-update) | async-done | bytes 524304 | tf_op jit(solution)/shard_map/reduce_scatter | solution.py:88
  365.3 2.4 convolution_convert_fusion.1
  367.7 4.4 copy.28
  372.9 9.0 %fusion.20 = f32[256,8192]{1,0:T(8,128)} fusion(bf16[256,512]{0,1:T(8,128)(2,1)S(1)} %fusion.5, bf16[8192,512]{0,1:T(8,128)(2,1)} %all-gather.11.cloned.1.call-done), kind=kOutput, calls=%fused_computation.42 | convolution fusion | flops 2147483648 | bytes 17039360 | tf_op jit(solution)/shard_map/dot_general | solution.py:77
  381.9 41.0 %reduce-scatter.11.cloned.1.call-done = bf16[4,64,64]{2,1,0:T(8,128)(2,1)} async-done(((bf16[64,64,64]{2,1,0:T(8,128)(2,1)}), bf16[4,64,64]{2,1,0:T(8,128)(2,1)}) %reduce-scatter.11.cloned.1.call-update) | async-done | bytes 32784 | tf_op jit(solution)/shard_map/reduce_scatter | solution.py:113
  422.9 1.5 convert_multiply_fusion.1
  424.4 62.8 %reduce-scatter.7.cloned.1.call-done = bf16[4,512,64]{1,2,0:T(8,128)(2,1)} async-done(((bf16[64,512,64]{1,2,0:T(8,128)(2,1)}), bf16[4,512,64]{1,2,0:T(8,128)(2,1)}) %reduce-scatter.7.cloned.1.call-update) | async-done | bytes 262160 | tf_op jit(solution)/shard_map/reduce_scatter | solution.py:110
  487.2 1.8 convert_multiply_fusion
  489.0 118.6 %all-gather.5.cloned.1.call-done = bf16[8192,1024]{1,0:T(8,128)(2,1)} async-done(((bf16[512,1024]{1,0:T(8,128)(2,1)}), bf16[8192,1024]{1,0:T(8,128)(2,1)}) %all-gather.5.cloned.1.call-update) | async-done | bytes 16777232 | tf_op jit(solution)/shard_map/all_gather | solution.py:73
  607.6 12.3 %fusion.1 = bf16[256,8192]{1,0:T(8,128)(2,1)} fusion(f32[256,8192]{1,0:T(8,128)} %fusion.20, bf16[256,1024]{1,0:T(8,128)(2,1)S(1)} %copy-done, bf16[8192,1024]{1,0:T(8,128)(2,1)} %all-gather.5.cloned.1.call-done), kind=kOutput, calls=%fused_computation.5 | convolution fusion | flops 4299161600 | bytes 29884416 | tf_op jit(solution)/shard_map/dot_general | solution.py:71
  (35 shorter events, 5.2 us)
Async XLA Ops:
  7.2 133.6 %copy-start = (bf16[256,1024]{1,0:T(8,128)(2,1)S(1)}, bf16[256,1024]{1,0:T(8,128)(2,1)}, u32[]{:S(2)}) copy-start(bf16[256,1024]{1,0:T(8,128)(2,1)} %param.9) | copy-start | bytes 1572868
  7.2 49.0 %all-gather.9.cloned.1.call-start = ((), (), s32[]{:S(2)}) async-start(), calls=%async_computation.6 | async-start | bytes 4456448 | tf_op jit(solution)/shard_map/all_gather | solution.py:44
  7.9 132.8 %all-gather.11.cloned.1.call-start = ((), (), s32[]{:S(2)}) async-start(), calls=%async_computation.7 | async-start | bytes 8912896 | tf_op jit(solution)/shard_map/all_gather | solution.py:54
  59.9 130.5 %all-gather.7.cloned.1.call-start = ((), (), s32[]{:S(2)}) async-start(), calls=%async_computation.5 | async-start | bytes 1114112 | tf_op jit(solution)/shard_map/all_gather | solution.py:55
  80.8 190.6 %reduce-scatter.9.cloned.1.call-start = ((), (), s32[]{:S(2)}) async-start(), calls=%async_computation.10 | async-start | bytes 1114112 | tf_op jit(solution)/shard_map/reduce_scatter | solution.py:91
  149.6 215.8 %reduce-scatter.5.cloned.1.call-start = ((), (), s32[]{:S(2)}) async-start(), calls=%async_computation.8 | async-start | bytes 8912896 | tf_op jit(solution)/shard_map/reduce_scatter | solution.py:88
  199.9 223.0 %reduce-scatter.11.cloned.1.call-start = ((), (), s32[]{:S(2)}) async-start(), calls=%async_computation.11 | async-start | bytes 1114112 | tf_op jit(solution)/shard_map/reduce_scatter | solution.py:113
  274.8 212.4 %reduce-scatter.7.cloned.1.call-start = ((), (), s32[]{:S(2)}) async-start(), calls=%async_computation.9 | async-start | bytes 4456448 | tf_op jit(solution)/shard_map/reduce_scatter | solution.py:110
  372.2 235.5 %all-gather.5.cloned.1.call-start = ((), (), s32[]{:S(2)}) async-start(), calls=%async_computation.4 | async-start | bytes 17825792 | tf_op jit(solution)/shard_map/all_gather | solution.py:73
Sparse Core Ops, SparseCore 0:
  9.8 46.3 all-gather.8
  60.0 80.6 all-gather.10
  143.7 46.5 all-gather.6
  194.3 77.0 reduce-scatter.8
  275.4 89.8 reduce-scatter.4
  367.9 54.9 reduce-scatter.10
  426.0 61.1 reduce-scatter.6
  489.6 117.9 all-gather.4
where the time goes:
time: 627 us
  waiting for transfers between devices  532 us (85%)
  matrix products  42.5 us (7%)
  blocking collectives  19.3 us (3%)
  between operations  14.2 us (2%)
  local copies, waits for them, and re-layouts  12.5 us (2%)
    all_gather x1, waiting for transfers between devices, local(): lax.all_gather(value_weight, 'fsdp', axis=0, tiled=True)  119 us
    reduce_scatter x1, waiting for transfers between devices, local(): lax.psum_scatter(part_down.astype(jnp.bfloat16), 'fsdp', scatter_dimensio...  90.5 us
    reduce_scatter x1, waiting for transfers between devices, local(): lax.psum_scatter(partial_up_gradient.astype(jnp.bfloat16), 'fsdp', scatte...  71.4 us
    reduce_scatter x1, waiting for transfers between devices, local(): lax.psum_scatter(table_down.astype(jnp.bfloat16), 'dp', scatter_dimension...  62.8 us
    all_gather x1, waiting for transfers between devices, local(): lax.all_gather(down_cols, 'fsdp', axis=0, tiled=True)  58.8 us
    all_gather x1, waiting for transfers between devices, local(): lax.all_gather(adapter_down_weight, 'dp', axis=0, tiled=True)  46.4 us
    reduce_scatter x1, waiting for transfers between devices, local(): lax.psum_scatter(table_up.astype(jnp.bfloat16), 'dp', scatter_dimension=0...  41 us
    all_gather x1, waiting for transfers between devices, local(): lax.all_gather(up_rows, 'fsdp', axis=1, tiled=True)  40.8 us
  transfers between devices with their start and end apart: 8, of which 8 were waited for; matrix products, arithmetic and copies ran while one was open for 7% of the time, Pallas kernels for 0%

commit v1 on v0

v1 whole, which is shorter than its diff:
```python
import functools

import jax
import jax.numpy as jnp
from jax import lax
from jax.experimental import pallas as pl
from jax.experimental.pallas import tpu as pltpu
from jax.sharding import PartitionSpec as P

ADAPTER_SCALE = 2.0
BF = jnp.bfloat16
F32 = jnp.float32
VMEM_BYTES = 40 * 1024 * 1024


def params():
    return pltpu.CompilerParams(vmem_limit_bytes=VMEM_BYTES)


def cost(flops, moved):
    return pl.CostEstimate(flops=flops, bytes_accessed=moved, transcendentals=0)


def inside_pair(meta, pair, first, shape, slots, rank):
    row = first + lax.broadcasted_iota(jnp.int32, shape, 0)
    low = lax.broadcasted_iota(jnp.int32, shape, 1) < rank
    begin = jnp.where(low, meta[2 + 2 * pair], meta[3 + 2 * pair])
    end = jnp.where(low, meta[2 + slots + 2 * pair], meta[3 + slots + 2 * pair])
    return (row >= begin) & (row < end)


def pack_kernel(tok, cot_t, out):
    rows = tok.shape[0]
    half = cot_t.shape[0] // 2
    out[0, :rows, :] = tok[...]
    out[0, rows:, :rows] = cot_t[:half, :]
    out[0, rows:, rows:] = cot_t[half:, :]


def pack(tokens, cot_t, n):
    rows, width = tokens.shape
    piece, v = width // n, cot_t.shape[0] // n
    extra = v * rows // piece
    return pl.pallas_call(
        pack_kernel,
        grid=(n,),
        in_specs=[
            pl.BlockSpec((rows, piece), lambda f: (0, f)),
            pl.BlockSpec((v, rows), lambda f: (f, 0)),
        ],
        out_specs=pl.BlockSpec((1, rows + extra, piece), lambda f: (f, 0, 0)),
        out_shape=jax.ShapeDtypeStruct((n, rows + extra, piece), BF),
        compiler_params=params(),
        cost_estimate=cost(0, 4 * rows * width),
        name="pack",
    )(tokens, cot_t)


def offer_kernel(slots, meta, down_t, up, out):
    piece, v = down_t.shape[2], up.shape[2]
    out[...] = jnp.zeros_like(out)
    for b in range(out.shape[0]):
        r = jnp.maximum(meta[2 + 3 * slots + b], 0)
        out[b, :, :piece] = down_t[r]
        out[b, :, piece:piece + v] = up[r]


def offer(meta, down_t, up, bins, slots):
    _, rank, piece = down_t.shape
    return pl.pallas_call(
        functools.partial(offer_kernel, slots),
        grid_spec=pltpu.PrefetchScalarGridSpec(
            num_scalar_prefetch=1,
            grid=(1,),
            in_specs=[
                pl.BlockSpec(down_t.shape, lambda i, m: (0, 0, 0)),
                pl.BlockSpec(up.shape, lambda i, m: (0, 0, 0)),
            ],
            out_specs=pl.BlockSpec((bins, rank, piece + 128), lambda i, m: (0, 0, 0)),
        ),
        out_shape=jax.ShapeDtypeStruct((bins, rank, piece + 128), BF),
        compiler_params=params(),
        cost_estimate=cost(0, 2 * bins * rank * piece),
        name="offer",
    )(meta, down_t, up)


def choose_kernel(slots, meta, got, down, up):
    rank, piece = got.shape[1], down.shape[1]
    for s in range(slots):
        block = got[meta[2 + 2 * slots + s]]
        down[s * rank:(s + 1) * rank, :] = block[:, :piece]
        up[s * rank:(s + 1) * rank, :] = block[:, piece:]


def choose(meta, got, slots):
    owners, rank, wide = got.shape
    piece = wide - 128
    return pl.pallas_call(
        functools.partial(choose_kernel, slots),
        grid_spec=pltpu.PrefetchScalarGridSpec(
            num_scalar_prefetch=1,
            grid=(1,),
            in_specs=[pl.BlockSpec(got.shape, lambda i, m: (0, 0, 0))],
            out_specs=[
                pl.BlockSpec((slots * rank, piece), lambda i, m: (0, 0)),
                pl.BlockSpec((slots * rank, 128), lambda i, m: (0, 0)),
            ],
        ),
        out_shape=[
            jax.ShapeDtypeStruct((slots * rank, piece), BF),
            jax.ShapeDtypeStruct((slots * rank, 128), BF),
        ],
        compiler_params=params(),
        cost_estimate=cost(0, 2 * owners * rank * wide),
        name="choose",
    )(meta, got)


def project_kernel(slots, rank, v, meta, part, down, up, out):
    rows = out.shape[1]
    first = pl.program_id(0) * rows
    tok = part[0, :rows, :]
    cot_t = jnp.concatenate([part[0, rows:, :rows], part[0, rows:, rows:]], axis=0)
    lr = lax.dot_general(tok, down[...], (((1,), (1,)), ((), ())), preferred_element_type=F32)
    lg = lax.dot_general(
        cot_t, up[:, :v], (((0,), (1,)), ((), ())), preferred_element_type=F32
    )
    shape = (rows, 2 * rank)
    lr_sum = jnp.zeros(shape, F32)
    lg_sum = jnp.zeros(shape, F32)
    for p in range(slots // 2):
        keep = inside_pair(meta, p, first, shape, slots, rank)
        cols = slice(2 * rank * p, 2 * rank * (p + 1))
        lr_sum += jnp.where(keep, lr[:, cols], 0.0)
        lg_sum += jnp.where(keep, lg[:, cols], 0.0)
    lr_sum += pltpu.roll(lr_sum, rank, 1)
    lg_sum += pltpu.roll(lg_sum, rank, 1)
    low = lax.broadcasted_iota(jnp.int32, shape, 1) < rank
    out[0] = jnp.where(low, lr_sum, ADAPTER_SCALE * lg_sum).astype(BF)


def project(meta, parts, down, up, rows, slots, rank, v):
    n, tall, piece = parts.shape
    return pl.pallas_call(
        functools.partial(project_kernel, slots, rank, v),
        grid_spec=pltpu.PrefetchScalarGridSpec(
            num_scalar_prefetch=1,
            grid=(n,),
            in_specs=[
                pl.BlockSpec((1, tall, piece), lambda j, m: (j, 0, 0)),
                pl.BlockSpec(down.shape, lambda j, m: (0, 0)),
                pl.BlockSpec(up.shape, lambda j, m: (0, 0)),
            ],
            out_specs=pl.BlockSpec((1, rows, 2 * rank), lambda j, m: (j, 0, 0)),
        ),
        out_shape=jax.ShapeDtypeStruct((n, rows, 2 * rank), BF),
        compiler_params=params(),
        cost_estimate=cost(2 * n * rows * (piece + v) * slots * rank, 2 * n * tall * piece),
        name="project",
    )(meta, parts, down, up)


def total_kernel(parts, out):
    acc = parts[0].astype(F32)
    for f in range(1, parts.shape[0]):
        acc += parts[f].astype(F32)
    acc = acc.astype(BF)
    for f in range(out.shape[0]):
        out[f] = acc


def total(parts):
    return pl.pallas_call(
        total_kernel,
        out_shape=jax.ShapeDtypeStruct(parts.shape, BF),
        compiler_params=params(),
        cost_estimate=cost(0, 4 * parts.size),
        name="total",
    )(parts)


def spread(meta, both, take_high, first, slots, rank):
    both = both.astype(F32)
    other = pltpu.roll(both, rank, 1)
    low = lax.broadcasted_iota(jnp.int32, both.shape, 1) < rank
    half = jnp.where(low != take_high, both, other)
    cols = [
        jnp.where(inside_pair(meta, p, first, both.shape, slots, rank), half, 0.0)
        for p in range(slots // 2)
    ]
    return jnp.concatenate(cols, axis=1).astype(BF)


def gradient_kernel(slots, rank, v, meta, part, low, out, acc_down, acc_up):
    rows = low.shape[1]
    step = pl.program_id(0)
    first = step * rows

    @pl.when(step == 0)
    def _():
        acc_down[...] = jnp.zeros_like(acc_down)
        acc_up[...] = jnp.zeros_like(acc_up)

    both = low[0]
    lr = spread(meta, both, False, first, slots, rank)
    lg = spread(meta, both, True, first, slots, rank)
    tok = part[0, :rows, :]
    cot_t = jnp.concatenate([part[0, rows:, :rows], part[0, rows:, rows:]], axis=0)
    acc_down[...] += lax.dot_general(
        lg, tok, (((0,), (0,)), ((), ())), preferred_element_type=F32
    )
    acc_up[...] += jnp.dot(cot_t, lr, preferred_element_type=F32)

    @pl.when(step == pl.num_programs(0) - 1)
    def _():
        piece = acc_down.shape[1]
        out[...] = jnp.zeros_like(out)
        up = jnp.transpose(ADAPTER_SCALE * acc_up[...]).astype(BF)
        for s in range(slots):
            at = meta[2 + 2 * slots + s]
            out[at, :, :piece] = acc_down[s * rank:(s + 1) * rank, :].astype(BF)
            out[at, :, piece:piece + v] = up[s * rank:(s + 1) * rank, :]


def gradient(meta, parts, low, owners, slots, rank, v):
    n, tall, piece = parts.shape
    rows = low.shape[1]
    return pl.pallas_call(
        functools.partial(gradient_kernel, slots, rank, v),
        grid_spec=pltpu.PrefetchScalarGridSpec(
            num_scalar_prefetch=1,
            grid=(n,),
            in_specs=[
                pl.BlockSpec((1, tall, piece), lambda j, m: (j, 0, 0)),
                pl.BlockSpec((1, rows, 2 * rank), lambda j, m: (j, 0, 0)),
            ],
            out_specs=pl.BlockSpec((owners, rank, piece + 128), lambda j, m: (0, 0, 0)),
            scratch_shapes=[
                pltpu.VMEM((slots * rank, piece), F32),
                pltpu.VMEM((v, slots * rank), F32),
            ],
        ),
        out_shape=jax.ShapeDtypeStruct((owners, rank, piece + 128), BF),
        compiler_params=params(),
        cost_estimate=cost(2 * n * rows * (piece + v) * slots * rank, 2 * n * tall * piece),
        name="gradient",
    )(meta, parts, low)


def collect_kernel(slots, scale, meta, got, down, up):
    piece, v = down.shape[2], up.shape[2]
    down[...] = jnp.zeros_like(down)
    up[...] = jnp.zeros_like(up)
    for b in range(got.shape[0]):
        r = meta[2 + 3 * slots + b]

        @pl.when(r >= 0)
        def _():
            down[r] += got[b, :, :piece].astype(F32)
            up[r] += got[b, :, piece:piece + v].astype(F32)

    down[...] = down[...] * scale
    up[...] = up[...] * scale


def collect(meta, got, rows, v, slots, scale):
    bins, rank, wide = got.shape
    piece = wide - 128
    return pl.pallas_call(
        functools.partial(collect_kernel, slots, scale),
        grid_spec=pltpu.PrefetchScalarGridSpec(
            num_scalar_prefetch=1,
            grid=(1,),
            in_specs=[pl.BlockSpec(got.shape, lambda i, m: (0, 0, 0))],
            out_specs=[
                pl.BlockSpec((rows, rank, piece), lambda i, m: (0, 0, 0)),
                pl.BlockSpec((rows, rank, v), lambda i, m: (0, 0, 0)),
            ],
        ),
        out_shape=[
            jax.ShapeDtypeStruct((rows, rank, piece), F32),
            jax.ShapeDtypeStruct((rows, rank, v), F32),
        ],
        compiler_params=params(),
        cost_estimate=cost(0, 2 * got.size),
        name="collect",
    )(meta, got)


def input_kernel(slots, rank, meta, cot, low, mine, other, down, out, lg):
    @pl.when(pl.program_id(0) == 0)
    def _():
        lg[...] = spread(meta, low[0], True, meta[1], slots, rank)

    nt = (((1,), (1,)), ((), ()))
    term = jnp.dot(lg[...], down[0], preferred_element_type=F32)
    a = lax.dot_general(cot[...], mine[0], nt, preferred_element_type=F32)
    b = lax.dot_general(cot[...], other[0], nt, preferred_element_type=F32)
    half = a.shape[1]
    lower = meta[0] == 0
    out[:, :half] = (jnp.where(lower, a, b) + term[:, :half]).astype(BF)
    out[:, half:] = (jnp.where(lower, b, a) + term[:, half:]).astype(BF)


def input_gradient(meta, cot, low, mine, other, down, slots, rank):
    n, half, width = mine.shape
    rows = cot.shape[0]
    piece = 2 * half
    return pl.pallas_call(
        functools.partial(input_kernel, slots, rank),
        grid_spec=pltpu.PrefetchScalarGridSpec(
            num_scalar_prefetch=1,
            grid=(n,),
            in_specs=[
                pl.BlockSpec(cot.shape, lambda f, m: (0, 0)),
                pl.BlockSpec((1, rows, 2 * rank), lambda f, m: (0, 0, 0)),
                pl.BlockSpec((1, half, width), lambda f, m: (f, 0, 0)),
                pl.BlockSpec((1, half, width), lambda f, m: (f, 0, 0)),
                pl.BlockSpec((1, slots * rank, piece), lambda f, m: (f, 0, 0)),
            ],
            out_specs=pl.BlockSpec((rows, piece), lambda f, m: (0, f)),
            scratch_shapes=[pltpu.VMEM((rows, slots * rank), BF)],
        ),
        out_shape=jax.ShapeDtypeStruct((rows, n * piece), BF),
        compiler_params=params(),
        cost_estimate=cost(
            2 * rows * n * piece * (width + slots * rank),
            2 * n * piece * (width + slots * rank + rows),
        ),
        name="input_gradient",
    )(meta, cot, low, mine, other, down)


def exchange(x, axis):
    return lax.all_to_all(x, axis, 0, 0, tiled=True)


def local(
    tokens,
    cotangent,
    value_weight,
    adapter_down_weight,
    adapter_up_weight,
    segment_tenant,
    segment_lengths,
    tenant_stored_row,
):
    own, piece, rank = adapter_down_weight.shape
    v = adapter_up_weight.shape[2]
    bins, slots = segment_tenant.shape
    rows = tokens.shape[0]
    n = lax.axis_size("fsdp")
    me_bin = lax.axis_index("dp")
    me_piece = lax.axis_index("fsdp")
    core = me_bin % 2
    scale = (n * rows) ** (-0.5)

    half = piece // 2
    half_weight = lax.dynamic_slice_in_dim(value_weight, core * half, half, 0)
    mine = lax.all_gather(half_weight, "fsdp", axis=0)
    other = lax.ppermute(mine, "dp", [(i, i ^ 1) for i in range(bins)])

    tenants = jnp.arange(tenant_stored_row.shape[0], dtype=jnp.int32)
    stored = jnp.sum(
        jnp.where(segment_tenant[:, :, None] == tenants, tenant_stored_row, 0), axis=2
    )
    my_stored = lax.dynamic_index_in_dim(stored, me_bin, 0, keepdims=False)
    lengths = lax.dynamic_index_in_dim(segment_lengths, me_bin, 0, keepdims=False)
    ends = jnp.cumsum(lengths)
    wanted = jnp.max(jnp.where(stored // own == me_bin, stored % own, -1), axis=1)
    meta = jnp.concatenate(
        [
            jnp.stack([core, me_piece * rows]),
            ends - lengths,
            ends,
            my_stored // own,
            wanted,
        ]
    ).astype(jnp.int32)

    got = exchange(
        offer(meta, jnp.swapaxes(adapter_down_weight, 1, 2), adapter_up_weight, bins, slots), "dp"
    )
    down, up = choose(meta, got, slots)
    down_all = lax.all_gather(down, "fsdp", axis=0)

    parts = exchange(pack(tokens, jnp.swapaxes(cotangent, 0, 1), n), "fsdp")
    low_own = total(exchange(project(meta, parts, down, up, rows, slots, rank, v), "fsdp"))
    low_all = exchange(low_own, "fsdp")
    sent = exchange(gradient(meta, parts, low_all, bins, slots, rank, v), "dp")
    down_grad, up_grad = collect(meta, sent, own, v, slots, scale)
    grad = input_gradient(meta, cotangent, low_own, mine, other, down_all, slots, rank)
    return grad, jnp.swapaxes(down_grad, 1, 2), up_grad


def solution(mesh):
    placed = (
        P(("dp", "fsdp"), None),
        P(("dp", "fsdp"), None),
        P("fsdp", None),
        P("dp", "fsdp", None),
        P("dp", None, "fsdp"),
        P(),
        P(),
        P(),
    )
    return jax.shard_map(
        local,
        mesh=mesh,
        in_specs=placed,
        out_specs=(P(("dp", "fsdp"), None), P("dp", "fsdp", None), P("dp", None, "fsdp")),
        check_vma=False,
    )
```

time: 627 us -> 310 us (0.49)
  waiting for transfers between devices: 532 us -> 83.4 us
  blocking collectives: 19.3 us -> 140 us
  Pallas kernels: 0 us -> 48.6 us
  matrix products: 42.5 us -> 0 us
  starting transfers between devices: 0.51 us -> 7.63 us
    reduce_scatter x4 -> x0, waiting for transfers between devices: 266 us -> none  [the longest x1 90.5 us: local(): lax.psum_scatter(part_down.astype(jnp.bfloat16), 'fsdp', scatter_dimensio...]
    all_gather x4 -> x2, waiting for transfers between devices: 265 us -> 67.3 us  [the longest x1 67.3 us: local(): mine = lax.all_gather(half_weight, 'fsdp', axis=0)]
    all_to_all x0 -> x4, blocking collectives: none -> 140 us  [exchange(): return lax.all_to_all(x, axis, 0, 0, tiled=True)]
    pallas_call x0 -> x8, Pallas kernels: none -> 48.6 us  [the longest x1 17.5 us: input_gradient(): pl.pallas_call(functools.partial(input_kernel, slots, rank), grid_spec=pl...]
    dot_general x7 -> x0, matrix products: 42.5 us -> none  [the longest x1 12.3 us: local(): lax.dot_general(cotangent, lax.all_gather(value_weight, 'fsdp', axis=0, t...]
    all_gather x1 -> x0, blocking collectives: 19.3 us -> none  [local(): lax.all_gather(adapter_up_weight, 'dp', axis=0, tiled=True)]
    all_to_all x0 -> x1, waiting for transfers between devices: none -> 16.1 us  [exchange(): return lax.all_to_all(x, axis, 0, 0, tiled=True)]
    unnamed x4 -> x16, local copies, waits for them, and re-layouts: 0.85 us -> 11.6 us
  transfers between devices with their start and end apart: 8 -> 4, of which waited for: 8 -> 2; matrix products, arithmetic and copies ran while one was open for 7% -> 1% of each run, Pallas kernels for 0% -> 10%
where the time goes in v1:
time: 310 us; the launch traced here: 308 us
  blocking collectives  140 us (45%)
  waiting for transfers between devices  83.4 us (27%)
  Pallas kernels  48.6 us (16%)
  between operations  14.2 us (5%)
  local copies, waits for them, and re-layouts  13.4 us (4%)
  starting transfers between devices  7.63 us (2%)
    all_to_all x4, blocking collectives, exchange(): return lax.all_to_all(x, axis, 0, 0, tiled=True)  140 us
    all_gather x1, waiting for transfers between devices, local(): mine = lax.all_gather(half_weight, 'fsdp', axis=0)  67.3 us
    pallas_call x1, Pallas kernels, input_gradient(): pl.pallas_call(functools.partial(input_kernel, slots, rank), grid_spec=pl...  17.5 us
    all_to_all x1, waiting for transfers between devices, exchange(): return lax.all_to_all(x, axis, 0, 0, tiled=True)  16.1 us
    pallas_call x1, Pallas kernels, gradient(): pl.pallas_call(functools.partial(gradient_kernel, slots, rank, v), grid_s...  13.2 us
    pallas_call x1, Pallas kernels, project(): pl.pallas_call(functools.partial(project_kernel, slots, rank, v), grid_sp...  13.1 us
    unnamed x16, local copies, waits for them, and re-layouts  11.6 us
    all_to_all x1, starting transfers between devices, exchange(): return lax.all_to_all(x, axis, 0, 0, tiled=True)  6.87 us
  transfers between devices with their start and end apart: 4, of which 2 were waited for; matrix products, arithmetic and copies ran while one was open for 1% of the time, Pallas kernels for 10%

profile of v1, /device:TPU:1, one launch (start us, length us, event | category | flops | bytes accessed | tf_op | source)
XLA Modules:
  0.0 308.2 jit_solution(1691462391572080641)
XLA Ops:
  7.3 1.1 copy-done
  8.4 0.8 constant_dynamic-slice_fusion.1
  9.3 0.9 dynamic-slice_reduce_fusion
  10.4 0.8 copy.13
  11.1 1.1 select_reduce_fusion
  12.4 1.0 copy-done.5
  13.4 0.8 copy-done.6
  14.9 43.9 %all_to_all.25.got = bf16[16,64,640]{2,1,0:T(8,128)(2,1)S(1)} all-to-all(bf16[16,64,640]{2,1,0:T(8,128)(2,1)S(1)} %offer.1), channel_id=1, replica_groups=mesh['dp'=16,'fsdp'=16] {'dp'}, dimensions={0} | all-to-all | bytes 2621440 | tf_op jit(solution)/shard_map/all_to_all | solution.py:336
  58.9 1.4 choose.1
  60.5 2.2 copy-done.3
  62.7 0.9 pack.1
  63.7 2.1 copy-done.1
  65.7 6.9 %all-to-all-start = ((bf16[16,288,512]{2,1,0:T(8,128)(2,1)}), bf16[16,288,512]{2,1,0:T(8,128)(2,1)}, u32[]{:S(2)}, u32[]{:S(2)}) async-start(bf16[16,288,512]{2,1,0:T(8,128)(2,1)} %copy-done.1), calls=%async_computation | async-start | bytes 9437184 | tf_op jit(solution)/shard_map/all_to_all | solution.py:336
  72.6 67.3 %all-gather.5.cloned.1.call-done = bf16[4096,1024]{1,0:T(8,128)(2,1)} async-done(((bf16[256,1024]{1,0:T(8,128)(2,1)}), bf16[4096,1024]{1,0:T(8,128)(2,1)}) %all-gather.5.cloned.1.call-update) | async-done | bytes 8388624 | tf_op jit(solution)/shard_map/all_gather | solution.py:361
  139.9 0.7 collective-permute-start
  140.6 16.1 %all-to-all-done.part = bf16[16,288,512]{2,1,0:T(8,128)(2,1)} async-done(((bf16[16,288,512]{2,1,0:T(8,128)(2,1)}), bf16[16,288,512]{2,1,0:T(8,128)(2,1)}, u32[]{:S(2)}, u32[]{:S(2)}) %all-to-all-start) | async-done | bytes 4718624 | tf_op jit(solution)/shard_map/all_to_all | solution.py:336
  156.6 13.1 %project.1 = bf16[16,256,128]{2,1,0:T(8,128)(2,1)S(1)} custom-call(s32[42]{0:T(128)S(1)} %concatenate.3.meta, bf16[16,288,512]{2,1,0:T(8,128)(2,1)} %all-to-all-done.part, bf16[512,512]{1,0:T(8,128)(2,1)} %get-tuple-element.7.down, bf16[512,128]{1,0:T(8,128)(2,1)S(1)} %get-tuple-element.8.up), custom_call_target="tpu_custom_call" | custom-call | flops 2415919104 | bytes 4718592 | tf_op jit(solution)/shard_map/project/pallas_call | solution.py:145
  169.7 23.3 %all_to_all.26.parts = bf16[16,256,128]{2,1,0:T(8,128)(2,1)S(1)} all-to-all(bf16[16,256,128]{2,1,0:T(8,128)(2,1)S(1)} %project.1), channel_id=1, replica_groups=mesh['dp'=16,'fsdp'=16] {'fsdp'}, dimensions={0} | all-to-all | bytes 2097152 | tf_op jit(solution)/shard_map/all_to_all | solution.py:336
  193.2 29.7 %all_to_all.27.low = bf16[16,256,128]{2,1,0:T(8,128)(2,1)S(1)} all-to-all(bf16[16,256,128]{2,1,0:T(8,128)(2,1)S(1)} %total.1.low), channel_id=1, replica_groups=mesh['dp'=16,'fsdp'=16] {'fsdp'}, dimensions={0} | all-to-all | bytes 2097152 | tf_op jit(solution)/shard_map/all_to_all | solution.py:336
  222.9 13.2 %gradient.1 = bf16[16,64,640]{2,1,0:T(8,128)(2,1)S(1)} custom-call(s32[42]{0:T(128)S(1)} %concatenate.3.meta, bf16[16,288,512]{2,1,0:T(8,128)(2,1)} %all-to-all-done.part, bf16[16,256,128]{2,1,0:T(8,128)(2,1)S(1)} %all_to_all.27.low), custom_call_target="tpu_custom_call" | custom-call | flops 2415919104 | bytes 4718592 | tf_op jit(solution)/shard_map/gradient/pallas_call | solution.py:229
  236.1 42.7 %all_to_all.28.got = bf16[16,64,640]{2,1,0:T(8,128)(2,1)S(1)} all-to-all(bf16[16,64,640]{2,1,0:T(8,128)(2,1)S(1)} %gradient.1), channel_id=1, replica_groups=mesh['dp'=16,'fsdp'=16] {'dp'}, dimensions={0} | all-to-all | bytes 2621440 | tf_op jit(solution)/shard_map/all_to_all | solution.py:336
  278.8 1.7 collect.1
  280.5 3.4 %copy-done.2 = bf16[4096,1024]{1,0:T(8,128)(2,1)S(1)} copy-done((bf16[4096,1024]{1,0:T(8,128)(2,1)S(1)}, bf16[4096,1024]{1,0:T(8,128)(2,1)}, u32[]{:S(2)}) %copy-start.2) | copy-done | bytes 8388632
  283.9 17.5 %input_gradient.1 = bf16[256,8192]{1,0:T(8,128)(2,1)} custom-call(s32[42]{0:T(128)S(1)} %concatenate.3.meta, bf16[256,1024]{1,0:T(8,128)(2,1)S(1)} %copy-done.4, bf16[16,256,128]{2,1,0:T(8,128)(2,1)S(1)} %total.1.low, bf16[16,256,1024]{2,1,0:T(8,128)(2,1)S(1)} %bitcast.15, bf16[16,256,1024]{2,1,0:T(8,128)(2,1)} %collective-permute-done.other, ...), custom_call_target="tpu_custom_call" | custom-call | flops 6442450944 | bytes 29360128 | tf_op jit(solution)/shard_map/input_gradient/pallas_call | solution.py:310
  (21 shorter events, 1.6 us)
Async XLA Ops:
  7.2 1.2 copy-start
  7.2 53.1 %copy-start.4 = (bf16[256,1024]{1,0:T(8,128)(2,1)S(1)}, bf16[256,1024]{1,0:T(8,128)(2,1)}, u32[]{:S(2)}) copy-start(bf16[256,1024]{1,0:T(8,128)(2,1)} %cot.1) | copy-start | bytes 1572868
  7.2 132.7 %all-gather.5.cloned.1.call-start = ((), (), s32[]{:S(2)}) async-start(), calls=%async_computation.5 | async-start | bytes 8912896 | tf_op jit(solution)/shard_map/all_gather | solution.py:361
  9.2 271.2 %all-gather.7.cloned.1.call-start = ((), (), s32[]{:S(2)}) async-start(), calls=%async_computation.6 | async-start | bytes 8912896 | tf_op jit(solution)/shard_map/all_gather | solution.py:386
  12.4 1.0 copy-start.5
  13.4 0.8 copy-start.6
  60.5 2.3 copy-start.3
  63.7 2.1 copy-start.1
  65.7 90.9 %all-to-all-start = ((bf16[16,288,512]{2,1,0:T(8,128)(2,1)}), bf16[16,288,512]{2,1,0:T(8,128)(2,1)}, u32[]{:S(2)}, u32[]{:S(2)}) async-start(bf16[16,288,512]{2,1,0:T(8,128)(2,1)} %copy-done.1), calls=%async_computation | async-start | bytes 9437184 | tf_op jit(solution)/shard_map/all_to_all | solution.py:336
  139.9 140.6 %collective-permute-start = (bf16[16,256,1024]{2,1,0:T(8,128)(2,1)}, bf16[16,256,1024]{2,1,0:T(8,128)(2,1)}, u32[]{:S(2)}, u32[]{:S(2)}) collective-permute-start(bf16[16,256,1024]{2,1,0:T(8,128)(2,1)} %bitcast.14), channel_id=1, source_target_pairs={{0,16},{16,0},{32,48},{48,32},{64,80},{80,64},{96,112},{112,96},{1... | collective-permute-start | bytes 25165832 | tf_op jit(solution)/shard_map/ppermute | solution.py:362
  280.5 3.4 %copy-start.2 = (bf16[4096,1024]{1,0:T(8,128)(2,1)S(1)}, bf16[4096,1024]{1,0:T(8,128)(2,1)}, u32[]{:S(2)}) copy-start(bf16[4096,1024]{1,0:T(8,128)(2,1)} %all-gather.5.cloned.1.call-done) | copy-start | bytes 25165828
Sparse Core Ops, SparseCore 0:
  11.0 128.8 all-gather.4
  142.9 92.1 all-gather.6

commit v2 on v0

v2 whole, which is shorter than its diff:
```python
import functools

import jax
import jax.numpy as jnp
from jax import lax
from jax.experimental import pallas as pl
from jax.experimental.pallas import tpu as pltpu
from jax.sharding import PartitionSpec as P

ADAPTER_SCALE = 2.0
BF = jnp.bfloat16
F32 = jnp.float32
VMEM_BYTES = 40 * 1024 * 1024
GROUP = 4
CORE, FIRST, CHIP, LIST = 0, 1, 2, 3


def call(kernel, name, flops=0, moved=0, **kw):
    return pl.pallas_call(
        kernel,
        compiler_params=pltpu.CompilerParams(vmem_limit_bytes=VMEM_BYTES),
        cost_estimate=pl.CostEstimate(flops=flops, bytes_accessed=moved, transcendentals=0),
        name=name,
        **kw,
    )


def whole(shape):
    return pl.BlockSpec(shape, lambda i, m: (0,) * len(shape))


def with_meta(grid, in_specs, out_specs, scratch=()):
    return pltpu.PrefetchScalarGridSpec(
        num_scalar_prefetch=1,
        grid=grid,
        in_specs=in_specs,
        out_specs=out_specs,
        scratch_shapes=list(scratch),
    )


def start_of(meta, s):
    return meta[LIST + s]


def end_of(meta, s, slots):
    return meta[LIST + slots + s]


def owner_of(meta, s, slots):
    return meta[LIST + 2 * slots + s]


def wanted_by(meta, b, slots):
    return meta[LIST + 3 * slots + b]


def segment_at(meta, owner, slots, bins):
    return meta[LIST + 3 * slots + bins + owner]


def inside_pair(meta, pair, first, shape, slots, rank):
    row = first + lax.broadcasted_iota(jnp.int32, shape, 0)
    low = lax.broadcasted_iota(jnp.int32, shape, 1) < rank
    begin = jnp.where(low, start_of(meta, 2 * pair), start_of(meta, 2 * pair + 1))
    end = jnp.where(low, end_of(meta, 2 * pair, slots), end_of(meta, 2 * pair + 1, slots))
    return (row >= begin) & (row < end)


def turn_kernel(meta, w, out):
    out[...] = jnp.transpose(w[...].astype(F32)).astype(BF)


def turn(meta, w):
    piece, width = w.shape
    half = piece // 2
    return call(
        turn_kernel,
        "turn",
        moved=4 * half * width,
        grid_spec=with_meta(
            (1,),
            [pl.BlockSpec((half, width), lambda i, m: (m[CORE], 0))],
            whole((width, half)),
        ),
        out_shape=jax.ShapeDtypeStruct((width, half), BF),
    )(meta, w)


def pack_kernel(tok, cot_t, out):
    rows = tok.shape[0]
    n, _, piece = out.shape
    v = cot_t.shape[0] // n
    for f in range(n):
        out[f, :rows, :] = tok[:, f * piece:(f + 1) * piece]
        out[f, rows:, :rows] = cot_t[f * v:f * v + v // 2, :]
        out[f, rows:, rows:] = cot_t[f * v + v // 2:(f + 1) * v, :]


def pack(tokens, cot_t, n):
    rows, width = tokens.shape
    piece, v = width // n, cot_t.shape[0] // n
    tall = rows + v * rows // piece
    return call(
        pack_kernel,
        "pack",
        moved=4 * rows * width,
        grid=(n // GROUP,),
        in_specs=[
            pl.BlockSpec((rows, GROUP * piece), lambda f: (0, f)),
            pl.BlockSpec((GROUP * v, rows), lambda f: (f, 0)),
        ],
        out_specs=pl.BlockSpec((GROUP, tall, piece), lambda f: (f, 0, 0)),
        out_shape=jax.ShapeDtypeStruct((n, tall, piece), BF),
    )(tokens, cot_t)


def offer_kernel(slots, meta, down_t, up, keep, give):
    piece, v = down_t.shape[2], up.shape[2]
    keep[...] = jnp.zeros_like(keep)
    give[...] = jnp.zeros_like(give)
    for z in range(keep.shape[0]):
        for out, core in ((keep, meta[CORE]), (give, 1 - meta[CORE])):
            r = jnp.maximum(wanted_by(meta, 2 * z + core, slots), 0)
            out[z, :, :piece] = down_t[r]
            out[z, :, piece:piece + v] = up[r]


def offer(meta, down_t, up, chips, slots):
    _, rank, piece = down_t.shape
    shape = (chips, rank, piece + 128)
    return call(
        functools.partial(offer_kernel, slots),
        "offer",
        moved=8 * chips * rank * piece,
        grid_spec=with_meta(
            (1,), [whole(down_t.shape), whole(up.shape)], [whole(shape), whole(shape)]
        ),
        out_shape=[jax.ShapeDtypeStruct(shape, BF)] * 2,
    )(meta, down_t, up)


def merge_kernel(meta, keep, taken, *outs):
    chips = len(outs)
    for k, out in enumerate(outs):
        z = lax.rem(meta[CHIP] + k, chips)
        out[meta[CORE]] = keep[z]
        out[1 - meta[CORE]] = taken[z]


def merge(meta, keep, taken):
    chips, rank, wide = keep.shape
    shape = (2, rank, wide)
    return call(
        merge_kernel,
        "merge",
        moved=4 * keep.size,
        grid_spec=with_meta(
            (1,), [whole(keep.shape), whole(taken.shape)], [whole(shape)] * chips
        ),
        out_shape=[jax.ShapeDtypeStruct(shape, BF)] * chips,
    )(meta, keep, taken)


def choose_kernel(slots, meta, *refs):
    chips = len(refs) - 3
    got, (down, turned, up) = refs[:chips], refs[chips:]
    piece, v, rank = down.shape[2], up.shape[0], down.shape[1]
    for k in range(chips):
        z = lax.rem(meta[CHIP] + chips - k, chips)
        for core in range(2):
            s = segment_at(meta, 2 * z + core, slots, 2 * chips)

            @pl.when(s >= 0)
            def _():
                down[s] = got[k][core]

    for p in range(slots // 2):
        pair = jnp.concatenate([down[2 * p], down[2 * p + 1]], axis=0).astype(F32)
        cols = slice(2 * rank * p, 2 * rank * (p + 1))
        turned[:, cols] = jnp.transpose(pair[:, :turned.shape[0]]).astype(BF)
        up[:, cols] = jnp.transpose(pair[:, turned.shape[0]:])[:v].astype(BF)


def choose(meta, got, slots, v):
    _, rank, wide = got[0].shape
    piece = wide - 128
    shapes = [(slots, rank, wide), (piece, slots * rank), (v, slots * rank)]
    return call(
        functools.partial(choose_kernel, slots),
        "choose",
        moved=4 * slots * rank * wide,
        grid_spec=with_meta((1,), [whole(g.shape) for g in got], [whole(s) for s in shapes]),
        out_shape=[jax.ShapeDtypeStruct(s, BF) for s in shapes],
    )(meta, *got)


def cot_of(part, rows):
    return jnp.concatenate([part[rows:, :rows], part[rows:, rows:]], axis=0)


def project_kernel(slots, rank, meta, part, down_t, up_t, out):
    group, rows, _ = out.shape
    shape = (rows, 2 * rank)
    low = lax.broadcasted_iota(jnp.int32, shape, 1) < rank
    for g in range(group):
        first = (pl.program_id(0) * group + g) * rows
        block = part[g]
        lr = jnp.dot(block[:rows], down_t[...], preferred_element_type=F32)
        lg = lax.dot_general(
            cot_of(block, rows), up_t[...], (((0,), (0,)), ((), ())), preferred_element_type=F32
        )
        lr_sum = jnp.zeros(shape, F32)
        lg_sum = jnp.zeros(shape, F32)
        for p in range(slots // 2):
            keep = inside_pair(meta, p, first, shape, slots, rank)
            cols = slice(2 * rank * p, 2 * rank * (p + 1))
            lr_sum += jnp.where(keep, lr[:, cols], 0.0)
            lg_sum += jnp.where(keep, lg[:, cols], 0.0)
        lr_sum += pltpu.roll(lr_sum, rank, 1)
        lg_sum += pltpu.roll(lg_sum, rank, 1)
        out[g] = jnp.where(low, lr_sum, ADAPTER_SCALE * lg_sum).astype(BF)


def project(meta, parts, down_t, up_t, rows, slots, rank):
    n, tall, piece = parts.shape
    return call(
        functools.partial(project_kernel, slots, rank),
        "project",
        flops=2 * n * rows * piece * slots * rank,
        moved=2 * n * tall * piece,
        grid_spec=with_meta(
            (n // GROUP,),
            [
                pl.BlockSpec((GROUP, tall, piece), lambda j, m: (j, 0, 0)),
                whole(down_t.shape),
                whole(up_t.shape),
            ],
            pl.BlockSpec((GROUP, rows, 2 * rank), lambda j, m: (j, 0, 0)),
        ),
        out_shape=jax.ShapeDtypeStruct((n, rows, 2 * rank), BF),
    )(meta, parts, down_t, up_t)


def total_kernel(parts, out, copies):
    acc = parts[0].astype(F32)
    for f in range(1, parts.shape[0]):
        acc += parts[f].astype(F32)
    out[...] = acc.astype(BF)
    turned = jnp.transpose(acc).astype(BF)
    for f in range(copies.shape[0]):
        copies[f] = turned


def total(parts):
    n, rows, wide = parts.shape
    return call(
        total_kernel,
        "total",
        moved=4 * parts.size,
        out_shape=[
            jax.ShapeDtypeStruct((rows, wide), BF),
            jax.ShapeDtypeStruct((n, wide, rows), BF),
        ],
    )(parts)


def gradient_kernel(slots, rank, v, meta, part, low, out, acc_down, acc_up):
    group, _, rows = low.shape
    step = pl.program_id(0)

    @pl.when(step == 0)
    def _():
        acc_down[...] = jnp.zeros_like(acc_down)
        acc_up[...] = jnp.zeros_like(acc_up)

    for g in range(group):
        first = (step * group + g) * rows
        for s in range(slots):
            start, end = start_of(meta, s), end_of(meta, s, slots)

            @pl.when((start < first + rows) & (end > first))
            def _():
                token = first + lax.broadcasted_iota(jnp.int32, (2 * rank, rows), 1)
                both = low[g].astype(F32)
                both = jnp.where((token >= start) & (token < end), both, 0.0).astype(BF)
                at = slice(s * rank, (s + 1) * rank)
                acc_down[at, :] += jnp.dot(
                    both[rank:], part[g, :rows, :], preferred_element_type=F32
                )
                acc_up[at, :] += lax.dot_general(
                    both[:rank],
                    cot_of(part[g], rows),
                    (((1,), (1,)), ((), ())),
                    preferred_element_type=F32,
                )

    @pl.when(step == pl.num_programs(0) - 1)
    def _():
        piece = acc_down.shape[1]
        out[...] = jnp.zeros_like(out)
        for s in range(slots):
            at = owner_of(meta, s, slots)
            rows_of = slice(s * rank, (s + 1) * rank)
            out[at, :, :piece] = acc_down[rows_of, :].astype(BF)
            out[at, :, piece:piece + v] = (ADAPTER_SCALE * acc_up[rows_of, :]).astype(BF)


def gradient(meta, parts, low, owners, slots, rank, v):
    n, tall, piece = parts.shape
    rows = low.shape[2]
    shape = (owners, rank, piece + 128)
    return call(
        functools.partial(gradient_kernel, slots, rank, v),
        "gradient",
        flops=2 * n * rows * piece * slots * rank,
        moved=2 * n * tall * piece,
        grid_spec=with_meta(
            (n // GROUP,),
            [
                pl.BlockSpec((GROUP, tall, piece), lambda j, m: (j, 0, 0)),
                pl.BlockSpec((GROUP, 2 * rank, rows), lambda j, m: (j, 0, 0)),
            ],
            whole(shape),
            [pltpu.VMEM((slots * rank, piece), F32), pltpu.VMEM((slots * rank, v), F32)],
        ),
        out_shape=jax.ShapeDtypeStruct(shape, BF),
    )(meta, parts, low)


def collect_kernel(slots, scale, meta, got, down, up):
    piece, v = down.shape[2], up.shape[2]
    down[...] = jnp.zeros_like(down)
    up[...] = jnp.zeros_like(up)
    for b in range(got.shape[0]):
        r = wanted_by(meta, b, slots)

        @pl.when(r >= 0)
        def _():
            down[r] += got[b, :, :piece].astype(F32) * scale
            up[r] += got[b, :, piece:piece + v].astype(F32) * scale


def collect(meta, got, rows, v, slots, scale):
    _, rank, wide = got.shape
    shapes = [(rows, rank, wide - 128), (rows, rank, v)]
    return call(
        functools.partial(collect_kernel, slots, scale),
        "collect",
        moved=2 * got.size,
        grid_spec=with_meta((1,), [whole(got.shape)], [whole(s) for s in shapes]),
        out_shape=[jax.ShapeDtypeStruct(s, F32) for s in shapes],
    )(meta, got)


def input_kernel(slots, rank, meta, cot, low, mine, other, down, out, lg):
    @pl.when(pl.program_id(0) == 0)
    def _():
        both = low[...].astype(F32)
        half = jnp.where(
            lax.broadcasted_iota(jnp.int32, both.shape, 1) < rank,
            pltpu.roll(both, rank, 1),
            both,
        )
        for p in range(slots // 2):
            keep = inside_pair(meta, p, meta[FIRST], both.shape, slots, rank)
            lg[:, 2 * rank * p:2 * rank * (p + 1)] = jnp.where(keep, half, 0.0).astype(BF)

    lower = meta[CORE] == 0
    group, _, half = mine.shape
    for g in range(group):
        at = 2 * g * half
        term = jnp.dot(lg[...], down[g], preferred_element_type=F32)
        a = jnp.dot(cot[...], mine[g], preferred_element_type=F32)
        b = jnp.dot(cot[...], other[g], preferred_element_type=F32)
        out[:, at:at + half] = (jnp.where(lower, a, b) + term[:, :half]).astype(BF)
        out[:, at + half:at + 2 * half] = (jnp.where(lower, b, a) + term[:, half:]).astype(BF)


def input_gradient(meta, cot, low, mine, other, down, slots, rank):
    n, width, half = mine.shape
    rows = cot.shape[0]
    piece = 2 * half
    group = 2
    return call(
        functools.partial(input_kernel, slots, rank),
        "input_gradient",
        flops=2 * rows * n * piece * (width + slots * rank),
        moved=2 * n * piece * (width + slots * rank + rows),
        grid_spec=with_meta(
            (n // group,),
            [
                whole(cot.shape),
                whole(low.shape),
                pl.BlockSpec((group, width, half), lambda f, m: (f, 0, 0)),
                pl.BlockSpec((group, width, half), lambda f, m: (f, 0, 0)),
                pl.BlockSpec((group, slots * rank, piece), lambda f, m: (f, 0, 0)),
            ],
            pl.BlockSpec((rows, group * piece), lambda f, m: (0, f)),
            [pltpu.VMEM((rows, slots * rank), BF)],
        ),
        out_shape=jax.ShapeDtypeStruct((rows, n * piece), BF),
    )(meta, cot, low, mine, other, down)


def exchange(x, axis):
    return lax.all_to_all(x, axis, 0, 0, tiled=True)


def swap(x, bins):
    return lax.ppermute(x, "dp", [(i, i ^ 1) for i in range(bins)])


def shift(x, k, bins):
    chips = bins // 2
    return lax.ppermute(
        x, "dp", [(i, (i // 2 + k) % chips * 2 + i % 2) for i in range(bins)]
    )


def scalars(segment_tenant, segment_lengths, tenant_stored_row, own, rows):
    bins, slots = segment_tenant.shape
    me = lax.axis_index("dp")
    tenants = jnp.arange(tenant_stored_row.shape[0], dtype=jnp.int32)
    stored = jnp.sum(
        jnp.where(segment_tenant[:, :, None] == tenants, tenant_stored_row, 0), axis=2
    )
    owners = lax.dynamic_index_in_dim(stored, me, 0, keepdims=False) // own
    lengths = lax.dynamic_index_in_dim(segment_lengths, me, 0, keepdims=False)
    place = jnp.arange(slots, dtype=jnp.int32)
    starts = jnp.sum(jnp.where(place[None, :] < place[:, None], lengths[None, :], 0), axis=1)
    wanted = jnp.max(jnp.where(stored // own == me, stored % own, -1), axis=1)
    every = jnp.arange(bins, dtype=jnp.int32)
    segment = jnp.max(jnp.where(owners[None, :] == every[:, None], place[None, :], -1), axis=1)
    head = jnp.stack([me % 2, lax.axis_index("fsdp") * rows, me // 2])
    return jnp.concatenate([head, starts, starts + lengths, owners, wanted, segment]).astype(
        jnp.int32
    )


def local(
    tokens,
    cotangent,
    value_weight,
    adapter_down_weight,
    adapter_up_weight,
    segment_tenant,
    segment_lengths,
    tenant_stored_row,
):
    own, piece, rank = adapter_down_weight.shape
    v = adapter_up_weight.shape[2]
    bins, slots = segment_tenant.shape
    chips = bins // 2
    rows = tokens.shape[0]
    n = lax.axis_size("fsdp")
    scale = (n * rows) ** (-0.5)
    meta = scalars(segment_tenant, segment_lengths, tenant_stored_row, own, rows)

    parts = exchange(pack(tokens, jnp.swapaxes(cotangent, 0, 1), n), "fsdp")
    mine = lax.all_gather(turn(meta, value_weight), "fsdp", axis=0)

    keep, give = offer(
        meta, jnp.swapaxes(adapter_down_weight, 1, 2), adapter_up_weight, chips, slots
    )
    blocks = merge(meta, keep, swap(give, bins))
    got = [blocks[0]] + [shift(blocks[k], k, bins) for k in range(1, chips)]
    parts, got = lax.optimization_barrier((parts, got))
    down, down_t, up_t = choose(meta, got, slots, v)
    down_all = lax.all_gather(
        down[:, :, :piece].reshape(slots * rank, piece), "fsdp", axis=0
    )

    low, copies = total(
        exchange(project(meta, parts, down_t, up_t, rows, slots, rank), "fsdp")
    )
    mine, copies = lax.optimization_barrier((mine, copies))
    other = swap(mine, bins)
    sent = exchange(
        gradient(meta, parts, exchange(copies, "fsdp"), bins, slots, rank, v), "dp"
    )
    grad = input_gradient(meta, cotangent, low, mine, other, down_all, slots, rank)
    sent, grad = lax.optimization_barrier((sent, grad))
    down_grad, up_grad = collect(meta, sent, own, v, slots, scale)
    return grad, jnp.swapaxes(down_grad, 1, 2), up_grad


def solution(mesh):
    placed = (
        P(("dp", "fsdp"), None),
        P(("dp", "fsdp"), None),
        P("fsdp", None),
        P("dp", "fsdp", None),
        P("dp", None, "fsdp"),
        P(),
        P(),
        P(),
    )
    return jax.shard_map(
        local,
        mesh=mesh,
        in_specs=placed,
        out_specs=(P(("dp", "fsdp"), None), P("dp", "fsdp", None), P("dp", None, "fsdp")),
        check_vma=False,
    )
```

time: 627 us -> 258 us (0.41)
  waiting for transfers between devices: 532 us -> 102 us
  matrix products: 42.5 us -> 0 us
  starting transfers between devices: 0.51 us -> 39 us
  Pallas kernels: 0 us -> 35.5 us
  blocking collectives: 19.3 us -> 52.4 us
    reduce_scatter x4 -> x0, waiting for transfers between devices: 266 us -> none  [the longest x1 90.5 us: local(): lax.psum_scatter(part_down.astype(jnp.bfloat16), 'fsdp', scatter_dimensio...]
    all_gather x4 -> x2, waiting for transfers between devices: 265 us -> 47.5 us  [the longest x1 38.8 us: local(): lax.all_gather(down[:, :, :piece].reshape(slots * rank, piece), 'fsdp', a...]
    all_to_all x0 -> x2, blocking collectives: none -> 52.4 us  [exchange(): return lax.all_to_all(x, axis, 0, 0, tiled=True)]
    dot_general x7 -> x0, matrix products: 42.5 us -> none  [the longest x1 12.3 us: local(): lax.dot_general(cotangent, lax.all_gather(value_weight, 'fsdp', axis=0, t...]
    pallas_call x0 -> x10, Pallas kernels: none -> 35.5 us  [the longest x1 13.7 us: input_gradient(): call(functools.partial(input_kernel, slots, rank), 'input_gradient', flop...]
    all_to_all x0 -> x2, waiting for transfers between devices: none -> 33.1 us  [exchange(): return lax.all_to_all(x, axis, 0, 0, tiled=True)]
    ppermute x0 -> x9, waiting for transfers between devices: none -> 21.6 us  [the longest x7 19.9 us: shift(): lax.ppermute(x, 'dp', [(i, (i // 2 + k) % chips * 2 + i % 2) for i in ran...]
    ppermute x0 -> x9, starting transfers between devices: none -> 21.4 us  [the longest x7 19.6 us: shift(): lax.ppermute(x, 'dp', [(i, (i // 2 + k) % chips * 2 + i % 2) for i in ran...]
  transfers between devices with their start and end apart: 8 -> 13, of which waited for: 8 -> 8; matrix products, arithmetic and copies ran while one was open for 7% -> 1% of each run, Pallas kernels for 0% -> 13%
where the time goes in v2:
time: 258 us; the launch traced here: 257 us
  waiting for transfers between devices  102 us (40%)
  blocking collectives  52.4 us (20%)
  starting transfers between devices  39 us (15%)
  Pallas kernels  35.5 us (14%)
  between operations  14.2 us (6%)
  local copies, waits for them, and re-layouts  12.1 us (5%)
    all_to_all x2, blocking collectives, exchange(): return lax.all_to_all(x, axis, 0, 0, tiled=True)  52.4 us
    all_gather x1, waiting for transfers between devices, local(): lax.all_gather(down[:, :, :piece].reshape(slots * rank, piece), 'fsdp', a...  38.8 us
    all_to_all x2, waiting for transfers between devices, exchange(): return lax.all_to_all(x, axis, 0, 0, tiled=True)  33.1 us
    ppermute x7, waiting for transfers between devices, shift(): lax.ppermute(x, 'dp', [(i, (i // 2 + k) % chips * 2 + i % 2) for i in ran...  19.9 us
    ppermute x7, starting transfers between devices, shift(): lax.ppermute(x, 'dp', [(i, (i // 2 + k) % chips * 2 + i % 2) for i in ran...  19.6 us
    all_to_all x2, starting transfers between devices, exchange(): return lax.all_to_all(x, axis, 0, 0, tiled=True)  17.6 us
    pallas_call x1, Pallas kernels, input_gradient(): call(functools.partial(input_kernel, slots, rank), 'input_gradient', flop...  13.7 us
    unnamed x18, local copies, waits for them, and re-layouts  11 us
  transfers between devices with their start and end apart: 13, of which 8 were waited for; matrix products, arithmetic and copies ran while one was open for 1% of the time, Pallas kernels for 13%

profile of v2, /device:TPU:1, one launch (start us, length us, event | category | flops | bytes accessed | tf_op | source)
XLA Modules:
  0.0 256.9 jit_solution(15512993455026266526)
XLA Ops:
  13.7 2.2 copy-done.3
  16.6 2.2 copy-done.1
  18.8 7.8 %all-to-all-start = ((bf16[16,288,512]{2,1,0:T(8,128)(2,1)}), bf16[16,288,512]{2,1,0:T(8,128)(2,1)}, u32[]{:S(2)}, u32[]{:S(2)}) async-start(bf16[16,288,512]{2,1,0:T(8,128)(2,1)} %copy-done.1), calls=%async_computation | async-start | bytes 9437184 | tf_op jit(solution)/shard_map/all_to_all | solution.py:407
  28.4 1.7 collective-permute-done.taken
  30.8 1.7 collective-permute-start.1
  32.5 3.0 %collective-permute-start.2 = (bf16[2,64,640]{2,1,0:T(8,128)(2,1)S(1)}, bf16[2,64,640]{2,1,0:T(8,128)(2,1)S(1)}, u32[]{:S(2)}, u32[]{:S(2)}) collective-permute-start(bf16[2,64,640]{2,1,0:T(8,128)(2,1)S(1)} %get-tuple-element.37), channel_id=1, source_target_pairs={{0,64},{16,80},{32,96},{48,112},{64,128},{80,144},{96,160},{112,17... | collective-permute-start | bytes 491528 | tf_op jit(solution)/shard_map/ppermute | solution.py:416
  35.5 3.8 %collective-permute-start.3 = (bf16[2,64,640]{2,1,0:T(8,128)(2,1)S(1)}, bf16[2,64,640]{2,1,0:T(8,128)(2,1)S(1)}, u32[]{:S(2)}, u32[]{:S(2)}) collective-permute-start(bf16[2,64,640]{2,1,0:T(8,128)(2,1)S(1)} %get-tuple-element.38), channel_id=1, source_target_pairs={{0,96},{16,112},{32,128},{48,144},{64,160},{80,176},{96,192},{112,... | collective-permute-start | bytes 491528 | tf_op jit(solution)/shard_map/ppermute | solution.py:416
  39.7 4.5 %collective-permute-start.5 = (bf16[2,64,640]{2,1,0:T(8,128)(2,1)S(1)}, bf16[2,64,640]{2,1,0:T(8,128)(2,1)S(1)}, u32[]{:S(2)}, u32[]{:S(2)}) collective-permute-start(bf16[2,64,640]{2,1,0:T(8,128)(2,1)S(1)} %get-tuple-element.40), channel_id=1, source_target_pairs={{0,160},{16,176},{32,192},{48,208},{64,224},{80,240},{96,0},{112,1... | collective-permute-start | bytes 491528 | tf_op jit(solution)/shard_map/ppermute | solution.py:416
  44.2 2.4 collective-permute-start.6
  46.6 3.9 %collective-permute-start.7 = (bf16[2,64,640]{2,1,0:T(8,128)(2,1)S(1)}, bf16[2,64,640]{2,1,0:T(8,128)(2,1)S(1)}, u32[]{:S(2)}, u32[]{:S(2)}) collective-permute-start(bf16[2,64,640]{2,1,0:T(8,128)(2,1)S(1)} %get-tuple-element.42), channel_id=1, source_target_pairs={{0,224},{16,240},{32,0},{48,16},{64,32},{80,48},{96,64},{112,80},{... | collective-permute-start | bytes 491528 | tf_op jit(solution)/shard_map/ppermute | solution.py:416
  50.4 8.3 %collective-permute-done.3.refs_3_ = bf16[2,64,640]{2,1,0:T(8,128)(2,1)S(1)} collective-permute-done((bf16[2,64,640]{2,1,0:T(8,128)(2,1)S(1)}, bf16[2,64,640]{2,1,0:T(8,128)(2,1)S(1)}, u32[]{:S(2)}, u32[]{:S(2)}) %collective-permute-start.3) | collective-permute-done | bytes 163872 | tf_op jit(solution)/shard_map/ppermute | solution.py:416
  58.7 2.7 %collective-permute-done.4.refs_4_ = bf16[2,64,640]{2,1,0:T(8,128)(2,1)S(1)} collective-permute-done((bf16[2,64,640]{2,1,0:T(8,128)(2,1)S(1)}, bf16[2,64,640]{2,1,0:T(8,128)(2,1)S(1)}, u32[]{:S(2)}, u32[]{:S(2)}) %collective-permute-start.4) | collective-permute-done | bytes 163872 | tf_op jit(solution)/shard_map/ppermute | solution.py:416
  61.4 7.9 %collective-permute-done.6.refs_6_ = bf16[2,64,640]{2,1,0:T(8,128)(2,1)S(1)} collective-permute-done((bf16[2,64,640]{2,1,0:T(8,128)(2,1)S(1)}, bf16[2,64,640]{2,1,0:T(8,128)(2,1)S(1)}, u32[]{:S(2)}, u32[]{:S(2)}) %collective-permute-start.6) | collective-permute-done | bytes 163872 | tf_op jit(solution)/shard_map/ppermute | solution.py:416
  70.3 33.1 %all-to-all-done.part = bf16[16,288,512]{2,1,0:T(8,128)(2,1)} async-done(((bf16[16,288,512]{2,1,0:T(8,128)(2,1)}), bf16[16,288,512]{2,1,0:T(8,128)(2,1)}, u32[]{:S(2)}, u32[]{:S(2)}) %all-to-all-start) | async-done | bytes 4718624 | tf_op jit(solution)/shard_map/all_to_all | solution.py:407
  105.3 6.8 %project.1 = bf16[16,256,128]{2,1,0:T(8,128)(2,1)S(1)} custom-call(s32[59]{0:T(128)S(1)} %concatenate.3.meta, bf16[16,288,512]{2,1,0:T(8,128)(2,1)} %all-to-all-done.part, bf16[512,512]{1,0:T(8,128)(2,1)S(1)} %get-tuple-element.52.down_t, bf16[64,512]{1,0:T(8,128)(2,1)S(1)} %get-tuple-element.53.up_t), custom_call_target="tpu_custom_call" | custom-call | flops 2147483648 | bytes 4718592 | tf_op jit(solution)/shard_map/project/pallas_call | solution.py:227
  112.1 30.5 %all_to_all.20.parts = bf16[16,256,128]{2,1,0:T(8,128)(2,1)S(1)} all-to-all(bf16[16,256,128]{2,1,0:T(8,128)(2,1)S(1)} %project.1), channel_id=1, replica_groups=mesh['dp'=16,'fsdp'=16] {'fsdp'}, dimensions={0} | all-to-all | bytes 2097152 | tf_op jit(solution)/shard_map/all_to_all | solution.py:407
  142.9 8.7 %all-gather.6.cloned.1.call-done = bf16[16384,256]{1,0:T(8,128)(2,1)} async-done(((bf16[1024,256]{1,0:T(8,128)(2,1)}), bf16[16384,256]{1,0:T(8,128)(2,1)}) %all-gather.6.cloned.1.call-update) | async-done | bytes 8388624 | tf_op jit(solution)/shard_map/all_gather | solution.py:461
  152.3 21.9 %all_to_all.21.low = bf16[16,128,256]{2,1,0:T(8,128)(2,1)S(1)} all-to-all(bf16[16,128,256]{2,1,0:T(8,128)(2,1)S(1)} %get-tuple-element.55), channel_id=1, replica_groups=mesh['dp'=16,'fsdp'=16] {'fsdp'}, dimensions={0} | all-to-all | bytes 2097152 | tf_op jit(solution)/shard_map/all_to_all | solution.py:407
  174.2 8.5 %gradient.1 = bf16[16,64,640]{2,1,0:T(8,128)(2,1)} custom-call(s32[59]{0:T(128)S(1)} %concatenate.3.meta, bf16[16,288,512]{2,1,0:T(8,128)(2,1)} %all-to-all-done.part, bf16[16,128,256]{2,1,0:T(8,128)(2,1)S(1)} %all_to_all.21.low), custom_call_target="tpu_custom_call" | custom-call | flops 2147483648 | bytes 4718592 | tf_op jit(solution)/shard_map/gradient/pallas_call | solution.py:313
  182.7 9.8 %all-to-all-start.3 = ((bf16[16,64,640]{2,1,0:T(8,128)(2,1)}), bf16[16,64,640]{2,1,0:T(8,128)(2,1)S(1)}, u32[]{:S(2)}, u32[]{:S(2)}) async-start(bf16[16,64,640]{2,1,0:T(8,128)(2,1)} %gradient.1), calls=%async_computation.3 | async-start | bytes 2621440 | tf_op jit(solution)/shard_map/all_to_all | solution.py:407
  192.5 38.8 %all-gather.4.cloned.1.call-done.down = bf16[16,512,512]{2,1,0:T(8,128)(2,1)} async-done(((bf16[1,512,512]{2,1,0:T(8,128)(2,1)}), bf16[16,512,512]{2,1,0:T(8,128)(2,1)}) %all-gather.4.cloned.1.call-update) | async-done | bytes 8388624 | tf_op jit(solution)/shard_map/all_gather | solution.py:470
  231.3 3.4 %copy-done.2 = bf16[16384,256]{1,0:T(8,128)(2,1)S(1)} copy-done((bf16[16384,256]{1,0:T(8,128)(2,1)S(1)}, bf16[16384,256]{1,0:T(8,128)(2,1)}, u32[]{:S(2)}) %copy-start.2) | copy-done | bytes 8388632
  234.7 13.7 %input_gradient.1 = bf16[256,8192]{1,0:T(8,128)(2,1)} custom-call(s32[59]{0:T(128)S(1)} %concatenate.3.meta, bf16[256,1024]{1,0:T(8,128)(2,1)S(1)} %copy-done.4, bf16[256,128]{1,0:T(8,128)(2,1)S(1)} %get-tuple-element.56.low, bf16[16,1024,256]{2,1,0:T(8,128)(2,1)S(1)} %bitcast.19, bf16[16,1024,256]{2,1,0:T(8,128)(2,1)} %collective-permute-done.8.other, ...), custom_call_target="tpu_custom_call" | custom-call | flops 6442450944 | bytes 29360128 | tf_op jit(solution)/shard_map/input_gradient/pallas_call | solution.py:385
  248.4 1.7 collect.1
  (43 shorter events, 13.9 us)
Async XLA Ops:
  7.2 2.0 copy-start
  7.2 144.5 %all-gather.6.cloned.1.call-start = ((), (), s32[]{:S(2)}) async-start(), calls=%async_computation.5 | async-start | bytes 8912896 | tf_op jit(solution)/shard_map/all_gather | solution.py:461
  9.7 1.2 copy-start.5
  13.7 2.2 copy-start.3
  16.6 2.2 copy-start.1
  18.8 7.8 %copy-start.6 = (bf16[4,512,64]{1,2,0:T(8,128)(2,1)S(1)}, bf16[4,512,64]{1,2,0:T(8,128)(2,1)}, u32[]{:S(2)}) copy-start(bf16[4,512,64]{1,2,0:T(8,128)(2,1)} %param.11) | copy-start | bytes 786436
  18.8 7.8 %copy-start.7 = (bf16[4,64,64]{2,1,0:T(8,128)(2,1)S(1)}, bf16[4,64,64]{2,1,0:T(8,128)(2,1)}, u32[]{:S(2)}) copy-start(bf16[4,64,64]{2,1,0:T(8,128)(2,1)} %up.1) | copy-start | bytes 98308
  18.8 84.6 %all-to-all-start = ((bf16[16,288,512]{2,1,0:T(8,128)(2,1)}), bf16[16,288,512]{2,1,0:T(8,128)(2,1)}, u32[]{:S(2)}, u32[]{:S(2)}) async-start(bf16[16,288,512]{2,1,0:T(8,128)(2,1)} %copy-done.1), calls=%async_computation | async-start | bytes 9437184 | tf_op jit(solution)/shard_map/all_to_all | solution.py:407
  26.6 204.7 %all-gather.4.cloned.1.call-start = ((), (), s32[]{:S(2)}) async-start(), calls=%async_computation.4 | async-start | bytes 8912896 | tf_op jit(solution)/shard_map/all_gather | solution.py:470
  27.4 2.8 %collective-permute-start = (bf16[8,64,640]{2,1,0:T(8,128)(2,1)S(1)}, bf16[8,64,640]{2,1,0:T(8,128)(2,1)S(1)}, u32[]{:S(2)}, u32[]{:S(2)}) collective-permute-start(bf16[8,64,640]{2,1,0:T(8,128)(2,1)S(1)} %get-tuple-element.34), channel_id=1, source_target_pairs={{0,16},{16,0},{32,48},{48,32},{64,80},{80,64},{96,112},{112,96},{1... | collective-permute-start | bytes 1966088 | tf_op jit(solution)/shard_map/ppermute | solution.py:411
  30.8 13.4 %collective-permute-start.1 = (bf16[2,64,640]{2,1,0:T(8,128)(2,1)S(1)}, bf16[2,64,640]{2,1,0:T(8,128)(2,1)S(1)}, u32[]{:S(2)}, u32[]{:S(2)}) collective-permute-start(bf16[2,64,640]{2,1,0:T(8,128)(2,1)S(1)} %get-tuple-element.36), channel_id=1, source_target_pairs={{0,32},{16,48},{32,64},{48,80},{64,96},{80,112},{96,128},{112,144}... | collective-permute-start | bytes 491528 | tf_op jit(solution)/shard_map/ppermute | solution.py:416
  32.5 14.1 %collective-permute-start.2 = (bf16[2,64,640]{2,1,0:T(8,128)(2,1)S(1)}, bf16[2,64,640]{2,1,0:T(8,128)(2,1)S(1)}, u32[]{:S(2)}, u32[]{:S(2)}) collective-permute-start(bf16[2,64,640]{2,1,0:T(8,128)(2,1)S(1)} %get-tuple-element.37), channel_id=1, source_target_pairs={{0,64},{16,80},{32,96},{48,112},{64,128},{80,144},{96,160},{112,17... | collective-permute-start | bytes 491528 | tf_op jit(solution)/shard_map/ppermute | solution.py:416
  35.5 23.2 %collective-permute-start.3 = (bf16[2,64,640]{2,1,0:T(8,128)(2,1)S(1)}, bf16[2,64,640]{2,1,0:T(8,128)(2,1)S(1)}, u32[]{:S(2)}, u32[]{:S(2)}) collective-permute-start(bf16[2,64,640]{2,1,0:T(8,128)(2,1)S(1)} %get-tuple-element.38), channel_id=1, source_target_pairs={{0,96},{16,112},{32,128},{48,144},{64,160},{80,176},{96,192},{112,... | collective-permute-start | bytes 491528 | tf_op jit(solution)/shard_map/ppermute | solution.py:416
  39.3 22.2 %collective-permute-start.4 = (bf16[2,64,640]{2,1,0:T(8,128)(2,1)S(1)}, bf16[2,64,640]{2,1,0:T(8,128)(2,1)S(1)}, u32[]{:S(2)}, u32[]{:S(2)}) collective-permute-start(bf16[2,64,640]{2,1,0:T(8,128)(2,1)S(1)} %get-tuple-element.39), channel_id=1, source_target_pairs={{0,128},{16,144},{32,160},{48,176},{64,192},{80,208},{96,224},{112... | collective-permute-start | bytes 491528 | tf_op jit(solution)/shard_map/ppermute | solution.py:416
  39.7 21.7 %collective-permute-start.5 = (bf16[2,64,640]{2,1,0:T(8,128)(2,1)S(1)}, bf16[2,64,640]{2,1,0:T(8,128)(2,1)S(1)}, u32[]{:S(2)}, u32[]{:S(2)}) collective-permute-start(bf16[2,64,640]{2,1,0:T(8,128)(2,1)S(1)} %get-tuple-element.40), channel_id=1, source_target_pairs={{0,160},{16,176},{32,192},{48,208},{64,224},{80,240},{96,0},{112,1... | collective-permute-start | bytes 491528 | tf_op jit(solution)/shard_map/ppermute | solution.py:416
  44.2 25.1 %collective-permute-start.6 = (bf16[2,64,640]{2,1,0:T(8,128)(2,1)S(1)}, bf16[2,64,640]{2,1,0:T(8,128)(2,1)S(1)}, u32[]{:S(2)}, u32[]{:S(2)}) collective-permute-start(bf16[2,64,640]{2,1,0:T(8,128)(2,1)S(1)} %get-tuple-element.41), channel_id=1, source_target_pairs={{0,192},{16,208},{32,224},{48,240},{64,0},{80,16},{96,32},{112,48}... | collective-permute-start | bytes 491528 | tf_op jit(solution)/shard_map/ppermute | solution.py:416
  46.6 23.8 %collective-permute-start.7 = (bf16[2,64,640]{2,1,0:T(8,128)(2,1)S(1)}, bf16[2,64,640]{2,1,0:T(8,128)(2,1)S(1)}, u32[]{:S(2)}, u32[]{:S(2)}) collective-permute-start(bf16[2,64,640]{2,1,0:T(8,128)(2,1)S(1)} %get-tuple-element.42), channel_id=1, source_target_pairs={{0,224},{16,240},{32,0},{48,16},{64,32},{80,48},{96,64},{112,80},{... | collective-permute-start | bytes 491528 | tf_op jit(solution)/shard_map/ppermute | solution.py:416
  151.6 79.7 %collective-permute-start.8 = (bf16[16,1024,256]{2,1,0:T(8,128)(2,1)}, bf16[16,1024,256]{2,1,0:T(8,128)(2,1)}, u32[]{:S(2)}, u32[]{:S(2)}) collective-permute-start(bf16[16,1024,256]{2,1,0:T(8,128)(2,1)} %bitcast.18), channel_id=1, source_target_pairs={{0,16},{16,0},{32,48},{48,32},{64,80},{80,64},{96,112},{112,96},{1... | collective-permute-start | bytes 25165832 | tf_op jit(solution)/shard_map/ppermute | solution.py:411
  174.2 57.1 %copy-start.4 = (bf16[256,1024]{1,0:T(8,128)(2,1)S(1)}, bf16[256,1024]{1,0:T(8,128)(2,1)}, u32[]{:S(2)}) copy-start(bf16[256,1024]{1,0:T(8,128)(2,1)} %cot.1) | copy-start | bytes 1572868
  182.7 65.7 %all-to-all-start.3 = ((bf16[16,64,640]{2,1,0:T(8,128)(2,1)}), bf16[16,64,640]{2,1,0:T(8,128)(2,1)S(1)}, u32[]{:S(2)}, u32[]{:S(2)}) async-start(bf16[16,64,640]{2,1,0:T(8,128)(2,1)} %gradient.1), calls=%async_computation.3 | async-start | bytes 2621440 | tf_op jit(solution)/shard_map/all_to_all | solution.py:407
  231.3 3.4 %copy-start.2 = (bf16[16384,256]{1,0:T(8,128)(2,1)S(1)}, bf16[16384,256]{1,0:T(8,128)(2,1)}, u32[]{:S(2)}) copy-start(bf16[16384,256]{1,0:T(8,128)(2,1)} %all-gather.6.cloned.1.call-done) | copy-start | bytes 25165828
Sparse Core Ops, SparseCore 0:
  12.6 138.9 all-gather.5
  154.6 76.6 all-gather.3

commit v3 on v2

--- a/solution.py
+++ b/solution.py
@@ -67,24 +67,24 @@
     return (row >= begin) & (row < end)
 
 
-def turn_kernel(meta, w, out):
+def turn_kernel(at, w, out):
     out[...] = jnp.transpose(w[...].astype(F32)).astype(BF)
 
 
-def turn(meta, w):
+def turn(at, w):
     piece, width = w.shape
-    half = piece // 2
+    part = piece // 4
     return call(
         turn_kernel,
         "turn",
-        moved=4 * half * width,
+        moved=4 * part * width,
         grid_spec=with_meta(
             (1,),
-            [pl.BlockSpec((half, width), lambda i, m: (m[CORE], 0))],
-            whole((width, half)),
-        ),
-        out_shape=jax.ShapeDtypeStruct((width, half), BF),
-    )(meta, w)
+            [pl.BlockSpec((part, width), lambda i, m: (m[0], 0))],
+            whole((width, part)),
+        ),
+        out_shape=jax.ShapeDtypeStruct((width, part), BF),
+    )(at, w)
 
 
 def pack_kernel(tok, cot_t, out):
@@ -353,7 +353,47 @@
     )(meta, got)
 
 
-def input_kernel(slots, rank, meta, cot, low, mine, other, down, out, lg):
+def base_kernel(meta, cot, mine, near, mine_o, near_o, out):
+    group, _, part = mine.shape
+    even = lax.rem(meta[CHIP], 2) == 0
+    lower = meta[CORE] == 0
+    for g in range(group):
+        w = jnp.concatenate([mine[g], near[g], mine_o[g], near_o[g]], axis=1)
+        r = jnp.dot(cot[...], w, preferred_element_type=F32)
+        r = [r[:, part * q:part * (q + 1)] for q in range(4)]
+        r = [
+            jnp.where(even, r[0], r[1]),
+            jnp.where(even, r[1], r[0]),
+            jnp.where(even, r[2], r[3]),
+            jnp.where(even, r[3], r[2]),
+        ]
+        for q in range(4):
+            at = (4 * g + q) * part
+            out[:, at:at + part] = jnp.where(lower, r[q], r[(q + 2) % 4])
+
+
+def base(meta, cot, mine, near, mine_o, near_o, upper):
+    n, width, part = near.shape
+    rows = cot.shape[0]
+    group = 2
+    skip = n // group if upper else 0
+    spec = pl.BlockSpec((group, width, part), lambda f, m: (f, 0, 0))
+    offset = pl.BlockSpec((group, width, part), lambda f, m: (f + skip, 0, 0))
+    return call(
+        base_kernel,
+        "base",
+        flops=8 * rows * n * part * width,
+        moved=8 * n * part * width + 16 * rows * n * part,
+        grid_spec=with_meta(
+            (n // group,),
+            [whole(cot.shape), offset, spec, offset, spec],
+            pl.BlockSpec((rows, 4 * group * part), lambda f, m: (0, f)),
+        ),
+        out_shape=jax.ShapeDtypeStruct((rows, 4 * n * part), F32),
+    )(meta, cot, mine, near, mine_o, near_o)
+
+
+def input_kernel(slots, rank, meta, low, base_a, base_b, down, out, lg):
     @pl.when(pl.program_id(0) == 0)
     def _():
         both = low[...].astype(F32)
@@ -366,41 +406,41 @@
             keep = inside_pair(meta, p, meta[FIRST], both.shape, slots, rank)
             lg[:, 2 * rank * p:2 * rank * (p + 1)] = jnp.where(keep, half, 0.0).astype(BF)
 
-    lower = meta[CORE] == 0
-    group, _, half = mine.shape
+    group, _, piece = down.shape
+    first = pl.program_id(0) < pl.num_programs(0) // 2
     for g in range(group):
-        at = 2 * g * half
+        cols = slice(g * piece, (g + 1) * piece)
         term = jnp.dot(lg[...], down[g], preferred_element_type=F32)
-        a = jnp.dot(cot[...], mine[g], preferred_element_type=F32)
-        b = jnp.dot(cot[...], other[g], preferred_element_type=F32)
-        out[:, at:at + half] = (jnp.where(lower, a, b) + term[:, :half]).astype(BF)
-        out[:, at + half:at + 2 * half] = (jnp.where(lower, b, a) + term[:, half:]).astype(BF)
-
-
-def input_gradient(meta, cot, low, mine, other, down, slots, rank):
-    n, width, half = mine.shape
-    rows = cot.shape[0]
-    piece = 2 * half
+        out[:, cols] = (term + jnp.where(first, base_a[:, cols], base_b[:, cols])).astype(BF)
+
+
+def input_gradient(meta, low, base_a, base_b, down, slots, rank):
+    n, _, piece = down.shape
+    rows = base_a.shape[0]
     group = 2
+    steps = n // group
     return call(
         functools.partial(input_kernel, slots, rank),
         "input_gradient",
-        flops=2 * rows * n * piece * (width + slots * rank),
-        moved=2 * n * piece * (width + slots * rank + rows),
-        grid_spec=with_meta(
-            (n // group,),
+        flops=2 * rows * n * piece * slots * rank,
+        moved=2 * n * piece * (slots * rank + 3 * rows),
+        grid_spec=with_meta(
+            (steps,),
             [
-                whole(cot.shape),
                 whole(low.shape),
-                pl.BlockSpec((group, width, half), lambda f, m: (f, 0, 0)),
-                pl.BlockSpec((group, width, half), lambda f, m: (f, 0, 0)),
+                pl.BlockSpec(
+                    (rows, group * piece), lambda f, m: (0, jnp.minimum(f, steps // 2 - 1))
+                ),
+                pl.BlockSpec(
+                    (rows, group * piece), lambda f, m: (0, jnp.maximum(f - steps // 2, 0))
+                ),
                 pl.BlockSpec((group, slots * rank, piece), lambda f, m: (f, 0, 0)),
             ],
             pl.BlockSpec((rows, group * piece), lambda f, m: (0, f)),
             [pltpu.VMEM((rows, slots * rank), BF)],
         ),
         out_shape=jax.ShapeDtypeStruct((rows, n * piece), BF),
-    )(meta, cot, low, mine, other, down)
+    )(meta, low, base_a, base_b, down)
 
 
 def exchange(x, axis):
@@ -457,29 +497,37 @@
     scale = (n * rows) ** (-0.5)
     meta = scalars(segment_tenant, segment_lengths, tenant_stored_row, own, rows)
 
+    me = lax.axis_index("dp")
+    quarter = 2 * (me % 2) + me // 2 % 2
+    mine = lax.all_gather(
+        turn(quarter.astype(jnp.int32).reshape(1), value_weight), "fsdp", axis=0
+    )
     parts = exchange(pack(tokens, jnp.swapaxes(cotangent, 0, 1), n), "fsdp")
-    mine = lax.all_gather(turn(meta, value_weight), "fsdp", axis=0)
 
     keep, give = offer(
         meta, jnp.swapaxes(adapter_down_weight, 1, 2), adapter_up_weight, chips, slots
     )
     blocks = merge(meta, keep, swap(give, bins))
     got = [blocks[0]] + [shift(blocks[k], k, bins) for k in range(1, chips)]
-    parts, got = lax.optimization_barrier((parts, got))
+    parts, got, mine = lax.optimization_barrier((parts, got, mine))
     down, down_t, up_t = choose(meta, got, slots, v)
     down_all = lax.all_gather(
         down[:, :, :piece].reshape(slots * rank, piece), "fsdp", axis=0
     )
 
-    low, copies = total(
-        exchange(project(meta, parts, down_t, up_t, rows, slots, rank), "fsdp")
-    )
-    mine, copies = lax.optimization_barrier((mine, copies))
-    other = swap(mine, bins)
-    sent = exchange(
-        gradient(meta, parts, exchange(copies, "fsdp"), bins, slots, rank, v), "dp"
-    )
-    grad = input_gradient(meta, cotangent, low, mine, other, down_all, slots, rank)
+    sums = exchange(project(meta, parts, down_t, up_t, rows, slots, rank), "fsdp")
+    near_a = shift(mine[:n // 2], chips - 1, bins)
+    near_b = shift(mine[n // 2:], 1, bins)
+    mine_o = swap(mine, bins)
+    sums, near_a, near_b, mine_o = lax.optimization_barrier((sums, near_a, near_b, mine_o))
+    low, copies = total(sums)
+    low_all = exchange(copies, "fsdp")
+    near_ao, near_bo = swap(near_a, bins), swap(near_b, bins)
+    low_all, near_ao, near_bo = lax.optimization_barrier((low_all, near_ao, near_bo))
+    sent = exchange(gradient(meta, parts, low_all, bins, slots, rank, v), "dp")
+    base_a = base(meta, cotangent, mine, near_a, mine_o, near_ao, False)
+    base_b = base(meta, cotangent, mine, near_b, mine_o, near_bo, True)
+    grad = input_gradient(meta, low, base_a, base_b, down_all, slots, rank)
     sent, grad = lax.optimization_barrier((sent, grad))
     down_grad, up_grad = collect(meta, sent, own, v, slots, scale)
     return grad, jnp.swapaxes(down_grad, 1, 2), up_grad

time: 258 us -> 270 us (1.047)
  local copies, waits for them, and re-layouts: 12.1 us -> 30.1 us
  waiting for transfers between devices: 102 us -> 87.6 us
  Pallas kernels: 35.5 us -> 41.1 us
    all_gather x1, waiting for transfers between devices: 38.8 us -> 0.01 us  [local(): lax.all_gather(down[:, :, :piece].reshape(slots * rank, piece), 'fsdp', a...]
    ppermute x7 -> x9, waiting for transfers between devices: 19.9 us -> 38.5 us  [shift(): lax.ppermute(x, 'dp', [(i, (i // 2 + k) % chips * 2 + i % 2) for i in ran...]
    unnamed x18 -> x50, local copies, waits for them, and re-layouts: 11 us -> 26.4 us
    all_gather x1, waiting for transfers between devices: 8.7 us -> 18.6 us  [local(): lax.all_gather(turn(quarter.astype(jnp.int32).reshape(1), value_weight),...]
    pallas_call x1 -> x3, Pallas kernels: 1.54 us -> 11.3 us  [the longest x2 10.5 us: base(): call(base_kernel, 'base', flops=8 * rows * n * part * width, moved=8 * n...]
    ppermute x7 -> x9, starting transfers between devices: 19.6 us -> 25.3 us  [shift(): lax.ppermute(x, 'dp', [(i, (i // 2 + k) % chips * 2 + i % 2) for i in ran...]
    all_to_all x2, waiting for transfers between devices: 33.1 us -> 28.6 us  [exchange(): return lax.all_to_all(x, axis, 0, 0, tiled=True)]
    all_to_all x2, starting transfers between devices: 17.6 us -> 13.4 us  [exchange(): return lax.all_to_all(x, axis, 0, 0, tiled=True)]
  transfers between devices with their start and end apart: 13 -> 17, of which waited for: 8 -> 9; matrix products, arithmetic and copies ran while one was open for 1% -> 2% of each run, Pallas kernels for 13% -> 14%
where the time goes in v3:
time: 270 us; the launch traced here: 269 us
  waiting for transfers between devices  87.6 us (32%)
  blocking collectives  53.8 us (20%)
  starting transfers between devices  41.4 us (15%)
  Pallas kernels  41.1 us (15%)
  local copies, waits for them, and re-layouts  30.1 us (11%)
  between operations  14.3 us (5%)
    all_to_all x2, blocking collectives, exchange(): return lax.all_to_all(x, axis, 0, 0, tiled=True)  53.8 us
    ppermute x9, waiting for transfers between devices, shift(): lax.ppermute(x, 'dp', [(i, (i // 2 + k) % chips * 2 + i % 2) for i in ran...  38.5 us
    all_to_all x2, waiting for transfers between devices, exchange(): return lax.all_to_all(x, axis, 0, 0, tiled=True)  28.6 us
    unnamed x50, local copies, waits for them, and re-layouts  26.4 us
    ppermute x9, starting transfers between devices, shift(): lax.ppermute(x, 'dp', [(i, (i // 2 + k) % chips * 2 + i % 2) for i in ran...  25.3 us
    all_gather x1, waiting for transfers between devices, local(): lax.all_gather(turn(quarter.astype(jnp.int32).reshape(1), value_weight),...  18.6 us
    all_to_all x2, starting transfers between devices, exchange(): return lax.all_to_all(x, axis, 0, 0, tiled=True)  13.4 us
    pallas_call x2, Pallas kernels, base(): call(base_kernel, 'base', flops=8 * rows * n * part * width, moved=8 * n...  10.5 us
  transfers between devices with their start and end apart: 17, of which 9 were waited for; matrix products, arithmetic and copies ran while one was open for 2% of the time, Pallas kernels for 14%

profile of v3, /device:TPU:1, one launch (start us, length us, event | category | flops | bytes accessed | tf_op | source)
XLA Modules:
  0.0 269.0 jit_solution(3275485797393785399)
XLA Ops:
  15.7 7.8 %all-to-all-start = ((bf16[16,288,512]{2,1,0:T(8,128)(2,1)}), bf16[16,288,512]{2,1,0:T(8,128)(2,1)}, u32[]{:S(2)}, u32[]{:S(2)}) async-start(bf16[16,288,512]{2,1,0:T(8,128)(2,1)} %copy-done.3), calls=%async_computation | async-start | bytes 9437184 | tf_op jit(solution)/shard_map/all_to_all | solution.py:447
  30.4 3.0 %collective-permute-start.2 = (bf16[2,64,640]{2,1,0:T(8,128)(2,1)S(1)}, bf16[2,64,640]{2,1,0:T(8,128)(2,1)S(1)}, u32[]{:S(2)}, u32[]{:S(2)}) collective-permute-start(bf16[2,64,640]{2,1,0:T(8,128)(2,1)S(1)} %get-tuple-element.43), channel_id=1, source_target_pairs={{0,64},{16,80},{32,96},{48,112},{64,128},{80,144},{96,160},{112,17... | collective-permute-start | bytes 491528 | tf_op jit(solution)/shard_map/ppermute | solution.py:456
  33.4 3.8 %collective-permute-start.3 = (bf16[2,64,640]{2,1,0:T(8,128)(2,1)S(1)}, bf16[2,64,640]{2,1,0:T(8,128)(2,1)S(1)}, u32[]{:S(2)}, u32[]{:S(2)}) collective-permute-start(bf16[2,64,640]{2,1,0:T(8,128)(2,1)S(1)} %get-tuple-element.44), channel_id=1, source_target_pairs={{0,96},{16,112},{32,128},{48,144},{64,160},{80,176},{96,192},{112,... | collective-permute-start | bytes 491528 | tf_op jit(solution)/shard_map/ppermute | solution.py:456
  37.6 4.5 %collective-permute-start.5 = (bf16[2,64,640]{2,1,0:T(8,128)(2,1)S(1)}, bf16[2,64,640]{2,1,0:T(8,128)(2,1)S(1)}, u32[]{:S(2)}, u32[]{:S(2)}) collective-permute-start(bf16[2,64,640]{2,1,0:T(8,128)(2,1)S(1)} %get-tuple-element.46), channel_id=1, source_target_pairs={{0,160},{16,176},{32,192},{48,208},{64,224},{80,240},{96,0},{112,1... | collective-permute-start | bytes 491528 | tf_op jit(solution)/shard_map/ppermute | solution.py:456
  42.1 2.4 collective-permute-start.6
  44.5 3.9 %collective-permute-start.7 = (bf16[2,64,640]{2,1,0:T(8,128)(2,1)S(1)}, bf16[2,64,640]{2,1,0:T(8,128)(2,1)S(1)}, u32[]{:S(2)}, u32[]{:S(2)}) collective-permute-start(bf16[2,64,640]{2,1,0:T(8,128)(2,1)S(1)} %get-tuple-element.48), channel_id=1, source_target_pairs={{0,224},{16,240},{32,0},{48,16},{64,32},{80,48},{96,64},{112,80},{... | collective-permute-start | bytes 491528 | tf_op jit(solution)/shard_map/ppermute | solution.py:456
  48.3 8.3 %collective-permute-done.3.refs_3_ = bf16[2,64,640]{2,1,0:T(8,128)(2,1)S(1)} collective-permute-done((bf16[2,64,640]{2,1,0:T(8,128)(2,1)S(1)}, bf16[2,64,640]{2,1,0:T(8,128)(2,1)S(1)}, u32[]{:S(2)}, u32[]{:S(2)}) %collective-permute-start.3) | collective-permute-done | bytes 163872 | tf_op jit(solution)/shard_map/ppermute | solution.py:456
  56.6 2.7 %collective-permute-done.4.refs_4_ = bf16[2,64,640]{2,1,0:T(8,128)(2,1)S(1)} collective-permute-done((bf16[2,64,640]{2,1,0:T(8,128)(2,1)S(1)}, bf16[2,64,640]{2,1,0:T(8,128)(2,1)S(1)}, u32[]{:S(2)}, u32[]{:S(2)}) %collective-permute-start.4) | collective-permute-done | bytes 163872 | tf_op jit(solution)/shard_map/ppermute | solution.py:456
  59.3 7.9 %collective-permute-done.6.refs_6_ = bf16[2,64,640]{2,1,0:T(8,128)(2,1)S(1)} collective-permute-done((bf16[2,64,640]{2,1,0:T(8,128)(2,1)S(1)}, bf16[2,64,640]{2,1,0:T(8,128)(2,1)S(1)}, u32[]{:S(2)}, u32[]{:S(2)}) %collective-permute-start.6) | collective-permute-done | bytes 163872 | tf_op jit(solution)/shard_map/ppermute | solution.py:456
  68.2 28.6 %all-to-all-done.part = bf16[16,288,512]{2,1,0:T(8,128)(2,1)} async-done(((bf16[16,288,512]{2,1,0:T(8,128)(2,1)}), bf16[16,288,512]{2,1,0:T(8,128)(2,1)}, u32[]{:S(2)}, u32[]{:S(2)}) %all-to-all-start) | async-done | bytes 4718624 | tf_op jit(solution)/shard_map/all_to_all | solution.py:447
  96.9 18.6 %all-gather.6.cloned.1.call-done = bf16[16384,128]{1,0:T(8,128)(2,1)} async-done(((bf16[1024,128]{1,0:T(8,128)(2,1)}), bf16[16384,128]{1,0:T(8,128)(2,1)}) %all-gather.6.cloned.1.call-update) | async-done | bytes 4194320 | tf_op jit(solution)/shard_map/all_gather | solution.py:502
  117.9 2.6 fusion.6
  120.6 5.7 %collective-permute-start.8 = (bf16[8,1024,128]{2,1,0:T(8,128)(2,1)S(1)}, bf16[8,1024,128]{2,1,0:T(8,128)(2,1)S(1)}, u32[]{:S(2)}, u32[]{:S(2)}) collective-permute-start(bf16[8,1024,128]{2,1,0:T(8,128)(2,1)S(1)} %get-tuple-element.76), channel_id=1, source_target_pairs={{0,224},{16,240},{32,0},{48,16},{64,32},{80,48},{96,64},{112,80},{... | collective-permute-start | bytes 6291464 | tf_op jit(solution)/shard_map/ppermute | solution.py:456
  126.2 6.8 %project.1 = bf16[16,256,128]{2,1,0:T(8,128)(2,1)S(1)} custom-call(s32[59]{0:T(128)S(1)} %concatenate.3.meta, bf16[16,288,512]{2,1,0:T(8,128)(2,1)} %all-to-all-done.part, bf16[512,512]{1,0:T(8,128)(2,1)S(1)} %get-tuple-element.58.down_t, bf16[64,512]{1,0:T(8,128)(2,1)S(1)} %get-tuple-element.59.up_t), custom_call_target="tpu_custom_call" | custom-call | flops 2147483648 | bytes 4718592 | tf_op jit(solution)/shard_map/project/pallas_call | solution.py:227
  133.0 22.8 %all_to_all.20.parts = bf16[16,256,128]{2,1,0:T(8,128)(2,1)S(1)} all-to-all(bf16[16,256,128]{2,1,0:T(8,128)(2,1)S(1)} %project.1), channel_id=1, replica_groups=mesh['dp'=16,'fsdp'=16] {'fsdp'}, dimensions={0} | all-to-all | bytes 2097152 | tf_op jit(solution)/shard_map/all_to_all | solution.py:447
  155.8 15.4 %collective-permute-done.8.near = bf16[8,1024,128]{2,1,0:T(8,128)(2,1)S(1)} collective-permute-done((bf16[8,1024,128]{2,1,0:T(8,128)(2,1)S(1)}, bf16[8,1024,128]{2,1,0:T(8,128)(2,1)S(1)}, u32[]{:S(2)}, u32[]{:S(2)}) %collective-permute-start.8) | collective-permute-done | bytes 2097184 | tf_op jit(solution)/shard_map/ppermute | solution.py:456
  171.2 3.2 %collective-permute-done.9.near = bf16[8,1024,128]{2,1,0:T(8,128)(2,1)S(1)} collective-permute-done((bf16[8,1024,128]{2,1,0:T(8,128)(2,1)S(1)}, bf16[8,1024,128]{2,1,0:T(8,128)(2,1)S(1)}, u32[]{:S(2)}, u32[]{:S(2)}) %collective-permute-start.9) | collective-permute-done | bytes 2097184 | tf_op jit(solution)/shard_map/ppermute | solution.py:456
  178.8 31.1 %all_to_all.21.low = bf16[16,128,256]{2,1,0:T(8,128)(2,1)S(1)} all-to-all(bf16[16,128,256]{2,1,0:T(8,128)(2,1)S(1)} %get-tuple-element.62), channel_id=1, replica_groups=mesh['dp'=16,'fsdp'=16] {'fsdp'}, dimensions={0} | all-to-all | bytes 2097152 | tf_op jit(solution)/shard_map/all_to_all | solution.py:447
  212.6 8.2 %gradient.1 = bf16[16,64,640]{2,1,0:T(8,128)(2,1)} custom-call(s32[59]{0:T(128)S(1)} %concatenate.3.meta, bf16[16,288,512]{2,1,0:T(8,128)(2,1)} %all-to-all-done.part, bf16[16,128,256]{2,1,0:T(8,128)(2,1)S(1)} %all_to_all.21.low), custom_call_target="tpu_custom_call" | custom-call | flops 2147483648 | bytes 4718592 | tf_op jit(solution)/shard_map/gradient/pallas_call | solution.py:313
  220.8 5.6 %all-to-all-start.3 = ((bf16[16,64,640]{2,1,0:T(8,128)(2,1)}), bf16[16,64,640]{2,1,0:T(8,128)(2,1)S(1)}, u32[]{:S(2)}, u32[]{:S(2)}) async-start(bf16[16,64,640]{2,1,0:T(8,128)(2,1)} %gradient.1), calls=%async_computation.3 | async-start | bytes 2621440 | tf_op jit(solution)/shard_map/all_to_all | solution.py:447
  231.8 5.4 %base.2.base_a = f32[256,4096]{1,0:T(8,128)S(1)} custom-call(s32[59]{0:T(128)S(1)} %concatenate.3.meta, bf16[256,1024]{1,0:T(8,128)(2,1)S(1)} %copy-done.8, bf16[16,1024,128]{2,1,0:T(8,128)(2,1)S(1)} %bitcast.21, bf16[8,1024,128]{2,1,0:T(8,128)(2,1)S(1)} %copy-done.11, bf16[16,1024,128]{2,1,0:T(8,128)(2,1)} %copy-done.21, bf16[8,1024,128]{2,1,0:T(8,128)(2,1)S(1)} %copy-done.17), custom_call_target="tpu_custom_call" | custom-call | flops 2147483648 | bytes 12582912 | tf_op jit(solution)/shard_map/base/pallas_call | solution.py:382
  239.2 5.1 %base.3.base_b = f32[256,4096]{1,0:T(8,128)S(1)} custom-call(s32[59]{0:T(128)S(1)} %concatenate.3.meta, bf16[256,1024]{1,0:T(8,128)(2,1)S(1)} %copy-done.8, bf16[16,1024,128]{2,1,0:T(8,128)(2,1)S(1)} %bitcast.22, bf16[8,1024,128]{2,1,0:T(8,128)(2,1)S(1)} %copy-done.13, bf16[16,1024,128]{2,1,0:T(8,128)(2,1)} %copy-done.21, bf16[8,1024,128]{2,1,0:T(8,128)(2,1)S(1)} %copy-done.15), custom_call_target="tpu_custom_call" | custom-call | flops 2147483648 | bytes 12582912 | tf_op jit(solution)/shard_map/base/pallas_call | solution.py:382
  246.3 2.2 copy-done.5
  250.7 9.8 %input_gradient.1 = bf16[256,8192]{1,0:T(8,128)(2,1)} custom-call(s32[59]{0:T(128)S(1)} %concatenate.3.meta, bf16[256,128]{1,0:T(8,128)(2,1)S(1)} %get-tuple-element.66.low, f32[256,4096]{1,0:T(8,128)S(1)} %copy-done.5, f32[256,4096]{1,0:T(8,128)S(1)} %copy-done.7, bf16[16,512,512]{2,1,0:T(8,128)(2,1)} %all-gather.4.cloned.1.call-done.down), custom_call_target="tpu_custom_call" | custom-call | flops 2147483648 | bytes 20971520 | tf_op jit(solution)/shard_map/input_gradient/pallas_call | solution.py:422
  (86 shorter events, 39.4 us)
Async XLA Ops:
  7.2 16.3 %copy-start = (s32[16,8]{0,1:T(8,128)S(1)}, s32[16,8]{0,1:T(8,128)}, u32[]{:S(2)}) copy-start(s32[16,8]{0,1:T(8,128)} %param.14) | copy-start | bytes 1540
  7.2 108.3 %all-gather.6.cloned.1.call-start = ((), (), s32[]{:S(2)}) async-start(), calls=%async_computation.5 | async-start | bytes 4456448 | tf_op jit(solution)/shard_map/all_gather | solution.py:502
  15.6 8.2 %copy-start.22 = (s32[16,8]{0,1:T(8,128)S(1)}, s32[16,8]{0,1:T(8,128)}, u32[]{:S(2)}) copy-start(s32[16,8]{0,1:T(8,128)} %param.13) | copy-start | bytes 1540
  15.6 8.2 %copy-start.23 = (s32[64]{0:T(128)S(1)}, s32[64]{0:T(128)}, u32[]{:S(2)}) copy-start(s32[64]{0:T(128)} %param.15) | copy-start | bytes 772
  15.6 8.9 %copy-start.19 = (bf16[4,512,64]{1,2,0:T(8,128)(2,1)S(1)}, bf16[4,512,64]{1,2,0:T(8,128)(2,1)}, u32[]{:S(2)}) copy-start(bf16[4,512,64]{1,2,0:T(8,128)(2,1)} %param.11) | copy-start | bytes 786436
  15.6 8.9 %copy-start.20 = (bf16[4,64,64]{2,1,0:T(8,128)(2,1)S(1)}, bf16[4,64,64]{2,1,0:T(8,128)(2,1)}, u32[]{:S(2)}) copy-start(bf16[4,64,64]{2,1,0:T(8,128)(2,1)} %up.1) | copy-start | bytes 98308
  15.7 81.2 %all-to-all-start = ((bf16[16,288,512]{2,1,0:T(8,128)(2,1)}), bf16[16,288,512]{2,1,0:T(8,128)(2,1)}, u32[]{:S(2)}, u32[]{:S(2)}) async-start(bf16[16,288,512]{2,1,0:T(8,128)(2,1)} %copy-done.3), calls=%async_computation | async-start | bytes 9437184 | tf_op jit(solution)/shard_map/all_to_all | solution.py:447
  23.4 222.9 %all-gather.4.cloned.1.call-start = ((), (), s32[]{:S(2)}) async-start(), calls=%async_computation.4 | async-start | bytes 8912896 | tf_op jit(solution)/shard_map/all_gather | solution.py:514
  25.3 2.8 %collective-permute-start = (bf16[8,64,640]{2,1,0:T(8,128)(2,1)S(1)}, bf16[8,64,640]{2,1,0:T(8,128)(2,1)S(1)}, u32[]{:S(2)}, u32[]{:S(2)}) collective-permute-start(bf16[8,64,640]{2,1,0:T(8,128)(2,1)S(1)} %get-tuple-element.40), channel_id=1, source_target_pairs={{0,16},{16,0},{32,48},{48,32},{64,80},{80,64},{96,112},{112,96},{1... | collective-permute-start | bytes 1966088 | tf_op jit(solution)/shard_map/ppermute | solution.py:451
  28.7 13.4 %collective-permute-start.1 = (bf16[2,64,640]{2,1,0:T(8,128)(2,1)S(1)}, bf16[2,64,640]{2,1,0:T(8,128)(2,1)S(1)}, u32[]{:S(2)}, u32[]{:S(2)}) collective-permute-start(bf16[2,64,640]{2,1,0:T(8,128)(2,1)S(1)} %get-tuple-element.42), channel_id=1, source_target_pairs={{0,32},{16,48},{32,64},{48,80},{64,96},{80,112},{96,128},{112,144}... | collective-permute-start | bytes 491528 | tf_op jit(solution)/shard_map/ppermute | solution.py:456
  30.4 14.1 %collective-permute-start.2 = (bf16[2,64,640]{2,1,0:T(8,128)(2,1)S(1)}, bf16[2,64,640]{2,1,0:T(8,128)(2,1)S(1)}, u32[]{:S(2)}, u32[]{:S(2)}) collective-permute-start(bf16[2,64,640]{2,1,0:T(8,128)(2,1)S(1)} %get-tuple-element.43), channel_id=1, source_target_pairs={{0,64},{16,80},{32,96},{48,112},{64,128},{80,144},{96,160},{112,17... | collective-permute-start | bytes 491528 | tf_op jit(solution)/shard_map/ppermute | solution.py:456
  33.4 23.2 %collective-permute-start.3 = (bf16[2,64,640]{2,1,0:T(8,128)(2,1)S(1)}, bf16[2,64,640]{2,1,0:T(8,128)(2,1)S(1)}, u32[]{:S(2)}, u32[]{:S(2)}) collective-permute-start(bf16[2,64,640]{2,1,0:T(8,128)(2,1)S(1)} %get-tuple-element.44), channel_id=1, source_target_pairs={{0,96},{16,112},{32,128},{48,144},{64,160},{80,176},{96,192},{112,... | collective-permute-start | bytes 491528 | tf_op jit(solution)/shard_map/ppermute | solution.py:456
  37.2 22.2 %collective-permute-start.4 = (bf16[2,64,640]{2,1,0:T(8,128)(2,1)S(1)}, bf16[2,64,640]{2,1,0:T(8,128)(2,1)S(1)}, u32[]{:S(2)}, u32[]{:S(2)}) collective-permute-start(bf16[2,64,640]{2,1,0:T(8,128)(2,1)S(1)} %get-tuple-element.45), channel_id=1, source_target_pairs={{0,128},{16,144},{32,160},{48,176},{64,192},{80,208},{96,224},{112... | collective-permute-start | bytes 491528 | tf_op jit(solution)/shard_map/ppermute | solution.py:456
  37.6 21.7 %collective-permute-start.5 = (bf16[2,64,640]{2,1,0:T(8,128)(2,1)S(1)}, bf16[2,64,640]{2,1,0:T(8,128)(2,1)S(1)}, u32[]{:S(2)}, u32[]{:S(2)}) collective-permute-start(bf16[2,64,640]{2,1,0:T(8,128)(2,1)S(1)} %get-tuple-element.46), channel_id=1, source_target_pairs={{0,160},{16,176},{32,192},{48,208},{64,224},{80,240},{96,0},{112,1... | collective-permute-start | bytes 491528 | tf_op jit(solution)/shard_map/ppermute | solution.py:456
  42.1 25.1 %collective-permute-start.6 = (bf16[2,64,640]{2,1,0:T(8,128)(2,1)S(1)}, bf16[2,64,640]{2,1,0:T(8,128)(2,1)S(1)}, u32[]{:S(2)}, u32[]{:S(2)}) collective-permute-start(bf16[2,64,640]{2,1,0:T(8,128)(2,1)S(1)} %get-tuple-element.47), channel_id=1, source_target_pairs={{0,192},{16,208},{32,224},{48,240},{64,0},{80,16},{96,32},{112,48}... | collective-permute-start | bytes 491528 | tf_op jit(solution)/shard_map/ppermute | solution.py:456
  44.5 23.8 %collective-permute-start.7 = (bf16[2,64,640]{2,1,0:T(8,128)(2,1)S(1)}, bf16[2,64,640]{2,1,0:T(8,128)(2,1)S(1)}, u32[]{:S(2)}, u32[]{:S(2)}) collective-permute-start(bf16[2,64,640]{2,1,0:T(8,128)(2,1)S(1)} %get-tuple-element.48), channel_id=1, source_target_pairs={{0,224},{16,240},{32,0},{48,16},{64,32},{80,48},{96,64},{112,80},{... | collective-permute-start | bytes 491528 | tf_op jit(solution)/shard_map/ppermute | solution.py:456
  117.4 57.0 %collective-permute-start.10 = (bf16[16,1024,128]{2,1,0:T(8,128)(2,1)}, bf16[16,1024,128]{2,1,0:T(8,128)(2,1)S(1)}, u32[]{:S(2)}, u32[]{:S(2)}) collective-permute-start(bf16[16,1024,128]{2,1,0:T(8,128)(2,1)} %bitcast.19), channel_id=1, source_target_pairs={{0,16},{16,0},{32,48},{48,32},{64,80},{80,64},{96,112},{112,96},{1... | collective-permute-start | bytes 12582920 | tf_op jit(solution)/shard_map/ppermute | solution.py:451
  120.6 50.7 %collective-permute-start.8 = (bf16[8,1024,128]{2,1,0:T(8,128)(2,1)S(1)}, bf16[8,1024,128]{2,1,0:T(8,128)(2,1)S(1)}, u32[]{:S(2)}, u32[]{:S(2)}) collective-permute-start(bf16[8,1024,128]{2,1,0:T(8,128)(2,1)S(1)} %get-tuple-element.76), channel_id=1, source_target_pairs={{0,224},{16,240},{32,0},{48,16},{64,32},{80,48},{96,64},{112,80},{... | collective-permute-start | bytes 6291464 | tf_op jit(solution)/shard_map/ppermute | solution.py:456
  126.2 48.2 %collective-permute-start.9 = (bf16[8,1024,128]{2,1,0:T(8,128)(2,1)S(1)}, bf16[8,1024,128]{2,1,0:T(8,128)(2,1)S(1)}, u32[]{:S(2)}, u32[]{:S(2)}) collective-permute-start(bf16[8,1024,128]{2,1,0:T(8,128)(2,1)S(1)} %get-tuple-element.75), channel_id=1, source_target_pairs={{0,32},{16,48},{32,64},{48,80},{64,96},{80,112},{96,128},{112,144}... | collective-permute-start | bytes 6291464 | tf_op jit(solution)/shard_map/ppermute | solution.py:456
  174.4 35.4 %collective-permute-start.11 = (bf16[8,1024,128]{2,1,0:T(8,128)(2,1)S(1)}, bf16[8,1024,128]{2,1,0:T(8,128)(2,1)S(1)}, u32[]{:S(2)}, u32[]{:S(2)}) collective-permute-start(bf16[8,1024,128]{2,1,0:T(8,128)(2,1)S(1)} %collective-permute-done.8.near), channel_id=1, source_target_pairs={{0,16},{16,0},{32,48},{48,32},{64,80},{80,64},{96,112},{112,96},{1... | collective-permute-start | bytes 6291464 | tf_op jit(solution)/shard_map/ppermute | solution.py:451
  177.1 34.1 %collective-permute-start.12 = (bf16[8,1024,128]{2,1,0:T(8,128)(2,1)S(1)}, bf16[8,1024,128]{2,1,0:T(8,128)(2,1)S(1)}, u32[]{:S(2)}, u32[]{:S(2)}) collective-permute-start(bf16[8,1024,128]{2,1,0:T(8,128)(2,1)S(1)} %collective-permute-done.9.near), channel_id=1, source_target_pairs={{0,16},{16,0},{32,48},{48,32},{64,80},{80,64},{96,112},{112,96},{1... | collective-permute-start | bytes 6291464 | tf_op jit(solution)/shard_map/ppermute | solution.py:451
  209.8 16.6 %copy-start.8 = (bf16[256,1024]{1,0:T(8,128)(2,1)S(1)}, bf16[256,1024]{1,0:T(8,128)(2,1)}, u32[]{:S(2)}) copy-start(bf16[256,1024]{1,0:T(8,128)(2,1)} %cot.3) | copy-start | bytes 1572868
  220.8 39.7 %all-to-all-start.3 = ((bf16[16,64,640]{2,1,0:T(8,128)(2,1)}), bf16[16,64,640]{2,1,0:T(8,128)(2,1)S(1)}, u32[]{:S(2)}, u32[]{:S(2)}) async-start(bf16[16,64,640]{2,1,0:T(8,128)(2,1)} %gradient.1), calls=%async_computation.3 | async-start | bytes 2621440 | tf_op jit(solution)/shard_map/all_to_all | solution.py:447
  250.7 11.4 %copy-start.1 = (s32[16,8]{0,1:T(8,128)S(1)}, s32[16,8]{0,1:T(8,128)}, u32[]{:S(2)}) copy-start(s32[16,8]{0,1:T(8,128)} %param.14) | copy-start | bytes 1540
  (17 other events, 44.2 us)
Sparse Core Ops, SparseCore 0:
  11.0 104.4 all-gather.5
  118.5 95.0 all-gather.3

commit v4 on v2

--- a/solution.py
+++ b/solution.py
@@ -11,14 +11,16 @@
 BF = jnp.bfloat16
 F32 = jnp.float32
 VMEM_BYTES = 40 * 1024 * 1024
+VMEM_MOST = 58 * 1024 * 1024
+WINDOW = 4
 GROUP = 4
 CORE, FIRST, CHIP, LIST = 0, 1, 2, 3
 
 
-def call(kernel, name, flops=0, moved=0, **kw):
+def call(kernel, name, flops=0, moved=0, vmem=VMEM_BYTES, **kw):
     return pl.pallas_call(
         kernel,
-        compiler_params=pltpu.CompilerParams(vmem_limit_bytes=VMEM_BYTES),
+        compiler_params=pltpu.CompilerParams(vmem_limit_bytes=vmem),
         cost_estimate=pl.CostEstimate(flops=flops, bytes_accessed=moved, transcendentals=0),
         name=name,
         **kw,
@@ -67,24 +69,24 @@
     return (row >= begin) & (row < end)
 
 
-def turn_kernel(meta, w, out):
+def turn_kernel(at, w, out):
     out[...] = jnp.transpose(w[...].astype(F32)).astype(BF)
 
 
-def turn(meta, w):
+def turn(at, w, slices):
     piece, width = w.shape
-    half = piece // 2
+    part = width // slices
     return call(
         turn_kernel,
         "turn",
-        moved=4 * half * width,
+        moved=4 * part * piece,
         grid_spec=with_meta(
             (1,),
-            [pl.BlockSpec((half, width), lambda i, m: (m[CORE], 0))],
-            whole((width, half)),
-        ),
-        out_shape=jax.ShapeDtypeStruct((width, half), BF),
-    )(meta, w)
+            [pl.BlockSpec((piece, part), lambda i, m: (0, m[0]))],
+            whole((part, piece)),
+        ),
+        out_shape=jax.ShapeDtypeStruct((part, piece), BF),
+    )(at, w)
 
 
 def pack_kernel(tok, cot_t, out):
@@ -105,6 +107,7 @@
         pack_kernel,
         "pack",
         moved=4 * rows * width,
+        vmem=VMEM_MOST,
         grid=(n // GROUP,),
         in_specs=[
             pl.BlockSpec((rows, GROUP * piece), lambda f: (0, f)),
@@ -353,9 +356,62 @@
     )(meta, got)
 
 
-def input_kernel(slots, rank, meta, cot, low, mine, other, down, out, lg):
+def slice_columns(cot, meta, step, core, part):
+    chip = lax.rem(meta[CHIP] + step + WINDOW, WINDOW)
+    at = pl.multiple_of((2 * chip + core) * part, part)
+    return cot[:, pl.ds(at, part)]
+
+
+def base_kernel(steps, meta, cot, *refs):
+    slices, (out, lhs) = refs[:-2], refs[-2:]
+    group, part, piece = slices[0].shape
+
     @pl.when(pl.program_id(0) == 0)
     def _():
+        for k, step in enumerate(steps):
+            for j in range(2):
+                core = meta[CORE] if j == 0 else 1 - meta[CORE]
+                at = (2 * k + j) * part
+                lhs[:, at:at + part] = slice_columns(cot, meta, step, core, part)
+
+    for g in range(group):
+        w = jnp.concatenate([x[g] for x in slices], axis=0)
+        out[:, g * piece:(g + 1) * piece] = jnp.dot(
+            lhs[...], w, preferred_element_type=F32
+        )
+
+
+def base(meta, cot, steps, slices):
+    n, part, piece = slices[0].shape
+    rows = cot.shape[0]
+    group = 2
+    return call(
+        functools.partial(base_kernel, steps),
+        "base",
+        flops=2 * rows * n * part * piece * len(slices),
+        moved=2 * n * part * piece * len(slices) + 4 * rows * n * piece,
+        vmem=VMEM_MOST,
+        grid_spec=with_meta(
+            (n // group,),
+            [whole(cot.shape)]
+            + [pl.BlockSpec((group, part, piece), lambda f, m: (f, 0, 0))] * len(slices),
+            pl.BlockSpec((rows, group * piece), lambda f, m: (0, f)),
+            [pltpu.VMEM((rows, part * len(slices)), BF)],
+        ),
+        out_shape=jax.ShapeDtypeStruct((rows, n * piece), F32),
+    )(meta, cot, *slices)
+
+
+def input_kernel(slots, rank, meta, low, cot, done, table, *refs):
+    far, (out, lhs) = refs[:-2], refs[-2:]
+    group, part, piece = far[0].shape
+    quarters = len(far) // 2
+    each = pl.num_programs(0) // quarters
+
+    @pl.when(pl.program_id(0) == 0)
+    def _():
+        lhs[:, :part] = slice_columns(cot, meta, WINDOW // 2, meta[CORE], part)
+        lhs[:, part:2 * part] = slice_columns(cot, meta, WINDOW // 2, 1 - meta[CORE], part)
         both = low[...].astype(F32)
         half = jnp.where(
             lax.broadcasted_iota(jnp.int32, both.shape, 1) < rank,
@@ -364,43 +420,56 @@
         )
         for p in range(slots // 2):
             keep = inside_pair(meta, p, meta[FIRST], both.shape, slots, rank)
-            lg[:, 2 * rank * p:2 * rank * (p + 1)] = jnp.where(keep, half, 0.0).astype(BF)
-
-    lower = meta[CORE] == 0
-    group, _, half = mine.shape
-    for g in range(group):
-        at = 2 * g * half
-        term = jnp.dot(lg[...], down[g], preferred_element_type=F32)
-        a = jnp.dot(cot[...], mine[g], preferred_element_type=F32)
-        b = jnp.dot(cot[...], other[g], preferred_element_type=F32)
-        out[:, at:at + half] = (jnp.where(lower, a, b) + term[:, :half]).astype(BF)
-        out[:, at + half:at + 2 * half] = (jnp.where(lower, b, a) + term[:, half:]).astype(BF)
-
-
-def input_gradient(meta, cot, low, mine, other, down, slots, rank):
-    n, width, half = mine.shape
+            at = 2 * part + 2 * rank * p
+            lhs[:, at:at + 2 * rank] = jnp.where(keep, half, 0.0).astype(BF)
+
+    def add(mine, other):
+        for g in range(group):
+            cols = slice(g * piece, (g + 1) * piece)
+            w = jnp.concatenate([mine[g], other[g], table[g]], axis=0)
+            term = jnp.dot(lhs[...], w, preferred_element_type=F32)
+            out[:, cols] = (done[:, cols] + term).astype(BF)
+
+    for q in range(quarters):
+        pl.when(pl.program_id(0) // each == q)(
+            functools.partial(add, far[q], far[quarters + q])
+        )
+
+
+def input_gradient(meta, low, cot, done, table, far, far_o, slots, rank):
+    n, _, piece = table.shape
+    part = far[0].shape[1]
     rows = cot.shape[0]
-    piece = 2 * half
     group = 2
+    steps = n // group
+    each = steps // len(far)
+
+    def quarter(q):
+        return pl.BlockSpec(
+            (group, part, piece),
+            lambda f, m: (jnp.clip(f - q * each, 0, each - 1), 0, 0),
+        )
+
     return call(
         functools.partial(input_kernel, slots, rank),
         "input_gradient",
-        flops=2 * rows * n * piece * (width + slots * rank),
-        moved=2 * n * piece * (width + slots * rank + rows),
-        grid_spec=with_meta(
-            (n // group,),
+        flops=2 * rows * n * piece * (slots * rank + 2 * part),
+        moved=2 * n * piece * (slots * rank + 2 * part + 3 * rows),
+        vmem=VMEM_MOST,
+        grid_spec=with_meta(
+            (steps,),
             [
+                whole(low.shape),
                 whole(cot.shape),
-                whole(low.shape),
-                pl.BlockSpec((group, width, half), lambda f, m: (f, 0, 0)),
-                pl.BlockSpec((group, width, half), lambda f, m: (f, 0, 0)),
+                pl.BlockSpec((rows, group * piece), lambda f, m: (0, f)),
                 pl.BlockSpec((group, slots * rank, piece), lambda f, m: (f, 0, 0)),
-            ],
+            ]
+            + [quarter(q) for q in range(len(far))] * 2,
             pl.BlockSpec((rows, group * piece), lambda f, m: (0, f)),
-            [pltpu.VMEM((rows, slots * rank), BF)],
+            [pltpu.VMEM((rows, slots * rank + 2 * part), BF)],
         ),
         out_shape=jax.ShapeDtypeStruct((rows, n * piece), BF),
-    )(meta, cot, low, mine, other, down)
+    )(meta, low, cot, done, table, *far, *far_o)
 
 
 def exchange(x, axis):
@@ -457,29 +526,43 @@
     scale = (n * rows) ** (-0.5)
     meta = scalars(segment_tenant, segment_lengths, tenant_stored_row, own, rows)
 
+    me = lax.axis_index("dp")
+    at = 2 * (me // 2 % WINDOW) + me % 2
+    mine = lax.all_gather(
+        turn(at.astype(jnp.int32).reshape(1), value_weight, 2 * WINDOW), "fsdp", axis=0
+    )
     parts = exchange(pack(tokens, jnp.swapaxes(cotangent, 0, 1), n), "fsdp")
-    mine = lax.all_gather(turn(meta, value_weight), "fsdp", axis=0)
 
     keep, give = offer(
         meta, jnp.swapaxes(adapter_down_weight, 1, 2), adapter_up_weight, chips, slots
     )
     blocks = merge(meta, keep, swap(give, bins))
     got = [blocks[0]] + [shift(blocks[k], k, bins) for k in range(1, chips)]
-    parts, got = lax.optimization_barrier((parts, got))
+    parts, got, mine = lax.optimization_barrier((parts, got, mine))
     down, down_t, up_t = choose(meta, got, slots, v)
-    down_all = lax.all_gather(
-        down[:, :, :piece].reshape(slots * rank, piece), "fsdp", axis=0
-    )
-
-    low, copies = total(
-        exchange(project(meta, parts, down_t, up_t, rows, slots, rank), "fsdp")
-    )
-    mine, copies = lax.optimization_barrier((mine, copies))
-    other = swap(mine, bins)
-    sent = exchange(
-        gradient(meta, parts, exchange(copies, "fsdp"), bins, slots, rank, v), "dp"
-    )
-    grad = input_gradient(meta, cotangent, low, mine, other, down_all, slots, rank)
+    table = lax.all_gather(down[:, :, :piece].reshape(slots * rank, piece), "fsdp", axis=0)
+
+    above, below = shift(mine, chips - 1, bins), shift(mine, 1, bins)
+    sums = exchange(project(meta, parts, down_t, up_t, rows, slots, rank), "fsdp")
+    sums, above, below = lax.optimization_barrier((sums, above, below))
+    low, copies = total(sums)
+    part = n // 4
+    far = [
+        shift(mine[q * part:(q + 1) * part], chips - 2 if q < 2 else 2, bins) for q in range(4)
+    ]
+    mine_o, above_o, below_o = swap(mine, bins), swap(above, bins), swap(below, bins)
+    low_all = exchange(copies, "fsdp")
+    low_all, mine_o, above_o, below_o, far[0], far[2] = lax.optimization_barrier(
+        (low_all, mine_o, above_o, below_o, far[0], far[2])
+    )
+    due = gradient(meta, parts, low_all, bins, slots, rank, v)
+    sent = exchange(due, "dp")
+    done = base(
+        meta, cotangent, (0, 1, -1), [mine, mine_o, above, above_o, below, below_o]
+    )
+    far[1], far[3], _ = lax.optimization_barrier((far[1], far[3], due))
+    far_o = [swap(x, bins) for x in far]
+    grad = input_gradient(meta, low, cotangent, done, table, far, far_o, slots, rank)
     sent, grad = lax.optimization_barrier((sent, grad))
     down_grad, up_grad = collect(meta, sent, own, v, slots, scale)
     return grad, jnp.swapaxes(down_grad, 1, 2), up_grad

time: 258 us -> 308 us (1.19)
  waiting for transfers between devices: 102 us -> 172 us
  blocking collectives: 52.4 us -> 0 us
  starting transfers between devices: 39 us -> 58.9 us
  Pallas kernels: 35.5 us -> 53.3 us
  local copies, waits for them, and re-layouts: 12.1 us -> 7.67 us
    ppermute x7 -> x13, waiting for transfers between devices: 19.9 us -> 107 us  [shift(): lax.ppermute(x, 'dp', [(i, (i // 2 + k) % chips * 2 + i % 2) for i in ran...]
    all_to_all x2 -> x0, blocking collectives: 52.4 us -> none  [exchange(): return lax.all_to_all(x, axis, 0, 0, tiled=True)]
    all_gather x1, waiting for transfers between devices: 38.8 us -> 0.01 us  [local(): lax.all_gather(down[:, :, :piece].reshape(slots * rank, piece), 'fsdp', a...]
    all_gather x1, waiting for transfers between devices: 8.7 us -> 43.1 us  [local(): lax.all_gather(turn(at.astype(jnp.int32).reshape(1), value_weight, 2 * WI...]
    pallas_call x2 -> x3, Pallas kernels: 2.23 us -> 18.5 us  [the longest x1 12.7 us: base(): call(functools.partial(base_kernel, steps), 'base', flops=2 * rows * n *...]
    all_to_all x2 -> x4, waiting for transfers between devices: 33.1 us -> 20.4 us  [exchange(): return lax.all_to_all(x, axis, 0, 0, tiled=True)]
    ppermute x7 -> x13, starting transfers between devices: 19.6 us -> 28.7 us  [shift(): lax.ppermute(x, 'dp', [(i, (i // 2 + k) % chips * 2 + i % 2) for i in ran...]
    ppermute x2 -> x8, starting transfers between devices: 1.72 us -> 7.47 us  [swap(): return lax.ppermute(x, 'dp', [(i, i ^ 1) for i in range(bins)])]
  transfers between devices with their start and end apart: 13 -> 27, of which waited for: 8 -> 12; matrix products, arithmetic and copies ran while one was open for 1% -> 1% of each run, Pallas kernels for 13% -> 15%
where the time goes in v4:
time: 308 us; the launch traced here: 307 us
  waiting for transfers between devices  172 us (56%)
  starting transfers between devices  58.9 us (19%)
  Pallas kernels  53.3 us (17%)
  between operations  14.3 us (5%)
  local copies, waits for them, and re-layouts  7.67 us (2%)
    ppermute x13, waiting for transfers between devices, shift(): lax.ppermute(x, 'dp', [(i, (i // 2 + k) % chips * 2 + i % 2) for i in ran...  107 us
    all_gather x1, waiting for transfers between devices, local(): lax.all_gather(turn(at.astype(jnp.int32).reshape(1), value_weight, 2 * WI...  43.1 us
    ppermute x13, starting transfers between devices, shift(): lax.ppermute(x, 'dp', [(i, (i // 2 + k) % chips * 2 + i % 2) for i in ran...  28.7 us
    all_to_all x4, starting transfers between devices, exchange(): return lax.all_to_all(x, axis, 0, 0, tiled=True)  22.7 us
    all_to_all x4, waiting for transfers between devices, exchange(): return lax.all_to_all(x, axis, 0, 0, tiled=True)  20.4 us
    pallas_call x1, Pallas kernels, input_gradient(): call(functools.partial(input_kernel, slots, rank), 'input_gradient', flop...  13.6 us
    pallas_call x1, Pallas kernels, base(): call(functools.partial(base_kernel, steps), 'base', flops=2 * rows * n *...  12.7 us
    pallas_call x1, Pallas kernels, gradient(): call(functools.partial(gradient_kernel, slots, rank, v), 'gradient', flop...  8.43 us
  transfers between devices with their start and end apart: 27, of which 12 were waited for; matrix products, arithmetic and copies ran while one was open for 1% of the time, Pallas kernels for 15%

profile of v4, /device:TPU:1, one launch (start us, length us, event | category | flops | bytes accessed | tf_op | source)
XLA Modules:
  0.0 307.1 jit_solution(13174357582038583720)
XLA Ops:
  9.2 5.0 %pack.1 = bf16[16,288,512]{2,1,0:T(8,128)(2,1)} custom-call(bf16[256,8192]{1,0:T(8,128)(2,1)} %tok.1, bf16[1024,256]{1,0:T(8,128)(2,1)} %bitcast.25), custom_call_target="tpu_custom_call" | custom-call | bytes 8388608 | tf_op jit(solution)/shard_map/pack/pallas_call | solution.py:106
  14.3 7.8 %all-to-all-start = ((bf16[16,288,512]{2,1,0:T(8,128)(2,1)}), bf16[16,288,512]{2,1,0:T(8,128)(2,1)}, u32[]{:S(2)}, u32[]{:S(2)}) async-start(bf16[16,288,512]{2,1,0:T(8,128)(2,1)} %pack.1), calls=%async_computation | async-start | bytes 9437184 | tf_op jit(solution)/shard_map/all_to_all | solution.py:476
  29.9 3.0 collective-permute-start.2
  32.9 3.8 %collective-permute-start.3 = (bf16[2,64,640]{2,1,0:T(8,128)(2,1)S(1)}, bf16[2,64,640]{2,1,0:T(8,128)(2,1)S(1)}, u32[]{:S(2)}, u32[]{:S(2)}) collective-permute-start(bf16[2,64,640]{2,1,0:T(8,128)(2,1)S(1)} %get-tuple-element.48), channel_id=1, source_target_pairs={{0,96},{16,112},{32,128},{48,144},{64,160},{80,176},{96,192},{112,... | collective-permute-start | bytes 491528 | tf_op jit(solution)/shard_map/ppermute | solution.py:485
  37.1 4.5 %collective-permute-start.5 = (bf16[2,64,640]{2,1,0:T(8,128)(2,1)S(1)}, bf16[2,64,640]{2,1,0:T(8,128)(2,1)S(1)}, u32[]{:S(2)}, u32[]{:S(2)}) collective-permute-start(bf16[2,64,640]{2,1,0:T(8,128)(2,1)S(1)} %get-tuple-element.50), channel_id=1, source_target_pairs={{0,160},{16,176},{32,192},{48,208},{64,224},{80,240},{96,0},{112,1... | collective-permute-start | bytes 491528 | tf_op jit(solution)/shard_map/ppermute | solution.py:485
  44.0 3.9 %collective-permute-start.7 = (bf16[2,64,640]{2,1,0:T(8,128)(2,1)S(1)}, bf16[2,64,640]{2,1,0:T(8,128)(2,1)S(1)}, u32[]{:S(2)}, u32[]{:S(2)}) collective-permute-start(bf16[2,64,640]{2,1,0:T(8,128)(2,1)S(1)} %get-tuple-element.52), channel_id=1, source_target_pairs={{0,224},{16,240},{32,0},{48,16},{64,32},{80,48},{96,64},{112,80},{... | collective-permute-start | bytes 491528 | tf_op jit(solution)/shard_map/ppermute | solution.py:485
  47.9 8.2 %collective-permute-done.3.refs_3_ = bf16[2,64,640]{2,1,0:T(8,128)(2,1)S(1)} collective-permute-done((bf16[2,64,640]{2,1,0:T(8,128)(2,1)S(1)}, bf16[2,64,640]{2,1,0:T(8,128)(2,1)S(1)}, u32[]{:S(2)}, u32[]{:S(2)}) %collective-permute-start.3) | collective-permute-done | bytes 163872 | tf_op jit(solution)/shard_map/ppermute | solution.py:485
  58.9 7.8 %collective-permute-done.6.refs_6_ = bf16[2,64,640]{2,1,0:T(8,128)(2,1)S(1)} collective-permute-done((bf16[2,64,640]{2,1,0:T(8,128)(2,1)S(1)}, bf16[2,64,640]{2,1,0:T(8,128)(2,1)S(1)}, u32[]{:S(2)}, u32[]{:S(2)}) %collective-permute-start.6) | collective-permute-done | bytes 163872 | tf_op jit(solution)/shard_map/ppermute | solution.py:485
  67.8 43.1 %all-gather.6.cloned.1.call-done = bf16[2048,512]{1,0:T(8,128)(2,1)} async-done(((bf16[128,512]{1,0:T(8,128)(2,1)}), bf16[2048,512]{1,0:T(8,128)(2,1)}) %all-gather.6.cloned.1.call-update) | async-done | bytes 2097168 | tf_op jit(solution)/shard_map/all_gather | solution.py:531
  112.7 3.1 %collective-permute-start.8 = (bf16[16,128,512]{2,1,0:T(8,128)(2,1)}, bf16[16,128,512]{2,1,0:T(8,128)(2,1)}, u32[]{:S(2)}, u32[]{:S(2)}) collective-permute-start(bf16[16,128,512]{2,1,0:T(8,128)(2,1)} %bitcast.20), channel_id=1, source_target_pairs={{0,224},{16,240},{32,0},{48,16},{64,32},{80,48},{96,64},{112,80},{... | collective-permute-start | bytes 6291464 | tf_op jit(solution)/shard_map/ppermute | solution.py:485
  115.9 7.6 %project.1 = bf16[16,256,128]{2,1,0:T(8,128)(2,1)} custom-call(s32[59]{0:T(128)S(1)} %concatenate.3.meta, bf16[16,288,512]{2,1,0:T(8,128)(2,1)} %all-to-all-done.part, bf16[512,512]{1,0:T(8,128)(2,1)S(1)} %get-tuple-element.62.down_t, bf16[64,512]{1,0:T(8,128)(2,1)S(1)} %get-tuple-element.63.up_t), custom_call_target="tpu_custom_call" | custom-call | flops 2147483648 | bytes 4718592 | tf_op jit(solution)/shard_map/project/pallas_call | solution.py:230
  123.4 4.8 %all-to-all-start.1 = ((bf16[16,256,128]{2,1,0:T(8,128)(2,1)}), bf16[16,256,128]{2,1,0:T(8,128)(2,1)S(1)}, u32[]{:S(2)}, u32[]{:S(2)}) async-start(bf16[16,256,128]{2,1,0:T(8,128)(2,1)} %project.1), calls=%async_computation.1 | async-start | bytes 2097152 | tf_op jit(solution)/shard_map/all_to_all | solution.py:476
  130.4 20.4 %all-to-all-done.1.parts = bf16[16,256,128]{2,1,0:T(8,128)(2,1)S(1)} async-done(((bf16[16,256,128]{2,1,0:T(8,128)(2,1)}), bf16[16,256,128]{2,1,0:T(8,128)(2,1)S(1)}, u32[]{:S(2)}, u32[]{:S(2)}) %all-to-all-start.1) | async-done | bytes 1048608 | tf_op jit(solution)/shard_map/all_to_all | solution.py:476
  150.8 8.8 %collective-permute-done.8.refs_2_ = bf16[16,128,512]{2,1,0:T(8,128)(2,1)} collective-permute-done((bf16[16,128,512]{2,1,0:T(8,128)(2,1)}, bf16[16,128,512]{2,1,0:T(8,128)(2,1)}, u32[]{:S(2)}, u32[]{:S(2)}) %collective-permute-start.8) | collective-permute-done | bytes 2097184 | tf_op jit(solution)/shard_map/ppermute | solution.py:485
  159.6 3.1 %collective-permute-done.9.refs_4_ = bf16[16,128,512]{2,1,0:T(8,128)(2,1)} collective-permute-done((bf16[16,128,512]{2,1,0:T(8,128)(2,1)}, bf16[16,128,512]{2,1,0:T(8,128)(2,1)}, u32[]{:S(2)}, u32[]{:S(2)}) %collective-permute-start.9) | collective-permute-done | bytes 2097184 | tf_op jit(solution)/shard_map/ppermute | solution.py:485
  167.3 4.7 %all-to-all-start.2 = ((bf16[16,128,256]{2,1,0:T(8,128)(2,1)}), bf16[16,128,256]{2,1,0:T(8,128)(2,1)S(1)}, u32[]{:S(2)}, u32[]{:S(2)}) async-start(bf16[16,128,256]{2,1,0:T(8,128)(2,1)} %get-tuple-element.66), calls=%async_computation.2 | async-start | bytes 2097152 | tf_op jit(solution)/shard_map/all_to_all | solution.py:476
  175.5 21.5 %collective-permute-done.13.refs_0_ = bf16[4,128,512]{2,1,0:T(8,128)(2,1)S(1)} collective-permute-done((bf16[4,128,512]{2,1,0:T(8,128)(2,1)S(1)}, bf16[4,128,512]{2,1,0:T(8,128)(2,1)S(1)}, u32[]{:S(2)}, u32[]{:S(2)}) %collective-permute-start.13) | collective-permute-done | bytes 524320 | tf_op jit(solution)/shard_map/ppermute | solution.py:485
  197.0 3.2 %collective-permute-done.14.refs_2_ = bf16[4,128,512]{2,1,0:T(8,128)(2,1)S(1)} collective-permute-done((bf16[4,128,512]{2,1,0:T(8,128)(2,1)S(1)}, bf16[4,128,512]{2,1,0:T(8,128)(2,1)S(1)}, u32[]{:S(2)}, u32[]{:S(2)}) %collective-permute-start.14) | collective-permute-done | bytes 524320 | tf_op jit(solution)/shard_map/ppermute | solution.py:485
  201.0 8.4 %gradient.1 = bf16[16,64,640]{2,1,0:T(8,128)(2,1)} custom-call(s32[59]{0:T(128)S(1)} %concatenate.3.meta, bf16[16,288,512]{2,1,0:T(8,128)(2,1)} %all-to-all-done.part, bf16[16,128,256]{2,1,0:T(8,128)(2,1)S(1)} %all-to-all-done.2.low), custom_call_target="tpu_custom_call" | custom-call | flops 2147483648 | bytes 4718592 | tf_op jit(solution)/shard_map/gradient/pallas_call | solution.py:316
  209.4 5.4 %all-to-all-start.3 = ((bf16[16,64,640]{2,1,0:T(8,128)(2,1)}), bf16[16,64,640]{2,1,0:T(8,128)(2,1)S(1)}, u32[]{:S(2)}, u32[]{:S(2)}) async-start(bf16[16,64,640]{2,1,0:T(8,128)(2,1)} %gradient.1), calls=%async_computation.3 | async-start | bytes 2621440 | tf_op jit(solution)/shard_map/all_to_all | solution.py:476
  214.9 3.6 %collective-permute-start.15 = (bf16[4,128,512]{2,1,0:T(8,128)(2,1)S(1)}, bf16[4,128,512]{2,1,0:T(8,128)(2,1)S(1)}, u32[]{:S(2)}, u32[]{:S(2)}) collective-permute-start(bf16[4,128,512]{2,1,0:T(8,128)(2,1)S(1)} %copy-done.19), channel_id=1, source_target_pairs={{0,192},{16,208},{32,224},{48,240},{64,0},{80,16},{96,32},{112,48}... | collective-permute-start | bytes 1572872 | tf_op jit(solution)/shard_map/ppermute | solution.py:485
  218.5 50.4 %collective-permute-done.15.refs_1_ = bf16[4,128,512]{2,1,0:T(8,128)(2,1)S(1)} collective-permute-done((bf16[4,128,512]{2,1,0:T(8,128)(2,1)S(1)}, bf16[4,128,512]{2,1,0:T(8,128)(2,1)S(1)}, u32[]{:S(2)}, u32[]{:S(2)}) %collective-permute-start.15) | collective-permute-done | bytes 524320 | tf_op jit(solution)/shard_map/ppermute | solution.py:485
  270.4 12.7 %base.1.done = f32[256,8192]{1,0:T(8,128)} custom-call(s32[59]{0:T(128)} %copy-done.6, bf16[256,1024]{1,0:T(8,128)(2,1)} %cot.3, bf16[16,128,512]{2,1,0:T(8,128)(2,1)} %bitcast.22, bf16[16,128,512]{2,1,0:T(8,128)(2,1)} %collective-permute-done.10.refs_1_, bf16[16,128,512]{2,1,0:T(8,128)(2,1)} %collective-permute-done.8.refs_2_, ...), custom_call_target="tpu_custom_call" | custom-call | flops 3221225472 | bytes 20971520 | tf_op jit(solution)/shard_map/base/pallas_call | solution.py:388
  285.0 13.6 %input_gradient.1 = bf16[256,8192]{1,0:T(8,128)(2,1)} custom-call(s32[59]{0:T(128)} %copy-done.6, bf16[256,128]{1,0:T(8,128)(2,1)} %copy-done.4, bf16[256,1024]{1,0:T(8,128)(2,1)} %cot.3, f32[256,8192]{1,0:T(8,128)} %base.1.done, bf16[16,512,512]{2,1,0:T(8,128)(2,1)} %all-gather.4.cloned.1.call-done.table, bf16[4,128,512]{2,1,0:T(8,128)(2,1)} %copy-done.9, ...), custom_call_target="tpu_custom_call" | custom-call | flops 3221225472 | bytes 25165824 | tf_op jit(solution)/shard_map/input_gradient/pallas_call | solution.py:453
  (99 shorter events, 34.5 us)
Async XLA Ops:
  14.3 96.6 %all-to-all-start = ((bf16[16,288,512]{2,1,0:T(8,128)(2,1)}), bf16[16,288,512]{2,1,0:T(8,128)(2,1)}, u32[]{:S(2)}, u32[]{:S(2)}) async-start(bf16[16,288,512]{2,1,0:T(8,128)(2,1)} %pack.1), calls=%async_computation | async-start | bytes 9437184 | tf_op jit(solution)/shard_map/all_to_all | solution.py:476
  22.0 88.8 %all-gather.6.cloned.1.call-start = ((), (), s32[]{:S(2)}) async-start(), calls=%async_computation.5 | async-start | bytes 2228224 | tf_op jit(solution)/shard_map/all_gather | solution.py:531
  23.0 262.0 %all-gather.4.cloned.1.call-start = ((), (), s32[]{:S(2)}) async-start(), calls=%async_computation.4 | async-start | bytes 8912896 | tf_op jit(solution)/shard_map/all_gather | solution.py:543
  29.9 14.1 %collective-permute-start.2 = (bf16[2,64,640]{2,1,0:T(8,128)(2,1)S(1)}, bf16[2,64,640]{2,1,0:T(8,128)(2,1)S(1)}, u32[]{:S(2)}, u32[]{:S(2)}) collective-permute-start(bf16[2,64,640]{2,1,0:T(8,128)(2,1)S(1)} %get-tuple-element.47), channel_id=1, source_target_pairs={{0,64},{16,80},{32,96},{48,112},{64,128},{80,144},{96,160},{112,17... | collective-permute-start | bytes 491528 | tf_op jit(solution)/shard_map/ppermute | solution.py:485
  32.9 23.2 %collective-permute-start.3 = (bf16[2,64,640]{2,1,0:T(8,128)(2,1)S(1)}, bf16[2,64,640]{2,1,0:T(8,128)(2,1)S(1)}, u32[]{:S(2)}, u32[]{:S(2)}) collective-permute-start(bf16[2,64,640]{2,1,0:T(8,128)(2,1)S(1)} %get-tuple-element.48), channel_id=1, source_target_pairs={{0,96},{16,112},{32,128},{48,144},{64,160},{80,176},{96,192},{112,... | collective-permute-start | bytes 491528 | tf_op jit(solution)/shard_map/ppermute | solution.py:485
  36.7 22.3 %collective-permute-start.4 = (bf16[2,64,640]{2,1,0:T(8,128)(2,1)S(1)}, bf16[2,64,640]{2,1,0:T(8,128)(2,1)S(1)}, u32[]{:S(2)}, u32[]{:S(2)}) collective-permute-start(bf16[2,64,640]{2,1,0:T(8,128)(2,1)S(1)} %get-tuple-element.49), channel_id=1, source_target_pairs={{0,128},{16,144},{32,160},{48,176},{64,192},{80,208},{96,224},{112... | collective-permute-start | bytes 491528 | tf_op jit(solution)/shard_map/ppermute | solution.py:485
  37.1 21.8 %collective-permute-start.5 = (bf16[2,64,640]{2,1,0:T(8,128)(2,1)S(1)}, bf16[2,64,640]{2,1,0:T(8,128)(2,1)S(1)}, u32[]{:S(2)}, u32[]{:S(2)}) collective-permute-start(bf16[2,64,640]{2,1,0:T(8,128)(2,1)S(1)} %get-tuple-element.50), channel_id=1, source_target_pairs={{0,160},{16,176},{32,192},{48,208},{64,224},{80,240},{96,0},{112,1... | collective-permute-start | bytes 491528 | tf_op jit(solution)/shard_map/ppermute | solution.py:485
  41.6 25.1 %collective-permute-start.6 = (bf16[2,64,640]{2,1,0:T(8,128)(2,1)S(1)}, bf16[2,64,640]{2,1,0:T(8,128)(2,1)S(1)}, u32[]{:S(2)}, u32[]{:S(2)}) collective-permute-start(bf16[2,64,640]{2,1,0:T(8,128)(2,1)S(1)} %get-tuple-element.51), channel_id=1, source_target_pairs={{0,192},{16,208},{32,224},{48,240},{64,0},{80,16},{96,32},{112,48}... | collective-permute-start | bytes 491528 | tf_op jit(solution)/shard_map/ppermute | solution.py:485
  44.0 23.8 %collective-permute-start.7 = (bf16[2,64,640]{2,1,0:T(8,128)(2,1)S(1)}, bf16[2,64,640]{2,1,0:T(8,128)(2,1)S(1)}, u32[]{:S(2)}, u32[]{:S(2)}) collective-permute-start(bf16[2,64,640]{2,1,0:T(8,128)(2,1)S(1)} %get-tuple-element.52), channel_id=1, source_target_pairs={{0,224},{16,240},{32,0},{48,16},{64,32},{80,48},{96,64},{112,80},{... | collective-permute-start | bytes 491528 | tf_op jit(solution)/shard_map/ppermute | solution.py:485
  112.7 46.8 %collective-permute-start.8 = (bf16[16,128,512]{2,1,0:T(8,128)(2,1)}, bf16[16,128,512]{2,1,0:T(8,128)(2,1)}, u32[]{:S(2)}, u32[]{:S(2)}) collective-permute-start(bf16[16,128,512]{2,1,0:T(8,128)(2,1)} %bitcast.20), channel_id=1, source_target_pairs={{0,224},{16,240},{32,0},{48,16},{64,32},{80,48},{96,64},{112,80},{... | collective-permute-start | bytes 6291464 | tf_op jit(solution)/shard_map/ppermute | solution.py:485
  115.9 46.9 %collective-permute-start.9 = (bf16[16,128,512]{2,1,0:T(8,128)(2,1)}, bf16[16,128,512]{2,1,0:T(8,128)(2,1)}, u32[]{:S(2)}, u32[]{:S(2)}) collective-permute-start(bf16[16,128,512]{2,1,0:T(8,128)(2,1)} %bitcast.21), channel_id=1, source_target_pairs={{0,32},{16,48},{32,64},{48,80},{64,96},{80,112},{96,128},{112,144}... | collective-permute-start | bytes 6291464 | tf_op jit(solution)/shard_map/ppermute | solution.py:485
  123.4 27.4 %all-to-all-start.1 = ((bf16[16,256,128]{2,1,0:T(8,128)(2,1)}), bf16[16,256,128]{2,1,0:T(8,128)(2,1)S(1)}, u32[]{:S(2)}, u32[]{:S(2)}) async-start(bf16[16,256,128]{2,1,0:T(8,128)(2,1)} %project.1), calls=%async_computation.1 | async-start | bytes 2097152 | tf_op jit(solution)/shard_map/all_to_all | solution.py:476
  128.3 72.7 %collective-permute-start.10 = (bf16[16,128,512]{2,1,0:T(8,128)(2,1)S(1)}, bf16[16,128,512]{2,1,0:T(8,128)(2,1)}, u32[]{:S(2)}, u32[]{:S(2)}) collective-permute-start(bf16[16,128,512]{2,1,0:T(8,128)(2,1)S(1)} %bitcast.23), channel_id=1, source_target_pairs={{0,16},{16,0},{32,48},{48,32},{64,80},{80,64},{96,112},{112,96},{1... | collective-permute-start | bytes 6291464 | tf_op jit(solution)/shard_map/ppermute | solution.py:480
  162.7 38.3 %collective-permute-start.11 = (bf16[16,128,512]{2,1,0:T(8,128)(2,1)}, bf16[16,128,512]{2,1,0:T(8,128)(2,1)}, u32[]{:S(2)}, u32[]{:S(2)}) collective-permute-start(bf16[16,128,512]{2,1,0:T(8,128)(2,1)} %collective-permute-done.8.refs_2_), channel_id=1, source_target_pairs={{0,16},{16,0},{32,48},{48,32},{64,80},{80,64},{96,112},{112,96},{1... | collective-permute-start | bytes 6291464 | tf_op jit(solution)/shard_map/ppermute | solution.py:480
  165.4 35.6 %collective-permute-start.12 = (bf16[16,128,512]{2,1,0:T(8,128)(2,1)}, bf16[16,128,512]{2,1,0:T(8,128)(2,1)}, u32[]{:S(2)}, u32[]{:S(2)}) collective-permute-start(bf16[16,128,512]{2,1,0:T(8,128)(2,1)} %collective-permute-done.9.refs_4_), channel_id=1, source_target_pairs={{0,16},{16,0},{32,48},{48,32},{64,80},{80,64},{96,112},{112,96},{1... | collective-permute-start | bytes 6291464 | tf_op jit(solution)/shard_map/ppermute | solution.py:480
  167.3 33.7 %all-to-all-start.2 = ((bf16[16,128,256]{2,1,0:T(8,128)(2,1)}), bf16[16,128,256]{2,1,0:T(8,128)(2,1)S(1)}, u32[]{:S(2)}, u32[]{:S(2)}) async-start(bf16[16,128,256]{2,1,0:T(8,128)(2,1)} %get-tuple-element.66), calls=%async_computation.2 | async-start | bytes 2097152 | tf_op jit(solution)/shard_map/all_to_all | solution.py:476
  173.1 23.8 %collective-permute-start.13 = (bf16[4,128,512]{2,1,0:T(8,128)(2,1)S(1)}, bf16[4,128,512]{2,1,0:T(8,128)(2,1)S(1)}, u32[]{:S(2)}, u32[]{:S(2)}) collective-permute-start(bf16[4,128,512]{2,1,0:T(8,128)(2,1)S(1)} %get-tuple-element.86), channel_id=1, source_target_pairs={{0,192},{16,208},{32,224},{48,240},{64,0},{80,16},{96,32},{112,48}... | collective-permute-start | bytes 1572872 | tf_op jit(solution)/shard_map/ppermute | solution.py:485
  173.8 26.3 %collective-permute-start.14 = (bf16[4,128,512]{2,1,0:T(8,128)(2,1)S(1)}, bf16[4,128,512]{2,1,0:T(8,128)(2,1)S(1)}, u32[]{:S(2)}, u32[]{:S(2)}) collective-permute-start(bf16[4,128,512]{2,1,0:T(8,128)(2,1)S(1)} %get-tuple-element.85), channel_id=1, source_target_pairs={{0,64},{16,80},{32,96},{48,112},{64,128},{80,144},{96,160},{112,17... | collective-permute-start | bytes 1572872 | tf_op jit(solution)/shard_map/ppermute | solution.py:485
  209.4 89.2 %all-to-all-start.3 = ((bf16[16,64,640]{2,1,0:T(8,128)(2,1)}), bf16[16,64,640]{2,1,0:T(8,128)(2,1)S(1)}, u32[]{:S(2)}, u32[]{:S(2)}) async-start(bf16[16,64,640]{2,1,0:T(8,128)(2,1)} %gradient.1), calls=%async_computation.3 | async-start | bytes 2621440 | tf_op jit(solution)/shard_map/all_to_all | solution.py:476
  214.9 54.0 %collective-permute-start.15 = (bf16[4,128,512]{2,1,0:T(8,128)(2,1)S(1)}, bf16[4,128,512]{2,1,0:T(8,128)(2,1)S(1)}, u32[]{:S(2)}, u32[]{:S(2)}) collective-permute-start(bf16[4,128,512]{2,1,0:T(8,128)(2,1)S(1)} %copy-done.19), channel_id=1, source_target_pairs={{0,192},{16,208},{32,224},{48,240},{64,0},{80,16},{96,32},{112,48}... | collective-permute-start | bytes 1572872 | tf_op jit(solution)/shard_map/ppermute | solution.py:485
  218.5 50.4 %collective-permute-start.16 = (bf16[4,128,512]{2,1,0:T(8,128)(2,1)S(1)}, bf16[4,128,512]{2,1,0:T(8,128)(2,1)S(1)}, u32[]{:S(2)}, u32[]{:S(2)}) collective-permute-start(bf16[4,128,512]{2,1,0:T(8,128)(2,1)S(1)} %copy-done.18), channel_id=1, source_target_pairs={{0,64},{16,80},{32,96},{48,112},{64,128},{80,144},{96,160},{112,17... | collective-permute-start | bytes 1572872 | tf_op jit(solution)/shard_map/ppermute | solution.py:485
  268.8 14.3 %collective-permute-start.18 = (bf16[4,128,512]{2,1,0:T(8,128)(2,1)S(1)}, bf16[4,128,512]{2,1,0:T(8,128)(2,1)S(1)}, u32[]{:S(2)}, u32[]{:S(2)}) collective-permute-start(bf16[4,128,512]{2,1,0:T(8,128)(2,1)S(1)} %collective-permute-done.15.refs_1_), channel_id=1, source_target_pairs={{0,16},{16,0},{32,48},{48,32},{64,80},{80,64},{96,112},{112,96},{1... | collective-permute-start | bytes 1572872 | tf_op jit(solution)/shard_map/ppermute | solution.py:480
  269.8 13.4 %collective-permute-start.20 = (bf16[4,128,512]{2,1,0:T(8,128)(2,1)S(1)}, bf16[4,128,512]{2,1,0:T(8,128)(2,1)S(1)}, u32[]{:S(2)}, u32[]{:S(2)}) collective-permute-start(bf16[4,128,512]{2,1,0:T(8,128)(2,1)S(1)} %collective-permute-done.16.refs_3_), channel_id=1, source_target_pairs={{0,16},{16,0},{32,48},{48,32},{64,80},{80,64},{96,112},{112,96},{1... | collective-permute-start | bytes 1572872 | tf_op jit(solution)/shard_map/ppermute | solution.py:480
  270.3 14.7 %collective-permute-start.19 = (bf16[4,128,512]{2,1,0:T(8,128)(2,1)S(1)}, bf16[4,128,512]{2,1,0:T(8,128)(2,1)}, u32[]{:S(2)}, u32[]{:S(2)}) collective-permute-start(bf16[4,128,512]{2,1,0:T(8,128)(2,1)S(1)} %copy-done.12), channel_id=1, source_target_pairs={{0,16},{16,0},{32,48},{48,32},{64,80},{80,64},{96,112},{112,96},{1... | collective-permute-start | bytes 1572872 | tf_op jit(solution)/shard_map/ppermute | solution.py:480
  (25 other events, 473.5 us)
Sparse Core Ops, SparseCore 0:
  25.9 84.9 all-gather.5
  113.9 96.6 all-gather.3

commit v5 on v2

--- a/solution.py
+++ b/solution.py
@@ -11,14 +11,16 @@
 BF = jnp.bfloat16
 F32 = jnp.float32
 VMEM_BYTES = 40 * 1024 * 1024
+VMEM_MOST = 58 * 1024 * 1024
 GROUP = 4
-CORE, FIRST, CHIP, LIST = 0, 1, 2, 3
-
-
-def call(kernel, name, flops=0, moved=0, **kw):
+SIDE = 4
+CORE, FIRST, CHIP, PIECE, LIST = 0, 1, 2, 3, 4
+
+
+def call(kernel, name, flops=0, moved=0, vmem=VMEM_BYTES, **kw):
     return pl.pallas_call(
         kernel,
-        compiler_params=pltpu.CompilerParams(vmem_limit_bytes=VMEM_BYTES),
+        compiler_params=pltpu.CompilerParams(vmem_limit_bytes=vmem),
         cost_estimate=pl.CostEstimate(flops=flops, bytes_accessed=moved, transcendentals=0),
         name=name,
         **kw,
@@ -67,24 +69,27 @@
     return (row >= begin) & (row < end)
 
 
-def turn_kernel(meta, w, out):
-    out[...] = jnp.transpose(w[...].astype(F32)).astype(BF)
-
-
-def turn(meta, w):
+def turn_kernel(at, w, out):
+    both = jnp.transpose(w[...].astype(F32)).astype(BF)
+    part = out.shape[0]
+    low = lax.rem(at[0], 2) == 0
+    out[...] = jnp.where(low, both[:part], both[part:])
+
+
+def turn(at, w, slices):
     piece, width = w.shape
-    half = piece // 2
+    part = width // slices
     return call(
         turn_kernel,
         "turn",
-        moved=4 * half * width,
+        moved=4 * part * piece,
         grid_spec=with_meta(
             (1,),
-            [pl.BlockSpec((half, width), lambda i, m: (m[CORE], 0))],
-            whole((width, half)),
-        ),
-        out_shape=jax.ShapeDtypeStruct((width, half), BF),
-    )(meta, w)
+            [pl.BlockSpec((piece, 2 * part), lambda i, m: (0, m[0] // 2))],
+            whole((part, piece)),
+        ),
+        out_shape=jax.ShapeDtypeStruct((part, piece), BF),
+    )(at, w)
 
 
 def pack_kernel(tok, cot_t, out):
@@ -105,6 +110,7 @@
         pack_kernel,
         "pack",
         moved=4 * rows * width,
+        vmem=VMEM_MOST,
         grid=(n // GROUP,),
         in_specs=[
             pl.BlockSpec((rows, GROUP * piece), lambda f: (0, f)),
@@ -242,11 +248,10 @@
     )(meta, parts, down_t, up_t)
 
 
-def total_kernel(parts, out, copies):
+def total_kernel(parts, copies):
     acc = parts[0].astype(F32)
     for f in range(1, parts.shape[0]):
         acc += parts[f].astype(F32)
-    out[...] = acc.astype(BF)
     turned = jnp.transpose(acc).astype(BF)
     for f in range(copies.shape[0]):
         copies[f] = turned
@@ -258,14 +263,11 @@
         total_kernel,
         "total",
         moved=4 * parts.size,
-        out_shape=[
-            jax.ShapeDtypeStruct((rows, wide), BF),
-            jax.ShapeDtypeStruct((n, wide, rows), BF),
-        ],
+        out_shape=jax.ShapeDtypeStruct((n, wide, rows), BF),
     )(parts)
 
 
-def gradient_kernel(slots, rank, v, meta, part, low, out, acc_down, acc_up):
+def gradient_kernel(slots, rank, v, meta, part, low, keep, give, acc_down, acc_up):
     group, _, rows = low.shape
     step = pl.program_id(0)
 
@@ -298,18 +300,25 @@
     @pl.when(step == pl.num_programs(0) - 1)
     def _():
         piece = acc_down.shape[1]
-        out[...] = jnp.zeros_like(out)
+        keep[...] = jnp.zeros_like(keep)
+        give[...] = jnp.zeros_like(give)
         for s in range(slots):
-            at = owner_of(meta, s, slots)
+            owner = owner_of(meta, s, slots)
+            chip, same = owner // 2, lax.rem(owner, 2) == meta[CORE]
             rows_of = slice(s * rank, (s + 1) * rank)
-            out[at, :, :piece] = acc_down[rows_of, :].astype(BF)
-            out[at, :, piece:piece + v] = (ADAPTER_SCALE * acc_up[rows_of, :]).astype(BF)
-
-
-def gradient(meta, parts, low, owners, slots, rank, v):
+
+            def put(out):
+                out[chip, :, :piece] = acc_down[rows_of, :].astype(BF)
+                out[chip, :, piece:piece + v] = (ADAPTER_SCALE * acc_up[rows_of, :]).astype(BF)
+
+            pl.when(same)(functools.partial(put, keep))
+            pl.when(jnp.logical_not(same))(functools.partial(put, give))
+
+
+def gradient(meta, parts, low, chips, slots, rank, v):
     n, tall, piece = parts.shape
     rows = low.shape[2]
-    shape = (owners, rank, piece + 128)
+    shape = (chips, rank, piece + 128)
     return call(
         functools.partial(gradient_kernel, slots, rank, v),
         "gradient",
@@ -321,86 +330,136 @@
                 pl.BlockSpec((GROUP, tall, piece), lambda j, m: (j, 0, 0)),
                 pl.BlockSpec((GROUP, 2 * rank, rows), lambda j, m: (j, 0, 0)),
             ],
-            whole(shape),
+            [whole(shape), whole(shape)],
             [pltpu.VMEM((slots * rank, piece), F32), pltpu.VMEM((slots * rank, v), F32)],
         ),
-        out_shape=jax.ShapeDtypeStruct(shape, BF),
+        out_shape=[jax.ShapeDtypeStruct(shape, BF)] * 2,
     )(meta, parts, low)
 
 
-def collect_kernel(slots, scale, meta, got, down, up):
+def collect_kernel(slots, scale, meta, *refs):
+    got, (down, up) = refs[:-2], refs[-2:]
+    chips = len(got)
     piece, v = down.shape[2], up.shape[2]
     down[...] = jnp.zeros_like(down)
     up[...] = jnp.zeros_like(up)
-    for b in range(got.shape[0]):
-        r = wanted_by(meta, b, slots)
-
-        @pl.when(r >= 0)
-        def _():
-            down[r] += got[b, :, :piece].astype(F32) * scale
-            up[r] += got[b, :, piece:piece + v].astype(F32) * scale
+    for k in range(chips):
+        z = lax.rem(meta[CHIP] + chips - k, chips)
+        for core in range(2):
+            r = wanted_by(meta, 2 * z + core, slots)
+
+            @pl.when(r >= 0)
+            def _():
+                down[r] += got[k][core, :, :piece].astype(F32) * scale
+                up[r] += got[k][core, :, piece:piece + v].astype(F32) * scale
 
 
 def collect(meta, got, rows, v, slots, scale):
-    _, rank, wide = got.shape
+    _, rank, wide = got[0].shape
     shapes = [(rows, rank, wide - 128), (rows, rank, v)]
     return call(
         functools.partial(collect_kernel, slots, scale),
         "collect",
-        moved=2 * got.size,
-        grid_spec=with_meta((1,), [whole(got.shape)], [whole(s) for s in shapes]),
+        moved=2 * len(got) * got[0].size,
+        grid_spec=with_meta((1,), [whole(g.shape) for g in got], [whole(s) for s in shapes]),
         out_shape=[jax.ShapeDtypeStruct(s, F32) for s in shapes],
-    )(meta, got)
-
-
-def input_kernel(slots, rank, meta, cot, low, mine, other, down, out, lg):
-    @pl.when(pl.program_id(0) == 0)
-    def _():
-        both = low[...].astype(F32)
-        half = jnp.where(
-            lax.broadcasted_iota(jnp.int32, both.shape, 1) < rank,
-            pltpu.roll(both, rank, 1),
-            both,
-        )
-        for p in range(slots // 2):
-            keep = inside_pair(meta, p, meta[FIRST], both.shape, slots, rank)
-            lg[:, 2 * rank * p:2 * rank * (p + 1)] = jnp.where(keep, half, 0.0).astype(BF)
-
-    lower = meta[CORE] == 0
-    group, _, half = mine.shape
+    )(meta, *got)
+
+
+def term_kernel(slots, rank, meta, low, down, out, acc):
+    group, _, rows = low.shape
+    piece = out.shape[2]
     for g in range(group):
-        at = 2 * g * half
-        term = jnp.dot(lg[...], down[g], preferred_element_type=F32)
-        a = jnp.dot(cot[...], mine[g], preferred_element_type=F32)
-        b = jnp.dot(cot[...], other[g], preferred_element_type=F32)
-        out[:, at:at + half] = (jnp.where(lower, a, b) + term[:, :half]).astype(BF)
-        out[:, at + half:at + 2 * half] = (jnp.where(lower, b, a) + term[:, half:]).astype(BF)
-
-
-def input_gradient(meta, cot, low, mine, other, down, slots, rank):
-    n, width, half = mine.shape
-    rows = cot.shape[0]
-    piece = 2 * half
-    group = 2
-    return call(
-        functools.partial(input_kernel, slots, rank),
-        "input_gradient",
-        flops=2 * rows * n * piece * (width + slots * rank),
-        moved=2 * n * piece * (width + slots * rank + rows),
-        grid_spec=with_meta(
-            (n // group,),
+        first = (pl.program_id(0) * group + g) * rows
+        acc[...] = jnp.zeros_like(acc)
+        for s in range(slots):
+            start, end = start_of(meta, s), end_of(meta, s, slots)
+
+            @pl.when((start < first + rows) & (end > first))
+            def _():
+                token = first + lax.broadcasted_iota(jnp.int32, (rank, rows), 1)
+                lg = low[g, rank:, :].astype(F32)
+                lg = jnp.where((token >= start) & (token < end), lg, 0.0).astype(BF)
+                acc[...] += lax.dot_general(
+                    lg, down[s, :, :piece], (((0,), (0,)), ((), ())), preferred_element_type=F32
+                )
+
+        out[g] = acc[...].astype(BF)
+
+
+def term(meta, low, down, piece, slots, rank):
+    n, wide, rows = low.shape
+    return call(
+        functools.partial(term_kernel, slots, rank),
+        "term",
+        flops=2 * n * rows * piece * 2 * rank,
+        moved=2 * n * rows * piece,
+        grid_spec=with_meta(
+            (n // GROUP,),
+            [pl.BlockSpec((GROUP, wide, rows), lambda j, m: (j, 0, 0)), whole(down.shape)],
+            pl.BlockSpec((GROUP, rows, piece), lambda j, m: (j, 0, 0)),
+            [pltpu.VMEM((rows, piece), F32)],
+        ),
+        out_shape=jax.ShapeDtypeStruct((n, rows, piece), BF),
+    )(meta, low, down)
+
+
+def base_kernel(meta, cot, w, out):
+    out[...] = jnp.dot(
+        cot[...],
+        jnp.concatenate([w[e, 0] for e in range(w.shape[0])], axis=0),
+        preferred_element_type=F32,
+    )
+
+
+def base(meta, cot, w):
+    slices, n, part, piece = w.shape
+    rows, width = cot.shape
+
+    def place(f, m):
+        y = lax.rem(m[PIECE] // SIDE + SIDE - f // SIDE, SIDE)
+        x = lax.rem(lax.rem(m[PIECE], SIDE) + SIDE - lax.rem(f, SIDE), SIDE)
+        return (0, y * SIDE + x)
+
+    return call(
+        base_kernel,
+        "base",
+        flops=2 * rows * n * piece * width,
+        moved=2 * n * piece * width + 4 * rows * n * piece,
+        grid_spec=with_meta(
+            (n,),
             [
                 whole(cot.shape),
-                whole(low.shape),
-                pl.BlockSpec((group, width, half), lambda f, m: (f, 0, 0)),
-                pl.BlockSpec((group, width, half), lambda f, m: (f, 0, 0)),
-                pl.BlockSpec((group, slots * rank, piece), lambda f, m: (f, 0, 0)),
+                pl.BlockSpec((slices, 1, part, piece), lambda f, m: (0, f, 0, 0)),
             ],
-            pl.BlockSpec((rows, group * piece), lambda f, m: (0, f)),
-            [pltpu.VMEM((rows, slots * rank), BF)],
-        ),
+            pl.BlockSpec((rows, piece), place),
+        ),
+        out_shape=jax.ShapeDtypeStruct((rows, n * piece), F32),
+    )(meta, cot, w)
+
+
+def join_kernel(done, terms, out):
+    group, _, piece = terms.shape
+    for g in range(group):
+        cols = slice(g * piece, (g + 1) * piece)
+        out[:, cols] = (done[:, cols] + terms[g].astype(F32)).astype(BF)
+
+
+def join(done, terms):
+    n, rows, piece = terms.shape
+    group = 2
+    return call(
+        join_kernel,
+        "join",
+        moved=8 * n * rows * piece,
+        grid=(n // group,),
+        in_specs=[
+            pl.BlockSpec((rows, group * piece), lambda f: (0, f)),
+            pl.BlockSpec((group, rows, piece), lambda f: (f, 0, 0)),
+        ],
+        out_specs=pl.BlockSpec((rows, group * piece), lambda f: (0, f)),
         out_shape=jax.ShapeDtypeStruct((rows, n * piece), BF),
-    )(meta, cot, low, mine, other, down)
+    )(done, terms)
 
 
 def exchange(x, axis):
@@ -415,6 +474,22 @@
     chips = bins // 2
     return lax.ppermute(
         x, "dp", [(i, (i // 2 + k) % chips * 2 + i % 2) for i in range(bins)]
+    )
+
+
+def spread(meta, keep, give, bins):
+    blocks = merge(meta, keep, swap(give, bins))
+    return [blocks[0]] + [shift(blocks[k], k, bins) for k in range(1, bins // 2)]
+
+
+def across(x, dy, dx, n):
+    return lax.ppermute(
+        x,
+        "fsdp",
+        [
+            (i, (i // SIDE + dy) % SIDE * SIDE + (i % SIDE + dx) % SIDE)
+            for i in range(n)
+        ],
     )
 
 
@@ -432,7 +507,8 @@
     wanted = jnp.max(jnp.where(stored // own == me, stored % own, -1), axis=1)
     every = jnp.arange(bins, dtype=jnp.int32)
     segment = jnp.max(jnp.where(owners[None, :] == every[:, None], place[None, :], -1), axis=1)
-    head = jnp.stack([me % 2, lax.axis_index("fsdp") * rows, me // 2])
+    place_f = lax.axis_index("fsdp")
+    head = jnp.stack([me % 2, place_f * rows, me // 2, place_f])
     return jnp.concatenate([head, starts, starts + lengths, owners, wanted, segment]).astype(
         jnp.int32
     )
@@ -457,30 +533,31 @@
     scale = (n * rows) ** (-0.5)
     meta = scalars(segment_tenant, segment_lengths, tenant_stored_row, own, rows)
 
-    parts = exchange(pack(tokens, jnp.swapaxes(cotangent, 0, 1), n), "fsdp")
-    mine = lax.all_gather(turn(meta, value_weight), "fsdp", axis=0)
+    packed = pack(tokens, jnp.swapaxes(cotangent, 0, 1), n)
+    me = lax.axis_index("dp").astype(jnp.int32).reshape(1)
+    packed, me = lax.optimization_barrier((packed, me))
+    parts = exchange(packed, "fsdp")
+    mine = turn(me, value_weight, bins)[None]
+    mine = jnp.concatenate([mine] + [across(mine, 0, k, n) for k in range(1, SIDE)])
+    mine = jnp.concatenate([mine] + [across(mine, k, 0, n) for k in range(1, SIDE)])
+    weight = lax.all_gather(mine, "dp", axis=0)
 
     keep, give = offer(
         meta, jnp.swapaxes(adapter_down_weight, 1, 2), adapter_up_weight, chips, slots
     )
-    blocks = merge(meta, keep, swap(give, bins))
-    got = [blocks[0]] + [shift(blocks[k], k, bins) for k in range(1, chips)]
-    parts, got = lax.optimization_barrier((parts, got))
+    got = spread(meta, keep, give, bins)
+    parts, got, mine = lax.optimization_barrier((parts, got, mine))
     down, down_t, up_t = choose(meta, got, slots, v)
-    down_all = lax.all_gather(
-        down[:, :, :piece].reshape(slots * rank, piece), "fsdp", axis=0
-    )
-
-    low, copies = total(
-        exchange(project(meta, parts, down_t, up_t, rows, slots, rank), "fsdp")
-    )
-    mine, copies = lax.optimization_barrier((mine, copies))
-    other = swap(mine, bins)
-    sent = exchange(
-        gradient(meta, parts, exchange(copies, "fsdp"), bins, slots, rank, v), "dp"
-    )
-    grad = input_gradient(meta, cotangent, low, mine, other, down_all, slots, rank)
-    sent, grad = lax.optimization_barrier((sent, grad))
+
+    sums = exchange(project(meta, parts, down_t, up_t, rows, slots, rank), "fsdp")
+    low_all = exchange(total(sums), "fsdp")
+    terms = term(meta, low_all, down, piece, slots, rank)
+    terms, low_all = lax.optimization_barrier((terms, low_all))
+    terms = exchange(terms, "fsdp")
+    sent = spread(meta, *gradient(meta, parts, low_all, chips, slots, rank, v), bins)
+    done = base(meta, cotangent, weight)
+    terms, sent, done = lax.optimization_barrier((terms, sent, done))
+    grad = join(done, terms)
     down_grad, up_grad = collect(meta, sent, own, v, slots, scale)
     return grad, jnp.swapaxes(down_grad, 1, 2), up_grad
 

time: 258 us -> 243 us (0.942)
  waiting for transfers between devices: 102 us -> 58.4 us
  starting transfers between devices: 39 us -> 66.2 us
  Pallas kernels: 35.5 us -> 55.5 us
  blocking collectives: 52.4 us -> 33.7 us
    all_gather x2 -> x1, waiting for transfers between devices: 47.5 us -> 0.01 us  [local(): weight = lax.all_gather(mine, 'dp', axis=0)]
    all_to_all x2, waiting for transfers between devices: 33.1 us -> 6.5 us  [exchange(): return lax.all_to_all(x, axis, 0, 0, tiled=True)]
    pallas_call x4 -> x6, Pallas kernels: 16.2 us -> 36.3 us  [the longest x1 15.7 us: base(): call(base_kernel, 'base', flops=2 * rows * n * piece * width, moved=2 * n...]
    all_to_all x2, blocking collectives: 52.4 us -> 33.7 us  [exchange(): return lax.all_to_all(x, axis, 0, 0, tiled=True)]
    ppermute x7 -> x14, waiting for transfers between devices: 19.9 us -> 37.2 us  [shift(): lax.ppermute(x, 'dp', [(i, (i // 2 + k) % chips * 2 + i % 2) for i in ran...]
    ppermute x7 -> x14, starting transfers between devices: 19.6 us -> 36.6 us  [shift(): lax.ppermute(x, 'dp', [(i, (i // 2 + k) % chips * 2 + i % 2) for i in ran...]
    ppermute x0 -> x6, waiting for transfers between devices: none -> 11.2 us  [across(): lax.ppermute(x, 'fsdp', [(i, (i // SIDE + dy) % SIDE * SIDE + (i % SIDE +...]
    ppermute x0 -> x6, starting transfers between devices: none -> 11 us  [across(): lax.ppermute(x, 'fsdp', [(i, (i // SIDE + dy) % SIDE * SIDE + (i % SIDE +...]
  transfers between devices with their start and end apart: 13 -> 25, of which waited for: 8 -> 13; matrix products, arithmetic and copies ran while one was open for 1% -> 0% of each run, Pallas kernels for 13% -> 17%
where the time goes in v5:
time: 243 us; the launch traced here: 241 us
  starting transfers between devices  66.2 us (27%)
  waiting for transfers between devices  58.4 us (24%)
  Pallas kernels  55.5 us (23%)
  blocking collectives  33.7 us (14%)
  between operations  14.3 us (6%)
  local copies, waits for them, and re-layouts  12.2 us (5%)
    ppermute x14, waiting for transfers between devices, shift(): lax.ppermute(x, 'dp', [(i, (i // 2 + k) % chips * 2 + i % 2) for i in ran...  37.2 us
    ppermute x14, starting transfers between devices, shift(): lax.ppermute(x, 'dp', [(i, (i // 2 + k) % chips * 2 + i % 2) for i in ran...  36.6 us
    all_to_all x2, blocking collectives, exchange(): return lax.all_to_all(x, axis, 0, 0, tiled=True)  33.7 us
    pallas_call x1, Pallas kernels, base(): call(base_kernel, 'base', flops=2 * rows * n * piece * width, moved=2 * n...  15.7 us
    unnamed x32, local copies, waits for them, and re-layouts  11.9 us
    ppermute x6, waiting for transfers between devices, across(): lax.ppermute(x, 'fsdp', [(i, (i // SIDE + dy) % SIDE * SIDE + (i % SIDE +...  11.2 us
    ppermute x6, starting transfers between devices, across(): lax.ppermute(x, 'fsdp', [(i, (i // SIDE + dy) % SIDE * SIDE + (i % SIDE +...  11 us
    all_to_all x2, starting transfers between devices, exchange(): return lax.all_to_all(x, axis, 0, 0, tiled=True)  10.9 us
  transfers between devices with their start and end apart: 25, of which 13 were waited for; matrix products, arithmetic and copies ran while one was open for 0% of the time, Pallas kernels for 17%

profile of v5, /device:TPU:1, one launch (start us, length us, event | category | flops | bytes accessed | tf_op | source)
XLA Modules:
  0.0 241.0 jit_solution(5779415808401855559)
XLA Ops:
  9.3 5.1 %pack.1 = bf16[16,288,512]{2,1,0:T(8,128)(2,1)} custom-call(bf16[256,8192]{1,0:T(8,128)(2,1)} %tok.1, bf16[1024,256]{1,0:T(8,128)(2,1)} %bitcast.27), custom_call_target="tpu_custom_call" | custom-call | bytes 8388608 | tf_op jit(solution)/shard_map/pack/pallas_call | solution.py:109
  29.9 7.0 %collective-permute-done.12 = bf16[4,64,512]{2,1,0:T(8,128)(2,1)S(1)} collective-permute-done((bf16[4,64,512]{2,1,0:T(8,128)(2,1)S(1)}, bf16[4,64,512]{2,1,0:T(8,128)(2,1)S(1)}, u32[]{:S(2)}, u32[]{:S(2)}) %collective-permute-start.12) | collective-permute-done | bytes 262176 | tf_op jit(solution)/shard_map/ppermute | solution.py:486
  38.0 6.3 %all-to-all-start = ((bf16[16,288,512]{2,1,0:T(8,128)(2,1)}), bf16[16,288,512]{2,1,0:T(8,128)(2,1)}, u32[]{:S(2)}, u32[]{:S(2)}) async-start(bf16[16,288,512]{2,1,0:T(8,128)(2,1)} %pack.1), calls=%async_computation | async-start | bytes 9437184 | tf_op jit(solution)/shard_map/all_to_all | solution.py:466
  55.7 3.8 %collective-permute-start.3 = (bf16[2,64,640]{2,1,0:T(8,128)(2,1)S(1)}, bf16[2,64,640]{2,1,0:T(8,128)(2,1)S(1)}, u32[]{:S(2)}, u32[]{:S(2)}) collective-permute-start(bf16[2,64,640]{2,1,0:T(8,128)(2,1)S(1)} %get-tuple-element.57), channel_id=1, source_target_pairs={{0,96},{16,112},{32,128},{48,144},{64,160},{80,176},{96,192},{112,... | collective-permute-start | bytes 491528 | tf_op jit(solution)/shard_map/ppermute | solution.py:475
  59.9 4.5 %collective-permute-start.5 = (bf16[2,64,640]{2,1,0:T(8,128)(2,1)S(1)}, bf16[2,64,640]{2,1,0:T(8,128)(2,1)S(1)}, u32[]{:S(2)}, u32[]{:S(2)}) collective-permute-start(bf16[2,64,640]{2,1,0:T(8,128)(2,1)S(1)} %get-tuple-element.59), channel_id=1, source_target_pairs={{0,160},{16,176},{32,192},{48,208},{64,224},{80,240},{96,0},{112,1... | collective-permute-start | bytes 491528 | tf_op jit(solution)/shard_map/ppermute | solution.py:475
  66.8 8.6 %collective-permute-done.2.refs_2_ = bf16[2,64,640]{2,1,0:T(8,128)(2,1)S(1)} collective-permute-done((bf16[2,64,640]{2,1,0:T(8,128)(2,1)S(1)}, bf16[2,64,640]{2,1,0:T(8,128)(2,1)S(1)}, u32[]{:S(2)}, u32[]{:S(2)}) %collective-permute-start.2) | collective-permute-done | bytes 163872 | tf_op jit(solution)/shard_map/ppermute | solution.py:475
  76.8 12.1 %collective-permute-done.3.refs_3_ = bf16[2,64,640]{2,1,0:T(8,128)(2,1)S(1)} collective-permute-done((bf16[2,64,640]{2,1,0:T(8,128)(2,1)S(1)}, bf16[2,64,640]{2,1,0:T(8,128)(2,1)S(1)}, u32[]{:S(2)}, u32[]{:S(2)}) %collective-permute-start.3) | collective-permute-done | bytes 163872 | tf_op jit(solution)/shard_map/ppermute | solution.py:475
  88.9 12.2 %collective-permute-done.4.refs_4_ = bf16[2,64,640]{2,1,0:T(8,128)(2,1)S(1)} collective-permute-done((bf16[2,64,640]{2,1,0:T(8,128)(2,1)S(1)}, bf16[2,64,640]{2,1,0:T(8,128)(2,1)S(1)}, u32[]{:S(2)}, u32[]{:S(2)}) %collective-permute-start.4) | collective-permute-done | bytes 163872 | tf_op jit(solution)/shard_map/ppermute | solution.py:475
  101.1 3.1 %collective-permute-done.7.refs_7_ = bf16[2,64,640]{2,1,0:T(8,128)(2,1)S(1)} collective-permute-done((bf16[2,64,640]{2,1,0:T(8,128)(2,1)S(1)}, bf16[2,64,640]{2,1,0:T(8,128)(2,1)S(1)}, u32[]{:S(2)}, u32[]{:S(2)}) %collective-permute-start.7) | collective-permute-done | bytes 163872 | tf_op jit(solution)/shard_map/ppermute | solution.py:475
  104.2 6.5 %all-to-all-done.part = bf16[16,288,512]{2,1,0:T(8,128)(2,1)} async-done(((bf16[16,288,512]{2,1,0:T(8,128)(2,1)}), bf16[16,288,512]{2,1,0:T(8,128)(2,1)}, u32[]{:S(2)}, u32[]{:S(2)}) %all-to-all-start) | async-done | bytes 4718624 | tf_op jit(solution)/shard_map/all_to_all | solution.py:466
  111.9 6.9 %project.1 = bf16[16,256,128]{2,1,0:T(8,128)(2,1)S(1)} custom-call(s32[60]{0:T(128)S(1)} %concatenate.10.meta, bf16[16,288,512]{2,1,0:T(8,128)(2,1)} %all-to-all-done.part, bf16[512,512]{1,0:T(8,128)(2,1)S(1)} %get-tuple-element.72.down_t, bf16[64,512]{1,0:T(8,128)(2,1)S(1)} %get-tuple-element.73.up_t), custom_call_target="tpu_custom_call" | custom-call | flops 2147483648 | bytes 4718592 | tf_op jit(solution)/shard_map/project/pallas_call | solution.py:233
  118.8 17.3 %all_to_all.20.parts = bf16[16,256,128]{2,1,0:T(8,128)(2,1)S(1)} all-to-all(bf16[16,256,128]{2,1,0:T(8,128)(2,1)S(1)} %project.1), channel_id=1, replica_groups=mesh['dp'=16,'fsdp'=16] {'fsdp'}, dimensions={0} | all-to-all | bytes 2097152 | tf_op jit(solution)/shard_map/all_to_all | solution.py:466
  136.4 16.3 %all_to_all.21.low = bf16[16,128,256]{2,1,0:T(8,128)(2,1)S(1)} all-to-all(bf16[16,128,256]{2,1,0:T(8,128)(2,1)S(1)} %total.1), channel_id=1, replica_groups=mesh['dp'=16,'fsdp'=16] {'fsdp'}, dimensions={0} | all-to-all | bytes 2097152 | tf_op jit(solution)/shard_map/all_to_all | solution.py:466
  152.7 8.1 %term.1 = bf16[16,256,512]{2,1,0:T(8,128)(2,1)S(1)} custom-call(s32[60]{0:T(128)S(1)} %concatenate.10.meta, bf16[16,128,256]{2,1,0:T(8,128)(2,1)S(1)} %all_to_all.21.low, bf16[8,64,640]{2,1,0:T(8,128)(2,1)S(1)} %get-tuple-element.74.down), custom_call_target="tpu_custom_call" | custom-call | flops 536870912 | bytes 4194304 | tf_op jit(solution)/shard_map/term/pallas_call | solution.py:392
  162.9 4.5 %all-to-all-start.3 = ((bf16[16,256,512]{2,1,0:T(8,128)(2,1)}), bf16[16,256,512]{2,1,0:T(8,128)(2,1)}, u32[]{:S(2)}, u32[]{:S(2)}) async-start(bf16[16,256,512]{2,1,0:T(8,128)(2,1)} %copy-done.4), calls=%async_computation.3 | async-start | bytes 8388608 | tf_op jit(solution)/shard_map/all_to_all | solution.py:466
  167.5 7.5 %gradient.1 = (bf16[8,64,640]{2,1,0:T(8,128)(2,1)S(1)}, bf16[8,64,640]{2,1,0:T(8,128)(2,1)S(1)}) custom-call(s32[60]{0:T(128)S(1)} %concatenate.10.meta, bf16[16,288,512]{2,1,0:T(8,128)(2,1)} %all-to-all-done.part, bf16[16,128,256]{2,1,0:T(8,128)(2,1)S(1)} %all_to_all.21.low), custom_call_target="tpu_custom_call" | custom-call | flops 2147483648 | bytes 4718592 | tf_op jit(solution)/shard_map/gradient/pallas_call | solution.py:322
  175.0 5.2 %collective-permute-start.14 = (bf16[8,64,640]{2,1,0:T(8,128)(2,1)S(1)}, bf16[8,64,640]{2,1,0:T(8,128)(2,1)S(1)}, u32[]{:S(2)}, u32[]{:S(2)}) collective-permute-start(bf16[8,64,640]{2,1,0:T(8,128)(2,1)S(1)} %get-tuple-element.78), channel_id=1, source_target_pairs={{0,16},{16,0},{32,48},{48,32},{64,80},{80,64},{96,112},{112,96},{1... | collective-permute-start | bytes 1966088 | tf_op jit(solution)/shard_map/ppermute | solution.py:470
  187.3 3.6 %collective-permute-start.17 = (bf16[2,64,640]{2,1,0:T(8,128)(2,1)S(1)}, bf16[2,64,640]{2,1,0:T(8,128)(2,1)S(1)}, u32[]{:S(2)}, u32[]{:S(2)}) collective-permute-start(bf16[2,64,640]{2,1,0:T(8,128)(2,1)S(1)} %get-tuple-element.82), channel_id=1, source_target_pairs={{0,96},{16,112},{32,128},{48,144},{64,160},{80,176},{96,192},{112,... | collective-permute-start | bytes 491528 | tf_op jit(solution)/shard_map/ppermute | solution.py:475
  191.6 4.5 %collective-permute-start.19 = (bf16[2,64,640]{2,1,0:T(8,128)(2,1)S(1)}, bf16[2,64,640]{2,1,0:T(8,128)(2,1)S(1)}, u32[]{:S(2)}, u32[]{:S(2)}) collective-permute-start(bf16[2,64,640]{2,1,0:T(8,128)(2,1)S(1)} %get-tuple-element.84), channel_id=1, source_target_pairs={{0,160},{16,176},{32,192},{48,208},{64,224},{80,240},{96,0},{112,1... | collective-permute-start | bytes 491528 | tf_op jit(solution)/shard_map/ppermute | solution.py:475
  198.7 3.3 %collective-permute-start.21 = (bf16[2,64,640]{2,1,0:T(8,128)(2,1)S(1)}, bf16[2,64,640]{2,1,0:T(8,128)(2,1)S(1)}, u32[]{:S(2)}, u32[]{:S(2)}) collective-permute-start(bf16[2,64,640]{2,1,0:T(8,128)(2,1)S(1)} %get-tuple-element.86), channel_id=1, source_target_pairs={{0,224},{16,240},{32,0},{48,16},{64,32},{80,48},{96,64},{112,80},{... | collective-permute-start | bytes 491528 | tf_op jit(solution)/shard_map/ppermute | solution.py:475
  202.0 15.7 %base.1.done = f32[256,8192]{1,0:T(8,128)S(1)} custom-call(s32[60]{0:T(128)S(1)} %concatenate.10.meta, bf16[256,1024]{1,0:T(8,128)(2,1)S(1)} %copy-done.5, bf16[16,16,64,512]{3,2,1,0:T(8,128)(2,1)} %bitcast.26), custom_call_target="tpu_custom_call" | custom-call | flops 4294967296 | bytes 25165824 | tf_op jit(solution)/shard_map/base/pallas_call | solution.py:424
  217.7 3.3 %copy-done.2 = f32[256,8192]{1,0:T(8,128)} copy-done((f32[256,8192]{1,0:T(8,128)}, f32[256,8192]{1,0:T(8,128)S(1)}, u32[]{:S(2)}) %copy-start.2) | copy-done | bytes 8388632
  222.2 3.4 %copy-done.3 = f32[256,8192]{1,0:T(8,128)S(1)} copy-done((f32[256,8192]{1,0:T(8,128)S(1)}, f32[256,8192]{1,0:T(8,128)}, u32[]{:S(2)}) %copy-start.3) | copy-done | bytes 8388632
  225.6 6.9 %join.1 = bf16[256,8192]{1,0:T(8,128)(2,1)} custom-call(f32[256,8192]{1,0:T(8,128)S(1)} %copy-done.3, bf16[16,256,512]{2,1,0:T(8,128)(2,1)} %all-to-all-done.3.terms), custom_call_target="tpu_custom_call" | custom-call | bytes 16777216 | tf_op jit(solution)/shard_map/join/pallas_call | solution.py:451
  (84 shorter events, 51.0 us)
Async XLA Ops:
  7.2 194.8 %all-gather.3.cloned.1.call-start = ((), (), s32[]{:S(2)}) async-start(), calls=%async_computation.4 | async-start | bytes 17825792 | tf_op jit(solution)/shard_map/all_gather | solution.py:543
  14.5 5.7 %collective-permute-start.8 = (bf16[1,64,512]{2,1,0:T(8,128)(2,1)S(1)}, bf16[1,64,512]{2,1,0:T(8,128)(2,1)S(1)}, u32[]{:S(2)}, u32[]{:S(2)}) collective-permute-start(bf16[1,64,512]{2,1,0:T(8,128)(2,1)S(1)} %bitcast.21), channel_id=1, source_target_pairs={{0,1},{1,2},{2,3},{3,0},{4,5},{5,6},{6,7},{7,4},{8,9},{9,10},{10,1... | collective-permute-start | bytes 196616 | tf_op jit(solution)/shard_map/ppermute | solution.py:486
  16.6 5.1 %collective-permute-start.9 = (bf16[1,64,512]{2,1,0:T(8,128)(2,1)S(1)}, bf16[1,64,512]{2,1,0:T(8,128)(2,1)S(1)}, u32[]{:S(2)}, u32[]{:S(2)}) collective-permute-start(bf16[1,64,512]{2,1,0:T(8,128)(2,1)S(1)} %bitcast.22), channel_id=1, source_target_pairs={{0,2},{1,3},{2,0},{3,1},{4,6},{5,7},{6,4},{7,5},{8,10},{9,11},{10,... | collective-permute-start | bytes 196616 | tf_op jit(solution)/shard_map/ppermute | solution.py:486
  22.5 7.3 %collective-permute-start.11 = (bf16[4,64,512]{2,1,0:T(8,128)(2,1)S(1)}, bf16[4,64,512]{2,1,0:T(8,128)(2,1)S(1)}, u32[]{:S(2)}, u32[]{:S(2)}) collective-permute-start(bf16[4,64,512]{2,1,0:T(8,128)(2,1)S(1)} %pad_maximum_fusion), channel_id=1, source_target_pairs={{0,4},{1,5},{2,6},{3,7},{4,8},{5,9},{6,10},{7,11},{8,12},{9,13},{1... | collective-permute-start | bytes 786440 | tf_op jit(solution)/shard_map/ppermute | solution.py:486
  24.2 12.7 %collective-permute-start.12 = (bf16[4,64,512]{2,1,0:T(8,128)(2,1)S(1)}, bf16[4,64,512]{2,1,0:T(8,128)(2,1)S(1)}, u32[]{:S(2)}, u32[]{:S(2)}) collective-permute-start(bf16[4,64,512]{2,1,0:T(8,128)(2,1)S(1)} %pad_maximum_fusion), channel_id=1, source_target_pairs={{0,8},{1,9},{2,10},{3,11},{4,12},{5,13},{6,14},{7,15},{8,0},{9,1},... | collective-permute-start | bytes 786440 | tf_op jit(solution)/shard_map/ppermute | solution.py:486
  26.8 10.1 %collective-permute-start.13 = (bf16[4,64,512]{2,1,0:T(8,128)(2,1)S(1)}, bf16[4,64,512]{2,1,0:T(8,128)(2,1)S(1)}, u32[]{:S(2)}, u32[]{:S(2)}) collective-permute-start(bf16[4,64,512]{2,1,0:T(8,128)(2,1)S(1)} %pad_maximum_fusion), channel_id=1, source_target_pairs={{0,12},{1,13},{2,14},{3,15},{4,0},{5,1},{6,2},{7,3},{8,4},{9,5},{1... | collective-permute-start | bytes 786440 | tf_op jit(solution)/shard_map/ppermute | solution.py:486
  38.0 72.7 %all-to-all-start = ((bf16[16,288,512]{2,1,0:T(8,128)(2,1)}), bf16[16,288,512]{2,1,0:T(8,128)(2,1)}, u32[]{:S(2)}, u32[]{:S(2)}) async-start(bf16[16,288,512]{2,1,0:T(8,128)(2,1)} %pack.1), calls=%async_computation | async-start | bytes 9437184 | tf_op jit(solution)/shard_map/all_to_all | solution.py:466
  46.1 4.2 %collective-permute-start = (bf16[8,64,640]{2,1,0:T(8,128)(2,1)S(1)}, bf16[8,64,640]{2,1,0:T(8,128)(2,1)S(1)}, u32[]{:S(2)}, u32[]{:S(2)}) collective-permute-start(bf16[8,64,640]{2,1,0:T(8,128)(2,1)S(1)} %get-tuple-element.53), channel_id=1, source_target_pairs={{0,16},{16,0},{32,48},{48,32},{64,80},{80,64},{96,112},{112,96},{1... | collective-permute-start | bytes 1966088 | tf_op jit(solution)/shard_map/ppermute | solution.py:470
  51.0 13.5 %collective-permute-start.1 = (bf16[2,64,640]{2,1,0:T(8,128)(2,1)S(1)}, bf16[2,64,640]{2,1,0:T(8,128)(2,1)S(1)}, u32[]{:S(2)}, u32[]{:S(2)}) collective-permute-start(bf16[2,64,640]{2,1,0:T(8,128)(2,1)S(1)} %get-tuple-element.55), channel_id=1, source_target_pairs={{0,32},{16,48},{32,64},{48,80},{64,96},{80,112},{96,128},{112,144}... | collective-permute-start | bytes 491528 | tf_op jit(solution)/shard_map/ppermute | solution.py:475
  52.7 22.6 %collective-permute-start.2 = (bf16[2,64,640]{2,1,0:T(8,128)(2,1)S(1)}, bf16[2,64,640]{2,1,0:T(8,128)(2,1)S(1)}, u32[]{:S(2)}, u32[]{:S(2)}) collective-permute-start(bf16[2,64,640]{2,1,0:T(8,128)(2,1)S(1)} %get-tuple-element.56), channel_id=1, source_target_pairs={{0,64},{16,80},{32,96},{48,112},{64,128},{80,144},{96,160},{112,17... | collective-permute-start | bytes 491528 | tf_op jit(solution)/shard_map/ppermute | solution.py:475
  55.7 33.2 %collective-permute-start.3 = (bf16[2,64,640]{2,1,0:T(8,128)(2,1)S(1)}, bf16[2,64,640]{2,1,0:T(8,128)(2,1)S(1)}, u32[]{:S(2)}, u32[]{:S(2)}) collective-permute-start(bf16[2,64,640]{2,1,0:T(8,128)(2,1)S(1)} %get-tuple-element.57), channel_id=1, source_target_pairs={{0,96},{16,112},{32,128},{48,144},{64,160},{80,176},{96,192},{112,... | collective-permute-start | bytes 491528 | tf_op jit(solution)/shard_map/ppermute | solution.py:475
  59.4 41.7 %collective-permute-start.4 = (bf16[2,64,640]{2,1,0:T(8,128)(2,1)S(1)}, bf16[2,64,640]{2,1,0:T(8,128)(2,1)S(1)}, u32[]{:S(2)}, u32[]{:S(2)}) collective-permute-start(bf16[2,64,640]{2,1,0:T(8,128)(2,1)S(1)} %get-tuple-element.58), channel_id=1, source_target_pairs={{0,128},{16,144},{32,160},{48,176},{64,192},{80,208},{96,224},{112... | collective-permute-start | bytes 491528 | tf_op jit(solution)/shard_map/ppermute | solution.py:475
  59.9 41.2 %collective-permute-start.5 = (bf16[2,64,640]{2,1,0:T(8,128)(2,1)S(1)}, bf16[2,64,640]{2,1,0:T(8,128)(2,1)S(1)}, u32[]{:S(2)}, u32[]{:S(2)}) collective-permute-start(bf16[2,64,640]{2,1,0:T(8,128)(2,1)S(1)} %get-tuple-element.59), channel_id=1, source_target_pairs={{0,160},{16,176},{32,192},{48,208},{64,224},{80,240},{96,0},{112,1... | collective-permute-start | bytes 491528 | tf_op jit(solution)/shard_map/ppermute | solution.py:475
  64.4 36.7 %collective-permute-start.6 = (bf16[2,64,640]{2,1,0:T(8,128)(2,1)S(1)}, bf16[2,64,640]{2,1,0:T(8,128)(2,1)S(1)}, u32[]{:S(2)}, u32[]{:S(2)}) collective-permute-start(bf16[2,64,640]{2,1,0:T(8,128)(2,1)S(1)} %get-tuple-element.60), channel_id=1, source_target_pairs={{0,192},{16,208},{32,224},{48,240},{64,0},{80,16},{96,32},{112,48}... | collective-permute-start | bytes 491528 | tf_op jit(solution)/shard_map/ppermute | solution.py:475
  75.3 28.9 %collective-permute-start.7 = (bf16[2,64,640]{2,1,0:T(8,128)(2,1)S(1)}, bf16[2,64,640]{2,1,0:T(8,128)(2,1)S(1)}, u32[]{:S(2)}, u32[]{:S(2)}) collective-permute-start(bf16[2,64,640]{2,1,0:T(8,128)(2,1)S(1)} %get-tuple-element.61), channel_id=1, source_target_pairs={{0,224},{16,240},{32,0},{48,16},{64,32},{80,48},{96,64},{112,80},{... | collective-permute-start | bytes 491528 | tf_op jit(solution)/shard_map/ppermute | solution.py:475
  162.9 59.3 %all-to-all-start.3 = ((bf16[16,256,512]{2,1,0:T(8,128)(2,1)}), bf16[16,256,512]{2,1,0:T(8,128)(2,1)}, u32[]{:S(2)}, u32[]{:S(2)}) async-start(bf16[16,256,512]{2,1,0:T(8,128)(2,1)} %copy-done.4), calls=%async_computation.3 | async-start | bytes 8388608 | tf_op jit(solution)/shard_map/all_to_all | solution.py:466
  175.0 6.9 %collective-permute-start.14 = (bf16[8,64,640]{2,1,0:T(8,128)(2,1)S(1)}, bf16[8,64,640]{2,1,0:T(8,128)(2,1)S(1)}, u32[]{:S(2)}, u32[]{:S(2)}) collective-permute-start(bf16[8,64,640]{2,1,0:T(8,128)(2,1)S(1)} %get-tuple-element.78), channel_id=1, source_target_pairs={{0,16},{16,0},{32,48},{48,32},{64,80},{80,64},{96,112},{112,96},{1... | collective-permute-start | bytes 1966088 | tf_op jit(solution)/shard_map/ppermute | solution.py:470
  182.6 13.4 %collective-permute-start.15 = (bf16[2,64,640]{2,1,0:T(8,128)(2,1)S(1)}, bf16[2,64,640]{2,1,0:T(8,128)(2,1)S(1)}, u32[]{:S(2)}, u32[]{:S(2)}) collective-permute-start(bf16[2,64,640]{2,1,0:T(8,128)(2,1)S(1)} %get-tuple-element.80), channel_id=1, source_target_pairs={{0,32},{16,48},{32,64},{48,80},{64,96},{80,112},{96,128},{112,144}... | collective-permute-start | bytes 491528 | tf_op jit(solution)/shard_map/ppermute | solution.py:475
  184.7 14.0 %collective-permute-start.16 = (bf16[2,64,640]{2,1,0:T(8,128)(2,1)S(1)}, bf16[2,64,640]{2,1,0:T(8,128)(2,1)S(1)}, u32[]{:S(2)}, u32[]{:S(2)}) collective-permute-start(bf16[2,64,640]{2,1,0:T(8,128)(2,1)S(1)} %get-tuple-element.81), channel_id=1, source_target_pairs={{0,64},{16,80},{32,96},{48,112},{64,128},{80,144},{96,160},{112,17... | collective-permute-start | bytes 491528 | tf_op jit(solution)/shard_map/ppermute | solution.py:475
  187.3 33.7 %collective-permute-start.17 = (bf16[2,64,640]{2,1,0:T(8,128)(2,1)S(1)}, bf16[2,64,640]{2,1,0:T(8,128)(2,1)S(1)}, u32[]{:S(2)}, u32[]{:S(2)}) collective-permute-start(bf16[2,64,640]{2,1,0:T(8,128)(2,1)S(1)} %get-tuple-element.82), channel_id=1, source_target_pairs={{0,96},{16,112},{32,128},{48,144},{64,160},{80,176},{96,192},{112,... | collective-permute-start | bytes 491528 | tf_op jit(solution)/shard_map/ppermute | solution.py:475
  190.9 30.1 %collective-permute-start.18 = (bf16[2,64,640]{2,1,0:T(8,128)(2,1)S(1)}, bf16[2,64,640]{2,1,0:T(8,128)(2,1)S(1)}, u32[]{:S(2)}, u32[]{:S(2)}) collective-permute-start(bf16[2,64,640]{2,1,0:T(8,128)(2,1)S(1)} %get-tuple-element.83), channel_id=1, source_target_pairs={{0,128},{16,144},{32,160},{48,176},{64,192},{80,208},{96,224},{112... | collective-permute-start | bytes 491528 | tf_op jit(solution)/shard_map/ppermute | solution.py:475
  191.6 29.4 %collective-permute-start.19 = (bf16[2,64,640]{2,1,0:T(8,128)(2,1)S(1)}, bf16[2,64,640]{2,1,0:T(8,128)(2,1)S(1)}, u32[]{:S(2)}, u32[]{:S(2)}) collective-permute-start(bf16[2,64,640]{2,1,0:T(8,128)(2,1)S(1)} %get-tuple-element.84), channel_id=1, source_target_pairs={{0,160},{16,176},{32,192},{48,208},{64,224},{80,240},{96,0},{112,1... | collective-permute-start | bytes 491528 | tf_op jit(solution)/shard_map/ppermute | solution.py:475
  196.0 25.0 %collective-permute-start.20 = (bf16[2,64,640]{2,1,0:T(8,128)(2,1)S(1)}, bf16[2,64,640]{2,1,0:T(8,128)(2,1)S(1)}, u32[]{:S(2)}, u32[]{:S(2)}) collective-permute-start(bf16[2,64,640]{2,1,0:T(8,128)(2,1)S(1)} %get-tuple-element.85), channel_id=1, source_target_pairs={{0,192},{16,208},{32,224},{48,240},{64,0},{80,16},{96,32},{112,48}... | collective-permute-start | bytes 491528 | tf_op jit(solution)/shard_map/ppermute | solution.py:475
  198.7 23.5 %collective-permute-start.21 = (bf16[2,64,640]{2,1,0:T(8,128)(2,1)S(1)}, bf16[2,64,640]{2,1,0:T(8,128)(2,1)S(1)}, u32[]{:S(2)}, u32[]{:S(2)}) collective-permute-start(bf16[2,64,640]{2,1,0:T(8,128)(2,1)S(1)} %get-tuple-element.86), channel_id=1, source_target_pairs={{0,224},{16,240},{32,0},{48,16},{64,32},{80,48},{96,64},{112,80},{... | collective-permute-start | bytes 491528 | tf_op jit(solution)/shard_map/ppermute | solution.py:475
  (13 other events, 126.9 us)
Sparse Core Ops, SparseCore 0:
  38.1 127.6 all-gather.2

commit v6 on v5

--- a/solution.py
+++ b/solution.py
@@ -13,8 +13,7 @@
 VMEM_BYTES = 40 * 1024 * 1024
 VMEM_MOST = 58 * 1024 * 1024
 GROUP = 4
-SIDE = 4
-CORE, FIRST, CHIP, PIECE, LIST = 0, 1, 2, 3, 4
+CORE, CHIP, LIST = 0, 1, 2
 
 
 def call(kernel, name, flops=0, moved=0, vmem=VMEM_BYTES, **kw):
@@ -69,27 +68,22 @@
     return (row >= begin) & (row < end)
 
 
-def turn_kernel(at, w, out):
-    both = jnp.transpose(w[...].astype(F32)).astype(BF)
-    part = out.shape[0]
-    low = lax.rem(at[0], 2) == 0
-    out[...] = jnp.where(low, both[:part], both[part:])
-
-
-def turn(at, w, slices):
+def turn_kernel(w, out):
+    out[...] = jnp.transpose(w[...].astype(F32)).astype(BF)
+
+
+def turn(w):
     piece, width = w.shape
-    part = width // slices
+    block = width // GROUP
     return call(
         turn_kernel,
         "turn",
-        moved=4 * part * piece,
-        grid_spec=with_meta(
-            (1,),
-            [pl.BlockSpec((piece, 2 * part), lambda i, m: (0, m[0] // 2))],
-            whole((part, piece)),
-        ),
-        out_shape=jax.ShapeDtypeStruct((part, piece), BF),
-    )(at, w)
+        moved=4 * width * piece,
+        grid=(GROUP,),
+        in_specs=[pl.BlockSpec((piece, block), lambda i: (0, i))],
+        out_specs=pl.BlockSpec((block, piece), lambda i: (i, 0)),
+        out_shape=jax.ShapeDtypeStruct((width, piece), BF),
+    )(w)
 
 
 def pack_kernel(tok, cot_t, out):
@@ -366,100 +360,66 @@
     )(meta, *got)
 
 
-def term_kernel(slots, rank, meta, low, down, out, acc):
+def term_kernel(slots, rank, meta, low, cot, w, down, out):
     group, _, rows = low.shape
     piece = out.shape[2]
+    table = jnp.concatenate([down[s, :, :piece] for s in range(slots)], axis=0)
     for g in range(group):
         first = (pl.program_id(0) * group + g) * rows
-        acc[...] = jnp.zeros_like(acc)
-        for s in range(slots):
-            start, end = start_of(meta, s), end_of(meta, s, slots)
-
-            @pl.when((start < first + rows) & (end > first))
-            def _():
-                token = first + lax.broadcasted_iota(jnp.int32, (rank, rows), 1)
-                lg = low[g, rank:, :].astype(F32)
-                lg = jnp.where((token >= start) & (token < end), lg, 0.0).astype(BF)
-                acc[...] += lax.dot_general(
-                    lg, down[s, :, :piece], (((0,), (0,)), ((), ())), preferred_element_type=F32
-                )
-
-        out[g] = acc[...].astype(BF)
-
-
-def term(meta, low, down, piece, slots, rank):
+        lg = low[g, rank:, :].astype(F32)
+        lg = jnp.transpose(jnp.concatenate([lg, lg], axis=0))
+        lg = [
+            jnp.where(inside_pair(meta, p, first, lg.shape, slots, rank), lg, 0.0)
+            for p in range(slots // 2)
+        ]
+        lg = jnp.concatenate(lg, axis=1).astype(BF)
+        acc = jnp.dot(cot[g], w[...], preferred_element_type=F32)
+        acc += jnp.dot(lg, table, preferred_element_type=F32)
+        out[g] = acc.astype(BF)
+
+
+def term(meta, low, cot, w, down, slots, rank):
     n, wide, rows = low.shape
+    width, piece = w.shape
+    group = 2
     return call(
         functools.partial(term_kernel, slots, rank),
         "term",
-        flops=2 * n * rows * piece * 2 * rank,
-        moved=2 * n * rows * piece,
+        flops=2 * n * rows * piece * (width + slots * rank),
+        moved=2 * n * rows * (piece + width),
+        vmem=VMEM_MOST,
         grid_spec=with_meta(
-            (n // GROUP,),
-            [pl.BlockSpec((GROUP, wide, rows), lambda j, m: (j, 0, 0)), whole(down.shape)],
-            pl.BlockSpec((GROUP, rows, piece), lambda j, m: (j, 0, 0)),
-            [pltpu.VMEM((rows, piece), F32)],
+            (n // group,),
+            [
+                pl.BlockSpec((group, wide, rows), lambda j, m: (j, 0, 0)),
+                pl.BlockSpec((group, rows, width), lambda j, m: (j, 0, 0)),
+                whole(w.shape),
+                whole(down.shape),
+            ],
+            pl.BlockSpec((group, rows, piece), lambda j, m: (j, 0, 0)),
         ),
         out_shape=jax.ShapeDtypeStruct((n, rows, piece), BF),
-    )(meta, low, down)
-
-
-def base_kernel(meta, cot, w, out):
-    out[...] = jnp.dot(
-        cot[...],
-        jnp.concatenate([w[e, 0] for e in range(w.shape[0])], axis=0),
-        preferred_element_type=F32,
-    )
-
-
-def base(meta, cot, w):
-    slices, n, part, piece = w.shape
-    rows, width = cot.shape
-
-    def place(f, m):
-        y = lax.rem(m[PIECE] // SIDE + SIDE - f // SIDE, SIDE)
-        x = lax.rem(lax.rem(m[PIECE], SIDE) + SIDE - lax.rem(f, SIDE), SIDE)
-        return (0, y * SIDE + x)
-
-    return call(
-        base_kernel,
-        "base",
-        flops=2 * rows * n * piece * width,
-        moved=2 * n * piece * width + 4 * rows * n * piece,
-        grid_spec=with_meta(
-            (n,),
-            [
-                whole(cot.shape),
-                pl.BlockSpec((slices, 1, part, piece), lambda f, m: (0, f, 0, 0)),
-            ],
-            pl.BlockSpec((rows, piece), place),
-        ),
-        out_shape=jax.ShapeDtypeStruct((rows, n * piece), F32),
-    )(meta, cot, w)
-
-
-def join_kernel(done, terms, out):
-    group, _, piece = terms.shape
+    )(meta, low, cot, w, down)
+
+
+def lay_kernel(blocks, out):
+    group, _, piece = blocks.shape
     for g in range(group):
-        cols = slice(g * piece, (g + 1) * piece)
-        out[:, cols] = (done[:, cols] + terms[g].astype(F32)).astype(BF)
-
-
-def join(done, terms):
-    n, rows, piece = terms.shape
-    group = 2
-    return call(
-        join_kernel,
-        "join",
-        moved=8 * n * rows * piece,
-        grid=(n // group,),
-        in_specs=[
-            pl.BlockSpec((rows, group * piece), lambda f: (0, f)),
-            pl.BlockSpec((group, rows, piece), lambda f: (f, 0, 0)),
-        ],
-        out_specs=pl.BlockSpec((rows, group * piece), lambda f: (0, f)),
+        out[:, g * piece:(g + 1) * piece] = blocks[g]
+
+
+def lay(blocks):
+    n, rows, piece = blocks.shape
+    return call(
+        lay_kernel,
+        "lay",
+        moved=4 * n * rows * piece,
+        vmem=VMEM_MOST,
+        grid=(n // GROUP,),
+        in_specs=[pl.BlockSpec((GROUP, rows, piece), lambda f: (f, 0, 0))],
+        out_specs=pl.BlockSpec((rows, GROUP * piece), lambda f: (0, f)),
         out_shape=jax.ShapeDtypeStruct((rows, n * piece), BF),
-    )(done, terms)
+    )(blocks)
 
 
 def exchange(x, axis):
@@ -482,18 +442,7 @@
     return [blocks[0]] + [shift(blocks[k], k, bins) for k in range(1, bins // 2)]
 
 
-def across(x, dy, dx, n):
-    return lax.ppermute(
-        x,
-        "fsdp",
-        [
-            (i, (i // SIDE + dy) % SIDE * SIDE + (i % SIDE + dx) % SIDE)
-            for i in range(n)
-        ],
-    )
-
-
-def scalars(segment_tenant, segment_lengths, tenant_stored_row, own, rows):
+def scalars(segment_tenant, segment_lengths, tenant_stored_row, own):
     bins, slots = segment_tenant.shape
     me = lax.axis_index("dp")
     tenants = jnp.arange(tenant_stored_row.shape[0], dtype=jnp.int32)
@@ -507,8 +456,7 @@
     wanted = jnp.max(jnp.where(stored // own == me, stored % own, -1), axis=1)
     every = jnp.arange(bins, dtype=jnp.int32)
     segment = jnp.max(jnp.where(owners[None, :] == every[:, None], place[None, :], -1), axis=1)
-    place_f = lax.axis_index("fsdp")
-    head = jnp.stack([me % 2, place_f * rows, me // 2, place_f])
+    head = jnp.stack([me % 2, me // 2])
     return jnp.concatenate([head, starts, starts + lengths, owners, wanted, segment]).astype(
         jnp.int32
     )
@@ -531,35 +479,26 @@
     rows = tokens.shape[0]
     n = lax.axis_size("fsdp")
     scale = (n * rows) ** (-0.5)
-    meta = scalars(segment_tenant, segment_lengths, tenant_stored_row, own, rows)
-
-    packed = pack(tokens, jnp.swapaxes(cotangent, 0, 1), n)
-    me = lax.axis_index("dp").astype(jnp.int32).reshape(1)
-    packed, me = lax.optimization_barrier((packed, me))
-    parts = exchange(packed, "fsdp")
-    mine = turn(me, value_weight, bins)[None]
-    mine = jnp.concatenate([mine] + [across(mine, 0, k, n) for k in range(1, SIDE)])
-    mine = jnp.concatenate([mine] + [across(mine, k, 0, n) for k in range(1, SIDE)])
-    weight = lax.all_gather(mine, "dp", axis=0)
-
+    meta = scalars(segment_tenant, segment_lengths, tenant_stored_row, own)
+
+    parts = exchange(pack(tokens, jnp.swapaxes(cotangent, 0, 1), n), "fsdp")
+    cot = lax.all_gather(cotangent, "fsdp", axis=0)
     keep, give = offer(
         meta, jnp.swapaxes(adapter_down_weight, 1, 2), adapter_up_weight, chips, slots
     )
     got = spread(meta, keep, give, bins)
-    parts, got, mine = lax.optimization_barrier((parts, got, mine))
+    parts, got = lax.optimization_barrier((parts, got))
     down, down_t, up_t = choose(meta, got, slots, v)
 
     sums = exchange(project(meta, parts, down_t, up_t, rows, slots, rank), "fsdp")
     low_all = exchange(total(sums), "fsdp")
-    terms = term(meta, low_all, down, piece, slots, rank)
+    terms = term(meta, low_all, cot, turn(value_weight), down, slots, rank)
     terms, low_all = lax.optimization_barrier((terms, low_all))
     terms = exchange(terms, "fsdp")
     sent = spread(meta, *gradient(meta, parts, low_all, chips, slots, rank, v), bins)
-    done = base(meta, cotangent, weight)
-    terms, sent, done = lax.optimization_barrier((terms, sent, done))
-    grad = join(done, terms)
     down_grad, up_grad = collect(meta, sent, own, v, slots, scale)
-    return grad, jnp.swapaxes(down_grad, 1, 2), up_grad
+    terms, down_grad, up_grad = lax.optimization_barrier((terms, down_grad, up_grad))
+    return lay(terms), jnp.swapaxes(down_grad, 1, 2), up_grad
 
 
 def solution(mesh):

time: 243 us -> 245 us (level)
  waiting for transfers between devices: 58.4 us -> 90.4 us
  Pallas kernels: 55.5 us -> 43.6 us
  starting transfers between devices: 66.2 us -> 56.9 us
  local copies, waits for them, and re-layouts: 12.2 us -> 4.36 us
    all_to_all x2 -> x3, waiting for transfers between devices: 6.5 us -> 43.7 us  [exchange(): return lax.all_to_all(x, axis, 0, 0, tiled=True)]
    pallas_call x3 -> x2, Pallas kernels: 22.8 us -> 5.48 us  [the longest x1 4.73 us: lay(): call(lay_kernel, 'lay', moved=4 * n * rows * piece, vmem=VMEM_MOST, grid=...]
    ppermute x6 -> x0, waiting for transfers between devices: 11.2 us -> none  [across(): lax.ppermute(x, 'fsdp', [(i, (i // SIDE + dy) % SIDE * SIDE + (i % SIDE +...]
    ppermute x6 -> x0, starting transfers between devices: 11 us -> none  [across(): lax.ppermute(x, 'fsdp', [(i, (i // SIDE + dy) % SIDE * SIDE + (i % SIDE +...]
    unnamed x32 -> x26, local copies, waits for them, and re-layouts: 11.9 us -> 4.1 us
    all_to_all x2 -> x3, starting transfers between devices: 10.9 us -> 16.3 us  [exchange(): return lax.all_to_all(x, axis, 0, 0, tiled=True)]
    ppermute x14, waiting for transfers between devices: 37.2 us -> 42.5 us  [shift(): lax.ppermute(x, 'dp', [(i, (i // 2 + k) % chips * 2 + i % 2) for i in ran...]
    pallas_call x1, Pallas kernels: 8.14 us -> 13.2 us  [term(): call(functools.partial(term_kernel, slots, rank), 'term', flops=2 * n * r...]
  transfers between devices with their start and end apart: 25 -> 20, of which waited for: 13 -> 11; matrix products, arithmetic and copies ran while one was open for 0% -> 1% of each run, Pallas kernels for 17% -> 11%
where the time goes in v6:
time: 245 us; the launch traced here: 242 us
  waiting for transfers between devices  90.4 us (37%)
  starting transfers between devices  56.9 us (23%)
  Pallas kernels  43.6 us (18%)
  blocking collectives  31.4 us (13%)
  between operations  14.3 us (6%)
  local copies, waits for them, and re-layouts  4.36 us (2%)
    all_to_all x3, waiting for transfers between devices, exchange(): return lax.all_to_all(x, axis, 0, 0, tiled=True)  43.7 us
    ppermute x14, waiting for transfers between devices, shift(): lax.ppermute(x, 'dp', [(i, (i // 2 + k) % chips * 2 + i % 2) for i in ran...  42.5 us
    ppermute x14, starting transfers between devices, shift(): lax.ppermute(x, 'dp', [(i, (i // 2 + k) % chips * 2 + i % 2) for i in ran...  34.6 us
    all_to_all x1, blocking collectives, exchange(): return lax.all_to_all(x, axis, 0, 0, tiled=True)  31.4 us
    all_to_all x3, starting transfers between devices, exchange(): return lax.all_to_all(x, axis, 0, 0, tiled=True)  16.3 us
    pallas_call x1, Pallas kernels, term(): call(functools.partial(term_kernel, slots, rank), 'term', flops=2 * n * r...  13.2 us
    pallas_call x1, Pallas kernels, gradient(): call(functools.partial(gradient_kernel, slots, rank, v), 'gradient', flop...  7.37 us
    pallas_call x1, Pallas kernels, project(): call(functools.partial(project_kernel, slots, rank), 'project', flops=2 *...  6.74 us
  transfers between devices with their start and end apart: 20, of which 11 were waited for; matrix products, arithmetic and copies ran while one was open for 1% of the time, Pallas kernels for 11%

profile of v6, /device:TPU:1, one launch (start us, length us, event | category | flops | bytes accessed | tf_op | source)
XLA Modules:
  0.0 241.6 jit_solution(15923580963920001560)
XLA Ops:
  10.0 5.0 %pack.1 = bf16[16,288,512]{2,1,0:T(8,128)(2,1)} custom-call(bf16[256,8192]{1,0:T(8,128)(2,1)} %tok.1, bf16[1024,256]{1,0:T(8,128)(2,1)} %bitcast.17), custom_call_target="tpu_custom_call" | custom-call | bytes 8388608 | tf_op jit(solution)/shard_map/pack/pallas_call | solution.py:103
  14.9 7.8 %all-to-all-start = ((bf16[16,288,512]{2,1,0:T(8,128)(2,1)}), bf16[16,288,512]{2,1,0:T(8,128)(2,1)}, u32[]{:S(2)}, u32[]{:S(2)}) async-start(bf16[16,288,512]{2,1,0:T(8,128)(2,1)} %pack.1), calls=%async_computation | async-start | bytes 9437184 | tf_op jit(solution)/shard_map/all_to_all | solution.py:426
  29.7 3.0 %collective-permute-start.2 = (bf16[2,64,640]{2,1,0:T(8,128)(2,1)S(1)}, bf16[2,64,640]{2,1,0:T(8,128)(2,1)S(1)}, u32[]{:S(2)}, u32[]{:S(2)}) collective-permute-start(bf16[2,64,640]{2,1,0:T(8,128)(2,1)S(1)} %get-tuple-element.46), channel_id=1, source_target_pairs={{0,64},{16,80},{32,96},{48,112},{64,128},{80,144},{96,160},{112,17... | collective-permute-start | bytes 491528 | tf_op jit(solution)/shard_map/ppermute | solution.py:435
  32.6 3.8 %collective-permute-start.3 = (bf16[2,64,640]{2,1,0:T(8,128)(2,1)S(1)}, bf16[2,64,640]{2,1,0:T(8,128)(2,1)S(1)}, u32[]{:S(2)}, u32[]{:S(2)}) collective-permute-start(bf16[2,64,640]{2,1,0:T(8,128)(2,1)S(1)} %get-tuple-element.47), channel_id=1, source_target_pairs={{0,96},{16,112},{32,128},{48,144},{64,160},{80,176},{96,192},{112,... | collective-permute-start | bytes 491528 | tf_op jit(solution)/shard_map/ppermute | solution.py:435
  36.9 4.5 %collective-permute-start.5 = (bf16[2,64,640]{2,1,0:T(8,128)(2,1)S(1)}, bf16[2,64,640]{2,1,0:T(8,128)(2,1)S(1)}, u32[]{:S(2)}, u32[]{:S(2)}) collective-permute-start(bf16[2,64,640]{2,1,0:T(8,128)(2,1)S(1)} %get-tuple-element.49), channel_id=1, source_target_pairs={{0,160},{16,176},{32,192},{48,208},{64,224},{80,240},{96,0},{112,1... | collective-permute-start | bytes 491528 | tf_op jit(solution)/shard_map/ppermute | solution.py:435
  43.7 3.9 %collective-permute-start.7 = (bf16[2,64,640]{2,1,0:T(8,128)(2,1)S(1)}, bf16[2,64,640]{2,1,0:T(8,128)(2,1)S(1)}, u32[]{:S(2)}, u32[]{:S(2)}) collective-permute-start(bf16[2,64,640]{2,1,0:T(8,128)(2,1)S(1)} %get-tuple-element.51), channel_id=1, source_target_pairs={{0,224},{16,240},{32,0},{48,16},{64,32},{80,48},{96,64},{112,80},{... | collective-permute-start | bytes 491528 | tf_op jit(solution)/shard_map/ppermute | solution.py:435
  47.6 8.3 %collective-permute-done.3.refs_3_ = bf16[2,64,640]{2,1,0:T(8,128)(2,1)S(1)} collective-permute-done((bf16[2,64,640]{2,1,0:T(8,128)(2,1)S(1)}, bf16[2,64,640]{2,1,0:T(8,128)(2,1)S(1)}, u32[]{:S(2)}, u32[]{:S(2)}) %collective-permute-start.3) | collective-permute-done | bytes 163872 | tf_op jit(solution)/shard_map/ppermute | solution.py:435
  55.8 2.7 %collective-permute-done.4.refs_4_ = bf16[2,64,640]{2,1,0:T(8,128)(2,1)S(1)} collective-permute-done((bf16[2,64,640]{2,1,0:T(8,128)(2,1)S(1)}, bf16[2,64,640]{2,1,0:T(8,128)(2,1)S(1)}, u32[]{:S(2)}, u32[]{:S(2)}) %collective-permute-start.4) | collective-permute-done | bytes 163872 | tf_op jit(solution)/shard_map/ppermute | solution.py:435
  58.6 7.9 %collective-permute-done.6.refs_6_ = bf16[2,64,640]{2,1,0:T(8,128)(2,1)S(1)} collective-permute-done((bf16[2,64,640]{2,1,0:T(8,128)(2,1)S(1)}, bf16[2,64,640]{2,1,0:T(8,128)(2,1)S(1)}, u32[]{:S(2)}, u32[]{:S(2)}) %collective-permute-start.6) | collective-permute-done | bytes 163872 | tf_op jit(solution)/shard_map/ppermute | solution.py:435
  67.5 31.5 %all-to-all-done.part = bf16[16,288,512]{2,1,0:T(8,128)(2,1)} async-done(((bf16[16,288,512]{2,1,0:T(8,128)(2,1)}), bf16[16,288,512]{2,1,0:T(8,128)(2,1)}, u32[]{:S(2)}, u32[]{:S(2)}) %all-to-all-start) | async-done | bytes 4718624 | tf_op jit(solution)/shard_map/all_to_all | solution.py:426
  100.0 6.7 %project.1 = bf16[16,256,128]{2,1,0:T(8,128)(2,1)S(1)} custom-call(s32[58]{0:T(128)S(1)} %concatenate.3.meta, bf16[16,288,512]{2,1,0:T(8,128)(2,1)} %all-to-all-done.part, bf16[512,512]{1,0:T(8,128)(2,1)S(1)} %get-tuple-element.61.down_t, bf16[64,512]{1,0:T(8,128)(2,1)S(1)} %get-tuple-element.62.up_t), custom_call_target="tpu_custom_call" | custom-call | flops 2147483648 | bytes 4718592 | tf_op jit(solution)/shard_map/project/pallas_call | solution.py:227
  106.8 31.4 %all_to_all.20.parts = bf16[16,256,128]{2,1,0:T(8,128)(2,1)S(1)} all-to-all(bf16[16,256,128]{2,1,0:T(8,128)(2,1)S(1)} %project.1), channel_id=1, replica_groups=mesh['dp'=16,'fsdp'=16] {'fsdp'}, dimensions={0} | all-to-all | bytes 2097152 | tf_op jit(solution)/shard_map/all_to_all | solution.py:426
  139.4 3.7 %all-to-all-start.2 = ((bf16[16,128,256]{2,1,0:T(8,128)(2,1)}), bf16[16,128,256]{2,1,0:T(8,128)(2,1)S(1)}, u32[]{:S(2)}, u32[]{:S(2)}) async-start(bf16[16,128,256]{2,1,0:T(8,128)(2,1)} %total.1), calls=%async_computation.2 | async-start | bytes 2097152 | tf_op jit(solution)/shard_map/all_to_all | solution.py:426
  144.9 12.2 %all-to-all-done.2.low = bf16[16,128,256]{2,1,0:T(8,128)(2,1)S(1)} async-done(((bf16[16,128,256]{2,1,0:T(8,128)(2,1)}), bf16[16,128,256]{2,1,0:T(8,128)(2,1)S(1)}, u32[]{:S(2)}, u32[]{:S(2)}) %all-to-all-start.2) | async-done | bytes 1048608 | tf_op jit(solution)/shard_map/all_to_all | solution.py:426
  158.0 13.2 %term.1 = bf16[16,256,512]{2,1,0:T(8,128)(2,1)} custom-call(s32[58]{0:T(128)} %copy-done.7, bf16[16,128,256]{2,1,0:T(8,128)(2,1)} %copy-done.2, bf16[16,256,1024]{2,1,0:T(8,128)(2,1)} %bitcast.18, bf16[1024,512]{1,0:T(8,128)(2,1)} %copy-done.4, bf16[8,64,640]{2,1,0:T(8,128)(2,1)} %copy-done.9), custom_call_target="tpu_custom_call" | custom-call | flops 6442450944 | bytes 12582912 | tf_op jit(solution)/shard_map/term/pallas_call | solution.py:385
  171.2 4.9 %all-to-all-start.3 = ((bf16[16,256,512]{2,1,0:T(8,128)(2,1)}), bf16[16,256,512]{2,1,0:T(8,128)(2,1)}, u32[]{:S(2)}, u32[]{:S(2)}) async-start(bf16[16,256,512]{2,1,0:T(8,128)(2,1)} %term.1), calls=%async_computation.3 | async-start | bytes 8388608 | tf_op jit(solution)/shard_map/all_to_all | solution.py:426
  176.1 7.4 %gradient.1 = (bf16[8,64,640]{2,1,0:T(8,128)(2,1)S(1)}, bf16[8,64,640]{2,1,0:T(8,128)(2,1)S(1)}) custom-call(s32[58]{0:T(128)S(1)} %copy-done.8, bf16[16,288,512]{2,1,0:T(8,128)(2,1)} %all-to-all-done.part, bf16[16,128,256]{2,1,0:T(8,128)(2,1)S(1)} %copy-done.3), custom_call_target="tpu_custom_call" | custom-call | flops 2147483648 | bytes 4718592 | tf_op jit(solution)/shard_map/gradient/pallas_call | solution.py:316
  183.4 4.9 %collective-permute-start.8 = (bf16[8,64,640]{2,1,0:T(8,128)(2,1)S(1)}, bf16[8,64,640]{2,1,0:T(8,128)(2,1)S(1)}, u32[]{:S(2)}, u32[]{:S(2)}) collective-permute-start(bf16[8,64,640]{2,1,0:T(8,128)(2,1)S(1)} %get-tuple-element.67), channel_id=1, source_target_pairs={{0,16},{16,0},{32,48},{48,32},{64,80},{80,64},{96,112},{112,96},{1... | collective-permute-start | bytes 1966088 | tf_op jit(solution)/shard_map/ppermute | solution.py:430
  190.7 2.8 %collective-permute-start.10 = (bf16[2,64,640]{2,1,0:T(8,128)(2,1)S(1)}, bf16[2,64,640]{2,1,0:T(8,128)(2,1)S(1)}, u32[]{:S(2)}, u32[]{:S(2)}) collective-permute-start(bf16[2,64,640]{2,1,0:T(8,128)(2,1)S(1)} %get-tuple-element.70), channel_id=1, source_target_pairs={{0,64},{16,80},{32,96},{48,112},{64,128},{80,144},{96,160},{112,17... | collective-permute-start | bytes 491528 | tf_op jit(solution)/shard_map/ppermute | solution.py:435
  193.5 4.8 %collective-permute-start.11 = (bf16[2,64,640]{2,1,0:T(8,128)(2,1)S(1)}, bf16[2,64,640]{2,1,0:T(8,128)(2,1)S(1)}, u32[]{:S(2)}, u32[]{:S(2)}) collective-permute-start(bf16[2,64,640]{2,1,0:T(8,128)(2,1)S(1)} %get-tuple-element.71), channel_id=1, source_target_pairs={{0,96},{16,112},{32,128},{48,144},{64,160},{80,176},{96,192},{112,... | collective-permute-start | bytes 491528 | tf_op jit(solution)/shard_map/ppermute | solution.py:435
  199.0 4.2 %collective-permute-start.13 = (bf16[2,64,640]{2,1,0:T(8,128)(2,1)S(1)}, bf16[2,64,640]{2,1,0:T(8,128)(2,1)S(1)}, u32[]{:S(2)}, u32[]{:S(2)}) collective-permute-start(bf16[2,64,640]{2,1,0:T(8,128)(2,1)S(1)} %get-tuple-element.73), channel_id=1, source_target_pairs={{0,160},{16,176},{32,192},{48,208},{64,224},{80,240},{96,0},{112,1... | collective-permute-start | bytes 491528 | tf_op jit(solution)/shard_map/ppermute | solution.py:435
  205.7 11.6 %collective-permute-done.11.refs_3_ = bf16[2,64,640]{2,1,0:T(8,128)(2,1)S(1)} collective-permute-done((bf16[2,64,640]{2,1,0:T(8,128)(2,1)S(1)}, bf16[2,64,640]{2,1,0:T(8,128)(2,1)S(1)}, u32[]{:S(2)}, u32[]{:S(2)}) %collective-permute-start.11) | collective-permute-done | bytes 163872 | tf_op jit(solution)/shard_map/ppermute | solution.py:435
  219.5 8.9 %collective-permute-done.14.refs_6_ = bf16[2,64,640]{2,1,0:T(8,128)(2,1)S(1)} collective-permute-done((bf16[2,64,640]{2,1,0:T(8,128)(2,1)S(1)}, bf16[2,64,640]{2,1,0:T(8,128)(2,1)S(1)}, u32[]{:S(2)}, u32[]{:S(2)}) %collective-permute-start.14) | collective-permute-done | bytes 163872 | tf_op jit(solution)/shard_map/ppermute | solution.py:435
  230.0 4.7 %lay.1 = bf16[256,8192]{1,0:T(8,128)(2,1)} custom-call(bf16[16,256,512]{2,1,0:T(8,128)(2,1)} %all-to-all-done.3.blocks), custom_call_target="tpu_custom_call" | custom-call | bytes 8388608 | tf_op jit(solution)/shard_map/lay/pallas_call | solution.py:413
  (64 shorter events, 27.9 us)
Async XLA Ops:
  7.2 15.6 %copy-start = (s32[16,8]{0,1:T(8,128)S(1)}, s32[16,8]{0,1:T(8,128)}, u32[]{:S(2)}) copy-start(s32[16,8]{0,1:T(8,128)} %param.14) | copy-start | bytes 1540
  7.2 149.9 %all-gather.3.cloned.1.call-start = ((), (), s32[]{:S(2)}) async-start(), calls=%async_computation.4 | async-start | bytes 8912896 | tf_op jit(solution)/shard_map/all_gather | solution.py:485
  14.9 84.0 %all-to-all-start = ((bf16[16,288,512]{2,1,0:T(8,128)(2,1)}), bf16[16,288,512]{2,1,0:T(8,128)(2,1)}, u32[]{:S(2)}, u32[]{:S(2)}) async-start(bf16[16,288,512]{2,1,0:T(8,128)(2,1)} %pack.1), calls=%async_computation | async-start | bytes 9437184 | tf_op jit(solution)/shard_map/all_to_all | solution.py:426
  23.8 82.9 %copy-start.7 = (s32[58]{0:T(128)}, s32[58]{0:T(128)S(1)}, u32[]{:S(2)}) copy-start(s32[58]{0:T(128)S(1)} %concatenate.3.meta) | copy-start | bytes 700
  24.5 2.8 %collective-permute-start = (bf16[8,64,640]{2,1,0:T(8,128)(2,1)S(1)}, bf16[8,64,640]{2,1,0:T(8,128)(2,1)S(1)}, u32[]{:S(2)}, u32[]{:S(2)}) collective-permute-start(bf16[8,64,640]{2,1,0:T(8,128)(2,1)S(1)} %get-tuple-element.43), channel_id=1, source_target_pairs={{0,16},{16,0},{32,48},{48,32},{64,80},{80,64},{96,112},{112,96},{1... | collective-permute-start | bytes 1966088 | tf_op jit(solution)/shard_map/ppermute | solution.py:430
  27.9 13.4 %collective-permute-start.1 = (bf16[2,64,640]{2,1,0:T(8,128)(2,1)S(1)}, bf16[2,64,640]{2,1,0:T(8,128)(2,1)S(1)}, u32[]{:S(2)}, u32[]{:S(2)}) collective-permute-start(bf16[2,64,640]{2,1,0:T(8,128)(2,1)S(1)} %get-tuple-element.45), channel_id=1, source_target_pairs={{0,32},{16,48},{32,64},{48,80},{64,96},{80,112},{96,128},{112,144}... | collective-permute-start | bytes 491528 | tf_op jit(solution)/shard_map/ppermute | solution.py:435
  29.7 14.1 %collective-permute-start.2 = (bf16[2,64,640]{2,1,0:T(8,128)(2,1)S(1)}, bf16[2,64,640]{2,1,0:T(8,128)(2,1)S(1)}, u32[]{:S(2)}, u32[]{:S(2)}) collective-permute-start(bf16[2,64,640]{2,1,0:T(8,128)(2,1)S(1)} %get-tuple-element.46), channel_id=1, source_target_pairs={{0,64},{16,80},{32,96},{48,112},{64,128},{80,144},{96,160},{112,17... | collective-permute-start | bytes 491528 | tf_op jit(solution)/shard_map/ppermute | solution.py:435
  32.6 23.2 %collective-permute-start.3 = (bf16[2,64,640]{2,1,0:T(8,128)(2,1)S(1)}, bf16[2,64,640]{2,1,0:T(8,128)(2,1)S(1)}, u32[]{:S(2)}, u32[]{:S(2)}) collective-permute-start(bf16[2,64,640]{2,1,0:T(8,128)(2,1)S(1)} %get-tuple-element.47), channel_id=1, source_target_pairs={{0,96},{16,112},{32,128},{48,144},{64,160},{80,176},{96,192},{112,... | collective-permute-start | bytes 491528 | tf_op jit(solution)/shard_map/ppermute | solution.py:435
  36.4 22.2 %collective-permute-start.4 = (bf16[2,64,640]{2,1,0:T(8,128)(2,1)S(1)}, bf16[2,64,640]{2,1,0:T(8,128)(2,1)S(1)}, u32[]{:S(2)}, u32[]{:S(2)}) collective-permute-start(bf16[2,64,640]{2,1,0:T(8,128)(2,1)S(1)} %get-tuple-element.48), channel_id=1, source_target_pairs={{0,128},{16,144},{32,160},{48,176},{64,192},{80,208},{96,224},{112... | collective-permute-start | bytes 491528 | tf_op jit(solution)/shard_map/ppermute | solution.py:435
  36.9 21.7 %collective-permute-start.5 = (bf16[2,64,640]{2,1,0:T(8,128)(2,1)S(1)}, bf16[2,64,640]{2,1,0:T(8,128)(2,1)S(1)}, u32[]{:S(2)}, u32[]{:S(2)}) collective-permute-start(bf16[2,64,640]{2,1,0:T(8,128)(2,1)S(1)} %get-tuple-element.49), channel_id=1, source_target_pairs={{0,160},{16,176},{32,192},{48,208},{64,224},{80,240},{96,0},{112,1... | collective-permute-start | bytes 491528 | tf_op jit(solution)/shard_map/ppermute | solution.py:435
  41.3 25.1 %collective-permute-start.6 = (bf16[2,64,640]{2,1,0:T(8,128)(2,1)S(1)}, bf16[2,64,640]{2,1,0:T(8,128)(2,1)S(1)}, u32[]{:S(2)}, u32[]{:S(2)}) collective-permute-start(bf16[2,64,640]{2,1,0:T(8,128)(2,1)S(1)} %get-tuple-element.50), channel_id=1, source_target_pairs={{0,192},{16,208},{32,224},{48,240},{64,0},{80,16},{96,32},{112,48}... | collective-permute-start | bytes 491528 | tf_op jit(solution)/shard_map/ppermute | solution.py:435
  43.7 23.8 %collective-permute-start.7 = (bf16[2,64,640]{2,1,0:T(8,128)(2,1)S(1)}, bf16[2,64,640]{2,1,0:T(8,128)(2,1)S(1)}, u32[]{:S(2)}, u32[]{:S(2)}) collective-permute-start(bf16[2,64,640]{2,1,0:T(8,128)(2,1)S(1)} %get-tuple-element.51), channel_id=1, source_target_pairs={{0,224},{16,240},{32,0},{48,16},{64,32},{80,48},{96,64},{112,80},{... | collective-permute-start | bytes 491528 | tf_op jit(solution)/shard_map/ppermute | solution.py:435
  100.0 38.2 %copy-start.9 = (bf16[8,64,640]{2,1,0:T(8,128)(2,1)}, bf16[8,64,640]{2,1,0:T(8,128)(2,1)S(1)}, u32[]{:S(2)}) copy-start(bf16[8,64,640]{2,1,0:T(8,128)(2,1)S(1)} %get-tuple-element.63.down) | copy-start | bytes 1966084
  106.8 36.3 %copy-start.1 = (bf16[512,1024]{1,0:T(8,128)(2,1)S(1)}, bf16[512,1024]{1,0:T(8,128)(2,1)}, u32[]{:S(2)}) copy-start(bf16[512,1024]{1,0:T(8,128)(2,1)} %w.1) | copy-start | bytes 3145732
  139.4 17.6 %all-to-all-start.2 = ((bf16[16,128,256]{2,1,0:T(8,128)(2,1)}), bf16[16,128,256]{2,1,0:T(8,128)(2,1)S(1)}, u32[]{:S(2)}, u32[]{:S(2)}) async-start(bf16[16,128,256]{2,1,0:T(8,128)(2,1)} %total.1), calls=%async_computation.2 | async-start | bytes 2097152 | tf_op jit(solution)/shard_map/all_to_all | solution.py:426
  171.2 58.9 %all-to-all-start.3 = ((bf16[16,256,512]{2,1,0:T(8,128)(2,1)}), bf16[16,256,512]{2,1,0:T(8,128)(2,1)}, u32[]{:S(2)}, u32[]{:S(2)}) async-start(bf16[16,256,512]{2,1,0:T(8,128)(2,1)} %term.1), calls=%async_computation.3 | async-start | bytes 8388608 | tf_op jit(solution)/shard_map/all_to_all | solution.py:426
  183.4 6.6 %collective-permute-start.8 = (bf16[8,64,640]{2,1,0:T(8,128)(2,1)S(1)}, bf16[8,64,640]{2,1,0:T(8,128)(2,1)S(1)}, u32[]{:S(2)}, u32[]{:S(2)}) collective-permute-start(bf16[8,64,640]{2,1,0:T(8,128)(2,1)S(1)} %get-tuple-element.67), channel_id=1, source_target_pairs={{0,16},{16,0},{32,48},{48,32},{64,80},{80,64},{96,112},{112,96},{1... | collective-permute-start | bytes 1966088 | tf_op jit(solution)/shard_map/ppermute | solution.py:430
  190.7 14.8 %collective-permute-start.10 = (bf16[2,64,640]{2,1,0:T(8,128)(2,1)S(1)}, bf16[2,64,640]{2,1,0:T(8,128)(2,1)S(1)}, u32[]{:S(2)}, u32[]{:S(2)}) collective-permute-start(bf16[2,64,640]{2,1,0:T(8,128)(2,1)S(1)} %get-tuple-element.70), channel_id=1, source_target_pairs={{0,64},{16,80},{32,96},{48,112},{64,128},{80,144},{96,160},{112,17... | collective-permute-start | bytes 491528 | tf_op jit(solution)/shard_map/ppermute | solution.py:435
  193.5 23.8 %collective-permute-start.11 = (bf16[2,64,640]{2,1,0:T(8,128)(2,1)S(1)}, bf16[2,64,640]{2,1,0:T(8,128)(2,1)S(1)}, u32[]{:S(2)}, u32[]{:S(2)}) collective-permute-start(bf16[2,64,640]{2,1,0:T(8,128)(2,1)S(1)} %get-tuple-element.71), channel_id=1, source_target_pairs={{0,96},{16,112},{32,128},{48,144},{64,160},{80,176},{96,192},{112,... | collective-permute-start | bytes 491528 | tf_op jit(solution)/shard_map/ppermute | solution.py:435
  198.3 21.1 %collective-permute-start.12 = (bf16[2,64,640]{2,1,0:T(8,128)(2,1)S(1)}, bf16[2,64,640]{2,1,0:T(8,128)(2,1)S(1)}, u32[]{:S(2)}, u32[]{:S(2)}) collective-permute-start(bf16[2,64,640]{2,1,0:T(8,128)(2,1)S(1)} %get-tuple-element.72), channel_id=1, source_target_pairs={{0,128},{16,144},{32,160},{48,176},{64,192},{80,208},{96,224},{112... | collective-permute-start | bytes 491528 | tf_op jit(solution)/shard_map/ppermute | solution.py:435
  199.0 20.4 %collective-permute-start.13 = (bf16[2,64,640]{2,1,0:T(8,128)(2,1)S(1)}, bf16[2,64,640]{2,1,0:T(8,128)(2,1)S(1)}, u32[]{:S(2)}, u32[]{:S(2)}) collective-permute-start(bf16[2,64,640]{2,1,0:T(8,128)(2,1)S(1)} %get-tuple-element.73), channel_id=1, source_target_pairs={{0,160},{16,176},{32,192},{48,208},{64,224},{80,240},{96,0},{112,1... | collective-permute-start | bytes 491528 | tf_op jit(solution)/shard_map/ppermute | solution.py:435
  203.2 25.2 %collective-permute-start.14 = (bf16[2,64,640]{2,1,0:T(8,128)(2,1)S(1)}, bf16[2,64,640]{2,1,0:T(8,128)(2,1)S(1)}, u32[]{:S(2)}, u32[]{:S(2)}) collective-permute-start(bf16[2,64,640]{2,1,0:T(8,128)(2,1)S(1)} %get-tuple-element.74), channel_id=1, source_target_pairs={{0,192},{16,208},{32,224},{48,240},{64,0},{80,16},{96,32},{112,48}... | collective-permute-start | bytes 491528 | tf_op jit(solution)/shard_map/ppermute | solution.py:435
  205.5 22.9 %collective-permute-start.15 = (bf16[2,64,640]{2,1,0:T(8,128)(2,1)S(1)}, bf16[2,64,640]{2,1,0:T(8,128)(2,1)S(1)}, u32[]{:S(2)}, u32[]{:S(2)}) collective-permute-start(bf16[2,64,640]{2,1,0:T(8,128)(2,1)S(1)} %get-tuple-element.75), channel_id=1, source_target_pairs={{0,224},{16,240},{32,0},{48,16},{64,32},{80,48},{96,64},{112,80},{... | collective-permute-start | bytes 491528 | tf_op jit(solution)/shard_map/ppermute | solution.py:435
  217.3 11.0 %collective-permute-start.9 = (bf16[2,64,640]{2,1,0:T(8,128)(2,1)S(1)}, bf16[2,64,640]{2,1,0:T(8,128)(2,1)S(1)}, u32[]{:S(2)}, u32[]{:S(2)}) collective-permute-start(bf16[2,64,640]{2,1,0:T(8,128)(2,1)S(1)} %get-tuple-element.69), channel_id=1, source_target_pairs={{0,32},{16,48},{32,64},{48,80},{64,96},{80,112},{96,128},{112,144}... | collective-permute-start | bytes 491528 | tf_op jit(solution)/shard_map/ppermute | solution.py:435
  (8 other events, 45.9 us)
Sparse Core Ops, SparseCore 0:
  10.4 136.3 all-gather.2

commit v7 on v5

--- a/solution.py
+++ b/solution.py
@@ -13,8 +13,7 @@
 VMEM_BYTES = 40 * 1024 * 1024
 VMEM_MOST = 58 * 1024 * 1024
 GROUP = 4
-SIDE = 4
-CORE, FIRST, CHIP, PIECE, LIST = 0, 1, 2, 3, 4
+CORE, CHIP, LIST = 0, 1, 2
 
 
 def call(kernel, name, flops=0, moved=0, vmem=VMEM_BYTES, **kw):
@@ -366,25 +365,20 @@
     )(meta, *got)
 
 
-def term_kernel(slots, rank, meta, low, down, out, acc):
+def term_kernel(slots, rank, meta, low, down, out):
     group, _, rows = low.shape
     piece = out.shape[2]
+    table = jnp.concatenate([down[s, :, :piece] for s in range(slots)], axis=0)
     for g in range(group):
         first = (pl.program_id(0) * group + g) * rows
-        acc[...] = jnp.zeros_like(acc)
-        for s in range(slots):
-            start, end = start_of(meta, s), end_of(meta, s, slots)
-
-            @pl.when((start < first + rows) & (end > first))
-            def _():
-                token = first + lax.broadcasted_iota(jnp.int32, (rank, rows), 1)
-                lg = low[g, rank:, :].astype(F32)
-                lg = jnp.where((token >= start) & (token < end), lg, 0.0).astype(BF)
-                acc[...] += lax.dot_general(
-                    lg, down[s, :, :piece], (((0,), (0,)), ((), ())), preferred_element_type=F32
-                )
-
-        out[g] = acc[...].astype(BF)
+        lg = low[g, rank:, :].astype(F32)
+        lg = jnp.transpose(jnp.concatenate([lg, lg], axis=0))
+        lg = [
+            jnp.where(inside_pair(meta, p, first, lg.shape, slots, rank), lg, 0.0)
+            for p in range(slots // 2)
+        ]
+        lg = jnp.concatenate(lg, axis=1).astype(BF)
+        out[g] = jnp.dot(lg, table, preferred_element_type=F32).astype(BF)
 
 
 def term(meta, low, down, piece, slots, rank):
@@ -392,50 +386,46 @@
     return call(
         functools.partial(term_kernel, slots, rank),
         "term",
-        flops=2 * n * rows * piece * 2 * rank,
+        flops=2 * n * rows * piece * slots * rank,
         moved=2 * n * rows * piece,
+        vmem=VMEM_MOST,
         grid_spec=with_meta(
             (n // GROUP,),
             [pl.BlockSpec((GROUP, wide, rows), lambda j, m: (j, 0, 0)), whole(down.shape)],
             pl.BlockSpec((GROUP, rows, piece), lambda j, m: (j, 0, 0)),
-            [pltpu.VMEM((rows, piece), F32)],
         ),
         out_shape=jax.ShapeDtypeStruct((n, rows, piece), BF),
     )(meta, low, down)
 
 
-def base_kernel(meta, cot, w, out):
-    out[...] = jnp.dot(
-        cot[...],
-        jnp.concatenate([w[e, 0] for e in range(w.shape[0])], axis=0),
-        preferred_element_type=F32,
-    )
-
-
-def base(meta, cot, w):
+def base_kernel(cot, w, out):
+    slices, group, _, piece = w.shape
+    for g in range(group):
+        out[:, g * piece:(g + 1) * piece] = jnp.dot(
+            cot[...],
+            jnp.concatenate([w[e, g] for e in range(slices)], axis=0),
+            preferred_element_type=F32,
+        )
+
+
+def base(cot, w):
     slices, n, part, piece = w.shape
     rows, width = cot.shape
-
-    def place(f, m):
-        y = lax.rem(m[PIECE] // SIDE + SIDE - f // SIDE, SIDE)
-        x = lax.rem(lax.rem(m[PIECE], SIDE) + SIDE - lax.rem(f, SIDE), SIDE)
-        return (0, y * SIDE + x)
-
+    group = 2
     return call(
         base_kernel,
         "base",
         flops=2 * rows * n * piece * width,
         moved=2 * n * piece * width + 4 * rows * n * piece,
-        grid_spec=with_meta(
-            (n,),
-            [
-                whole(cot.shape),
-                pl.BlockSpec((slices, 1, part, piece), lambda f, m: (0, f, 0, 0)),
-            ],
-            pl.BlockSpec((rows, piece), place),
-        ),
+        vmem=VMEM_MOST,
+        grid=(n // group,),
+        in_specs=[
+            pl.BlockSpec(cot.shape, lambda f: (0, 0)),
+            pl.BlockSpec((slices, group, part, piece), lambda f: (0, f, 0, 0)),
+        ],
+        out_specs=pl.BlockSpec((rows, group * piece), lambda f: (0, f)),
         out_shape=jax.ShapeDtypeStruct((rows, n * piece), F32),
-    )(meta, cot, w)
+    )(cot, w)
 
 
 def join_kernel(done, terms, out):
@@ -452,6 +442,7 @@
         join_kernel,
         "join",
         moved=8 * n * rows * piece,
+        vmem=VMEM_MOST,
         grid=(n // group,),
         in_specs=[
             pl.BlockSpec((rows, group * piece), lambda f: (0, f)),
@@ -482,18 +473,7 @@
     return [blocks[0]] + [shift(blocks[k], k, bins) for k in range(1, bins // 2)]
 
 
-def across(x, dy, dx, n):
-    return lax.ppermute(
-        x,
-        "fsdp",
-        [
-            (i, (i // SIDE + dy) % SIDE * SIDE + (i % SIDE + dx) % SIDE)
-            for i in range(n)
-        ],
-    )
-
-
-def scalars(segment_tenant, segment_lengths, tenant_stored_row, own, rows):
+def scalars(segment_tenant, segment_lengths, tenant_stored_row, own):
     bins, slots = segment_tenant.shape
     me = lax.axis_index("dp")
     tenants = jnp.arange(tenant_stored_row.shape[0], dtype=jnp.int32)
@@ -507,8 +487,7 @@
     wanted = jnp.max(jnp.where(stored // own == me, stored % own, -1), axis=1)
     every = jnp.arange(bins, dtype=jnp.int32)
     segment = jnp.max(jnp.where(owners[None, :] == every[:, None], place[None, :], -1), axis=1)
-    place_f = lax.axis_index("fsdp")
-    head = jnp.stack([me % 2, place_f * rows, me // 2, place_f])
+    head = jnp.stack([me % 2, me // 2])
     return jnp.concatenate([head, starts, starts + lengths, owners, wanted, segment]).astype(
         jnp.int32
     )
@@ -531,22 +510,18 @@
     rows = tokens.shape[0]
     n = lax.axis_size("fsdp")
     scale = (n * rows) ** (-0.5)
-    meta = scalars(segment_tenant, segment_lengths, tenant_stored_row, own, rows)
-
-    packed = pack(tokens, jnp.swapaxes(cotangent, 0, 1), n)
+    meta = scalars(segment_tenant, segment_lengths, tenant_stored_row, own)
+
     me = lax.axis_index("dp").astype(jnp.int32).reshape(1)
-    packed, me = lax.optimization_barrier((packed, me))
-    parts = exchange(packed, "fsdp")
-    mine = turn(me, value_weight, bins)[None]
-    mine = jnp.concatenate([mine] + [across(mine, 0, k, n) for k in range(1, SIDE)])
-    mine = jnp.concatenate([mine] + [across(mine, k, 0, n) for k in range(1, SIDE)])
-    weight = lax.all_gather(mine, "dp", axis=0)
-
+    weight = lax.all_gather(turn(me, value_weight, bins), ("dp", "fsdp"), axis=0)
+    weight = weight.reshape((bins, n) + weight.shape[1:])
+
+    parts = exchange(pack(tokens, jnp.swapaxes(cotangent, 0, 1), n), "fsdp")
     keep, give = offer(
         meta, jnp.swapaxes(adapter_down_weight, 1, 2), adapter_up_weight, chips, slots
     )
     got = spread(meta, keep, give, bins)
-    parts, got, mine = lax.optimization_barrier((parts, got, mine))
+    parts, got = lax.optimization_barrier((parts, got))
     down, down_t, up_t = choose(meta, got, slots, v)
 
     sums = exchange(project(meta, parts, down_t, up_t, rows, slots, rank), "fsdp")
@@ -555,11 +530,12 @@
     terms, low_all = lax.optimization_barrier((terms, low_all))
     terms = exchange(terms, "fsdp")
     sent = spread(meta, *gradient(meta, parts, low_all, chips, slots, rank, v), bins)
-    done = base(meta, cotangent, weight)
-    terms, sent, done = lax.optimization_barrier((terms, sent, done))
-    grad = join(done, terms)
     down_grad, up_grad = collect(meta, sent, own, v, slots, scale)
-    return grad, jnp.swapaxes(down_grad, 1, 2), up_grad
+    done = base(cotangent, weight)
+    terms, down_grad, up_grad, done = lax.optimization_barrier(
+        (terms, down_grad, up_grad, done)
+    )
+    return join(done, terms), jnp.swapaxes(down_grad, 1, 2), up_grad
 
 
 def solution(mesh):

time: 243 us -> 251 us (1.033)
  waiting for transfers between devices: 58.4 us -> 76.2 us
  starting transfers between devices: 66.2 us -> 58.3 us
  local copies, waits for them, and re-layouts: 12.2 us -> 4.49 us
  blocking collectives: 33.7 us -> 41.1 us
    all_to_all x2, waiting for transfers between devices: 6.5 us -> 24.8 us  [exchange(): return lax.all_to_all(x, axis, 0, 0, tiled=True)]
    ppermute x6 -> x0, waiting for transfers between devices: 11.2 us -> none  [across(): lax.ppermute(x, 'fsdp', [(i, (i // SIDE + dy) % SIDE * SIDE + (i % SIDE +...]
    ppermute x6 -> x0, starting transfers between devices: 11 us -> none  [across(): lax.ppermute(x, 'fsdp', [(i, (i // SIDE + dy) % SIDE * SIDE + (i % SIDE +...]
    ppermute x14, waiting for transfers between devices: 37.2 us -> 47.9 us  [shift(): lax.ppermute(x, 'dp', [(i, (i // 2 + k) % chips * 2 + i % 2) for i in ran...]
    unnamed x32 -> x24, local copies, waits for them, and re-layouts: 11.9 us -> 4.22 us
    all_to_all x2, blocking collectives: 33.7 us -> 41.1 us  [exchange(): return lax.all_to_all(x, axis, 0, 0, tiled=True)]
  transfers between devices with their start and end apart: 25 -> 19, of which waited for: 13 -> 12; matrix products, arithmetic and copies ran while one was open for 0% -> 1% of each run, Pallas kernels for 17% -> 18%
where the time goes in v7:
time: 251 us; the launch traced here: 249 us
  waiting for transfers between devices  76.2 us (30%)
  starting transfers between devices  58.3 us (23%)
  Pallas kernels  53.8 us (21%)
  blocking collectives  41.1 us (16%)
  between operations  14.2 us (6%)
  local copies, waits for them, and re-layouts  4.49 us (2%)
    ppermute x14, waiting for transfers between devices, shift(): lax.ppermute(x, 'dp', [(i, (i // 2 + k) % chips * 2 + i % 2) for i in ran...  47.9 us
    all_to_all x2, blocking collectives, exchange(): return lax.all_to_all(x, axis, 0, 0, tiled=True)  41.1 us
    ppermute x14, starting transfers between devices, shift(): lax.ppermute(x, 'dp', [(i, (i // 2 + k) % chips * 2 + i % 2) for i in ran...  36 us
    all_to_all x2, waiting for transfers between devices, exchange(): return lax.all_to_all(x, axis, 0, 0, tiled=True)  24.8 us
    pallas_call x1, Pallas kernels, base(): call(base_kernel, 'base', flops=2 * rows * n * piece * width, moved=2 * n...  13.3 us
    all_to_all x2, starting transfers between devices, exchange(): return lax.all_to_all(x, axis, 0, 0, tiled=True)  12.6 us
    ppermute x2, starting transfers between devices, swap(): return lax.ppermute(x, 'dp', [(i, i ^ 1) for i in range(bins)])  9.6 us
    pallas_call x1, Pallas kernels, join(): call(join_kernel, 'join', moved=8 * n * rows * piece, vmem=VMEM_MOST, gri...  8.5 us
  transfers between devices with their start and end apart: 19, of which 12 were waited for; matrix products, arithmetic and copies ran while one was open for 1% of the time, Pallas kernels for 18%

profile of v7, /device:TPU:1, one launch (start us, length us, event | category | flops | bytes accessed | tf_op | source)
XLA Modules:
  0.0 249.0 jit_solution(17390087407061463935)
XLA Ops:
  11.3 5.1 %pack.1 = bf16[16,288,512]{2,1,0:T(8,128)(2,1)} custom-call(bf16[256,8192]{1,0:T(8,128)(2,1)} %tok.1, bf16[1024,256]{1,0:T(8,128)(2,1)} %bitcast.19), custom_call_target="tpu_custom_call" | custom-call | bytes 8388608 | tf_op jit(solution)/shard_map/pack/pallas_call | solution.py:108
  16.4 7.8 %all-to-all-start = ((bf16[16,288,512]{2,1,0:T(8,128)(2,1)}), bf16[16,288,512]{2,1,0:T(8,128)(2,1)}, u32[]{:S(2)}, u32[]{:S(2)}) async-start(bf16[16,288,512]{2,1,0:T(8,128)(2,1)} %pack.1), calls=%async_computation | async-start | bytes 9437184 | tf_op jit(solution)/shard_map/all_to_all | solution.py:457
  31.2 3.0 %collective-permute-start.2 = (bf16[2,64,640]{2,1,0:T(8,128)(2,1)S(1)}, bf16[2,64,640]{2,1,0:T(8,128)(2,1)S(1)}, u32[]{:S(2)}, u32[]{:S(2)}) collective-permute-start(bf16[2,64,640]{2,1,0:T(8,128)(2,1)S(1)} %get-tuple-element.47), channel_id=1, source_target_pairs={{0,64},{16,80},{32,96},{48,112},{64,128},{80,144},{96,160},{112,17... | collective-permute-start | bytes 491528 | tf_op jit(solution)/shard_map/ppermute | solution.py:466
  34.2 3.8 %collective-permute-start.3 = (bf16[2,64,640]{2,1,0:T(8,128)(2,1)S(1)}, bf16[2,64,640]{2,1,0:T(8,128)(2,1)S(1)}, u32[]{:S(2)}, u32[]{:S(2)}) collective-permute-start(bf16[2,64,640]{2,1,0:T(8,128)(2,1)S(1)} %get-tuple-element.48), channel_id=1, source_target_pairs={{0,96},{16,112},{32,128},{48,144},{64,160},{80,176},{96,192},{112,... | collective-permute-start | bytes 491528 | tf_op jit(solution)/shard_map/ppermute | solution.py:466
  38.4 4.5 %collective-permute-start.5 = (bf16[2,64,640]{2,1,0:T(8,128)(2,1)S(1)}, bf16[2,64,640]{2,1,0:T(8,128)(2,1)S(1)}, u32[]{:S(2)}, u32[]{:S(2)}) collective-permute-start(bf16[2,64,640]{2,1,0:T(8,128)(2,1)S(1)} %get-tuple-element.50), channel_id=1, source_target_pairs={{0,160},{16,176},{32,192},{48,208},{64,224},{80,240},{96,0},{112,1... | collective-permute-start | bytes 491528 | tf_op jit(solution)/shard_map/ppermute | solution.py:466
  45.3 3.9 %collective-permute-start.7 = (bf16[2,64,640]{2,1,0:T(8,128)(2,1)S(1)}, bf16[2,64,640]{2,1,0:T(8,128)(2,1)S(1)}, u32[]{:S(2)}, u32[]{:S(2)}) collective-permute-start(bf16[2,64,640]{2,1,0:T(8,128)(2,1)S(1)} %get-tuple-element.52), channel_id=1, source_target_pairs={{0,224},{16,240},{32,0},{48,16},{64,32},{80,48},{96,64},{112,80},{... | collective-permute-start | bytes 491528 | tf_op jit(solution)/shard_map/ppermute | solution.py:466
  49.2 9.1 %collective-permute-done.3.refs_3_ = bf16[2,64,640]{2,1,0:T(8,128)(2,1)S(1)} collective-permute-done((bf16[2,64,640]{2,1,0:T(8,128)(2,1)S(1)}, bf16[2,64,640]{2,1,0:T(8,128)(2,1)S(1)}, u32[]{:S(2)}, u32[]{:S(2)}) %collective-permute-start.3) | collective-permute-done | bytes 163872 | tf_op jit(solution)/shard_map/ppermute | solution.py:466
  61.0 7.5 %collective-permute-done.6.refs_6_ = bf16[2,64,640]{2,1,0:T(8,128)(2,1)S(1)} collective-permute-done((bf16[2,64,640]{2,1,0:T(8,128)(2,1)S(1)}, bf16[2,64,640]{2,1,0:T(8,128)(2,1)S(1)}, u32[]{:S(2)}, u32[]{:S(2)}) %collective-permute-start.6) | collective-permute-done | bytes 163872 | tf_op jit(solution)/shard_map/ppermute | solution.py:466
  69.7 24.8 %all-to-all-done.part = bf16[16,288,512]{2,1,0:T(8,128)(2,1)} async-done(((bf16[16,288,512]{2,1,0:T(8,128)(2,1)}), bf16[16,288,512]{2,1,0:T(8,128)(2,1)}, u32[]{:S(2)}, u32[]{:S(2)}) %all-to-all-start) | async-done | bytes 4718624 | tf_op jit(solution)/shard_map/all_to_all | solution.py:457
  96.4 6.7 %project.1 = bf16[16,256,128]{2,1,0:T(8,128)(2,1)S(1)} custom-call(s32[58]{0:T(128)S(1)} %concatenate.3.meta, bf16[16,288,512]{2,1,0:T(8,128)(2,1)} %all-to-all-done.part, bf16[512,512]{1,0:T(8,128)(2,1)S(1)} %get-tuple-element.62.down_t, bf16[64,512]{1,0:T(8,128)(2,1)S(1)} %get-tuple-element.63.up_t), custom_call_target="tpu_custom_call" | custom-call | flops 2147483648 | bytes 4718592 | tf_op jit(solution)/shard_map/project/pallas_call | solution.py:232
  103.2 21.8 %all_to_all.20.parts = bf16[16,256,128]{2,1,0:T(8,128)(2,1)S(1)} all-to-all(bf16[16,256,128]{2,1,0:T(8,128)(2,1)S(1)} %project.1), channel_id=1, replica_groups=mesh['dp'=16,'fsdp'=16] {'fsdp'}, dimensions={0} | all-to-all | bytes 2097152 | tf_op jit(solution)/shard_map/all_to_all | solution.py:457
  125.3 19.3 %all_to_all.21.low = bf16[16,128,256]{2,1,0:T(8,128)(2,1)} all-to-all(bf16[16,128,256]{2,1,0:T(8,128)(2,1)S(1)} %total.1), channel_id=1, replica_groups=mesh['dp'=16,'fsdp'=16] {'fsdp'}, dimensions={0} | all-to-all | bytes 2097152 | tf_op jit(solution)/shard_map/all_to_all | solution.py:457
  144.6 6.7 %term.1 = bf16[16,256,512]{2,1,0:T(8,128)(2,1)} custom-call(s32[58]{0:T(128)} %copy-done.6, bf16[16,128,256]{2,1,0:T(8,128)(2,1)} %all_to_all.21.low, bf16[8,64,640]{2,1,0:T(8,128)(2,1)} %copy-done.8), custom_call_target="tpu_custom_call" | custom-call | flops 2147483648 | bytes 4194304 | tf_op jit(solution)/shard_map/term/pallas_call | solution.py:386
  151.3 4.9 %all-to-all-start.3 = ((bf16[16,256,512]{2,1,0:T(8,128)(2,1)}), bf16[16,256,512]{2,1,0:T(8,128)(2,1)}, u32[]{:S(2)}, u32[]{:S(2)}) async-start(bf16[16,256,512]{2,1,0:T(8,128)(2,1)} %term.1), calls=%async_computation.3 | async-start | bytes 8388608 | tf_op jit(solution)/shard_map/all_to_all | solution.py:457
  156.2 7.8 %gradient.1 = (bf16[8,64,640]{2,1,0:T(8,128)(2,1)S(1)}, bf16[8,64,640]{2,1,0:T(8,128)(2,1)S(1)}) custom-call(s32[58]{0:T(128)S(1)} %copy-done.7, bf16[16,288,512]{2,1,0:T(8,128)(2,1)} %all-to-all-done.part, bf16[16,128,256]{2,1,0:T(8,128)(2,1)S(1)} %copy-done.3), custom_call_target="tpu_custom_call" | custom-call | flops 2147483648 | bytes 4718592 | tf_op jit(solution)/shard_map/gradient/pallas_call | solution.py:321
  164.0 8.6 %collective-permute-start.8 = (bf16[8,64,640]{2,1,0:T(8,128)(2,1)S(1)}, bf16[8,64,640]{2,1,0:T(8,128)(2,1)S(1)}, u32[]{:S(2)}, u32[]{:S(2)}) collective-permute-start(bf16[8,64,640]{2,1,0:T(8,128)(2,1)S(1)} %get-tuple-element.68), channel_id=1, source_target_pairs={{0,16},{16,0},{32,48},{48,32},{64,80},{80,64},{96,112},{112,96},{1... | collective-permute-start | bytes 1966088 | tf_op jit(solution)/shard_map/ppermute | solution.py:461
  177.3 2.9 %collective-permute-start.10 = (bf16[2,64,640]{2,1,0:T(8,128)(2,1)S(1)}, bf16[2,64,640]{2,1,0:T(8,128)(2,1)S(1)}, u32[]{:S(2)}, u32[]{:S(2)}) collective-permute-start(bf16[2,64,640]{2,1,0:T(8,128)(2,1)S(1)} %get-tuple-element.71), channel_id=1, source_target_pairs={{0,64},{16,80},{32,96},{48,112},{64,128},{80,144},{96,160},{112,17... | collective-permute-start | bytes 491528 | tf_op jit(solution)/shard_map/ppermute | solution.py:466
  184.3 4.5 %collective-permute-start.13 = (bf16[2,64,640]{2,1,0:T(8,128)(2,1)S(1)}, bf16[2,64,640]{2,1,0:T(8,128)(2,1)S(1)}, u32[]{:S(2)}, u32[]{:S(2)}) collective-permute-start(bf16[2,64,640]{2,1,0:T(8,128)(2,1)S(1)} %get-tuple-element.74), channel_id=1, source_target_pairs={{0,160},{16,176},{32,192},{48,208},{64,224},{80,240},{96,0},{112,1... | collective-permute-start | bytes 491528 | tf_op jit(solution)/shard_map/ppermute | solution.py:466
  190.0 3.4 %collective-permute-done.10.refs_2_ = bf16[2,64,640]{2,1,0:T(8,128)(2,1)S(1)} collective-permute-done((bf16[2,64,640]{2,1,0:T(8,128)(2,1)S(1)}, bf16[2,64,640]{2,1,0:T(8,128)(2,1)S(1)}, u32[]{:S(2)}, u32[]{:S(2)}) %collective-permute-start.10) | collective-permute-done | bytes 163872 | tf_op jit(solution)/shard_map/ppermute | solution.py:466
  194.7 12.0 %collective-permute-done.11.refs_3_ = bf16[2,64,640]{2,1,0:T(8,128)(2,1)S(1)} collective-permute-done((bf16[2,64,640]{2,1,0:T(8,128)(2,1)S(1)}, bf16[2,64,640]{2,1,0:T(8,128)(2,1)S(1)}, u32[]{:S(2)}, u32[]{:S(2)}) %collective-permute-start.11) | collective-permute-done | bytes 163872 | tf_op jit(solution)/shard_map/ppermute | solution.py:466
  206.8 3.3 %collective-permute-done.12.refs_4_ = bf16[2,64,640]{2,1,0:T(8,128)(2,1)S(1)} collective-permute-done((bf16[2,64,640]{2,1,0:T(8,128)(2,1)S(1)}, bf16[2,64,640]{2,1,0:T(8,128)(2,1)S(1)}, u32[]{:S(2)}, u32[]{:S(2)}) %collective-permute-start.12) | collective-permute-done | bytes 163872 | tf_op jit(solution)/shard_map/ppermute | solution.py:466
  210.1 7.3 %collective-permute-done.14.refs_6_ = bf16[2,64,640]{2,1,0:T(8,128)(2,1)S(1)} collective-permute-done((bf16[2,64,640]{2,1,0:T(8,128)(2,1)S(1)}, bf16[2,64,640]{2,1,0:T(8,128)(2,1)S(1)}, u32[]{:S(2)}, u32[]{:S(2)}) %collective-permute-start.14) | collective-permute-done | bytes 163872 | tf_op jit(solution)/shard_map/ppermute | solution.py:466
  220.4 13.3 %base.1.done = f32[256,8192]{1,0:T(8,128)} custom-call(bf16[256,1024]{1,0:T(8,128)(2,1)} %cot.1, bf16[16,16,64,512]{3,2,1,0:T(8,128)(2,1)} %bitcast.18), custom_call_target="tpu_custom_call" | custom-call | flops 4294967296 | bytes 25165824 | tf_op jit(solution)/shard_map/base/pallas_call | solution.py:415
  233.6 8.5 %join.1 = bf16[256,8192]{1,0:T(8,128)(2,1)} custom-call(f32[256,8192]{1,0:T(8,128)} %base.1.done, bf16[16,256,512]{2,1,0:T(8,128)(2,1)} %all-to-all-done.3.terms), custom_call_target="tpu_custom_call" | custom-call | bytes 16777216 | tf_op jit(solution)/shard_map/join/pallas_call | solution.py:441
  (63 shorter events, 34.2 us)
Async XLA Ops:
  7.2 17.0 %copy-start = (s32[16,8]{0,1:T(8,128)S(1)}, s32[16,8]{0,1:T(8,128)}, u32[]{:S(2)}) copy-start(s32[16,8]{0,1:T(8,128)} %param.14) | copy-start | bytes 1540
  7.2 213.2 %all-gather.3.cloned.1.call-start = ((), (), s32[]{:S(2)}) async-start(), calls=%async_computation.4 | async-start | bytes 16842752 | tf_op jit(solution)/shard_map/all_gather | solution.py:516
  16.4 9.0 %copy-start.4 = (bf16[4,512,64]{1,2,0:T(8,128)(2,1)S(1)}, bf16[4,512,64]{1,2,0:T(8,128)(2,1)}, u32[]{:S(2)}) copy-start(bf16[4,512,64]{1,2,0:T(8,128)(2,1)} %param.11) | copy-start | bytes 786436
  16.4 9.0 %copy-start.5 = (bf16[4,64,64]{2,1,0:T(8,128)(2,1)S(1)}, bf16[4,64,64]{2,1,0:T(8,128)(2,1)}, u32[]{:S(2)}) copy-start(bf16[4,64,64]{2,1,0:T(8,128)(2,1)} %up.1) | copy-start | bytes 98308
  16.4 78.2 %all-to-all-start = ((bf16[16,288,512]{2,1,0:T(8,128)(2,1)}), bf16[16,288,512]{2,1,0:T(8,128)(2,1)}, u32[]{:S(2)}, u32[]{:S(2)}) async-start(bf16[16,288,512]{2,1,0:T(8,128)(2,1)} %pack.1), calls=%async_computation | async-start | bytes 9437184 | tf_op jit(solution)/shard_map/all_to_all | solution.py:457
  25.4 77.8 %copy-start.6 = (s32[58]{0:T(128)}, s32[58]{0:T(128)S(1)}, u32[]{:S(2)}) copy-start(s32[58]{0:T(128)S(1)} %concatenate.3.meta) | copy-start | bytes 700
  26.1 2.8 %collective-permute-start = (bf16[8,64,640]{2,1,0:T(8,128)(2,1)S(1)}, bf16[8,64,640]{2,1,0:T(8,128)(2,1)S(1)}, u32[]{:S(2)}, u32[]{:S(2)}) collective-permute-start(bf16[8,64,640]{2,1,0:T(8,128)(2,1)S(1)} %get-tuple-element.44), channel_id=1, source_target_pairs={{0,16},{16,0},{32,48},{48,32},{64,80},{80,64},{96,112},{112,96},{1... | collective-permute-start | bytes 1966088 | tf_op jit(solution)/shard_map/ppermute | solution.py:461
  29.5 13.4 %collective-permute-start.1 = (bf16[2,64,640]{2,1,0:T(8,128)(2,1)S(1)}, bf16[2,64,640]{2,1,0:T(8,128)(2,1)S(1)}, u32[]{:S(2)}, u32[]{:S(2)}) collective-permute-start(bf16[2,64,640]{2,1,0:T(8,128)(2,1)S(1)} %get-tuple-element.46), channel_id=1, source_target_pairs={{0,32},{16,48},{32,64},{48,80},{64,96},{80,112},{96,128},{112,144}... | collective-permute-start | bytes 491528 | tf_op jit(solution)/shard_map/ppermute | solution.py:466
  31.2 14.1 %collective-permute-start.2 = (bf16[2,64,640]{2,1,0:T(8,128)(2,1)S(1)}, bf16[2,64,640]{2,1,0:T(8,128)(2,1)S(1)}, u32[]{:S(2)}, u32[]{:S(2)}) collective-permute-start(bf16[2,64,640]{2,1,0:T(8,128)(2,1)S(1)} %get-tuple-element.47), channel_id=1, source_target_pairs={{0,64},{16,80},{32,96},{48,112},{64,128},{80,144},{96,160},{112,17... | collective-permute-start | bytes 491528 | tf_op jit(solution)/shard_map/ppermute | solution.py:466
  34.2 24.1 %collective-permute-start.3 = (bf16[2,64,640]{2,1,0:T(8,128)(2,1)S(1)}, bf16[2,64,640]{2,1,0:T(8,128)(2,1)S(1)}, u32[]{:S(2)}, u32[]{:S(2)}) collective-permute-start(bf16[2,64,640]{2,1,0:T(8,128)(2,1)S(1)} %get-tuple-element.48), channel_id=1, source_target_pairs={{0,96},{16,112},{32,128},{48,144},{64,160},{80,176},{96,192},{112,... | collective-permute-start | bytes 491528 | tf_op jit(solution)/shard_map/ppermute | solution.py:466
  37.9 23.0 %collective-permute-start.4 = (bf16[2,64,640]{2,1,0:T(8,128)(2,1)S(1)}, bf16[2,64,640]{2,1,0:T(8,128)(2,1)S(1)}, u32[]{:S(2)}, u32[]{:S(2)}) collective-permute-start(bf16[2,64,640]{2,1,0:T(8,128)(2,1)S(1)} %get-tuple-element.49), channel_id=1, source_target_pairs={{0,128},{16,144},{32,160},{48,176},{64,192},{80,208},{96,224},{112... | collective-permute-start | bytes 491528 | tf_op jit(solution)/shard_map/ppermute | solution.py:466
  38.4 22.6 %collective-permute-start.5 = (bf16[2,64,640]{2,1,0:T(8,128)(2,1)S(1)}, bf16[2,64,640]{2,1,0:T(8,128)(2,1)S(1)}, u32[]{:S(2)}, u32[]{:S(2)}) collective-permute-start(bf16[2,64,640]{2,1,0:T(8,128)(2,1)S(1)} %get-tuple-element.50), channel_id=1, source_target_pairs={{0,160},{16,176},{32,192},{48,208},{64,224},{80,240},{96,0},{112,1... | collective-permute-start | bytes 491528 | tf_op jit(solution)/shard_map/ppermute | solution.py:466
  42.9 25.7 %collective-permute-start.6 = (bf16[2,64,640]{2,1,0:T(8,128)(2,1)S(1)}, bf16[2,64,640]{2,1,0:T(8,128)(2,1)S(1)}, u32[]{:S(2)}, u32[]{:S(2)}) collective-permute-start(bf16[2,64,640]{2,1,0:T(8,128)(2,1)S(1)} %get-tuple-element.51), channel_id=1, source_target_pairs={{0,192},{16,208},{32,224},{48,240},{64,0},{80,16},{96,32},{112,48}... | collective-permute-start | bytes 491528 | tf_op jit(solution)/shard_map/ppermute | solution.py:466
  45.3 24.5 %collective-permute-start.7 = (bf16[2,64,640]{2,1,0:T(8,128)(2,1)S(1)}, bf16[2,64,640]{2,1,0:T(8,128)(2,1)S(1)}, u32[]{:S(2)}, u32[]{:S(2)}) collective-permute-start(bf16[2,64,640]{2,1,0:T(8,128)(2,1)S(1)} %get-tuple-element.52), channel_id=1, source_target_pairs={{0,224},{16,240},{32,0},{48,16},{64,32},{80,48},{96,64},{112,80},{... | collective-permute-start | bytes 491528 | tf_op jit(solution)/shard_map/ppermute | solution.py:466
  151.3 82.3 %all-to-all-start.3 = ((bf16[16,256,512]{2,1,0:T(8,128)(2,1)}), bf16[16,256,512]{2,1,0:T(8,128)(2,1)}, u32[]{:S(2)}, u32[]{:S(2)}) async-start(bf16[16,256,512]{2,1,0:T(8,128)(2,1)} %term.1), calls=%async_computation.3 | async-start | bytes 8388608 | tf_op jit(solution)/shard_map/all_to_all | solution.py:457
  164.0 10.3 %collective-permute-start.8 = (bf16[8,64,640]{2,1,0:T(8,128)(2,1)S(1)}, bf16[8,64,640]{2,1,0:T(8,128)(2,1)S(1)}, u32[]{:S(2)}, u32[]{:S(2)}) collective-permute-start(bf16[8,64,640]{2,1,0:T(8,128)(2,1)S(1)} %get-tuple-element.68), channel_id=1, source_target_pairs={{0,16},{16,0},{32,48},{48,32},{64,80},{80,64},{96,112},{112,96},{1... | collective-permute-start | bytes 1966088 | tf_op jit(solution)/shard_map/ppermute | solution.py:461
  175.0 13.8 %collective-permute-start.9 = (bf16[2,64,640]{2,1,0:T(8,128)(2,1)S(1)}, bf16[2,64,640]{2,1,0:T(8,128)(2,1)S(1)}, u32[]{:S(2)}, u32[]{:S(2)}) collective-permute-start(bf16[2,64,640]{2,1,0:T(8,128)(2,1)S(1)} %get-tuple-element.70), channel_id=1, source_target_pairs={{0,32},{16,48},{32,64},{48,80},{64,96},{80,112},{96,128},{112,144}... | collective-permute-start | bytes 491528 | tf_op jit(solution)/shard_map/ppermute | solution.py:466
  177.3 16.1 %collective-permute-start.10 = (bf16[2,64,640]{2,1,0:T(8,128)(2,1)S(1)}, bf16[2,64,640]{2,1,0:T(8,128)(2,1)S(1)}, u32[]{:S(2)}, u32[]{:S(2)}) collective-permute-start(bf16[2,64,640]{2,1,0:T(8,128)(2,1)S(1)} %get-tuple-element.71), channel_id=1, source_target_pairs={{0,64},{16,80},{32,96},{48,112},{64,128},{80,144},{96,160},{112,17... | collective-permute-start | bytes 491528 | tf_op jit(solution)/shard_map/ppermute | solution.py:466
  180.2 26.6 %collective-permute-start.11 = (bf16[2,64,640]{2,1,0:T(8,128)(2,1)S(1)}, bf16[2,64,640]{2,1,0:T(8,128)(2,1)S(1)}, u32[]{:S(2)}, u32[]{:S(2)}) collective-permute-start(bf16[2,64,640]{2,1,0:T(8,128)(2,1)S(1)} %get-tuple-element.72), channel_id=1, source_target_pairs={{0,96},{16,112},{32,128},{48,144},{64,160},{80,176},{96,192},{112,... | collective-permute-start | bytes 491528 | tf_op jit(solution)/shard_map/ppermute | solution.py:466
  182.7 27.4 %collective-permute-start.12 = (bf16[2,64,640]{2,1,0:T(8,128)(2,1)S(1)}, bf16[2,64,640]{2,1,0:T(8,128)(2,1)S(1)}, u32[]{:S(2)}, u32[]{:S(2)}) collective-permute-start(bf16[2,64,640]{2,1,0:T(8,128)(2,1)S(1)} %get-tuple-element.73), channel_id=1, source_target_pairs={{0,128},{16,144},{32,160},{48,176},{64,192},{80,208},{96,224},{112... | collective-permute-start | bytes 491528 | tf_op jit(solution)/shard_map/ppermute | solution.py:466
  184.3 25.8 %collective-permute-start.13 = (bf16[2,64,640]{2,1,0:T(8,128)(2,1)S(1)}, bf16[2,64,640]{2,1,0:T(8,128)(2,1)S(1)}, u32[]{:S(2)}, u32[]{:S(2)}) collective-permute-start(bf16[2,64,640]{2,1,0:T(8,128)(2,1)S(1)} %get-tuple-element.74), channel_id=1, source_target_pairs={{0,160},{16,176},{32,192},{48,208},{64,224},{80,240},{96,0},{112,1... | collective-permute-start | bytes 491528 | tf_op jit(solution)/shard_map/ppermute | solution.py:466
  188.8 28.7 %collective-permute-start.14 = (bf16[2,64,640]{2,1,0:T(8,128)(2,1)S(1)}, bf16[2,64,640]{2,1,0:T(8,128)(2,1)S(1)}, u32[]{:S(2)}, u32[]{:S(2)}) collective-permute-start(bf16[2,64,640]{2,1,0:T(8,128)(2,1)S(1)} %get-tuple-element.75), channel_id=1, source_target_pairs={{0,192},{16,208},{32,224},{48,240},{64,0},{80,16},{96,32},{112,48}... | collective-permute-start | bytes 491528 | tf_op jit(solution)/shard_map/ppermute | solution.py:466
  193.4 25.2 %collective-permute-start.15 = (bf16[2,64,640]{2,1,0:T(8,128)(2,1)S(1)}, bf16[2,64,640]{2,1,0:T(8,128)(2,1)S(1)}, u32[]{:S(2)}, u32[]{:S(2)}) collective-permute-start(bf16[2,64,640]{2,1,0:T(8,128)(2,1)S(1)} %get-tuple-element.76), channel_id=1, source_target_pairs={{0,224},{16,240},{32,0},{48,16},{64,32},{80,48},{96,64},{112,80},{... | collective-permute-start | bytes 491528 | tf_op jit(solution)/shard_map/ppermute | solution.py:466
  233.6 8.5 %copy-start.1 = (s32[16,8]{0,1:T(8,128)S(1)}, s32[16,8]{0,1:T(8,128)}, u32[]{:S(2)}) copy-start(s32[16,8]{0,1:T(8,128)} %param.14) | copy-start | bytes 1540
  (6 other events, 28.2 us)
Sparse Core Ops, SparseCore 0:
  11.7 203.6 all-gather.2

commit v8 on v5

--- a/solution.py
+++ b/solution.py
@@ -14,7 +14,7 @@
 VMEM_MOST = 58 * 1024 * 1024
 GROUP = 4
 SIDE = 4
-CORE, FIRST, CHIP, PIECE, LIST = 0, 1, 2, 3, 4
+CORE, CHIP, PIECE, LIST = 0, 1, 2, 3
 
 
 def call(kernel, name, flops=0, moved=0, vmem=VMEM_BYTES, **kw):
@@ -366,25 +366,20 @@
     )(meta, *got)
 
 
-def term_kernel(slots, rank, meta, low, down, out, acc):
+def term_kernel(slots, rank, meta, low, down, out):
     group, _, rows = low.shape
     piece = out.shape[2]
+    table = jnp.concatenate([down[s, :, :piece] for s in range(slots)], axis=0)
     for g in range(group):
         first = (pl.program_id(0) * group + g) * rows
-        acc[...] = jnp.zeros_like(acc)
-        for s in range(slots):
-            start, end = start_of(meta, s), end_of(meta, s, slots)
-
-            @pl.when((start < first + rows) & (end > first))
-            def _():
-                token = first + lax.broadcasted_iota(jnp.int32, (rank, rows), 1)
-                lg = low[g, rank:, :].astype(F32)
-                lg = jnp.where((token >= start) & (token < end), lg, 0.0).astype(BF)
-                acc[...] += lax.dot_general(
-                    lg, down[s, :, :piece], (((0,), (0,)), ((), ())), preferred_element_type=F32
-                )
-
-        out[g] = acc[...].astype(BF)
+        lg = low[g, rank:, :].astype(F32)
+        lg = jnp.transpose(jnp.concatenate([lg, lg], axis=0))
+        lg = [
+            jnp.where(inside_pair(meta, p, first, lg.shape, slots, rank), lg, 0.0)
+            for p in range(slots // 2)
+        ]
+        lg = jnp.concatenate(lg, axis=1).astype(BF)
+        out[g] = jnp.dot(lg, table, preferred_element_type=F32).astype(BF)
 
 
 def term(meta, low, down, piece, slots, rank):
@@ -392,13 +387,13 @@
     return call(
         functools.partial(term_kernel, slots, rank),
         "term",
-        flops=2 * n * rows * piece * 2 * rank,
+        flops=2 * n * rows * piece * slots * rank,
         moved=2 * n * rows * piece,
+        vmem=VMEM_MOST,
         grid_spec=with_meta(
             (n // GROUP,),
             [pl.BlockSpec((GROUP, wide, rows), lambda j, m: (j, 0, 0)), whole(down.shape)],
             pl.BlockSpec((GROUP, rows, piece), lambda j, m: (j, 0, 0)),
-            [pltpu.VMEM((rows, piece), F32)],
         ),
         out_shape=jax.ShapeDtypeStruct((n, rows, piece), BF),
     )(meta, low, down)
@@ -426,6 +421,7 @@
         "base",
         flops=2 * rows * n * piece * width,
         moved=2 * n * piece * width + 4 * rows * n * piece,
+        vmem=VMEM_MOST,
         grid_spec=with_meta(
             (n,),
             [
@@ -452,6 +448,7 @@
         join_kernel,
         "join",
         moved=8 * n * rows * piece,
+        vmem=VMEM_MOST,
         grid=(n // group,),
         in_specs=[
             pl.BlockSpec((rows, group * piece), lambda f: (0, f)),
@@ -493,7 +490,7 @@
     )
 
 
-def scalars(segment_tenant, segment_lengths, tenant_stored_row, own, rows):
+def scalars(segment_tenant, segment_lengths, tenant_stored_row, own):
     bins, slots = segment_tenant.shape
     me = lax.axis_index("dp")
     tenants = jnp.arange(tenant_stored_row.shape[0], dtype=jnp.int32)
@@ -507,8 +504,7 @@
     wanted = jnp.max(jnp.where(stored // own == me, stored % own, -1), axis=1)
     every = jnp.arange(bins, dtype=jnp.int32)
     segment = jnp.max(jnp.where(owners[None, :] == every[:, None], place[None, :], -1), axis=1)
-    place_f = lax.axis_index("fsdp")
-    head = jnp.stack([me % 2, place_f * rows, me // 2, place_f])
+    head = jnp.stack([me % 2, me // 2, lax.axis_index("fsdp")])
     return jnp.concatenate([head, starts, starts + lengths, owners, wanted, segment]).astype(
         jnp.int32
     )
@@ -531,22 +527,24 @@
     rows = tokens.shape[0]
     n = lax.axis_size("fsdp")
     scale = (n * rows) ** (-0.5)
-    meta = scalars(segment_tenant, segment_lengths, tenant_stored_row, own, rows)
-
+    meta = scalars(segment_tenant, segment_lengths, tenant_stored_row, own)
+
+    me = lax.axis_index("dp").astype(jnp.int32).reshape(1)
+    mine = turn(me, value_weight, bins)[None]
+    near = [across(mine, 0, k, n) for k in range(1, SIDE)]
     packed = pack(tokens, jnp.swapaxes(cotangent, 0, 1), n)
-    me = lax.axis_index("dp").astype(jnp.int32).reshape(1)
-    packed, me = lax.optimization_barrier((packed, me))
-    parts = exchange(packed, "fsdp")
-    mine = turn(me, value_weight, bins)[None]
-    mine = jnp.concatenate([mine] + [across(mine, 0, k, n) for k in range(1, SIDE)])
-    mine = jnp.concatenate([mine] + [across(mine, k, 0, n) for k in range(1, SIDE)])
-    weight = lax.all_gather(mine, "dp", axis=0)
-
+    packed, near, mine = lax.optimization_barrier((packed, near, mine))
+    mine = jnp.concatenate([mine] + near)
+    near = [across(mine, k, 0, n) for k in range(1, SIDE)]
     keep, give = offer(
         meta, jnp.swapaxes(adapter_down_weight, 1, 2), adapter_up_weight, chips, slots
     )
+    packed, keep, give, near, mine = lax.optimization_barrier((packed, keep, give, near, mine))
+    weight = lax.all_gather(jnp.concatenate([mine] + near), "dp", axis=0)
+
+    parts = exchange(packed, "fsdp")
     got = spread(meta, keep, give, bins)
-    parts, got, mine = lax.optimization_barrier((parts, got, mine))
+    parts, got = lax.optimization_barrier((parts, got))
     down, down_t, up_t = choose(meta, got, slots, v)
 
     sums = exchange(project(meta, parts, down_t, up_t, rows, slots, rank), "fsdp")
@@ -556,10 +554,10 @@
     terms = exchange(terms, "fsdp")
     sent = spread(meta, *gradient(meta, parts, low_all, chips, slots, rank, v), bins)
     done = base(meta, cotangent, weight)
-    terms, sent, done = lax.optimization_barrier((terms, sent, done))
-    grad = join(done, terms)
+    sent, done = lax.optimization_barrier((sent, done))
     down_grad, up_grad = collect(meta, sent, own, v, slots, scale)
-    return grad, jnp.swapaxes(down_grad, 1, 2), up_grad
+    terms, down_grad, up_grad = lax.optimization_barrier((terms, down_grad, up_grad))
+    return join(done, terms), jnp.swapaxes(down_grad, 1, 2), up_grad
 
 
 def solution(mesh):

time: 243 us -> 240 us (0.988)
  local copies, waits for them, and re-layouts: 12.2 us -> 5.19 us
  starting transfers between devices: 66.2 us -> 63.3 us
  waiting for transfers between devices: 58.4 us -> 61.1 us
    unnamed x32 -> x25, local copies, waits for them, and re-layouts: 11.9 us -> 4.92 us
    all_to_all x2, waiting for transfers between devices: 6.5 us -> 9.37 us  [exchange(): return lax.all_to_all(x, axis, 0, 0, tiled=True)]
    ppermute x6, waiting for transfers between devices: 11.2 us -> 8.38 us  [across(): lax.ppermute(x, 'fsdp', [(i, (i // SIDE + dy) % SIDE * SIDE + (i % SIDE +...]
    ppermute x14, waiting for transfers between devices: 37.2 us -> 39.9 us  [shift(): lax.ppermute(x, 'dp', [(i, (i // 2 + k) % chips * 2 + i % 2) for i in ran...]
  transfers between devices with their start and end apart: 25 -> 25, of which waited for: 13 -> 11; matrix products, arithmetic and copies ran while one was open for 0% -> 2% of each run, Pallas kernels for 17% -> 20%
where the time goes in v8:
time: 240 us; the launch traced here: 238 us
  starting transfers between devices  63.3 us (26%)
  waiting for transfers between devices  61.1 us (25%)
  Pallas kernels  57.3 us (24%)
  blocking collectives  33.8 us (14%)
  between operations  14.3 us (6%)
  local copies, waits for them, and re-layouts  5.19 us (2%)
  other arithmetic  2.47 us (1%)
    ppermute x14, waiting for transfers between devices, shift(): lax.ppermute(x, 'dp', [(i, (i // 2 + k) % chips * 2 + i % 2) for i in ran...  39.9 us
    ppermute x14, starting transfers between devices, shift(): lax.ppermute(x, 'dp', [(i, (i // 2 + k) % chips * 2 + i % 2) for i in ran...  35.2 us
    all_to_all x2, blocking collectives, exchange(): return lax.all_to_all(x, axis, 0, 0, tiled=True)  33.8 us
    pallas_call x1, Pallas kernels, base(): call(base_kernel, 'base', flops=2 * rows * n * piece * width, moved=2 * n...  17.7 us
    ppermute x6, starting transfers between devices, across(): lax.ppermute(x, 'fsdp', [(i, (i // SIDE + dy) % SIDE * SIDE + (i % SIDE +...  10.8 us
    all_to_all x2, starting transfers between devices, exchange(): return lax.all_to_all(x, axis, 0, 0, tiled=True)  9.56 us
    all_to_all x2, waiting for transfers between devices, exchange(): return lax.all_to_all(x, axis, 0, 0, tiled=True)  9.37 us
    pallas_call x1, Pallas kernels, join(): call(join_kernel, 'join', moved=8 * n * rows * piece, vmem=VMEM_MOST, gri...  8.5 us
  transfers between devices with their start and end apart: 25, of which 11 were waited for; matrix products, arithmetic and copies ran while one was open for 2% of the time, Pallas kernels for 20%

profile of v8, /device:TPU:1, one launch (start us, length us, event | category | flops | bytes accessed | tf_op | source)
XLA Modules:
  0.0 237.5 jit_solution(8377266420409117689)
XLA Ops:
  18.4 5.1 %pack.1 = bf16[16,288,512]{2,1,0:T(8,128)(2,1)} custom-call(bf16[256,8192]{1,0:T(8,128)(2,1)} %tok.1, bf16[1024,256]{1,0:T(8,128)(2,1)} %bitcast.25), custom_call_target="tpu_custom_call" | custom-call | bytes 8388608 | tf_op jit(solution)/shard_map/pack/pallas_call | solution.py:109
  31.4 6.7 %collective-permute-done.4 = bf16[4,64,512]{2,1,0:T(8,128)(2,1)S(1)} collective-permute-done((bf16[4,64,512]{2,1,0:T(8,128)(2,1)S(1)}, bf16[4,64,512]{2,1,0:T(8,128)(2,1)S(1)}, u32[]{:S(2)}, u32[]{:S(2)}) %collective-permute-start.4) | collective-permute-done | bytes 262176 | tf_op jit(solution)/shard_map/ppermute | solution.py:483
  39.3 4.9 %all-to-all-start = ((bf16[16,288,512]{2,1,0:T(8,128)(2,1)}), bf16[16,288,512]{2,1,0:T(8,128)(2,1)}, u32[]{:S(2)}, u32[]{:S(2)}) async-start(bf16[16,288,512]{2,1,0:T(8,128)(2,1)} %pack.1), calls=%async_computation | async-start | bytes 9437184 | tf_op jit(solution)/shard_map/all_to_all | solution.py:463
  50.5 3.0 %collective-permute-start.8 = (bf16[2,64,640]{2,1,0:T(8,128)(2,1)S(1)}, bf16[2,64,640]{2,1,0:T(8,128)(2,1)S(1)}, u32[]{:S(2)}, u32[]{:S(2)}) collective-permute-start(bf16[2,64,640]{2,1,0:T(8,128)(2,1)S(1)} %get-tuple-element.75), channel_id=1, source_target_pairs={{0,64},{16,80},{32,96},{48,112},{64,128},{80,144},{96,160},{112,17... | collective-permute-start | bytes 491528 | tf_op jit(solution)/shard_map/ppermute | solution.py:472
  53.5 3.8 %collective-permute-start.9 = (bf16[2,64,640]{2,1,0:T(8,128)(2,1)S(1)}, bf16[2,64,640]{2,1,0:T(8,128)(2,1)S(1)}, u32[]{:S(2)}, u32[]{:S(2)}) collective-permute-start(bf16[2,64,640]{2,1,0:T(8,128)(2,1)S(1)} %get-tuple-element.76), channel_id=1, source_target_pairs={{0,96},{16,112},{32,128},{48,144},{64,160},{80,176},{96,192},{112,... | collective-permute-start | bytes 491528 | tf_op jit(solution)/shard_map/ppermute | solution.py:472
  57.7 4.5 %collective-permute-start.11 = (bf16[2,64,640]{2,1,0:T(8,128)(2,1)S(1)}, bf16[2,64,640]{2,1,0:T(8,128)(2,1)S(1)}, u32[]{:S(2)}, u32[]{:S(2)}) collective-permute-start(bf16[2,64,640]{2,1,0:T(8,128)(2,1)S(1)} %get-tuple-element.78), channel_id=1, source_target_pairs={{0,160},{16,176},{32,192},{48,208},{64,224},{80,240},{96,0},{112,1... | collective-permute-start | bytes 491528 | tf_op jit(solution)/shard_map/ppermute | solution.py:472
  64.5 9.3 %collective-permute-done.8.refs_2_ = bf16[2,64,640]{2,1,0:T(8,128)(2,1)S(1)} collective-permute-done((bf16[2,64,640]{2,1,0:T(8,128)(2,1)S(1)}, bf16[2,64,640]{2,1,0:T(8,128)(2,1)S(1)}, u32[]{:S(2)}, u32[]{:S(2)}) %collective-permute-start.8) | collective-permute-done | bytes 163872 | tf_op jit(solution)/shard_map/ppermute | solution.py:472
  73.9 11.9 %collective-permute-done.9.refs_3_ = bf16[2,64,640]{2,1,0:T(8,128)(2,1)S(1)} collective-permute-done((bf16[2,64,640]{2,1,0:T(8,128)(2,1)S(1)}, bf16[2,64,640]{2,1,0:T(8,128)(2,1)S(1)}, u32[]{:S(2)}, u32[]{:S(2)}) %collective-permute-start.9) | collective-permute-done | bytes 163872 | tf_op jit(solution)/shard_map/ppermute | solution.py:472
  85.8 8.7 %collective-permute-done.10.refs_4_ = bf16[2,64,640]{2,1,0:T(8,128)(2,1)S(1)} collective-permute-done((bf16[2,64,640]{2,1,0:T(8,128)(2,1)S(1)}, bf16[2,64,640]{2,1,0:T(8,128)(2,1)S(1)}, u32[]{:S(2)}, u32[]{:S(2)}) %collective-permute-start.10) | collective-permute-done | bytes 163872 | tf_op jit(solution)/shard_map/ppermute | solution.py:472
  94.5 7.5 %collective-permute-done.13.refs_7_ = bf16[2,64,640]{2,1,0:T(8,128)(2,1)S(1)} collective-permute-done((bf16[2,64,640]{2,1,0:T(8,128)(2,1)S(1)}, bf16[2,64,640]{2,1,0:T(8,128)(2,1)S(1)}, u32[]{:S(2)}, u32[]{:S(2)}) %collective-permute-start.13) | collective-permute-done | bytes 163872 | tf_op jit(solution)/shard_map/ppermute | solution.py:472
  102.0 9.4 %all-to-all-done.part = bf16[16,288,512]{2,1,0:T(8,128)(2,1)} async-done(((bf16[16,288,512]{2,1,0:T(8,128)(2,1)}), bf16[16,288,512]{2,1,0:T(8,128)(2,1)}, u32[]{:S(2)}, u32[]{:S(2)}) %all-to-all-start) | async-done | bytes 4718624 | tf_op jit(solution)/shard_map/all_to_all | solution.py:463
  113.4 6.8 %project.1 = bf16[16,256,128]{2,1,0:T(8,128)(2,1)S(1)} custom-call(s32[59]{0:T(128)S(1)} %concatenate.9.meta, bf16[16,288,512]{2,1,0:T(8,128)(2,1)} %all-to-all-done.part, bf16[512,512]{1,0:T(8,128)(2,1)S(1)} %get-tuple-element.90.down_t, bf16[64,512]{1,0:T(8,128)(2,1)S(1)} %get-tuple-element.91.up_t), custom_call_target="tpu_custom_call" | custom-call | flops 2147483648 | bytes 4718592 | tf_op jit(solution)/shard_map/project/pallas_call | solution.py:233
  120.3 17.5 %all_to_all.20.parts = bf16[16,256,128]{2,1,0:T(8,128)(2,1)S(1)} all-to-all(bf16[16,256,128]{2,1,0:T(8,128)(2,1)S(1)} %project.1), channel_id=1, replica_groups=mesh['dp'=16,'fsdp'=16] {'fsdp'}, dimensions={0} | all-to-all | bytes 2097152 | tf_op jit(solution)/shard_map/all_to_all | solution.py:463
  138.1 16.3 %all_to_all.21.low = bf16[16,128,256]{2,1,0:T(8,128)(2,1)} all-to-all(bf16[16,128,256]{2,1,0:T(8,128)(2,1)S(1)} %total.1), channel_id=1, replica_groups=mesh['dp'=16,'fsdp'=16] {'fsdp'}, dimensions={0} | all-to-all | bytes 2097152 | tf_op jit(solution)/shard_map/all_to_all | solution.py:463
  154.4 6.5 %term.1 = bf16[16,256,512]{2,1,0:T(8,128)(2,1)} custom-call(s32[59]{0:T(128)} %copy-done.6, bf16[16,128,256]{2,1,0:T(8,128)(2,1)} %all_to_all.21.low, bf16[8,64,640]{2,1,0:T(8,128)(2,1)} %copy-done.9), custom_call_target="tpu_custom_call" | custom-call | flops 2147483648 | bytes 4194304 | tf_op jit(solution)/shard_map/term/pallas_call | solution.py:387
  160.9 4.7 %all-to-all-start.3 = ((bf16[16,256,512]{2,1,0:T(8,128)(2,1)}), bf16[16,256,512]{2,1,0:T(8,128)(2,1)}, u32[]{:S(2)}, u32[]{:S(2)}) async-start(bf16[16,256,512]{2,1,0:T(8,128)(2,1)} %term.1), calls=%async_computation.3 | async-start | bytes 8388608 | tf_op jit(solution)/shard_map/all_to_all | solution.py:463
  165.6 7.4 %gradient.1 = (bf16[8,64,640]{2,1,0:T(8,128)(2,1)S(1)}, bf16[8,64,640]{2,1,0:T(8,128)(2,1)S(1)}) custom-call(s32[59]{0:T(128)S(1)} %copy-done.7, bf16[16,288,512]{2,1,0:T(8,128)(2,1)} %all-to-all-done.part, bf16[16,128,256]{2,1,0:T(8,128)(2,1)S(1)} %copy-done.3), custom_call_target="tpu_custom_call" | custom-call | flops 2147483648 | bytes 4718592 | tf_op jit(solution)/shard_map/gradient/pallas_call | solution.py:322
  173.0 5.5 %collective-permute-start.14 = (bf16[8,64,640]{2,1,0:T(8,128)(2,1)S(1)}, bf16[8,64,640]{2,1,0:T(8,128)(2,1)S(1)}, u32[]{:S(2)}, u32[]{:S(2)}) collective-permute-start(bf16[8,64,640]{2,1,0:T(8,128)(2,1)S(1)} %get-tuple-element.95), channel_id=1, source_target_pairs={{0,16},{16,0},{32,48},{48,32},{64,80},{80,64},{96,112},{112,96},{1... | collective-permute-start | bytes 1966088 | tf_op jit(solution)/shard_map/ppermute | solution.py:467
  182.8 2.8 %collective-permute-start.16 = (bf16[2,64,640]{2,1,0:T(8,128)(2,1)S(1)}, bf16[2,64,640]{2,1,0:T(8,128)(2,1)S(1)}, u32[]{:S(2)}, u32[]{:S(2)}) collective-permute-start(bf16[2,64,640]{2,1,0:T(8,128)(2,1)S(1)} %get-tuple-element.98), channel_id=1, source_target_pairs={{0,64},{16,80},{32,96},{48,112},{64,128},{80,144},{96,160},{112,17... | collective-permute-start | bytes 491528 | tf_op jit(solution)/shard_map/ppermute | solution.py:472
  185.5 3.7 %collective-permute-start.17 = (bf16[2,64,640]{2,1,0:T(8,128)(2,1)S(1)}, bf16[2,64,640]{2,1,0:T(8,128)(2,1)S(1)}, u32[]{:S(2)}, u32[]{:S(2)}) collective-permute-start(bf16[2,64,640]{2,1,0:T(8,128)(2,1)S(1)} %get-tuple-element.99), channel_id=1, source_target_pairs={{0,96},{16,112},{32,128},{48,144},{64,160},{80,176},{96,192},{112,... | collective-permute-start | bytes 491528 | tf_op jit(solution)/shard_map/ppermute | solution.py:472
  189.8 4.5 %collective-permute-start.19 = (bf16[2,64,640]{2,1,0:T(8,128)(2,1)S(1)}, bf16[2,64,640]{2,1,0:T(8,128)(2,1)S(1)}, u32[]{:S(2)}, u32[]{:S(2)}) collective-permute-start(bf16[2,64,640]{2,1,0:T(8,128)(2,1)S(1)} %get-tuple-element.101), channel_id=1, source_target_pairs={{0,160},{16,176},{32,192},{48,208},{64,224},{80,240},{96,0},{112,1... | collective-permute-start | bytes 491528 | tf_op jit(solution)/shard_map/ppermute | solution.py:472
  196.8 3.5 %collective-permute-start.21 = (bf16[2,64,640]{2,1,0:T(8,128)(2,1)S(1)}, bf16[2,64,640]{2,1,0:T(8,128)(2,1)S(1)}, u32[]{:S(2)}, u32[]{:S(2)}) collective-permute-start(bf16[2,64,640]{2,1,0:T(8,128)(2,1)S(1)} %get-tuple-element.103), channel_id=1, source_target_pairs={{0,224},{16,240},{32,0},{48,16},{64,32},{80,48},{96,64},{112,80},{... | collective-permute-start | bytes 491528 | tf_op jit(solution)/shard_map/ppermute | solution.py:472
  200.3 17.7 %base.1.done = f32[256,8192]{1,0:T(8,128)} custom-call(s32[59]{0:T(128)} %copy-done.6, bf16[256,1024]{1,0:T(8,128)(2,1)} %cot.1, bf16[16,16,64,512]{3,2,1,0:T(8,128)(2,1)} %bitcast.24), custom_call_target="tpu_custom_call" | custom-call | flops 4294967296 | bytes 25165824 | tf_op jit(solution)/shard_map/base/pallas_call | solution.py:419
  222.2 8.5 %join.1 = bf16[256,8192]{1,0:T(8,128)(2,1)} custom-call(f32[256,8192]{1,0:T(8,128)} %base.1.done, bf16[16,256,512]{2,1,0:T(8,128)(2,1)} %all-to-all-done.3.terms), custom_call_target="tpu_custom_call" | custom-call | bytes 16777216 | tf_op jit(solution)/shard_map/join/pallas_call | solution.py:447
  (77 shorter events, 43.0 us)
Async XLA Ops:
  7.2 193.1 %all-gather.3.cloned.1.call-start = ((), (), s32[]{:S(2)}) async-start(), calls=%async_computation.4 | async-start | bytes 17825792 | tf_op jit(solution)/shard_map/all_gather | solution.py:543
  8.6 15.0 %collective-permute-start = (bf16[1,64,512]{2,1,0:T(8,128)(2,1)S(1)}, bf16[1,64,512]{2,1,0:T(8,128)(2,1)S(1)}, u32[]{:S(2)}, u32[]{:S(2)}) collective-permute-start(bf16[1,64,512]{2,1,0:T(8,128)(2,1)S(1)} %bitcast.20), channel_id=1, source_target_pairs={{0,1},{1,2},{2,3},{3,0},{4,5},{5,6},{6,7},{7,4},{8,9},{9,10},{10,1... | collective-permute-start | bytes 196616 | tf_op jit(solution)/shard_map/ppermute | solution.py:483
  10.7 12.9 %collective-permute-start.1 = (bf16[1,64,512]{2,1,0:T(8,128)(2,1)S(1)}, bf16[1,64,512]{2,1,0:T(8,128)(2,1)S(1)}, u32[]{:S(2)}, u32[]{:S(2)}) collective-permute-start(bf16[1,64,512]{2,1,0:T(8,128)(2,1)S(1)} %bitcast.21), channel_id=1, source_target_pairs={{0,2},{1,3},{2,0},{3,1},{4,6},{5,7},{6,4},{7,5},{8,10},{9,11},{10,... | collective-permute-start | bytes 196616 | tf_op jit(solution)/shard_map/ppermute | solution.py:483
  13.2 10.4 %collective-permute-start.2 = (bf16[1,64,512]{2,1,0:T(8,128)(2,1)S(1)}, bf16[1,64,512]{2,1,0:T(8,128)(2,1)S(1)}, u32[]{:S(2)}, u32[]{:S(2)}) collective-permute-start(bf16[1,64,512]{2,1,0:T(8,128)(2,1)S(1)} %bitcast.22), channel_id=1, source_target_pairs={{0,3},{1,0},{2,1},{3,2},{4,7},{5,4},{6,5},{7,6},{8,11},{9,8},{10,9... | collective-permute-start | bytes 196616 | tf_op jit(solution)/shard_map/ppermute | solution.py:483
  23.7 7.7 %collective-permute-start.3 = (bf16[4,64,512]{2,1,0:T(8,128)(2,1)S(1)}, bf16[4,64,512]{2,1,0:T(8,128)(2,1)S(1)}, u32[]{:S(2)}, u32[]{:S(2)}) collective-permute-start(bf16[4,64,512]{2,1,0:T(8,128)(2,1)S(1)} %constant_dynamic-update-slice_fusion), channel_id=1, source_target_pairs={{0,4},{1,5},{2,6},{3,7},{4,8},{5,9},{6,10},{7,11},{8,12},{9,13},{1... | collective-permute-start | bytes 786440 | tf_op jit(solution)/shard_map/ppermute | solution.py:483
  25.1 13.1 %collective-permute-start.4 = (bf16[4,64,512]{2,1,0:T(8,128)(2,1)S(1)}, bf16[4,64,512]{2,1,0:T(8,128)(2,1)S(1)}, u32[]{:S(2)}, u32[]{:S(2)}) collective-permute-start(bf16[4,64,512]{2,1,0:T(8,128)(2,1)S(1)} %constant_dynamic-update-slice_fusion), channel_id=1, source_target_pairs={{0,8},{1,9},{2,10},{3,11},{4,12},{5,13},{6,14},{7,15},{8,0},{9,1},... | collective-permute-start | bytes 786440 | tf_op jit(solution)/shard_map/ppermute | solution.py:483
  27.7 10.4 %collective-permute-start.5 = (bf16[4,64,512]{2,1,0:T(8,128)(2,1)S(1)}, bf16[4,64,512]{2,1,0:T(8,128)(2,1)S(1)}, u32[]{:S(2)}, u32[]{:S(2)}) collective-permute-start(bf16[4,64,512]{2,1,0:T(8,128)(2,1)S(1)} %constant_dynamic-update-slice_fusion), channel_id=1, source_target_pairs={{0,12},{1,13},{2,14},{3,15},{4,0},{5,1},{6,2},{7,3},{8,4},{9,5},{1... | collective-permute-start | bytes 786440 | tf_op jit(solution)/shard_map/ppermute | solution.py:483
  39.3 72.1 %all-to-all-start = ((bf16[16,288,512]{2,1,0:T(8,128)(2,1)}), bf16[16,288,512]{2,1,0:T(8,128)(2,1)}, u32[]{:S(2)}, u32[]{:S(2)}) async-start(bf16[16,288,512]{2,1,0:T(8,128)(2,1)} %pack.1), calls=%async_computation | async-start | bytes 9437184 | tf_op jit(solution)/shard_map/all_to_all | solution.py:463
  48.8 13.4 %collective-permute-start.7 = (bf16[2,64,640]{2,1,0:T(8,128)(2,1)S(1)}, bf16[2,64,640]{2,1,0:T(8,128)(2,1)S(1)}, u32[]{:S(2)}, u32[]{:S(2)}) collective-permute-start(bf16[2,64,640]{2,1,0:T(8,128)(2,1)S(1)} %get-tuple-element.74), channel_id=1, source_target_pairs={{0,32},{16,48},{32,64},{48,80},{64,96},{80,112},{96,128},{112,144}... | collective-permute-start | bytes 491528 | tf_op jit(solution)/shard_map/ppermute | solution.py:472
  50.5 23.4 %collective-permute-start.8 = (bf16[2,64,640]{2,1,0:T(8,128)(2,1)S(1)}, bf16[2,64,640]{2,1,0:T(8,128)(2,1)S(1)}, u32[]{:S(2)}, u32[]{:S(2)}) collective-permute-start(bf16[2,64,640]{2,1,0:T(8,128)(2,1)S(1)} %get-tuple-element.75), channel_id=1, source_target_pairs={{0,64},{16,80},{32,96},{48,112},{64,128},{80,144},{96,160},{112,17... | collective-permute-start | bytes 491528 | tf_op jit(solution)/shard_map/ppermute | solution.py:472
  53.5 32.3 %collective-permute-start.9 = (bf16[2,64,640]{2,1,0:T(8,128)(2,1)S(1)}, bf16[2,64,640]{2,1,0:T(8,128)(2,1)S(1)}, u32[]{:S(2)}, u32[]{:S(2)}) collective-permute-start(bf16[2,64,640]{2,1,0:T(8,128)(2,1)S(1)} %get-tuple-element.76), channel_id=1, source_target_pairs={{0,96},{16,112},{32,128},{48,144},{64,160},{80,176},{96,192},{112,... | collective-permute-start | bytes 491528 | tf_op jit(solution)/shard_map/ppermute | solution.py:472
  57.2 37.3 %collective-permute-start.10 = (bf16[2,64,640]{2,1,0:T(8,128)(2,1)S(1)}, bf16[2,64,640]{2,1,0:T(8,128)(2,1)S(1)}, u32[]{:S(2)}, u32[]{:S(2)}) collective-permute-start(bf16[2,64,640]{2,1,0:T(8,128)(2,1)S(1)} %get-tuple-element.77), channel_id=1, source_target_pairs={{0,128},{16,144},{32,160},{48,176},{64,192},{80,208},{96,224},{112... | collective-permute-start | bytes 491528 | tf_op jit(solution)/shard_map/ppermute | solution.py:472
  57.7 36.8 %collective-permute-start.11 = (bf16[2,64,640]{2,1,0:T(8,128)(2,1)S(1)}, bf16[2,64,640]{2,1,0:T(8,128)(2,1)S(1)}, u32[]{:S(2)}, u32[]{:S(2)}) collective-permute-start(bf16[2,64,640]{2,1,0:T(8,128)(2,1)S(1)} %get-tuple-element.78), channel_id=1, source_target_pairs={{0,160},{16,176},{32,192},{48,208},{64,224},{80,240},{96,0},{112,1... | collective-permute-start | bytes 491528 | tf_op jit(solution)/shard_map/ppermute | solution.py:472
  62.1 32.3 %collective-permute-start.12 = (bf16[2,64,640]{2,1,0:T(8,128)(2,1)S(1)}, bf16[2,64,640]{2,1,0:T(8,128)(2,1)S(1)}, u32[]{:S(2)}, u32[]{:S(2)}) collective-permute-start(bf16[2,64,640]{2,1,0:T(8,128)(2,1)S(1)} %get-tuple-element.79), channel_id=1, source_target_pairs={{0,192},{16,208},{32,224},{48,240},{64,0},{80,16},{96,32},{112,48}... | collective-permute-start | bytes 491528 | tf_op jit(solution)/shard_map/ppermute | solution.py:472
  73.9 28.1 %collective-permute-start.13 = (bf16[2,64,640]{2,1,0:T(8,128)(2,1)S(1)}, bf16[2,64,640]{2,1,0:T(8,128)(2,1)S(1)}, u32[]{:S(2)}, u32[]{:S(2)}) collective-permute-start(bf16[2,64,640]{2,1,0:T(8,128)(2,1)S(1)} %get-tuple-element.80), channel_id=1, source_target_pairs={{0,224},{16,240},{32,0},{48,16},{64,32},{80,48},{96,64},{112,80},{... | collective-permute-start | bytes 491528 | tf_op jit(solution)/shard_map/ppermute | solution.py:472
  160.9 61.3 %all-to-all-start.3 = ((bf16[16,256,512]{2,1,0:T(8,128)(2,1)}), bf16[16,256,512]{2,1,0:T(8,128)(2,1)}, u32[]{:S(2)}, u32[]{:S(2)}) async-start(bf16[16,256,512]{2,1,0:T(8,128)(2,1)} %term.1), calls=%async_computation.3 | async-start | bytes 8388608 | tf_op jit(solution)/shard_map/all_to_all | solution.py:463
  173.0 7.3 %collective-permute-start.14 = (bf16[8,64,640]{2,1,0:T(8,128)(2,1)S(1)}, bf16[8,64,640]{2,1,0:T(8,128)(2,1)S(1)}, u32[]{:S(2)}, u32[]{:S(2)}) collective-permute-start(bf16[8,64,640]{2,1,0:T(8,128)(2,1)S(1)} %get-tuple-element.95), channel_id=1, source_target_pairs={{0,16},{16,0},{32,48},{48,32},{64,80},{80,64},{96,112},{112,96},{1... | collective-permute-start | bytes 1966088 | tf_op jit(solution)/shard_map/ppermute | solution.py:467
  180.9 13.4 %collective-permute-start.15 = (bf16[2,64,640]{2,1,0:T(8,128)(2,1)S(1)}, bf16[2,64,640]{2,1,0:T(8,128)(2,1)S(1)}, u32[]{:S(2)}, u32[]{:S(2)}) collective-permute-start(bf16[2,64,640]{2,1,0:T(8,128)(2,1)S(1)} %get-tuple-element.97), channel_id=1, source_target_pairs={{0,32},{16,48},{32,64},{48,80},{64,96},{80,112},{96,128},{112,144}... | collective-permute-start | bytes 491528 | tf_op jit(solution)/shard_map/ppermute | solution.py:472
  182.8 14.0 %collective-permute-start.16 = (bf16[2,64,640]{2,1,0:T(8,128)(2,1)S(1)}, bf16[2,64,640]{2,1,0:T(8,128)(2,1)S(1)}, u32[]{:S(2)}, u32[]{:S(2)}) collective-permute-start(bf16[2,64,640]{2,1,0:T(8,128)(2,1)S(1)} %get-tuple-element.98), channel_id=1, source_target_pairs={{0,64},{16,80},{32,96},{48,112},{64,128},{80,144},{96,160},{112,17... | collective-permute-start | bytes 491528 | tf_op jit(solution)/shard_map/ppermute | solution.py:472
  185.5 32.5 %collective-permute-start.17 = (bf16[2,64,640]{2,1,0:T(8,128)(2,1)S(1)}, bf16[2,64,640]{2,1,0:T(8,128)(2,1)S(1)}, u32[]{:S(2)}, u32[]{:S(2)}) collective-permute-start(bf16[2,64,640]{2,1,0:T(8,128)(2,1)S(1)} %get-tuple-element.99), channel_id=1, source_target_pairs={{0,96},{16,112},{32,128},{48,144},{64,160},{80,176},{96,192},{112,... | collective-permute-start | bytes 491528 | tf_op jit(solution)/shard_map/ppermute | solution.py:472
  189.3 28.7 %collective-permute-start.18 = (bf16[2,64,640]{2,1,0:T(8,128)(2,1)S(1)}, bf16[2,64,640]{2,1,0:T(8,128)(2,1)S(1)}, u32[]{:S(2)}, u32[]{:S(2)}) collective-permute-start(bf16[2,64,640]{2,1,0:T(8,128)(2,1)S(1)} %get-tuple-element.100), channel_id=1, source_target_pairs={{0,128},{16,144},{32,160},{48,176},{64,192},{80,208},{96,224},{112... | collective-permute-start | bytes 491528 | tf_op jit(solution)/shard_map/ppermute | solution.py:472
  189.8 28.2 %collective-permute-start.19 = (bf16[2,64,640]{2,1,0:T(8,128)(2,1)S(1)}, bf16[2,64,640]{2,1,0:T(8,128)(2,1)S(1)}, u32[]{:S(2)}, u32[]{:S(2)}) collective-permute-start(bf16[2,64,640]{2,1,0:T(8,128)(2,1)S(1)} %get-tuple-element.101), channel_id=1, source_target_pairs={{0,160},{16,176},{32,192},{48,208},{64,224},{80,240},{96,0},{112,1... | collective-permute-start | bytes 491528 | tf_op jit(solution)/shard_map/ppermute | solution.py:472
  194.3 25.0 %collective-permute-start.20 = (bf16[2,64,640]{2,1,0:T(8,128)(2,1)S(1)}, bf16[2,64,640]{2,1,0:T(8,128)(2,1)S(1)}, u32[]{:S(2)}, u32[]{:S(2)}) collective-permute-start(bf16[2,64,640]{2,1,0:T(8,128)(2,1)S(1)} %get-tuple-element.102), channel_id=1, source_target_pairs={{0,192},{16,208},{32,224},{48,240},{64,0},{80,16},{96,32},{112,48}... | collective-permute-start | bytes 491528 | tf_op jit(solution)/shard_map/ppermute | solution.py:472
  196.8 23.6 %collective-permute-start.21 = (bf16[2,64,640]{2,1,0:T(8,128)(2,1)S(1)}, bf16[2,64,640]{2,1,0:T(8,128)(2,1)S(1)}, u32[]{:S(2)}, u32[]{:S(2)}) collective-permute-start(bf16[2,64,640]{2,1,0:T(8,128)(2,1)S(1)} %get-tuple-element.103), channel_id=1, source_target_pairs={{0,224},{16,240},{32,0},{48,16},{64,32},{80,48},{96,64},{112,80},{... | collective-permute-start | bytes 491528 | tf_op jit(solution)/shard_map/ppermute | solution.py:472
  (11 other events, 159.8 us)
Sparse Core Ops, SparseCore 0:
  39.4 124.9 all-gather.2

commit v9 on v8

--- a/solution.py
+++ b/solution.py
@@ -400,37 +400,41 @@
 
 
 def base_kernel(meta, cot, w, out):
-    out[...] = jnp.dot(
-        cot[...],
-        jnp.concatenate([w[e, 0] for e in range(w.shape[0])], axis=0),
-        preferred_element_type=F32,
-    )
+    slices, group, _, piece = w.shape
+    dx = lax.rem(pl.program_id(0) * group, SIDE)
+    for g in range(group):
+        x = lax.rem(lax.rem(meta[PIECE], SIDE) + SIDE - dx - g, SIDE)
+        r = jnp.dot(
+            cot[...],
+            jnp.concatenate([w[e, g] for e in range(slices)], axis=0),
+            preferred_element_type=F32,
+        )
+        out[:, pl.ds(pl.multiple_of(x * piece, piece), piece)] = r.astype(BF)
 
 
 def base(meta, cot, w):
     slices, n, part, piece = w.shape
     rows, width = cot.shape
+    group = SIDE // 2
 
     def place(f, m):
-        y = lax.rem(m[PIECE] // SIDE + SIDE - f // SIDE, SIDE)
-        x = lax.rem(lax.rem(m[PIECE], SIDE) + SIDE - lax.rem(f, SIDE), SIDE)
-        return (0, y * SIDE + x)
+        return (0, lax.rem(m[PIECE] // SIDE + SIDE - f * group // SIDE, SIDE))
 
     return call(
         base_kernel,
         "base",
         flops=2 * rows * n * piece * width,
-        moved=2 * n * piece * width + 4 * rows * n * piece,
+        moved=2 * n * piece * (width + rows),
         vmem=VMEM_MOST,
         grid_spec=with_meta(
-            (n,),
+            (n // group,),
             [
                 whole(cot.shape),
-                pl.BlockSpec((slices, 1, part, piece), lambda f, m: (0, f, 0, 0)),
+                pl.BlockSpec((slices, group, part, piece), lambda f, m: (0, f, 0, 0)),
             ],
-            pl.BlockSpec((rows, piece), place),
-        ),
-        out_shape=jax.ShapeDtypeStruct((rows, n * piece), F32),
+            pl.BlockSpec((rows, SIDE * piece), place),
+        ),
+        out_shape=jax.ShapeDtypeStruct((rows, n * piece), BF),
     )(meta, cot, w)
 
 
@@ -438,23 +442,22 @@
     group, _, piece = terms.shape
     for g in range(group):
         cols = slice(g * piece, (g + 1) * piece)
-        out[:, cols] = (done[:, cols] + terms[g].astype(F32)).astype(BF)
+        out[:, cols] = (done[:, cols].astype(F32) + terms[g].astype(F32)).astype(BF)
 
 
 def join(done, terms):
     n, rows, piece = terms.shape
-    group = 2
     return call(
         join_kernel,
         "join",
-        moved=8 * n * rows * piece,
+        moved=6 * n * rows * piece,
         vmem=VMEM_MOST,
-        grid=(n // group,),
+        grid=(n // GROUP,),
         in_specs=[
-            pl.BlockSpec((rows, group * piece), lambda f: (0, f)),
-            pl.BlockSpec((group, rows, piece), lambda f: (f, 0, 0)),
+            pl.BlockSpec((rows, GROUP * piece), lambda f: (0, f)),
+            pl.BlockSpec((GROUP, rows, piece), lambda f: (f, 0, 0)),
         ],
-        out_specs=pl.BlockSpec((rows, group * piece), lambda f: (0, f)),
+        out_specs=pl.BlockSpec((rows, GROUP * piece), lambda f: (0, f)),
         out_shape=jax.ShapeDtypeStruct((rows, n * piece), BF),
     )(done, terms)
 
@@ -532,10 +535,9 @@
     me = lax.axis_index("dp").astype(jnp.int32).reshape(1)
     mine = turn(me, value_weight, bins)[None]
     near = [across(mine, 0, k, n) for k in range(1, SIDE)]
-    packed = pack(tokens, jnp.swapaxes(cotangent, 0, 1), n)
-    packed, near, mine = lax.optimization_barrier((packed, near, mine))
     mine = jnp.concatenate([mine] + near)
     near = [across(mine, k, 0, n) for k in range(1, SIDE)]
+    packed = pack(tokens, jnp.swapaxes(cotangent, 0, 1), n)
     keep, give = offer(
         meta, jnp.swapaxes(adapter_down_weight, 1, 2), adapter_up_weight, chips, slots
     )

time: 240 us -> 233 us (0.971)
  Pallas kernels: 57.3 us -> 50.7 us
    ppermute x6, waiting for transfers between devices: 8.38 us -> 2.72 us  [across(): lax.ppermute(x, 'fsdp', [(i, (i // SIDE + dy) % SIDE * SIDE + (i % SIDE +...]
    pallas_call x1, Pallas kernels: 17.7 us -> 13.4 us  [base(): call(base_kernel, 'base', flops=2 * rows * n * piece * width, moved=2 * n...]
    ppermute x14, waiting for transfers between devices: 39.9 us -> 42.4 us  [shift(): lax.ppermute(x, 'dp', [(i, (i // 2 + k) % chips * 2 + i % 2) for i in ran...]
    pallas_call x1, Pallas kernels: 8.5 us -> 6.01 us  [join(): call(join_kernel, 'join', moved=6 * n * rows * piece, vmem=VMEM_MOST, gri...]
    unnamed x25 -> x20, local copies, waits for them, and re-layouts: 4.92 us -> 4.9 us
  transfers between devices with their start and end apart: 25 -> 25, of which waited for: 11 -> 12; matrix products, arithmetic and copies ran while one was open for 2% -> 2% of each run, Pallas kernels for 20% -> 19%
where the time goes in v9:
time: 233 us; the launch traced here: 231 us
  starting transfers between devices  64.5 us (28%)
  waiting for transfers between devices  59 us (25%)
  Pallas kernels  50.7 us (22%)
  blocking collectives  34.9 us (15%)
  between operations  14.3 us (6%)
  local copies, waits for them, and re-layouts  5.16 us (2%)
  other arithmetic  2.51 us (1%)
    ppermute x14, waiting for transfers between devices, shift(): lax.ppermute(x, 'dp', [(i, (i // 2 + k) % chips * 2 + i % 2) for i in ran...  42.4 us
    ppermute x14, starting transfers between devices, shift(): lax.ppermute(x, 'dp', [(i, (i // 2 + k) % chips * 2 + i % 2) for i in ran...  36.9 us
    all_to_all x2, blocking collectives, exchange(): return lax.all_to_all(x, axis, 0, 0, tiled=True)  34.9 us
    pallas_call x1, Pallas kernels, base(): call(base_kernel, 'base', flops=2 * rows * n * piece * width, moved=2 * n...  13.4 us
    all_to_all x2, starting transfers between devices, exchange(): return lax.all_to_all(x, axis, 0, 0, tiled=True)  11.2 us
    all_to_all x2, waiting for transfers between devices, exchange(): return lax.all_to_all(x, axis, 0, 0, tiled=True)  10.5 us
    ppermute x6, starting transfers between devices, across(): lax.ppermute(x, 'fsdp', [(i, (i // SIDE + dy) % SIDE * SIDE + (i % SIDE +...  9.57 us
    pallas_call x1, Pallas kernels, gradient(): call(functools.partial(gradient_kernel, slots, rank, v), 'gradient', flop...  7.52 us
  transfers between devices with their start and end apart: 25, of which 12 were waited for; matrix products, arithmetic and copies ran while one was open for 2% of the time, Pallas kernels for 19%

profile of v9, /device:TPU:1, one launch (start us, length us, event | category | flops | bytes accessed | tf_op | source)
XLA Modules:
  0.0 231.0 jit_solution(14702104422192842005)
XLA Ops:
  8.6 3.4 %collective-permute-start.2 = (bf16[1,64,512]{2,1,0:T(8,128)(2,1)S(1)}, bf16[1,64,512]{2,1,0:T(8,128)(2,1)S(1)}, u32[]{:S(2)}, u32[]{:S(2)}) collective-permute-start(bf16[1,64,512]{2,1,0:T(8,128)(2,1)S(1)} %bitcast.20), channel_id=1, source_target_pairs={{0,3},{1,0},{2,1},{3,2},{4,7},{5,4},{6,5},{7,6},{8,11},{9,8},{10,9... | collective-permute-start | bytes 196616 | tf_op jit(solution)/shard_map/ppermute | solution.py:486
  24.5 5.1 %pack.1 = bf16[16,288,512]{2,1,0:T(8,128)(2,1)} custom-call(bf16[256,8192]{1,0:T(8,128)(2,1)} %tok.1, bf16[1024,256]{1,0:T(8,128)(2,1)} %bitcast.25), custom_call_target="tpu_custom_call" | custom-call | bytes 8388608 | tf_op jit(solution)/shard_map/pack/pallas_call | solution.py:109
  32.3 6.6 %all-to-all-start = ((bf16[16,288,512]{2,1,0:T(8,128)(2,1)}), bf16[16,288,512]{2,1,0:T(8,128)(2,1)}, u32[]{:S(2)}, u32[]{:S(2)}) async-start(bf16[16,288,512]{2,1,0:T(8,128)(2,1)} %pack.1), calls=%async_computation | async-start | bytes 9437184 | tf_op jit(solution)/shard_map/all_to_all | solution.py:466
  44.8 3.0 %collective-permute-start.8 = (bf16[2,64,640]{2,1,0:T(8,128)(2,1)S(1)}, bf16[2,64,640]{2,1,0:T(8,128)(2,1)S(1)}, u32[]{:S(2)}, u32[]{:S(2)}) collective-permute-start(bf16[2,64,640]{2,1,0:T(8,128)(2,1)S(1)} %get-tuple-element.65), channel_id=1, source_target_pairs={{0,64},{16,80},{32,96},{48,112},{64,128},{80,144},{96,160},{112,17... | collective-permute-start | bytes 491528 | tf_op jit(solution)/shard_map/ppermute | solution.py:475
  47.8 3.8 %collective-permute-start.9 = (bf16[2,64,640]{2,1,0:T(8,128)(2,1)S(1)}, bf16[2,64,640]{2,1,0:T(8,128)(2,1)S(1)}, u32[]{:S(2)}, u32[]{:S(2)}) collective-permute-start(bf16[2,64,640]{2,1,0:T(8,128)(2,1)S(1)} %get-tuple-element.66), channel_id=1, source_target_pairs={{0,96},{16,112},{32,128},{48,144},{64,160},{80,176},{96,192},{112,... | collective-permute-start | bytes 491528 | tf_op jit(solution)/shard_map/ppermute | solution.py:475
  52.0 4.5 %collective-permute-start.11 = (bf16[2,64,640]{2,1,0:T(8,128)(2,1)S(1)}, bf16[2,64,640]{2,1,0:T(8,128)(2,1)S(1)}, u32[]{:S(2)}, u32[]{:S(2)}) collective-permute-start(bf16[2,64,640]{2,1,0:T(8,128)(2,1)S(1)} %get-tuple-element.68), channel_id=1, source_target_pairs={{0,160},{16,176},{32,192},{48,208},{64,224},{80,240},{96,0},{112,1... | collective-permute-start | bytes 491528 | tf_op jit(solution)/shard_map/ppermute | solution.py:475
  58.9 7.0 %collective-permute-done.8.refs_2_ = bf16[2,64,640]{2,1,0:T(8,128)(2,1)S(1)} collective-permute-done((bf16[2,64,640]{2,1,0:T(8,128)(2,1)S(1)}, bf16[2,64,640]{2,1,0:T(8,128)(2,1)S(1)}, u32[]{:S(2)}, u32[]{:S(2)}) %collective-permute-start.8) | collective-permute-done | bytes 163872 | tf_op jit(solution)/shard_map/ppermute | solution.py:475
  67.0 11.2 %collective-permute-done.9.refs_3_ = bf16[2,64,640]{2,1,0:T(8,128)(2,1)S(1)} collective-permute-done((bf16[2,64,640]{2,1,0:T(8,128)(2,1)S(1)}, bf16[2,64,640]{2,1,0:T(8,128)(2,1)S(1)}, u32[]{:S(2)}, u32[]{:S(2)}) %collective-permute-start.9) | collective-permute-done | bytes 163872 | tf_op jit(solution)/shard_map/ppermute | solution.py:475
  78.2 9.3 %collective-permute-done.10.refs_4_ = bf16[2,64,640]{2,1,0:T(8,128)(2,1)S(1)} collective-permute-done((bf16[2,64,640]{2,1,0:T(8,128)(2,1)S(1)}, bf16[2,64,640]{2,1,0:T(8,128)(2,1)S(1)}, u32[]{:S(2)}, u32[]{:S(2)}) %collective-permute-start.10) | collective-permute-done | bytes 163872 | tf_op jit(solution)/shard_map/ppermute | solution.py:475
  87.5 8.8 %collective-permute-done.13.refs_7_ = bf16[2,64,640]{2,1,0:T(8,128)(2,1)S(1)} collective-permute-done((bf16[2,64,640]{2,1,0:T(8,128)(2,1)S(1)}, bf16[2,64,640]{2,1,0:T(8,128)(2,1)S(1)}, u32[]{:S(2)}, u32[]{:S(2)}) %collective-permute-start.13) | collective-permute-done | bytes 163872 | tf_op jit(solution)/shard_map/ppermute | solution.py:475
  96.4 10.5 %all-to-all-done.part = bf16[16,288,512]{2,1,0:T(8,128)(2,1)} async-done(((bf16[16,288,512]{2,1,0:T(8,128)(2,1)}), bf16[16,288,512]{2,1,0:T(8,128)(2,1)}, u32[]{:S(2)}, u32[]{:S(2)}) %all-to-all-start) | async-done | bytes 4718624 | tf_op jit(solution)/shard_map/all_to_all | solution.py:466
  108.9 6.9 %project.1 = bf16[16,256,128]{2,1,0:T(8,128)(2,1)S(1)} custom-call(s32[59]{0:T(128)S(1)} %concatenate.9.meta, bf16[16,288,512]{2,1,0:T(8,128)(2,1)} %all-to-all-done.part, bf16[512,512]{1,0:T(8,128)(2,1)S(1)} %get-tuple-element.80.down_t, bf16[64,512]{1,0:T(8,128)(2,1)S(1)} %get-tuple-element.81.up_t), custom_call_target="tpu_custom_call" | custom-call | flops 2147483648 | bytes 4718592 | tf_op jit(solution)/shard_map/project/pallas_call | solution.py:233
  115.8 18.4 %all_to_all.20.parts = bf16[16,256,128]{2,1,0:T(8,128)(2,1)S(1)} all-to-all(bf16[16,256,128]{2,1,0:T(8,128)(2,1)S(1)} %project.1), channel_id=1, replica_groups=mesh['dp'=16,'fsdp'=16] {'fsdp'}, dimensions={0} | all-to-all | bytes 2097152 | tf_op jit(solution)/shard_map/all_to_all | solution.py:466
  134.5 16.5 %all_to_all.21.low = bf16[16,128,256]{2,1,0:T(8,128)(2,1)} all-to-all(bf16[16,128,256]{2,1,0:T(8,128)(2,1)S(1)} %total.1), channel_id=1, replica_groups=mesh['dp'=16,'fsdp'=16] {'fsdp'}, dimensions={0} | all-to-all | bytes 2097152 | tf_op jit(solution)/shard_map/all_to_all | solution.py:466
  151.0 6.5 %term.1 = bf16[16,256,512]{2,1,0:T(8,128)(2,1)} custom-call(s32[59]{0:T(128)} %copy-done.5, bf16[16,128,256]{2,1,0:T(8,128)(2,1)} %all_to_all.21.low, bf16[8,64,640]{2,1,0:T(8,128)(2,1)} %copy-done.8), custom_call_target="tpu_custom_call" | custom-call | flops 2147483648 | bytes 4194304 | tf_op jit(solution)/shard_map/term/pallas_call | solution.py:387
  157.5 4.7 %all-to-all-start.3 = ((bf16[16,256,512]{2,1,0:T(8,128)(2,1)}), bf16[16,256,512]{2,1,0:T(8,128)(2,1)}, u32[]{:S(2)}, u32[]{:S(2)}) async-start(bf16[16,256,512]{2,1,0:T(8,128)(2,1)} %term.1), calls=%async_computation.3 | async-start | bytes 8388608 | tf_op jit(solution)/shard_map/all_to_all | solution.py:466
  162.2 7.5 %gradient.1 = (bf16[8,64,640]{2,1,0:T(8,128)(2,1)S(1)}, bf16[8,64,640]{2,1,0:T(8,128)(2,1)S(1)}) custom-call(s32[59]{0:T(128)S(1)} %copy-done.6, bf16[16,288,512]{2,1,0:T(8,128)(2,1)} %all-to-all-done.part, bf16[16,128,256]{2,1,0:T(8,128)(2,1)S(1)} %copy-done.2), custom_call_target="tpu_custom_call" | custom-call | flops 2147483648 | bytes 4718592 | tf_op jit(solution)/shard_map/gradient/pallas_call | solution.py:322
  169.8 4.9 %collective-permute-start.14 = (bf16[8,64,640]{2,1,0:T(8,128)(2,1)S(1)}, bf16[8,64,640]{2,1,0:T(8,128)(2,1)S(1)}, u32[]{:S(2)}, u32[]{:S(2)}) collective-permute-start(bf16[8,64,640]{2,1,0:T(8,128)(2,1)S(1)} %get-tuple-element.85), channel_id=1, source_target_pairs={{0,16},{16,0},{32,48},{48,32},{64,80},{80,64},{96,112},{112,96},{1... | collective-permute-start | bytes 1966088 | tf_op jit(solution)/shard_map/ppermute | solution.py:470
  182.1 3.6 %collective-permute-start.17 = (bf16[2,64,640]{2,1,0:T(8,128)(2,1)S(1)}, bf16[2,64,640]{2,1,0:T(8,128)(2,1)S(1)}, u32[]{:S(2)}, u32[]{:S(2)}) collective-permute-start(bf16[2,64,640]{2,1,0:T(8,128)(2,1)S(1)} %get-tuple-element.89), channel_id=1, source_target_pairs={{0,96},{16,112},{32,128},{48,144},{64,160},{80,176},{96,192},{112,... | collective-permute-start | bytes 491528 | tf_op jit(solution)/shard_map/ppermute | solution.py:475
  186.0 4.4 %collective-permute-start.19 = (bf16[2,64,640]{2,1,0:T(8,128)(2,1)S(1)}, bf16[2,64,640]{2,1,0:T(8,128)(2,1)S(1)}, u32[]{:S(2)}, u32[]{:S(2)}) collective-permute-start(bf16[2,64,640]{2,1,0:T(8,128)(2,1)S(1)} %get-tuple-element.91), channel_id=1, source_target_pairs={{0,160},{16,176},{32,192},{48,208},{64,224},{80,240},{96,0},{112,1... | collective-permute-start | bytes 491528 | tf_op jit(solution)/shard_map/ppermute | solution.py:475
  193.0 4.0 %collective-permute-start.21 = (bf16[2,64,640]{2,1,0:T(8,128)(2,1)S(1)}, bf16[2,64,640]{2,1,0:T(8,128)(2,1)S(1)}, u32[]{:S(2)}, u32[]{:S(2)}) collective-permute-start(bf16[2,64,640]{2,1,0:T(8,128)(2,1)S(1)} %get-tuple-element.93), channel_id=1, source_target_pairs={{0,224},{16,240},{32,0},{48,16},{64,32},{80,48},{96,64},{112,80},{... | collective-permute-start | bytes 491528 | tf_op jit(solution)/shard_map/ppermute | solution.py:475
  197.0 13.4 %base.1.done = bf16[256,8192]{1,0:T(8,128)(2,1)} custom-call(s32[59]{0:T(128)} %copy-done.5, bf16[256,1024]{1,0:T(8,128)(2,1)} %cot.1, bf16[16,16,64,512]{3,2,1,0:T(8,128)(2,1)} %bitcast.24), custom_call_target="tpu_custom_call" | custom-call | flops 4294967296 | bytes 20971520 | tf_op jit(solution)/shard_map/base/pallas_call | solution.py:423
  210.4 4.7 %collective-permute-done.20.refs_6_ = bf16[2,64,640]{2,1,0:T(8,128)(2,1)S(1)} collective-permute-done((bf16[2,64,640]{2,1,0:T(8,128)(2,1)S(1)}, bf16[2,64,640]{2,1,0:T(8,128)(2,1)S(1)}, u32[]{:S(2)}, u32[]{:S(2)}) %collective-permute-start.20) | collective-permute-done | bytes 163872 | tf_op jit(solution)/shard_map/ppermute | solution.py:475
  218.1 6.0 %join.1 = bf16[256,8192]{1,0:T(8,128)(2,1)} custom-call(bf16[256,8192]{1,0:T(8,128)(2,1)} %base.1.done, bf16[16,256,512]{2,1,0:T(8,128)(2,1)} %all-to-all-done.3.terms), custom_call_target="tpu_custom_call" | custom-call | bytes 12582912 | tf_op jit(solution)/shard_map/join/pallas_call | solution.py:450
  (72 shorter events, 42.1 us)
Async XLA Ops:
  7.2 189.8 %all-gather.3.cloned.1.call-start = ((), (), s32[]{:S(2)}) async-start(), calls=%async_computation.4 | async-start | bytes 17825792 | tf_op jit(solution)/shard_map/all_gather | solution.py:545
  8.6 6.6 %collective-permute-start.2 = (bf16[1,64,512]{2,1,0:T(8,128)(2,1)S(1)}, bf16[1,64,512]{2,1,0:T(8,128)(2,1)S(1)}, u32[]{:S(2)}, u32[]{:S(2)}) collective-permute-start(bf16[1,64,512]{2,1,0:T(8,128)(2,1)S(1)} %bitcast.20), channel_id=1, source_target_pairs={{0,3},{1,0},{2,1},{3,2},{4,7},{5,4},{6,5},{7,6},{8,11},{9,8},{10,9... | collective-permute-start | bytes 196616 | tf_op jit(solution)/shard_map/ppermute | solution.py:486
  12.0 4.7 %collective-permute-start.1 = (bf16[1,64,512]{2,1,0:T(8,128)(2,1)S(1)}, bf16[1,64,512]{2,1,0:T(8,128)(2,1)S(1)}, u32[]{:S(2)}, u32[]{:S(2)}) collective-permute-start(bf16[1,64,512]{2,1,0:T(8,128)(2,1)S(1)} %bitcast.21), channel_id=1, source_target_pairs={{0,2},{1,3},{2,0},{3,1},{4,6},{5,7},{6,4},{7,5},{8,10},{9,11},{10,... | collective-permute-start | bytes 196616 | tf_op jit(solution)/shard_map/ppermute | solution.py:486
  12.5 4.8 %collective-permute-start = (bf16[1,64,512]{2,1,0:T(8,128)(2,1)S(1)}, bf16[1,64,512]{2,1,0:T(8,128)(2,1)S(1)}, u32[]{:S(2)}, u32[]{:S(2)}) collective-permute-start(bf16[1,64,512]{2,1,0:T(8,128)(2,1)S(1)} %bitcast.22), channel_id=1, source_target_pairs={{0,1},{1,2},{2,3},{3,0},{4,5},{5,6},{6,7},{7,4},{8,9},{9,10},{10,1... | collective-permute-start | bytes 196616 | tf_op jit(solution)/shard_map/ppermute | solution.py:486
  17.4 13.2 %collective-permute-start.3 = (bf16[4,64,512]{2,1,0:T(8,128)(2,1)S(1)}, bf16[4,64,512]{2,1,0:T(8,128)(2,1)S(1)}, u32[]{:S(2)}, u32[]{:S(2)}) collective-permute-start(bf16[4,64,512]{2,1,0:T(8,128)(2,1)S(1)} %pad_maximum_fusion.1), channel_id=1, source_target_pairs={{0,4},{1,5},{2,6},{3,7},{4,8},{5,9},{6,10},{7,11},{8,12},{9,13},{1... | collective-permute-start | bytes 786440 | tf_op jit(solution)/shard_map/ppermute | solution.py:486
  18.7 12.5 %collective-permute-start.4 = (bf16[4,64,512]{2,1,0:T(8,128)(2,1)S(1)}, bf16[4,64,512]{2,1,0:T(8,128)(2,1)S(1)}, u32[]{:S(2)}, u32[]{:S(2)}) collective-permute-start(bf16[4,64,512]{2,1,0:T(8,128)(2,1)S(1)} %pad_maximum_fusion.1), channel_id=1, source_target_pairs={{0,8},{1,9},{2,10},{3,11},{4,12},{5,13},{6,14},{7,15},{8,0},{9,1},... | collective-permute-start | bytes 786440 | tf_op jit(solution)/shard_map/ppermute | solution.py:486
  21.3 9.8 %collective-permute-start.5 = (bf16[4,64,512]{2,1,0:T(8,128)(2,1)S(1)}, bf16[4,64,512]{2,1,0:T(8,128)(2,1)S(1)}, u32[]{:S(2)}, u32[]{:S(2)}) collective-permute-start(bf16[4,64,512]{2,1,0:T(8,128)(2,1)S(1)} %pad_maximum_fusion.1), channel_id=1, source_target_pairs={{0,12},{1,13},{2,14},{3,15},{4,0},{5,1},{6,2},{7,3},{8,4},{9,5},{1... | collective-permute-start | bytes 786440 | tf_op jit(solution)/shard_map/ppermute | solution.py:486
  32.3 74.5 %all-to-all-start = ((bf16[16,288,512]{2,1,0:T(8,128)(2,1)}), bf16[16,288,512]{2,1,0:T(8,128)(2,1)}, u32[]{:S(2)}, u32[]{:S(2)}) async-start(bf16[16,288,512]{2,1,0:T(8,128)(2,1)} %pack.1), calls=%async_computation | async-start | bytes 9437184 | tf_op jit(solution)/shard_map/all_to_all | solution.py:466
  43.1 13.4 %collective-permute-start.7 = (bf16[2,64,640]{2,1,0:T(8,128)(2,1)S(1)}, bf16[2,64,640]{2,1,0:T(8,128)(2,1)S(1)}, u32[]{:S(2)}, u32[]{:S(2)}) collective-permute-start(bf16[2,64,640]{2,1,0:T(8,128)(2,1)S(1)} %get-tuple-element.64), channel_id=1, source_target_pairs={{0,32},{16,48},{32,64},{48,80},{64,96},{80,112},{96,128},{112,144}... | collective-permute-start | bytes 491528 | tf_op jit(solution)/shard_map/ppermute | solution.py:475
  44.8 21.1 %collective-permute-start.8 = (bf16[2,64,640]{2,1,0:T(8,128)(2,1)S(1)}, bf16[2,64,640]{2,1,0:T(8,128)(2,1)S(1)}, u32[]{:S(2)}, u32[]{:S(2)}) collective-permute-start(bf16[2,64,640]{2,1,0:T(8,128)(2,1)S(1)} %get-tuple-element.65), channel_id=1, source_target_pairs={{0,64},{16,80},{32,96},{48,112},{64,128},{80,144},{96,160},{112,17... | collective-permute-start | bytes 491528 | tf_op jit(solution)/shard_map/ppermute | solution.py:475
  47.8 30.4 %collective-permute-start.9 = (bf16[2,64,640]{2,1,0:T(8,128)(2,1)S(1)}, bf16[2,64,640]{2,1,0:T(8,128)(2,1)S(1)}, u32[]{:S(2)}, u32[]{:S(2)}) collective-permute-start(bf16[2,64,640]{2,1,0:T(8,128)(2,1)S(1)} %get-tuple-element.66), channel_id=1, source_target_pairs={{0,96},{16,112},{32,128},{48,144},{64,160},{80,176},{96,192},{112,... | collective-permute-start | bytes 491528 | tf_op jit(solution)/shard_map/ppermute | solution.py:475
  51.6 36.0 %collective-permute-start.10 = (bf16[2,64,640]{2,1,0:T(8,128)(2,1)S(1)}, bf16[2,64,640]{2,1,0:T(8,128)(2,1)S(1)}, u32[]{:S(2)}, u32[]{:S(2)}) collective-permute-start(bf16[2,64,640]{2,1,0:T(8,128)(2,1)S(1)} %get-tuple-element.67), channel_id=1, source_target_pairs={{0,128},{16,144},{32,160},{48,176},{64,192},{80,208},{96,224},{112... | collective-permute-start | bytes 491528 | tf_op jit(solution)/shard_map/ppermute | solution.py:475
  52.0 35.5 %collective-permute-start.11 = (bf16[2,64,640]{2,1,0:T(8,128)(2,1)S(1)}, bf16[2,64,640]{2,1,0:T(8,128)(2,1)S(1)}, u32[]{:S(2)}, u32[]{:S(2)}) collective-permute-start(bf16[2,64,640]{2,1,0:T(8,128)(2,1)S(1)} %get-tuple-element.68), channel_id=1, source_target_pairs={{0,160},{16,176},{32,192},{48,208},{64,224},{80,240},{96,0},{112,1... | collective-permute-start | bytes 491528 | tf_op jit(solution)/shard_map/ppermute | solution.py:475
  56.5 31.0 %collective-permute-start.12 = (bf16[2,64,640]{2,1,0:T(8,128)(2,1)S(1)}, bf16[2,64,640]{2,1,0:T(8,128)(2,1)S(1)}, u32[]{:S(2)}, u32[]{:S(2)}) collective-permute-start(bf16[2,64,640]{2,1,0:T(8,128)(2,1)S(1)} %get-tuple-element.69), channel_id=1, source_target_pairs={{0,192},{16,208},{32,224},{48,240},{64,0},{80,16},{96,32},{112,48}... | collective-permute-start | bytes 491528 | tf_op jit(solution)/shard_map/ppermute | solution.py:475
  65.9 30.5 %collective-permute-start.13 = (bf16[2,64,640]{2,1,0:T(8,128)(2,1)S(1)}, bf16[2,64,640]{2,1,0:T(8,128)(2,1)S(1)}, u32[]{:S(2)}, u32[]{:S(2)}) collective-permute-start(bf16[2,64,640]{2,1,0:T(8,128)(2,1)S(1)} %get-tuple-element.70), channel_id=1, source_target_pairs={{0,224},{16,240},{32,0},{48,16},{64,32},{80,48},{96,64},{112,80},{... | collective-permute-start | bytes 491528 | tf_op jit(solution)/shard_map/ppermute | solution.py:475
  157.5 60.6 %all-to-all-start.3 = ((bf16[16,256,512]{2,1,0:T(8,128)(2,1)}), bf16[16,256,512]{2,1,0:T(8,128)(2,1)}, u32[]{:S(2)}, u32[]{:S(2)}) async-start(bf16[16,256,512]{2,1,0:T(8,128)(2,1)} %term.1), calls=%async_computation.3 | async-start | bytes 8388608 | tf_op jit(solution)/shard_map/all_to_all | solution.py:466
  169.8 6.7 %collective-permute-start.14 = (bf16[8,64,640]{2,1,0:T(8,128)(2,1)S(1)}, bf16[8,64,640]{2,1,0:T(8,128)(2,1)S(1)}, u32[]{:S(2)}, u32[]{:S(2)}) collective-permute-start(bf16[8,64,640]{2,1,0:T(8,128)(2,1)S(1)} %get-tuple-element.85), channel_id=1, source_target_pairs={{0,16},{16,0},{32,48},{48,32},{64,80},{80,64},{96,112},{112,96},{1... | collective-permute-start | bytes 1966088 | tf_op jit(solution)/shard_map/ppermute | solution.py:470
  177.1 13.3 %collective-permute-start.15 = (bf16[2,64,640]{2,1,0:T(8,128)(2,1)S(1)}, bf16[2,64,640]{2,1,0:T(8,128)(2,1)S(1)}, u32[]{:S(2)}, u32[]{:S(2)}) collective-permute-start(bf16[2,64,640]{2,1,0:T(8,128)(2,1)S(1)} %get-tuple-element.87), channel_id=1, source_target_pairs={{0,32},{16,48},{32,64},{48,80},{64,96},{80,112},{96,128},{112,144}... | collective-permute-start | bytes 491528 | tf_op jit(solution)/shard_map/ppermute | solution.py:475
  179.1 13.9 %collective-permute-start.16 = (bf16[2,64,640]{2,1,0:T(8,128)(2,1)S(1)}, bf16[2,64,640]{2,1,0:T(8,128)(2,1)S(1)}, u32[]{:S(2)}, u32[]{:S(2)}) collective-permute-start(bf16[2,64,640]{2,1,0:T(8,128)(2,1)S(1)} %get-tuple-element.88), channel_id=1, source_target_pairs={{0,64},{16,80},{32,96},{48,112},{64,128},{80,144},{96,160},{112,17... | collective-permute-start | bytes 491528 | tf_op jit(solution)/shard_map/ppermute | solution.py:475
  182.1 28.4 %collective-permute-start.17 = (bf16[2,64,640]{2,1,0:T(8,128)(2,1)S(1)}, bf16[2,64,640]{2,1,0:T(8,128)(2,1)S(1)}, u32[]{:S(2)}, u32[]{:S(2)}) collective-permute-start(bf16[2,64,640]{2,1,0:T(8,128)(2,1)S(1)} %get-tuple-element.89), channel_id=1, source_target_pairs={{0,96},{16,112},{32,128},{48,144},{64,160},{80,176},{96,192},{112,... | collective-permute-start | bytes 491528 | tf_op jit(solution)/shard_map/ppermute | solution.py:475
  185.7 24.7 %collective-permute-start.18 = (bf16[2,64,640]{2,1,0:T(8,128)(2,1)S(1)}, bf16[2,64,640]{2,1,0:T(8,128)(2,1)S(1)}, u32[]{:S(2)}, u32[]{:S(2)}) collective-permute-start(bf16[2,64,640]{2,1,0:T(8,128)(2,1)S(1)} %get-tuple-element.90), channel_id=1, source_target_pairs={{0,128},{16,144},{32,160},{48,176},{64,192},{80,208},{96,224},{112... | collective-permute-start | bytes 491528 | tf_op jit(solution)/shard_map/ppermute | solution.py:475
  186.0 24.4 %collective-permute-start.19 = (bf16[2,64,640]{2,1,0:T(8,128)(2,1)S(1)}, bf16[2,64,640]{2,1,0:T(8,128)(2,1)S(1)}, u32[]{:S(2)}, u32[]{:S(2)}) collective-permute-start(bf16[2,64,640]{2,1,0:T(8,128)(2,1)S(1)} %get-tuple-element.91), channel_id=1, source_target_pairs={{0,160},{16,176},{32,192},{48,208},{64,224},{80,240},{96,0},{112,1... | collective-permute-start | bytes 491528 | tf_op jit(solution)/shard_map/ppermute | solution.py:475
  190.4 24.8 %collective-permute-start.20 = (bf16[2,64,640]{2,1,0:T(8,128)(2,1)S(1)}, bf16[2,64,640]{2,1,0:T(8,128)(2,1)S(1)}, u32[]{:S(2)}, u32[]{:S(2)}) collective-permute-start(bf16[2,64,640]{2,1,0:T(8,128)(2,1)S(1)} %get-tuple-element.92), channel_id=1, source_target_pairs={{0,192},{16,208},{32,224},{48,240},{64,0},{80,16},{96,32},{112,48}... | collective-permute-start | bytes 491528 | tf_op jit(solution)/shard_map/ppermute | solution.py:475
  193.0 23.5 %collective-permute-start.21 = (bf16[2,64,640]{2,1,0:T(8,128)(2,1)S(1)}, bf16[2,64,640]{2,1,0:T(8,128)(2,1)S(1)}, u32[]{:S(2)}, u32[]{:S(2)}) collective-permute-start(bf16[2,64,640]{2,1,0:T(8,128)(2,1)S(1)} %get-tuple-element.93), channel_id=1, source_target_pairs={{0,224},{16,240},{32,0},{48,16},{64,32},{80,48},{96,64},{112,80},{... | collective-permute-start | bytes 491528 | tf_op jit(solution)/shard_map/ppermute | solution.py:475
  (10 other events, 130.9 us)
Sparse Core Ops, SparseCore 0:
  32.5 126.2 all-gather.2

commit v10 on v9

--- a/solution.py
+++ b/solution.py
@@ -205,27 +205,42 @@
     return jnp.concatenate([part[rows:, :rows], part[rows:, rows:]], axis=0)
 
 
+def by_half(meta, first, rows, slots, body):
+    cut = start_of(meta, slots // 2)
+    low, high = first + rows <= cut, first >= cut
+    pl.when(low)(lambda: body(range(slots // 4)))
+    pl.when(high)(lambda: body(range(slots // 4, slots // 2)))
+    pl.when(jnp.logical_not(low | high))(lambda: body(range(slots // 2)))
+
+
 def project_kernel(slots, rank, meta, part, down_t, up_t, out):
     group, rows, _ = out.shape
     shape = (rows, 2 * rank)
-    low = lax.broadcasted_iota(jnp.int32, shape, 1) < rank
-    for g in range(group):
-        first = (pl.program_id(0) * group + g) * rows
-        block = part[g]
-        lr = jnp.dot(block[:rows], down_t[...], preferred_element_type=F32)
+
+    def block(g, first, pairs):
+        cols = slice(2 * rank * pairs[0], 2 * rank * (pairs[-1] + 1))
+        lr = jnp.dot(part[g, :rows, :], down_t[:, cols], preferred_element_type=F32)
         lg = lax.dot_general(
-            cot_of(block, rows), up_t[...], (((0,), (0,)), ((), ())), preferred_element_type=F32
+            cot_of(part[g], rows),
+            up_t[:, cols],
+            (((0,), (0,)), ((), ())),
+            preferred_element_type=F32,
         )
         lr_sum = jnp.zeros(shape, F32)
         lg_sum = jnp.zeros(shape, F32)
-        for p in range(slots // 2):
+        for k, p in enumerate(pairs):
             keep = inside_pair(meta, p, first, shape, slots, rank)
-            cols = slice(2 * rank * p, 2 * rank * (p + 1))
-            lr_sum += jnp.where(keep, lr[:, cols], 0.0)
-            lg_sum += jnp.where(keep, lg[:, cols], 0.0)
+            at = slice(2 * rank * k, 2 * rank * (k + 1))
+            lr_sum += jnp.where(keep, lr[:, at], 0.0)
+            lg_sum += jnp.where(keep, lg[:, at], 0.0)
         lr_sum += pltpu.roll(lr_sum, rank, 1)
         lg_sum += pltpu.roll(lg_sum, rank, 1)
+        low = lax.broadcasted_iota(jnp.int32, shape, 1) < rank
         out[g] = jnp.where(low, lr_sum, ADAPTER_SCALE * lg_sum).astype(BF)
+
+    for g in range(group):
+        first = (pl.program_id(0) * group + g) * rows
+        by_half(meta, first, rows, slots, functools.partial(block, g, first))
 
 
 def project(meta, parts, down_t, up_t, rows, slots, rank):
@@ -369,17 +384,22 @@
 def term_kernel(slots, rank, meta, low, down, out):
     group, _, rows = low.shape
     piece = out.shape[2]
-    table = jnp.concatenate([down[s, :, :piece] for s in range(slots)], axis=0)
-    for g in range(group):
-        first = (pl.program_id(0) * group + g) * rows
+
+    def block(g, first, pairs):
+        table = [down[2 * p + j, :, :piece] for p in pairs for j in range(2)]
         lg = low[g, rank:, :].astype(F32)
         lg = jnp.transpose(jnp.concatenate([lg, lg], axis=0))
         lg = [
             jnp.where(inside_pair(meta, p, first, lg.shape, slots, rank), lg, 0.0)
-            for p in range(slots // 2)
+            for p in pairs
         ]
         lg = jnp.concatenate(lg, axis=1).astype(BF)
+        table = jnp.concatenate(table, axis=0)
         out[g] = jnp.dot(lg, table, preferred_element_type=F32).astype(BF)
+
+    for g in range(group):
+        first = (pl.program_id(0) * group + g) * rows
+        by_half(meta, first, rows, slots, functools.partial(block, g, first))
 
 
 def term(meta, low, down, piece, slots, rank):
@@ -546,8 +566,8 @@
 
     parts = exchange(packed, "fsdp")
     got = spread(meta, keep, give, bins)
-    parts, got = lax.optimization_barrier((parts, got))
     down, down_t, up_t = choose(meta, got, slots, v)
+    parts, down, down_t, up_t = lax.optimization_barrier((parts, down, down_t, up_t))
 
     sums = exchange(project(meta, parts, down_t, up_t, rows, slots, rank), "fsdp")
     low_all = exchange(total(sums), "fsdp")

time: 233 us -> 233 us (level)
  transfers between devices with their start and end apart: 25 -> 25, of which waited for: 12 -> 12; matrix products, arithmetic and copies ran while one was open for 2% -> 2% of each run, Pallas kernels for 19% -> 20%
where the time goes in v10:
time: 233 us; the launch traced here: 231 us
  starting transfers between devices  64.4 us (28%)
  waiting for transfers between devices  57.6 us (25%)
  Pallas kernels  52.2 us (22%)
  blocking collectives  35.1 us (15%)
  between operations  14.3 us (6%)
  local copies, waits for them, and re-layouts  5.12 us (2%)
  other arithmetic  2.51 us (1%)
    ppermute x14, waiting for transfers between devices, shift(): lax.ppermute(x, 'dp', [(i, (i // 2 + k) % chips * 2 + i % 2) for i in ran...  43 us
    ppermute x14, starting transfers between devices, shift(): lax.ppermute(x, 'dp', [(i, (i // 2 + k) % chips * 2 + i % 2) for i in ran...  36.7 us
    all_to_all x2, blocking collectives, exchange(): return lax.all_to_all(x, axis, 0, 0, tiled=True)  35.1 us
    pallas_call x1, Pallas kernels, base(): call(base_kernel, 'base', flops=2 * rows * n * piece * width, moved=2 * n...  13.4 us
    all_to_all x2, starting transfers between devices, exchange(): return lax.all_to_all(x, axis, 0, 0, tiled=True)  11.2 us
    ppermute x6, starting transfers between devices, across(): lax.ppermute(x, 'fsdp', [(i, (i // SIDE + dy) % SIDE * SIDE + (i % SIDE +...  9.57 us
    all_to_all x2, waiting for transfers between devices, exchange(): return lax.all_to_all(x, axis, 0, 0, tiled=True)  8.45 us
    pallas_call x1, Pallas kernels, project(): call(functools.partial(project_kernel, slots, rank), 'project', flops=2 *...  7.67 us
  transfers between devices with their start and end apart: 25, of which 12 were waited for; matrix products, arithmetic and copies ran while one was open for 2% of the time, Pallas kernels for 20%

profile of v10, /device:TPU:1, one launch (start us, length us, event | category | flops | bytes accessed | tf_op | source)
XLA Modules:
  0.0 231.2 jit_solution(17556132336626465142)
XLA Ops:
  8.6 3.4 %collective-permute-start.2 = (bf16[1,64,512]{2,1,0:T(8,128)(2,1)S(1)}, bf16[1,64,512]{2,1,0:T(8,128)(2,1)S(1)}, u32[]{:S(2)}, u32[]{:S(2)}) collective-permute-start(bf16[1,64,512]{2,1,0:T(8,128)(2,1)S(1)} %bitcast.20), channel_id=1, source_target_pairs={{0,3},{1,0},{2,1},{3,2},{4,7},{5,4},{6,5},{7,6},{8,11},{9,8},{10,9... | collective-permute-start | bytes 196616 | tf_op jit(solution)/shard_map/ppermute | solution.py:506
  24.5 5.1 %pack.1 = bf16[16,288,512]{2,1,0:T(8,128)(2,1)} custom-call(bf16[256,8192]{1,0:T(8,128)(2,1)} %tok.1, bf16[1024,256]{1,0:T(8,128)(2,1)} %bitcast.25), custom_call_target="tpu_custom_call" | custom-call | bytes 8388608 | tf_op jit(solution)/shard_map/pack/pallas_call | solution.py:109
  32.3 6.6 %all-to-all-start = ((bf16[16,288,512]{2,1,0:T(8,128)(2,1)}), bf16[16,288,512]{2,1,0:T(8,128)(2,1)}, u32[]{:S(2)}, u32[]{:S(2)}) async-start(bf16[16,288,512]{2,1,0:T(8,128)(2,1)} %pack.1), calls=%async_computation | async-start | bytes 9437184 | tf_op jit(solution)/shard_map/all_to_all | solution.py:486
  47.8 3.8 %collective-permute-start.9 = (bf16[2,64,640]{2,1,0:T(8,128)(2,1)S(1)}, bf16[2,64,640]{2,1,0:T(8,128)(2,1)S(1)}, u32[]{:S(2)}, u32[]{:S(2)}) collective-permute-start(bf16[2,64,640]{2,1,0:T(8,128)(2,1)S(1)} %get-tuple-element.61), channel_id=1, source_target_pairs={{0,96},{16,112},{32,128},{48,144},{64,160},{80,176},{96,192},{112,... | collective-permute-start | bytes 491528 | tf_op jit(solution)/shard_map/ppermute | solution.py:495
  52.0 4.5 %collective-permute-start.11 = (bf16[2,64,640]{2,1,0:T(8,128)(2,1)S(1)}, bf16[2,64,640]{2,1,0:T(8,128)(2,1)S(1)}, u32[]{:S(2)}, u32[]{:S(2)}) collective-permute-start(bf16[2,64,640]{2,1,0:T(8,128)(2,1)S(1)} %get-tuple-element.63), channel_id=1, source_target_pairs={{0,160},{16,176},{32,192},{48,208},{64,224},{80,240},{96,0},{112,1... | collective-permute-start | bytes 491528 | tf_op jit(solution)/shard_map/ppermute | solution.py:495
  58.9 7.0 %collective-permute-done.8.refs_2_ = bf16[2,64,640]{2,1,0:T(8,128)(2,1)S(1)} collective-permute-done((bf16[2,64,640]{2,1,0:T(8,128)(2,1)S(1)}, bf16[2,64,640]{2,1,0:T(8,128)(2,1)S(1)}, u32[]{:S(2)}, u32[]{:S(2)}) %collective-permute-start.8) | collective-permute-done | bytes 163872 | tf_op jit(solution)/shard_map/ppermute | solution.py:495
  67.0 11.2 %collective-permute-done.9.refs_3_ = bf16[2,64,640]{2,1,0:T(8,128)(2,1)S(1)} collective-permute-done((bf16[2,64,640]{2,1,0:T(8,128)(2,1)S(1)}, bf16[2,64,640]{2,1,0:T(8,128)(2,1)S(1)}, u32[]{:S(2)}, u32[]{:S(2)}) %collective-permute-start.9) | collective-permute-done | bytes 163872 | tf_op jit(solution)/shard_map/ppermute | solution.py:495
  78.2 9.3 %collective-permute-done.10.refs_4_ = bf16[2,64,640]{2,1,0:T(8,128)(2,1)S(1)} collective-permute-done((bf16[2,64,640]{2,1,0:T(8,128)(2,1)S(1)}, bf16[2,64,640]{2,1,0:T(8,128)(2,1)S(1)}, u32[]{:S(2)}, u32[]{:S(2)}) %collective-permute-start.10) | collective-permute-done | bytes 163872 | tf_op jit(solution)/shard_map/ppermute | solution.py:495
  87.5 8.8 %collective-permute-done.13.refs_7_ = bf16[2,64,640]{2,1,0:T(8,128)(2,1)S(1)} collective-permute-done((bf16[2,64,640]{2,1,0:T(8,128)(2,1)S(1)}, bf16[2,64,640]{2,1,0:T(8,128)(2,1)S(1)}, u32[]{:S(2)}, u32[]{:S(2)}) %collective-permute-start.13) | collective-permute-done | bytes 163872 | tf_op jit(solution)/shard_map/ppermute | solution.py:495
  98.4 8.4 %all-to-all-done.part = bf16[16,288,512]{2,1,0:T(8,128)(2,1)} async-done(((bf16[16,288,512]{2,1,0:T(8,128)(2,1)}), bf16[16,288,512]{2,1,0:T(8,128)(2,1)}, u32[]{:S(2)}, u32[]{:S(2)}) %all-to-all-start) | async-done | bytes 4718624 | tf_op jit(solution)/shard_map/all_to_all | solution.py:486
  106.8 7.7 %project.1 = bf16[16,256,128]{2,1,0:T(8,128)(2,1)S(1)} custom-call(s32[59]{0:T(128)S(1)} %concatenate.9.meta, bf16[16,288,512]{2,1,0:T(8,128)(2,1)} %all-to-all-done.part, bf16[512,512]{1,0:T(8,128)(2,1)S(1)} %get-tuple-element.70.down_t, bf16[64,512]{1,0:T(8,128)(2,1)S(1)} %get-tuple-element.71.up_t), custom_call_target="tpu_custom_call" | custom-call | flops 2147483648 | bytes 4718592 | tf_op jit(solution)/shard_map/project/pallas_call | solution.py:248
  114.5 18.6 %all_to_all.20.parts = bf16[16,256,128]{2,1,0:T(8,128)(2,1)S(1)} all-to-all(bf16[16,256,128]{2,1,0:T(8,128)(2,1)S(1)} %project.1), channel_id=1, replica_groups=mesh['dp'=16,'fsdp'=16] {'fsdp'}, dimensions={0} | all-to-all | bytes 2097152 | tf_op jit(solution)/shard_map/all_to_all | solution.py:486
  133.4 16.5 %all_to_all.21.low = bf16[16,128,256]{2,1,0:T(8,128)(2,1)} all-to-all(bf16[16,128,256]{2,1,0:T(8,128)(2,1)S(1)} %total.1), channel_id=1, replica_groups=mesh['dp'=16,'fsdp'=16] {'fsdp'}, dimensions={0} | all-to-all | bytes 2097152 | tf_op jit(solution)/shard_map/all_to_all | solution.py:486
  149.9 7.5 %term.1 = bf16[16,256,512]{2,1,0:T(8,128)(2,1)} custom-call(s32[59]{0:T(128)} %copy-done.5, bf16[16,128,256]{2,1,0:T(8,128)(2,1)} %all_to_all.21.low, bf16[8,64,640]{2,1,0:T(8,128)(2,1)} %copy-done.8), custom_call_target="tpu_custom_call" | custom-call | flops 2147483648 | bytes 4194304 | tf_op jit(solution)/shard_map/term/pallas_call | solution.py:407
  157.3 4.7 %all-to-all-start.3 = ((bf16[16,256,512]{2,1,0:T(8,128)(2,1)}), bf16[16,256,512]{2,1,0:T(8,128)(2,1)}, u32[]{:S(2)}, u32[]{:S(2)}) async-start(bf16[16,256,512]{2,1,0:T(8,128)(2,1)} %term.1), calls=%async_computation.3 | async-start | bytes 8388608 | tf_op jit(solution)/shard_map/all_to_all | solution.py:486
  162.0 7.3 %gradient.1 = (bf16[8,64,640]{2,1,0:T(8,128)(2,1)S(1)}, bf16[8,64,640]{2,1,0:T(8,128)(2,1)S(1)}) custom-call(s32[59]{0:T(128)S(1)} %copy-done.6, bf16[16,288,512]{2,1,0:T(8,128)(2,1)} %all-to-all-done.part, bf16[16,128,256]{2,1,0:T(8,128)(2,1)S(1)} %copy-done.2), custom_call_target="tpu_custom_call" | custom-call | flops 2147483648 | bytes 4718592 | tf_op jit(solution)/shard_map/gradient/pallas_call | solution.py:337
  169.4 5.1 %collective-permute-start.14 = (bf16[8,64,640]{2,1,0:T(8,128)(2,1)S(1)}, bf16[8,64,640]{2,1,0:T(8,128)(2,1)S(1)}, u32[]{:S(2)}, u32[]{:S(2)}) collective-permute-start(bf16[8,64,640]{2,1,0:T(8,128)(2,1)S(1)} %get-tuple-element.75), channel_id=1, source_target_pairs={{0,16},{16,0},{32,48},{48,32},{64,80},{80,64},{96,112},{112,96},{1... | collective-permute-start | bytes 1966088 | tf_op jit(solution)/shard_map/ppermute | solution.py:490
  178.8 3.2 %collective-permute-start.16 = (bf16[2,64,640]{2,1,0:T(8,128)(2,1)S(1)}, bf16[2,64,640]{2,1,0:T(8,128)(2,1)S(1)}, u32[]{:S(2)}, u32[]{:S(2)}) collective-permute-start(bf16[2,64,640]{2,1,0:T(8,128)(2,1)S(1)} %get-tuple-element.78), channel_id=1, source_target_pairs={{0,64},{16,80},{32,96},{48,112},{64,128},{80,144},{96,160},{112,17... | collective-permute-start | bytes 491528 | tf_op jit(solution)/shard_map/ppermute | solution.py:495
  182.0 3.6 %collective-permute-start.17 = (bf16[2,64,640]{2,1,0:T(8,128)(2,1)S(1)}, bf16[2,64,640]{2,1,0:T(8,128)(2,1)S(1)}, u32[]{:S(2)}, u32[]{:S(2)}) collective-permute-start(bf16[2,64,640]{2,1,0:T(8,128)(2,1)S(1)} %get-tuple-element.79), channel_id=1, source_target_pairs={{0,96},{16,112},{32,128},{48,144},{64,160},{80,176},{96,192},{112,... | collective-permute-start | bytes 491528 | tf_op jit(solution)/shard_map/ppermute | solution.py:495
  186.0 4.5 %collective-permute-start.19 = (bf16[2,64,640]{2,1,0:T(8,128)(2,1)S(1)}, bf16[2,64,640]{2,1,0:T(8,128)(2,1)S(1)}, u32[]{:S(2)}, u32[]{:S(2)}) collective-permute-start(bf16[2,64,640]{2,1,0:T(8,128)(2,1)S(1)} %get-tuple-element.81), channel_id=1, source_target_pairs={{0,160},{16,176},{32,192},{48,208},{64,224},{80,240},{96,0},{112,1... | collective-permute-start | bytes 491528 | tf_op jit(solution)/shard_map/ppermute | solution.py:495
  192.9 3.7 %collective-permute-start.21 = (bf16[2,64,640]{2,1,0:T(8,128)(2,1)S(1)}, bf16[2,64,640]{2,1,0:T(8,128)(2,1)S(1)}, u32[]{:S(2)}, u32[]{:S(2)}) collective-permute-start(bf16[2,64,640]{2,1,0:T(8,128)(2,1)S(1)} %get-tuple-element.83), channel_id=1, source_target_pairs={{0,224},{16,240},{32,0},{48,16},{64,32},{80,48},{96,64},{112,80},{... | collective-permute-start | bytes 491528 | tf_op jit(solution)/shard_map/ppermute | solution.py:495
  196.6 13.4 %base.1.done = bf16[256,8192]{1,0:T(8,128)(2,1)} custom-call(s32[59]{0:T(128)} %copy-done.5, bf16[256,1024]{1,0:T(8,128)(2,1)} %cot.1, bf16[16,16,64,512]{3,2,1,0:T(8,128)(2,1)} %bitcast.24), custom_call_target="tpu_custom_call" | custom-call | flops 4294967296 | bytes 20971520 | tf_op jit(solution)/shard_map/base/pallas_call | solution.py:443
  210.0 5.5 %collective-permute-done.20.refs_6_ = bf16[2,64,640]{2,1,0:T(8,128)(2,1)S(1)} collective-permute-done((bf16[2,64,640]{2,1,0:T(8,128)(2,1)S(1)}, bf16[2,64,640]{2,1,0:T(8,128)(2,1)S(1)}, u32[]{:S(2)}, u32[]{:S(2)}) %collective-permute-start.20) | collective-permute-done | bytes 163872 | tf_op jit(solution)/shard_map/ppermute | solution.py:495
  218.3 6.0 %join.1 = bf16[256,8192]{1,0:T(8,128)(2,1)} custom-call(bf16[256,8192]{1,0:T(8,128)(2,1)} %base.1.done, bf16[16,256,512]{2,1,0:T(8,128)(2,1)} %all-to-all-done.3.terms), custom_call_target="tpu_custom_call" | custom-call | bytes 12582912 | tf_op jit(solution)/shard_map/join/pallas_call | solution.py:470
  (72 shorter events, 41.8 us)
Async XLA Ops:
  7.2 189.4 %all-gather.3.cloned.1.call-start = ((), (), s32[]{:S(2)}) async-start(), calls=%async_computation.4 | async-start | bytes 17825792 | tf_op jit(solution)/shard_map/all_gather | solution.py:565
  8.6 6.6 %collective-permute-start.2 = (bf16[1,64,512]{2,1,0:T(8,128)(2,1)S(1)}, bf16[1,64,512]{2,1,0:T(8,128)(2,1)S(1)}, u32[]{:S(2)}, u32[]{:S(2)}) collective-permute-start(bf16[1,64,512]{2,1,0:T(8,128)(2,1)S(1)} %bitcast.20), channel_id=1, source_target_pairs={{0,3},{1,0},{2,1},{3,2},{4,7},{5,4},{6,5},{7,6},{8,11},{9,8},{10,9... | collective-permute-start | bytes 196616 | tf_op jit(solution)/shard_map/ppermute | solution.py:506
  12.0 4.7 %collective-permute-start.1 = (bf16[1,64,512]{2,1,0:T(8,128)(2,1)S(1)}, bf16[1,64,512]{2,1,0:T(8,128)(2,1)S(1)}, u32[]{:S(2)}, u32[]{:S(2)}) collective-permute-start(bf16[1,64,512]{2,1,0:T(8,128)(2,1)S(1)} %bitcast.21), channel_id=1, source_target_pairs={{0,2},{1,3},{2,0},{3,1},{4,6},{5,7},{6,4},{7,5},{8,10},{9,11},{10,... | collective-permute-start | bytes 196616 | tf_op jit(solution)/shard_map/ppermute | solution.py:506
  12.5 4.8 %collective-permute-start = (bf16[1,64,512]{2,1,0:T(8,128)(2,1)S(1)}, bf16[1,64,512]{2,1,0:T(8,128)(2,1)S(1)}, u32[]{:S(2)}, u32[]{:S(2)}) collective-permute-start(bf16[1,64,512]{2,1,0:T(8,128)(2,1)S(1)} %bitcast.22), channel_id=1, source_target_pairs={{0,1},{1,2},{2,3},{3,0},{4,5},{5,6},{6,7},{7,4},{8,9},{9,10},{10,1... | collective-permute-start | bytes 196616 | tf_op jit(solution)/shard_map/ppermute | solution.py:506
  17.4 13.2 %collective-permute-start.3 = (bf16[4,64,512]{2,1,0:T(8,128)(2,1)S(1)}, bf16[4,64,512]{2,1,0:T(8,128)(2,1)S(1)}, u32[]{:S(2)}, u32[]{:S(2)}) collective-permute-start(bf16[4,64,512]{2,1,0:T(8,128)(2,1)S(1)} %pad_maximum_fusion.1), channel_id=1, source_target_pairs={{0,4},{1,5},{2,6},{3,7},{4,8},{5,9},{6,10},{7,11},{8,12},{9,13},{1... | collective-permute-start | bytes 786440 | tf_op jit(solution)/shard_map/ppermute | solution.py:506
  18.7 12.5 %collective-permute-start.4 = (bf16[4,64,512]{2,1,0:T(8,128)(2,1)S(1)}, bf16[4,64,512]{2,1,0:T(8,128)(2,1)S(1)}, u32[]{:S(2)}, u32[]{:S(2)}) collective-permute-start(bf16[4,64,512]{2,1,0:T(8,128)(2,1)S(1)} %pad_maximum_fusion.1), channel_id=1, source_target_pairs={{0,8},{1,9},{2,10},{3,11},{4,12},{5,13},{6,14},{7,15},{8,0},{9,1},... | collective-permute-start | bytes 786440 | tf_op jit(solution)/shard_map/ppermute | solution.py:506
  21.3 9.8 %collective-permute-start.5 = (bf16[4,64,512]{2,1,0:T(8,128)(2,1)S(1)}, bf16[4,64,512]{2,1,0:T(8,128)(2,1)S(1)}, u32[]{:S(2)}, u32[]{:S(2)}) collective-permute-start(bf16[4,64,512]{2,1,0:T(8,128)(2,1)S(1)} %pad_maximum_fusion.1), channel_id=1, source_target_pairs={{0,12},{1,13},{2,14},{3,15},{4,0},{5,1},{6,2},{7,3},{8,4},{9,5},{1... | collective-permute-start | bytes 786440 | tf_op jit(solution)/shard_map/ppermute | solution.py:506
  32.3 74.5 %all-to-all-start = ((bf16[16,288,512]{2,1,0:T(8,128)(2,1)}), bf16[16,288,512]{2,1,0:T(8,128)(2,1)}, u32[]{:S(2)}, u32[]{:S(2)}) async-start(bf16[16,288,512]{2,1,0:T(8,128)(2,1)} %pack.1), calls=%async_computation | async-start | bytes 9437184 | tf_op jit(solution)/shard_map/all_to_all | solution.py:486
  43.1 13.4 %collective-permute-start.7 = (bf16[2,64,640]{2,1,0:T(8,128)(2,1)S(1)}, bf16[2,64,640]{2,1,0:T(8,128)(2,1)S(1)}, u32[]{:S(2)}, u32[]{:S(2)}) collective-permute-start(bf16[2,64,640]{2,1,0:T(8,128)(2,1)S(1)} %get-tuple-element.59), channel_id=1, source_target_pairs={{0,32},{16,48},{32,64},{48,80},{64,96},{80,112},{96,128},{112,144}... | collective-permute-start | bytes 491528 | tf_op jit(solution)/shard_map/ppermute | solution.py:495
  44.8 21.1 %collective-permute-start.8 = (bf16[2,64,640]{2,1,0:T(8,128)(2,1)S(1)}, bf16[2,64,640]{2,1,0:T(8,128)(2,1)S(1)}, u32[]{:S(2)}, u32[]{:S(2)}) collective-permute-start(bf16[2,64,640]{2,1,0:T(8,128)(2,1)S(1)} %get-tuple-element.60), channel_id=1, source_target_pairs={{0,64},{16,80},{32,96},{48,112},{64,128},{80,144},{96,160},{112,17... | collective-permute-start | bytes 491528 | tf_op jit(solution)/shard_map/ppermute | solution.py:495
  47.8 30.4 %collective-permute-start.9 = (bf16[2,64,640]{2,1,0:T(8,128)(2,1)S(1)}, bf16[2,64,640]{2,1,0:T(8,128)(2,1)S(1)}, u32[]{:S(2)}, u32[]{:S(2)}) collective-permute-start(bf16[2,64,640]{2,1,0:T(8,128)(2,1)S(1)} %get-tuple-element.61), channel_id=1, source_target_pairs={{0,96},{16,112},{32,128},{48,144},{64,160},{80,176},{96,192},{112,... | collective-permute-start | bytes 491528 | tf_op jit(solution)/shard_map/ppermute | solution.py:495
  51.6 36.0 %collective-permute-start.10 = (bf16[2,64,640]{2,1,0:T(8,128)(2,1)S(1)}, bf16[2,64,640]{2,1,0:T(8,128)(2,1)S(1)}, u32[]{:S(2)}, u32[]{:S(2)}) collective-permute-start(bf16[2,64,640]{2,1,0:T(8,128)(2,1)S(1)} %get-tuple-element.62), channel_id=1, source_target_pairs={{0,128},{16,144},{32,160},{48,176},{64,192},{80,208},{96,224},{112... | collective-permute-start | bytes 491528 | tf_op jit(solution)/shard_map/ppermute | solution.py:495
  52.0 35.5 %collective-permute-start.11 = (bf16[2,64,640]{2,1,0:T(8,128)(2,1)S(1)}, bf16[2,64,640]{2,1,0:T(8,128)(2,1)S(1)}, u32[]{:S(2)}, u32[]{:S(2)}) collective-permute-start(bf16[2,64,640]{2,1,0:T(8,128)(2,1)S(1)} %get-tuple-element.63), channel_id=1, source_target_pairs={{0,160},{16,176},{32,192},{48,208},{64,224},{80,240},{96,0},{112,1... | collective-permute-start | bytes 491528 | tf_op jit(solution)/shard_map/ppermute | solution.py:495
  56.5 31.0 %collective-permute-start.12 = (bf16[2,64,640]{2,1,0:T(8,128)(2,1)S(1)}, bf16[2,64,640]{2,1,0:T(8,128)(2,1)S(1)}, u32[]{:S(2)}, u32[]{:S(2)}) collective-permute-start(bf16[2,64,640]{2,1,0:T(8,128)(2,1)S(1)} %get-tuple-element.64), channel_id=1, source_target_pairs={{0,192},{16,208},{32,224},{48,240},{64,0},{80,16},{96,32},{112,48}... | collective-permute-start | bytes 491528 | tf_op jit(solution)/shard_map/ppermute | solution.py:495
  65.9 30.5 %collective-permute-start.13 = (bf16[2,64,640]{2,1,0:T(8,128)(2,1)S(1)}, bf16[2,64,640]{2,1,0:T(8,128)(2,1)S(1)}, u32[]{:S(2)}, u32[]{:S(2)}) collective-permute-start(bf16[2,64,640]{2,1,0:T(8,128)(2,1)S(1)} %get-tuple-element.65), channel_id=1, source_target_pairs={{0,224},{16,240},{32,0},{48,16},{64,32},{80,48},{96,64},{112,80},{... | collective-permute-start | bytes 491528 | tf_op jit(solution)/shard_map/ppermute | solution.py:495
  157.3 61.0 %all-to-all-start.3 = ((bf16[16,256,512]{2,1,0:T(8,128)(2,1)}), bf16[16,256,512]{2,1,0:T(8,128)(2,1)}, u32[]{:S(2)}, u32[]{:S(2)}) async-start(bf16[16,256,512]{2,1,0:T(8,128)(2,1)} %term.1), calls=%async_computation.3 | async-start | bytes 8388608 | tf_op jit(solution)/shard_map/all_to_all | solution.py:486
  169.4 6.8 %collective-permute-start.14 = (bf16[8,64,640]{2,1,0:T(8,128)(2,1)S(1)}, bf16[8,64,640]{2,1,0:T(8,128)(2,1)S(1)}, u32[]{:S(2)}, u32[]{:S(2)}) collective-permute-start(bf16[8,64,640]{2,1,0:T(8,128)(2,1)S(1)} %get-tuple-element.75), channel_id=1, source_target_pairs={{0,16},{16,0},{32,48},{48,32},{64,80},{80,64},{96,112},{112,96},{1... | collective-permute-start | bytes 1966088 | tf_op jit(solution)/shard_map/ppermute | solution.py:490
  176.8 13.7 %collective-permute-start.15 = (bf16[2,64,640]{2,1,0:T(8,128)(2,1)S(1)}, bf16[2,64,640]{2,1,0:T(8,128)(2,1)S(1)}, u32[]{:S(2)}, u32[]{:S(2)}) collective-permute-start(bf16[2,64,640]{2,1,0:T(8,128)(2,1)S(1)} %get-tuple-element.77), channel_id=1, source_target_pairs={{0,32},{16,48},{32,64},{48,80},{64,96},{80,112},{96,128},{112,144}... | collective-permute-start | bytes 491528 | tf_op jit(solution)/shard_map/ppermute | solution.py:495
  178.8 14.1 %collective-permute-start.16 = (bf16[2,64,640]{2,1,0:T(8,128)(2,1)S(1)}, bf16[2,64,640]{2,1,0:T(8,128)(2,1)S(1)}, u32[]{:S(2)}, u32[]{:S(2)}) collective-permute-start(bf16[2,64,640]{2,1,0:T(8,128)(2,1)S(1)} %get-tuple-element.78), channel_id=1, source_target_pairs={{0,64},{16,80},{32,96},{48,112},{64,128},{80,144},{96,160},{112,17... | collective-permute-start | bytes 491528 | tf_op jit(solution)/shard_map/ppermute | solution.py:495
  182.0 28.0 %collective-permute-start.17 = (bf16[2,64,640]{2,1,0:T(8,128)(2,1)S(1)}, bf16[2,64,640]{2,1,0:T(8,128)(2,1)S(1)}, u32[]{:S(2)}, u32[]{:S(2)}) collective-permute-start(bf16[2,64,640]{2,1,0:T(8,128)(2,1)S(1)} %get-tuple-element.79), channel_id=1, source_target_pairs={{0,96},{16,112},{32,128},{48,144},{64,160},{80,176},{96,192},{112,... | collective-permute-start | bytes 491528 | tf_op jit(solution)/shard_map/ppermute | solution.py:495
  185.6 24.4 %collective-permute-start.18 = (bf16[2,64,640]{2,1,0:T(8,128)(2,1)S(1)}, bf16[2,64,640]{2,1,0:T(8,128)(2,1)S(1)}, u32[]{:S(2)}, u32[]{:S(2)}) collective-permute-start(bf16[2,64,640]{2,1,0:T(8,128)(2,1)S(1)} %get-tuple-element.80), channel_id=1, source_target_pairs={{0,128},{16,144},{32,160},{48,176},{64,192},{80,208},{96,224},{112... | collective-permute-start | bytes 491528 | tf_op jit(solution)/shard_map/ppermute | solution.py:495
  186.0 24.0 %collective-permute-start.19 = (bf16[2,64,640]{2,1,0:T(8,128)(2,1)S(1)}, bf16[2,64,640]{2,1,0:T(8,128)(2,1)S(1)}, u32[]{:S(2)}, u32[]{:S(2)}) collective-permute-start(bf16[2,64,640]{2,1,0:T(8,128)(2,1)S(1)} %get-tuple-element.81), channel_id=1, source_target_pairs={{0,160},{16,176},{32,192},{48,208},{64,224},{80,240},{96,0},{112,1... | collective-permute-start | bytes 491528 | tf_op jit(solution)/shard_map/ppermute | solution.py:495
  190.5 25.0 %collective-permute-start.20 = (bf16[2,64,640]{2,1,0:T(8,128)(2,1)S(1)}, bf16[2,64,640]{2,1,0:T(8,128)(2,1)S(1)}, u32[]{:S(2)}, u32[]{:S(2)}) collective-permute-start(bf16[2,64,640]{2,1,0:T(8,128)(2,1)S(1)} %get-tuple-element.82), channel_id=1, source_target_pairs={{0,192},{16,208},{32,224},{48,240},{64,0},{80,16},{96,32},{112,48}... | collective-permute-start | bytes 491528 | tf_op jit(solution)/shard_map/ppermute | solution.py:495
  192.9 23.7 %collective-permute-start.21 = (bf16[2,64,640]{2,1,0:T(8,128)(2,1)S(1)}, bf16[2,64,640]{2,1,0:T(8,128)(2,1)S(1)}, u32[]{:S(2)}, u32[]{:S(2)}) collective-permute-start(bf16[2,64,640]{2,1,0:T(8,128)(2,1)S(1)} %get-tuple-element.83), channel_id=1, source_target_pairs={{0,224},{16,240},{32,0},{48,16},{64,32},{80,48},{96,64},{112,80},{... | collective-permute-start | bytes 491528 | tf_op jit(solution)/shard_map/ppermute | solution.py:495
  (10 other events, 129.4 us)
Sparse Core Ops, SparseCore 0:
  32.5 126.2 all-gather.2

commit v11 on v9

--- a/solution.py
+++ b/solution.py
@@ -92,19 +92,20 @@
     )(at, w)
 
 
-def pack_kernel(tok, cot_t, out):
+def pack_kernel(tok, cot, out):
     rows = tok.shape[0]
-    n, _, piece = out.shape
-    v = cot_t.shape[0] // n
-    for f in range(n):
+    group, _, piece = out.shape
+    v = cot.shape[1] // group
+    cot_t = jnp.transpose(cot[...].astype(F32)).astype(BF)
+    for f in range(group):
         out[f, :rows, :] = tok[:, f * piece:(f + 1) * piece]
         out[f, rows:, :rows] = cot_t[f * v:f * v + v // 2, :]
         out[f, rows:, rows:] = cot_t[f * v + v // 2:(f + 1) * v, :]
 
 
-def pack(tokens, cot_t, n):
+def pack(tokens, cot, n):
     rows, width = tokens.shape
-    piece, v = width // n, cot_t.shape[0] // n
+    piece, v = width // n, cot.shape[1] // n
     tall = rows + v * rows // piece
     return call(
         pack_kernel,
@@ -114,11 +115,11 @@
         grid=(n // GROUP,),
         in_specs=[
             pl.BlockSpec((rows, GROUP * piece), lambda f: (0, f)),
-            pl.BlockSpec((GROUP * v, rows), lambda f: (f, 0)),
+            pl.BlockSpec((rows, GROUP * v), lambda f: (0, f)),
         ],
         out_specs=pl.BlockSpec((GROUP, tall, piece), lambda f: (f, 0, 0)),
         out_shape=jax.ShapeDtypeStruct((n, tall, piece), BF),
-    )(tokens, cot_t)
+    )(tokens, cot)
 
 
 def offer_kernel(slots, meta, down_t, up, keep, give):
@@ -536,18 +537,25 @@
     mine = turn(me, value_weight, bins)[None]
     near = [across(mine, 0, k, n) for k in range(1, SIDE)]
     mine = jnp.concatenate([mine] + near)
-    near = [across(mine, k, 0, n) for k in range(1, SIDE)]
-    packed = pack(tokens, jnp.swapaxes(cotangent, 0, 1), n)
+    below, above = across(mine, 1, 0, n), across(mine, SIDE - 1, 0, n)
+    half = SIDE // 2
+    near = [
+        below,
+        across(below[:half], 1, 0, n),
+        across(above[half:], SIDE - 1, 0, n),
+        above,
+    ]
+    packed = pack(tokens, cotangent, n)
+    packed, near, mine = lax.optimization_barrier((packed, near, mine))
+    weight = lax.all_gather(jnp.concatenate([mine] + near), "dp", axis=0)
+
     keep, give = offer(
         meta, jnp.swapaxes(adapter_down_weight, 1, 2), adapter_up_weight, chips, slots
     )
-    packed, keep, give, near, mine = lax.optimization_barrier((packed, keep, give, near, mine))
-    weight = lax.all_gather(jnp.concatenate([mine] + near), "dp", axis=0)
-
     parts = exchange(packed, "fsdp")
     got = spread(meta, keep, give, bins)
-    parts, got = lax.optimization_barrier((parts, got))
     down, down_t, up_t = choose(meta, got, slots, v)
+    parts, down, down_t, up_t = lax.optimization_barrier((parts, down, down_t, up_t))
 
     sums = exchange(project(meta, parts, down_t, up_t, rows, slots, rank), "fsdp")
     low_all = exchange(total(sums), "fsdp")

time: 233 us -> 225 us (0.966)
  waiting for transfers between devices: 59 us -> 54.8 us
    all_to_all x2, waiting for transfers between devices: 10.5 us -> 1.41 us  [exchange(): return lax.all_to_all(x, axis, 0, 0, tiled=True)]
    ppermute x6 -> x7, waiting for transfers between devices: 2.72 us -> 6.44 us  [across(): lax.ppermute(x, 'fsdp', [(i, (i // SIDE + dy) % SIDE * SIDE + (i % SIDE +...]
    ppermute x14, starting transfers between devices: 36.9 us -> 33.2 us  [shift(): lax.ppermute(x, 'dp', [(i, (i // 2 + k) % chips * 2 + i % 2) for i in ran...]
    ppermute x6 -> x7, starting transfers between devices: 9.57 us -> 11.7 us  [across(): lax.ppermute(x, 'fsdp', [(i, (i // SIDE + dy) % SIDE * SIDE + (i % SIDE +...]
    unnamed x20 -> x29, local copies, waits for them, and re-layouts: 4.9 us -> 3.2 us
  transfers between devices with their start and end apart: 25 -> 26, of which waited for: 12 -> 12; matrix products, arithmetic and copies ran while one was open for 2% -> 0% of each run, Pallas kernels for 19% -> 20%
where the time goes in v11:
time: 225 us; the launch traced here: 223 us
  starting transfers between devices  63.2 us (28%)
  waiting for transfers between devices  54.8 us (24%)
  Pallas kernels  50.3 us (22%)
  blocking collectives  35.8 us (16%)
  between operations  14.4 us (6%)
  local copies, waits for them, and re-layouts  3.5 us (2%)
    ppermute x14, waiting for transfers between devices, shift(): lax.ppermute(x, 'dp', [(i, (i // 2 + k) % chips * 2 + i % 2) for i in ran...  43.4 us
    all_to_all x2, blocking collectives, exchange(): return lax.all_to_all(x, axis, 0, 0, tiled=True)  35.8 us
    ppermute x14, starting transfers between devices, shift(): lax.ppermute(x, 'dp', [(i, (i // 2 + k) % chips * 2 + i % 2) for i in ran...  33.2 us
    pallas_call x1, Pallas kernels, base(): call(base_kernel, 'base', flops=2 * rows * n * piece * width, moved=2 * n...  13.4 us
    ppermute x7, starting transfers between devices, across(): lax.ppermute(x, 'fsdp', [(i, (i // SIDE + dy) % SIDE * SIDE + (i % SIDE +...  11.7 us
    all_to_all x2, starting transfers between devices, exchange(): return lax.all_to_all(x, axis, 0, 0, tiled=True)  9.39 us
    ppermute x2, starting transfers between devices, swap(): return lax.ppermute(x, 'dp', [(i, i ^ 1) for i in range(bins)])  8.93 us
    pallas_call x1, Pallas kernels, gradient(): call(functools.partial(gradient_kernel, slots, rank, v), 'gradient', flop...  7.54 us
  transfers between devices with their start and end apart: 26, of which 12 were waited for; matrix products, arithmetic and copies ran while one was open for 0% of the time, Pallas kernels for 20%

profile of v11, /device:TPU:1, one launch (start us, length us, event | category | flops | bytes accessed | tf_op | source)
XLA Modules:
  0.0 222.7 jit_solution(18149057101643976031)
XLA Ops:
  19.8 4.2 %collective-permute-done.3 = bf16[4,64,512]{2,1,0:T(8,128)(2,1)S(1)} collective-permute-done((bf16[4,64,512]{2,1,0:T(8,128)(2,1)S(1)}, bf16[4,64,512]{2,1,0:T(8,128)(2,1)S(1)}, u32[]{:S(2)}, u32[]{:S(2)}) %collective-permute-start.3) | collective-permute-done | bytes 262176 | tf_op jit(solution)/shard_map/ppermute | solution.py:487
  26.8 5.1 %pack.1 = bf16[16,288,512]{2,1,0:T(8,128)(2,1)} custom-call(bf16[256,8192]{1,0:T(8,128)(2,1)} %tok.1, bf16[256,1024]{1,0:T(8,128)(2,1)} %cot.3), custom_call_target="tpu_custom_call" | custom-call | bytes 8388608 | tf_op jit(solution)/shard_map/pack/pallas_call | solution.py:110
  33.1 4.7 %all-to-all-start = ((bf16[16,288,512]{2,1,0:T(8,128)(2,1)}), bf16[16,288,512]{2,1,0:T(8,128)(2,1)}, u32[]{:S(2)}, u32[]{:S(2)}) async-start(bf16[16,288,512]{2,1,0:T(8,128)(2,1)} %pack.1), calls=%async_computation | async-start | bytes 9437184 | tf_op jit(solution)/shard_map/all_to_all | solution.py:467
  39.6 3.6 %collective-permute-start.7 = (bf16[8,64,640]{2,1,0:T(8,128)(2,1)S(1)}, bf16[8,64,640]{2,1,0:T(8,128)(2,1)S(1)}, u32[]{:S(2)}, u32[]{:S(2)}) collective-permute-start(bf16[8,64,640]{2,1,0:T(8,128)(2,1)S(1)} %get-tuple-element.54), channel_id=1, source_target_pairs={{0,16},{16,0},{32,48},{48,32},{64,80},{80,64},{96,112},{112,96},{1... | collective-permute-start | bytes 1966088 | tf_op jit(solution)/shard_map/ppermute | solution.py:471
  45.6 4.4 %collective-permute-start.10 = (bf16[2,64,640]{2,1,0:T(8,128)(2,1)S(1)}, bf16[2,64,640]{2,1,0:T(8,128)(2,1)S(1)}, u32[]{:S(2)}, u32[]{:S(2)}) collective-permute-start(bf16[2,64,640]{2,1,0:T(8,128)(2,1)S(1)} %get-tuple-element.58), channel_id=1, source_target_pairs={{0,96},{16,112},{32,128},{48,144},{64,160},{80,176},{96,192},{112,... | collective-permute-start | bytes 491528 | tf_op jit(solution)/shard_map/ppermute | solution.py:476
  50.0 4.2 %collective-permute-start.11 = (bf16[2,64,640]{2,1,0:T(8,128)(2,1)S(1)}, bf16[2,64,640]{2,1,0:T(8,128)(2,1)S(1)}, u32[]{:S(2)}, u32[]{:S(2)}) collective-permute-start(bf16[2,64,640]{2,1,0:T(8,128)(2,1)S(1)} %get-tuple-element.59), channel_id=1, source_target_pairs={{0,128},{16,144},{32,160},{48,176},{64,192},{80,208},{96,224},{112... | collective-permute-start | bytes 491528 | tf_op jit(solution)/shard_map/ppermute | solution.py:476
  57.5 7.6 %collective-permute-done.10.refs_3_ = bf16[2,64,640]{2,1,0:T(8,128)(2,1)S(1)} collective-permute-done((bf16[2,64,640]{2,1,0:T(8,128)(2,1)S(1)}, bf16[2,64,640]{2,1,0:T(8,128)(2,1)S(1)}, u32[]{:S(2)}, u32[]{:S(2)}) %collective-permute-start.10) | collective-permute-done | bytes 163872 | tf_op jit(solution)/shard_map/ppermute | solution.py:476
  67.1 11.2 %collective-permute-done.11.refs_4_ = bf16[2,64,640]{2,1,0:T(8,128)(2,1)S(1)} collective-permute-done((bf16[2,64,640]{2,1,0:T(8,128)(2,1)S(1)}, bf16[2,64,640]{2,1,0:T(8,128)(2,1)S(1)}, u32[]{:S(2)}, u32[]{:S(2)}) %collective-permute-start.11) | collective-permute-done | bytes 163872 | tf_op jit(solution)/shard_map/ppermute | solution.py:476
  78.3 9.0 %collective-permute-done.13.refs_6_ = bf16[2,64,640]{2,1,0:T(8,128)(2,1)S(1)} collective-permute-done((bf16[2,64,640]{2,1,0:T(8,128)(2,1)S(1)}, bf16[2,64,640]{2,1,0:T(8,128)(2,1)S(1)}, u32[]{:S(2)}, u32[]{:S(2)}) %collective-permute-start.13) | collective-permute-done | bytes 163872 | tf_op jit(solution)/shard_map/ppermute | solution.py:476
  87.4 9.2 %collective-permute-done.14.refs_7_ = bf16[2,64,640]{2,1,0:T(8,128)(2,1)S(1)} collective-permute-done((bf16[2,64,640]{2,1,0:T(8,128)(2,1)S(1)}, bf16[2,64,640]{2,1,0:T(8,128)(2,1)S(1)}, u32[]{:S(2)}, u32[]{:S(2)}) %collective-permute-start.14) | collective-permute-done | bytes 163872 | tf_op jit(solution)/shard_map/ppermute | solution.py:476
  99.9 6.7 %project.1 = bf16[16,256,128]{2,1,0:T(8,128)(2,1)S(1)} custom-call(s32[59]{0:T(128)S(1)} %concatenate.9.meta, bf16[16,288,512]{2,1,0:T(8,128)(2,1)} %all-to-all-done.part, bf16[512,512]{1,0:T(8,128)(2,1)S(1)} %get-tuple-element.67.down_t, bf16[64,512]{1,0:T(8,128)(2,1)S(1)} %get-tuple-element.68.up_t), custom_call_target="tpu_custom_call" | custom-call | flops 2147483648 | bytes 4718592 | tf_op jit(solution)/shard_map/project/pallas_call | solution.py:234
  106.6 19.5 %all_to_all.20.parts = bf16[16,256,128]{2,1,0:T(8,128)(2,1)S(1)} all-to-all(bf16[16,256,128]{2,1,0:T(8,128)(2,1)S(1)} %project.1), channel_id=1, replica_groups=mesh['dp'=16,'fsdp'=16] {'fsdp'}, dimensions={0} | all-to-all | bytes 2097152 | tf_op jit(solution)/shard_map/all_to_all | solution.py:467
  126.3 16.3 %all_to_all.21.low = bf16[16,128,256]{2,1,0:T(8,128)(2,1)} all-to-all(bf16[16,128,256]{2,1,0:T(8,128)(2,1)S(1)} %total.1), channel_id=1, replica_groups=mesh['dp'=16,'fsdp'=16] {'fsdp'}, dimensions={0} | all-to-all | bytes 2097152 | tf_op jit(solution)/shard_map/all_to_all | solution.py:467
  142.7 6.5 %term.1 = bf16[16,256,512]{2,1,0:T(8,128)(2,1)} custom-call(s32[59]{0:T(128)} %copy-done.5, bf16[16,128,256]{2,1,0:T(8,128)(2,1)} %all_to_all.21.low, bf16[8,64,640]{2,1,0:T(8,128)(2,1)} %copy-done.8), custom_call_target="tpu_custom_call" | custom-call | flops 2147483648 | bytes 4194304 | tf_op jit(solution)/shard_map/term/pallas_call | solution.py:388
  149.2 4.7 %all-to-all-start.3 = ((bf16[16,256,512]{2,1,0:T(8,128)(2,1)}), bf16[16,256,512]{2,1,0:T(8,128)(2,1)}, u32[]{:S(2)}, u32[]{:S(2)}) async-start(bf16[16,256,512]{2,1,0:T(8,128)(2,1)} %term.1), calls=%async_computation.3 | async-start | bytes 8388608 | tf_op jit(solution)/shard_map/all_to_all | solution.py:467
  153.9 7.5 %gradient.1 = (bf16[8,64,640]{2,1,0:T(8,128)(2,1)S(1)}, bf16[8,64,640]{2,1,0:T(8,128)(2,1)S(1)}) custom-call(s32[59]{0:T(128)S(1)} %copy-done.6, bf16[16,288,512]{2,1,0:T(8,128)(2,1)} %all-to-all-done.part, bf16[16,128,256]{2,1,0:T(8,128)(2,1)S(1)} %copy-done.2), custom_call_target="tpu_custom_call" | custom-call | flops 2147483648 | bytes 4718592 | tf_op jit(solution)/shard_map/gradient/pallas_call | solution.py:323
  161.4 5.3 %collective-permute-start.15 = (bf16[8,64,640]{2,1,0:T(8,128)(2,1)S(1)}, bf16[8,64,640]{2,1,0:T(8,128)(2,1)S(1)}, u32[]{:S(2)}, u32[]{:S(2)}) collective-permute-start(bf16[8,64,640]{2,1,0:T(8,128)(2,1)S(1)} %get-tuple-element.72), channel_id=1, source_target_pairs={{0,16},{16,0},{32,48},{48,32},{64,80},{80,64},{96,112},{112,96},{1... | collective-permute-start | bytes 1966088 | tf_op jit(solution)/shard_map/ppermute | solution.py:471
  170.4 3.1 %collective-permute-start.17 = (bf16[2,64,640]{2,1,0:T(8,128)(2,1)S(1)}, bf16[2,64,640]{2,1,0:T(8,128)(2,1)S(1)}, u32[]{:S(2)}, u32[]{:S(2)}) collective-permute-start(bf16[2,64,640]{2,1,0:T(8,128)(2,1)S(1)} %get-tuple-element.75), channel_id=1, source_target_pairs={{0,64},{16,80},{32,96},{48,112},{64,128},{80,144},{96,160},{112,17... | collective-permute-start | bytes 491528 | tf_op jit(solution)/shard_map/ppermute | solution.py:476
  173.5 3.8 %collective-permute-start.18 = (bf16[2,64,640]{2,1,0:T(8,128)(2,1)S(1)}, bf16[2,64,640]{2,1,0:T(8,128)(2,1)S(1)}, u32[]{:S(2)}, u32[]{:S(2)}) collective-permute-start(bf16[2,64,640]{2,1,0:T(8,128)(2,1)S(1)} %get-tuple-element.76), channel_id=1, source_target_pairs={{0,96},{16,112},{32,128},{48,144},{64,160},{80,176},{96,192},{112,... | collective-permute-start | bytes 491528 | tf_op jit(solution)/shard_map/ppermute | solution.py:476
  177.6 4.5 %collective-permute-start.20 = (bf16[2,64,640]{2,1,0:T(8,128)(2,1)S(1)}, bf16[2,64,640]{2,1,0:T(8,128)(2,1)S(1)}, u32[]{:S(2)}, u32[]{:S(2)}) collective-permute-start(bf16[2,64,640]{2,1,0:T(8,128)(2,1)S(1)} %get-tuple-element.78), channel_id=1, source_target_pairs={{0,160},{16,176},{32,192},{48,208},{64,224},{80,240},{96,0},{112,1... | collective-permute-start | bytes 491528 | tf_op jit(solution)/shard_map/ppermute | solution.py:476
  184.5 3.9 %collective-permute-start.22 = (bf16[2,64,640]{2,1,0:T(8,128)(2,1)S(1)}, bf16[2,64,640]{2,1,0:T(8,128)(2,1)S(1)}, u32[]{:S(2)}, u32[]{:S(2)}) collective-permute-start(bf16[2,64,640]{2,1,0:T(8,128)(2,1)S(1)} %get-tuple-element.80), channel_id=1, source_target_pairs={{0,224},{16,240},{32,0},{48,16},{64,32},{80,48},{96,64},{112,80},{... | collective-permute-start | bytes 491528 | tf_op jit(solution)/shard_map/ppermute | solution.py:476
  188.4 13.4 %base.1.done = bf16[256,8192]{1,0:T(8,128)(2,1)} custom-call(s32[59]{0:T(128)} %copy-done.5, bf16[256,1024]{1,0:T(8,128)(2,1)} %cot.3, bf16[16,16,64,512]{3,2,1,0:T(8,128)(2,1)} %bitcast.23), custom_call_target="tpu_custom_call" | custom-call | flops 4294967296 | bytes 20971520 | tf_op jit(solution)/shard_map/base/pallas_call | solution.py:424
  201.8 5.3 %collective-permute-done.21.refs_6_ = bf16[2,64,640]{2,1,0:T(8,128)(2,1)S(1)} collective-permute-done((bf16[2,64,640]{2,1,0:T(8,128)(2,1)S(1)}, bf16[2,64,640]{2,1,0:T(8,128)(2,1)S(1)}, u32[]{:S(2)}, u32[]{:S(2)}) %collective-permute-start.21) | collective-permute-done | bytes 163872 | tf_op jit(solution)/shard_map/ppermute | solution.py:476
  209.9 6.0 %join.1 = bf16[256,8192]{1,0:T(8,128)(2,1)} custom-call(bf16[256,8192]{1,0:T(8,128)(2,1)} %base.1.done, bf16[16,256,512]{2,1,0:T(8,128)(2,1)} %all-to-all-done.3.terms), custom_call_target="tpu_custom_call" | custom-call | bytes 12582912 | tf_op jit(solution)/shard_map/join/pallas_call | solution.py:451
  (85 shorter events, 38.6 us)
Async XLA Ops:
  7.2 181.2 %all-gather.3.cloned.1.call-start = ((), (), s32[]{:S(2)}) async-start(), calls=%async_computation.4 | async-start | bytes 17825792 | tf_op jit(solution)/shard_map/all_gather | solution.py:550
  8.6 5.7 %collective-permute-start = (bf16[1,64,512]{2,1,0:T(8,128)(2,1)S(1)}, bf16[1,64,512]{2,1,0:T(8,128)(2,1)S(1)}, u32[]{:S(2)}, u32[]{:S(2)}) collective-permute-start(bf16[1,64,512]{2,1,0:T(8,128)(2,1)S(1)} %bitcast.19), channel_id=1, source_target_pairs={{0,1},{1,2},{2,3},{3,0},{4,5},{5,6},{6,7},{7,4},{8,9},{9,10},{10,1... | collective-permute-start | bytes 196616 | tf_op jit(solution)/shard_map/ppermute | solution.py:487
  16.6 7.3 %collective-permute-start.3 = (bf16[4,64,512]{2,1,0:T(8,128)(2,1)S(1)}, bf16[4,64,512]{2,1,0:T(8,128)(2,1)S(1)}, u32[]{:S(2)}, u32[]{:S(2)}) collective-permute-start(bf16[4,64,512]{2,1,0:T(8,128)(2,1)S(1)} %pad_maximum_fusion), channel_id=1, source_target_pairs={{0,4},{1,5},{2,6},{3,7},{4,8},{5,9},{6,10},{7,11},{8,12},{9,13},{1... | collective-permute-start | bytes 786440 | tf_op jit(solution)/shard_map/ppermute | solution.py:487
  18.2 6.0 %collective-permute-start.5 = (bf16[4,64,512]{2,1,0:T(8,128)(2,1)S(1)}, bf16[4,64,512]{2,1,0:T(8,128)(2,1)S(1)}, u32[]{:S(2)}, u32[]{:S(2)}) collective-permute-start(bf16[4,64,512]{2,1,0:T(8,128)(2,1)S(1)} %pad_maximum_fusion), channel_id=1, source_target_pairs={{0,12},{1,13},{2,14},{3,15},{4,0},{5,1},{6,2},{7,3},{8,4},{9,5},{1... | collective-permute-start | bytes 786440 | tf_op jit(solution)/shard_map/ppermute | solution.py:487
  24.0 7.9 %collective-permute-start.4 = (bf16[2,64,512]{2,1,0:T(8,128)(2,1)S(1)}, bf16[2,64,512]{2,1,0:T(8,128)(2,1)S(1)}, u32[]{:S(2)}, u32[]{:S(2)}) collective-permute-start(bf16[2,64,512]{2,1,0:T(8,128)(2,1)S(1)} %slice.8), channel_id=1, source_target_pairs={{0,4},{1,5},{2,6},{3,7},{4,8},{5,9},{6,10},{7,11},{8,12},{9,13},{1... | collective-permute-start | bytes 393224 | tf_op jit(solution)/shard_map/ppermute | solution.py:487
  24.3 7.6 %collective-permute-start.6 = (bf16[2,64,512]{2,1,0:T(8,128)(2,1)S(1)}, bf16[2,64,512]{2,1,0:T(8,128)(2,1)S(1)}, u32[]{:S(2)}, u32[]{:S(2)}) collective-permute-start(bf16[2,64,512]{2,1,0:T(8,128)(2,1)S(1)} %slice.9), channel_id=1, source_target_pairs={{0,12},{1,13},{2,14},{3,15},{4,0},{5,1},{6,2},{7,3},{8,4},{9,5},{1... | collective-permute-start | bytes 393224 | tf_op jit(solution)/shard_map/ppermute | solution.py:487
  33.1 66.8 %all-to-all-start = ((bf16[16,288,512]{2,1,0:T(8,128)(2,1)}), bf16[16,288,512]{2,1,0:T(8,128)(2,1)}, u32[]{:S(2)}, u32[]{:S(2)}) async-start(bf16[16,288,512]{2,1,0:T(8,128)(2,1)} %pack.1), calls=%async_computation | async-start | bytes 9437184 | tf_op jit(solution)/shard_map/all_to_all | solution.py:467
  39.6 5.4 %collective-permute-start.7 = (bf16[8,64,640]{2,1,0:T(8,128)(2,1)S(1)}, bf16[8,64,640]{2,1,0:T(8,128)(2,1)S(1)}, u32[]{:S(2)}, u32[]{:S(2)}) collective-permute-start(bf16[8,64,640]{2,1,0:T(8,128)(2,1)S(1)} %get-tuple-element.54), channel_id=1, source_target_pairs={{0,16},{16,0},{32,48},{48,32},{64,80},{80,64},{96,112},{112,96},{1... | collective-permute-start | bytes 1966088 | tf_op jit(solution)/shard_map/ppermute | solution.py:471
  45.6 19.4 %collective-permute-start.10 = (bf16[2,64,640]{2,1,0:T(8,128)(2,1)S(1)}, bf16[2,64,640]{2,1,0:T(8,128)(2,1)S(1)}, u32[]{:S(2)}, u32[]{:S(2)}) collective-permute-start(bf16[2,64,640]{2,1,0:T(8,128)(2,1)S(1)} %get-tuple-element.58), channel_id=1, source_target_pairs={{0,96},{16,112},{32,128},{48,144},{64,160},{80,176},{96,192},{112,... | collective-permute-start | bytes 491528 | tf_op jit(solution)/shard_map/ppermute | solution.py:476
  50.0 28.3 %collective-permute-start.11 = (bf16[2,64,640]{2,1,0:T(8,128)(2,1)S(1)}, bf16[2,64,640]{2,1,0:T(8,128)(2,1)S(1)}, u32[]{:S(2)}, u32[]{:S(2)}) collective-permute-start(bf16[2,64,640]{2,1,0:T(8,128)(2,1)S(1)} %get-tuple-element.59), channel_id=1, source_target_pairs={{0,128},{16,144},{32,160},{48,176},{64,192},{80,208},{96,224},{112... | collective-permute-start | bytes 491528 | tf_op jit(solution)/shard_map/ppermute | solution.py:476
  54.2 24.1 %collective-permute-start.12 = (bf16[2,64,640]{2,1,0:T(8,128)(2,1)S(1)}, bf16[2,64,640]{2,1,0:T(8,128)(2,1)S(1)}, u32[]{:S(2)}, u32[]{:S(2)}) collective-permute-start(bf16[2,64,640]{2,1,0:T(8,128)(2,1)S(1)} %get-tuple-element.60), channel_id=1, source_target_pairs={{0,160},{16,176},{32,192},{48,208},{64,224},{80,240},{96,0},{112,1... | collective-permute-start | bytes 491528 | tf_op jit(solution)/shard_map/ppermute | solution.py:476
  57.1 30.3 %collective-permute-start.13 = (bf16[2,64,640]{2,1,0:T(8,128)(2,1)S(1)}, bf16[2,64,640]{2,1,0:T(8,128)(2,1)S(1)}, u32[]{:S(2)}, u32[]{:S(2)}) collective-permute-start(bf16[2,64,640]{2,1,0:T(8,128)(2,1)S(1)} %get-tuple-element.61), channel_id=1, source_target_pairs={{0,192},{16,208},{32,224},{48,240},{64,0},{80,16},{96,32},{112,48}... | collective-permute-start | bytes 491528 | tf_op jit(solution)/shard_map/ppermute | solution.py:476
  57.1 39.5 %collective-permute-start.14 = (bf16[2,64,640]{2,1,0:T(8,128)(2,1)S(1)}, bf16[2,64,640]{2,1,0:T(8,128)(2,1)S(1)}, u32[]{:S(2)}, u32[]{:S(2)}) collective-permute-start(bf16[2,64,640]{2,1,0:T(8,128)(2,1)S(1)} %get-tuple-element.62), channel_id=1, source_target_pairs={{0,224},{16,240},{32,0},{48,16},{64,32},{80,48},{96,64},{112,80},{... | collective-permute-start | bytes 491528 | tf_op jit(solution)/shard_map/ppermute | solution.py:476
  65.0 31.6 %collective-permute-start.8 = (bf16[2,64,640]{2,1,0:T(8,128)(2,1)S(1)}, bf16[2,64,640]{2,1,0:T(8,128)(2,1)S(1)}, u32[]{:S(2)}, u32[]{:S(2)}) collective-permute-start(bf16[2,64,640]{2,1,0:T(8,128)(2,1)S(1)} %get-tuple-element.56), channel_id=1, source_target_pairs={{0,32},{16,48},{32,64},{48,80},{64,96},{80,112},{96,128},{112,144}... | collective-permute-start | bytes 491528 | tf_op jit(solution)/shard_map/ppermute | solution.py:476
  78.3 18.3 %collective-permute-start.9 = (bf16[2,64,640]{2,1,0:T(8,128)(2,1)S(1)}, bf16[2,64,640]{2,1,0:T(8,128)(2,1)S(1)}, u32[]{:S(2)}, u32[]{:S(2)}) collective-permute-start(bf16[2,64,640]{2,1,0:T(8,128)(2,1)S(1)} %get-tuple-element.57), channel_id=1, source_target_pairs={{0,64},{16,80},{32,96},{48,112},{64,128},{80,144},{96,160},{112,17... | collective-permute-start | bytes 491528 | tf_op jit(solution)/shard_map/ppermute | solution.py:476
  149.2 60.7 %all-to-all-start.3 = ((bf16[16,256,512]{2,1,0:T(8,128)(2,1)}), bf16[16,256,512]{2,1,0:T(8,128)(2,1)}, u32[]{:S(2)}, u32[]{:S(2)}) async-start(bf16[16,256,512]{2,1,0:T(8,128)(2,1)} %term.1), calls=%async_computation.3 | async-start | bytes 8388608 | tf_op jit(solution)/shard_map/all_to_all | solution.py:467
  161.4 7.0 %collective-permute-start.15 = (bf16[8,64,640]{2,1,0:T(8,128)(2,1)S(1)}, bf16[8,64,640]{2,1,0:T(8,128)(2,1)S(1)}, u32[]{:S(2)}, u32[]{:S(2)}) collective-permute-start(bf16[8,64,640]{2,1,0:T(8,128)(2,1)S(1)} %get-tuple-element.72), channel_id=1, source_target_pairs={{0,16},{16,0},{32,48},{48,32},{64,80},{80,64},{96,112},{112,96},{1... | collective-permute-start | bytes 1966088 | tf_op jit(solution)/shard_map/ppermute | solution.py:471
  169.1 12.9 %collective-permute-start.16 = (bf16[2,64,640]{2,1,0:T(8,128)(2,1)S(1)}, bf16[2,64,640]{2,1,0:T(8,128)(2,1)S(1)}, u32[]{:S(2)}, u32[]{:S(2)}) collective-permute-start(bf16[2,64,640]{2,1,0:T(8,128)(2,1)S(1)} %get-tuple-element.74), channel_id=1, source_target_pairs={{0,32},{16,48},{32,64},{48,80},{64,96},{80,112},{96,128},{112,144}... | collective-permute-start | bytes 491528 | tf_op jit(solution)/shard_map/ppermute | solution.py:476
  170.4 14.0 %collective-permute-start.17 = (bf16[2,64,640]{2,1,0:T(8,128)(2,1)S(1)}, bf16[2,64,640]{2,1,0:T(8,128)(2,1)S(1)}, u32[]{:S(2)}, u32[]{:S(2)}) collective-permute-start(bf16[2,64,640]{2,1,0:T(8,128)(2,1)S(1)} %get-tuple-element.75), channel_id=1, source_target_pairs={{0,64},{16,80},{32,96},{48,112},{64,128},{80,144},{96,160},{112,17... | collective-permute-start | bytes 491528 | tf_op jit(solution)/shard_map/ppermute | solution.py:476
  173.5 28.3 %collective-permute-start.18 = (bf16[2,64,640]{2,1,0:T(8,128)(2,1)S(1)}, bf16[2,64,640]{2,1,0:T(8,128)(2,1)S(1)}, u32[]{:S(2)}, u32[]{:S(2)}) collective-permute-start(bf16[2,64,640]{2,1,0:T(8,128)(2,1)S(1)} %get-tuple-element.76), channel_id=1, source_target_pairs={{0,96},{16,112},{32,128},{48,144},{64,160},{80,176},{96,192},{112,... | collective-permute-start | bytes 491528 | tf_op jit(solution)/shard_map/ppermute | solution.py:476
  177.3 24.5 %collective-permute-start.19 = (bf16[2,64,640]{2,1,0:T(8,128)(2,1)S(1)}, bf16[2,64,640]{2,1,0:T(8,128)(2,1)S(1)}, u32[]{:S(2)}, u32[]{:S(2)}) collective-permute-start(bf16[2,64,640]{2,1,0:T(8,128)(2,1)S(1)} %get-tuple-element.77), channel_id=1, source_target_pairs={{0,128},{16,144},{32,160},{48,176},{64,192},{80,208},{96,224},{112... | collective-permute-start | bytes 491528 | tf_op jit(solution)/shard_map/ppermute | solution.py:476
  177.6 24.2 %collective-permute-start.20 = (bf16[2,64,640]{2,1,0:T(8,128)(2,1)S(1)}, bf16[2,64,640]{2,1,0:T(8,128)(2,1)S(1)}, u32[]{:S(2)}, u32[]{:S(2)}) collective-permute-start(bf16[2,64,640]{2,1,0:T(8,128)(2,1)S(1)} %get-tuple-element.78), channel_id=1, source_target_pairs={{0,160},{16,176},{32,192},{48,208},{64,224},{80,240},{96,0},{112,1... | collective-permute-start | bytes 491528 | tf_op jit(solution)/shard_map/ppermute | solution.py:476
  182.1 25.0 %collective-permute-start.21 = (bf16[2,64,640]{2,1,0:T(8,128)(2,1)S(1)}, bf16[2,64,640]{2,1,0:T(8,128)(2,1)S(1)}, u32[]{:S(2)}, u32[]{:S(2)}) collective-permute-start(bf16[2,64,640]{2,1,0:T(8,128)(2,1)S(1)} %get-tuple-element.79), channel_id=1, source_target_pairs={{0,192},{16,208},{32,224},{48,240},{64,0},{80,16},{96,32},{112,48}... | collective-permute-start | bytes 491528 | tf_op jit(solution)/shard_map/ppermute | solution.py:476
  184.5 23.7 %collective-permute-start.22 = (bf16[2,64,640]{2,1,0:T(8,128)(2,1)S(1)}, bf16[2,64,640]{2,1,0:T(8,128)(2,1)S(1)}, u32[]{:S(2)}, u32[]{:S(2)}) collective-permute-start(bf16[2,64,640]{2,1,0:T(8,128)(2,1)S(1)} %get-tuple-element.80), channel_id=1, source_target_pairs={{0,224},{16,240},{32,0},{48,16},{64,32},{80,48},{96,64},{112,80},{... | collective-permute-start | bytes 491528 | tf_op jit(solution)/shard_map/ppermute | solution.py:476
  (14 other events, 161.0 us)
Sparse Core Ops, SparseCore 0:
  33.2 126.9 all-gather.2
